TPU v7x, 32 devices: a whole 2x2x4 slice. The times are simulated.
32 devices in a mesh: dp: 4 (over y, x), tensor: 8 (over z, core).
Axes of the slice: x: 2, y: 2, z: 4, core: 2. Of those that a mesh axis runs over, the one named last changes fastest.
Arguments:
- hidden: bfloat16 [512, 8192], P('dp', 'tensor')
- norm_gain: float32 [8192], P('tensor'), may hold values from 0.5 to 1.5
- head: bfloat16 [8192, 36864], P(None, ('dp', 'tensor'))
- targets: int32 [512], P('dp'), may hold values from 0 to 36863
- old_logprob: float32 [512], P('dp'), may hold values from -20 to -1
- lengths: int32 [4], P('dp'), may hold values from 1 to 128, as said below
Outputs:
- new_logprob: float32 [512], P('dp')
- log_ratio: float32 [512], P('dp')
Inputs may be any that keep to these rules, and one draw needn't show every extreme that they name: `lengths`: every length is at least 1 and at most 128; some sequence has 128 live tokens and some has 1.
All inputs are finite; a program needn't handle non-finite values.
Results may differ from a plain program's by a relative error of at most 0.00094.
Values may be sent and summed in bfloat16 or wider, within the bound.
No kernel may reach another device: no remote copies, remote signals or barrier semaphores. Data moves between devices by JAX's collectives and lax.ppermute only.
A program may use at most 128 MiB of HBM per device.

v0:
```python
import jax
import jax.numpy as jnp
from jax import lax
from jax.sharding import PartitionSpec as P

D = 8192
CORES = 2
X_ONLY, Y_ONLY = (0, 1), (1, 0)


class Grid:
    def __init__(self, n_dp, n_t):
        self.n_t = n_t
        self.cols = 2
        self.rows = n_dp // self.cols
        self.depth = n_t // CORES
        self.square = self.rows == self.cols
        self.first = (X_ONLY, Y_ONLY) if self.square else (X_ONLY, X_ONLY)
        self.second = (Y_ONLY, X_ONLY) if self.square else (Y_ONLY, Y_ONLY)
        self.spots = [(j, i) for j in range(self.rows) for i in range(self.cols)]

    def permute(self, a, place):
        perm = []
        for y in range(self.rows):
            for x in range(self.cols):
                for z in range(self.depth):
                    for c in range(CORES):
                        src = (y * self.cols + x) * self.n_t + z * CORES + c
                        v, u, w, d = place(y, x, z, c)
                        dst = (v % self.rows * self.cols + u % self.cols) * self.n_t
                        perm.append((src, dst + w % self.depth * CORES + d % CORES))
        return lax.ppermute(a, ("dp", "tensor"), perm)

    def plane(self, a, ways, step):
        def place(y, x, z, c):
            return y + ways[c][0] * step, x + ways[c][1] * step, z, c

        return self.permute(a, place)

    def along(self, a, step):
        return self.permute(a, lambda y, x, z, c: (y, x, z + step, c))

    def sibling(self, a):
        return self.permute(a, lambda y, x, z, c: (y, x, z, c + 1))

    def reach(self, a):
        got = {(0, 0): a}
        for i in range(1, self.cols):
            got[0, i] = self.plane(a, self.first, i)
        for j in range(1, self.rows):
            got[j, 0] = self.plane(a, self.second, j)
        return got

    def fill(self, got, *late):
        late = (*late, *got.values())
        for j in range(1, self.rows):
            for i in range(1, self.cols):
                got[j, i] = self.plane(after(got[0, i], *late), self.second, j)
        return [got[s] for s in self.spots]

    def owners(self, y, x, c):
        ways = [(self.first[k], self.second[k]) for k in range(CORES)]
        out = []
        for j, i in self.spots:
            at = [
                (y - f[0] * i - s[0] * j) % self.rows * self.cols + (x - f[1] * i - s[1] * j) % self.cols
                for f, s in ways
            ]
            out.append(jnp.where(c == 0, at[0], at[1]))
        return out


def after(a, *others):
    return lax.optimization_barrier((a, *others))[0] if others else a


def exchange(a, axis):
    copies = jnp.broadcast_to(a[None], (lax.axis_size(axis), *a.shape))
    return lax.all_to_all(copies, axis, 0, 0, tiled=True)


def merge(parts):
    top = jnp.max(parts[:, 0], axis=0)
    total = jnp.sum(parts[:, 1] * jnp.exp(parts[:, 0] - top[None]), axis=0)
    return top, total, jnp.sum(parts[:, 2], axis=0)


def body(hidden, norm_gain, head, targets, old_logprob, lengths):
    n_dp, n_t = lax.axis_size("dp"), lax.axis_size("tensor")
    grid = Grid(n_dp, n_t)
    depth = grid.depth
    tok, feat = hidden.shape
    plane, tensor = lax.axis_index("dp"), lax.axis_index("tensor")
    z_me, c_me = tensor // CORES, tensor % CORES
    owners = grid.owners(plane // grid.cols, plane % grid.cols, c_me)
    groups = [[0]] + [[d, depth - d] for d in range(1, (depth + 1) // 2)] + [[depth // 2]]

    layers = {0: hidden}
    before = []
    for group in groups[1:]:
        for dz in group:
            layers[dz] = grid.along(after(hidden, *before), dz)
        before = [layers[dz] for dz in group]
    reached = [grid.reach(hidden)]
    for at, group in enumerate(groups[1:]):
        sources = after(tuple(layers[dz] for dz in group), *reached[at].values())
        joined = jnp.concatenate(sources) if len(sources) > 1 else sources[0]
        reached.append(grid.reach(joined))

    values = hidden.astype(jnp.float32)
    packed = jnp.concatenate([norm_gain, jnp.sum(values * values, axis=1)])
    fine = exchange(packed, "tensor")
    gains = fine[:, :feat]
    scaled = lax.rsqrt(jnp.sum(fine[:, feat:], axis=0) / D + 1e-06)
    marks = exchange(jnp.stack([scaled, targets.astype(jnp.float32)]), "dp")
    scale_all = marks[:, 0].reshape(n_dp * tok)
    target_all = marks[:, 1].reshape(n_dp * tok).astype(jnp.int32)

    vocab_cols = head.shape[1]
    logits = None
    for at, group in enumerate(groups):
        final = at == len(groups) - 1
        held = [] if final or not at else [layers[dz] for dz in groups[at + 1]]
        if at == 1:
            held.append(logits)
        spread = grid.fill(dict(reached[at]), *held)
        size = len(group)
        block = jnp.zeros((size * n_dp * tok, feat), hidden.dtype)
        for owner, part in zip(owners, spread, strict=True):
            for j in range(size):
                piece = part[j * tok : (j + 1) * tok]
                block = lax.dynamic_update_slice_in_dim(block, piece, (j * n_dp + owner) * tok, 0)
        other = grid.sibling(block)
        for j, dz in enumerate(group):
            for dc, part in ((0, block), (1, other)):
                source = (z_me - dz) % depth * CORES + (c_me - dc) % CORES
                gain = lax.dynamic_index_in_dim(gains, source, 0, False)
                raw = part[j * n_dp * tok : (j + 1) * n_dp * tok].astype(jnp.float32)
                normed = (raw * scale_all[:, None] * gain[None, :]).astype(jnp.bfloat16)
                weights = lax.dynamic_slice_in_dim(head, source * feat, feat, 0)
                product = jnp.dot(normed, weights, preferred_element_type=jnp.float32)
                logits = product if logits is None else logits + product

    vocab_start = lax.axis_index(("dp", "tensor")) * vocab_cols
    block_top = jnp.max(logits, axis=1)
    block_total = jnp.sum(jnp.exp(logits - block_top[:, None]), axis=1)
    entry = vocab_start + jnp.arange(vocab_cols, dtype=jnp.int32)
    hits = entry[None, :] == target_all[:, None]
    block_pick = jnp.sum(jnp.where(hits, logits, jnp.float32(0.0)), axis=1)

    stats = jnp.stack([s.reshape(n_dp, tok) for s in (block_top, block_total, block_pick)], axis=1)
    stats = jnp.stack(merge(lax.all_to_all(stats, "dp", 0, 0, tiled=True)))
    top, total, picked = merge(exchange(stats, "tensor"))

    seq_count = lengths.shape[0]
    position = jnp.arange(tok // seq_count, dtype=jnp.int32)
    live = (position[None, :] < lengths[:, None]).reshape(-1).astype(jnp.float32)
    logprob = picked - top - jnp.log(total)
    return (live * logprob, live * (logprob - old_logprob))


def solution(mesh):
    in_specs = (
        P("dp", "tensor"),
        P("tensor"),
        P(None, ("dp", "tensor")),
        P("dp"),
        P("dp"),
        P("dp"),
    )
    out_specs = (P("dp"), P("dp"))
    return jax.shard_map(body, mesh=mesh, in_specs=in_specs, out_specs=out_specs, check_vma=False)
```

profile of v0, /device:TPU:0, one launch (start us, length us, event | category | flops | bytes accessed | tf_op | source)
XLA Modules:
  0.0 119.9 jit_solution(9858904204624372389)
XLA Ops:
  0.6 3.0 %collective-permute-start = (bf16[128,1024]{1,0:T(8,128)(2,1)}, bf16[128,1024]{1,0:T(8,128)(2,1)S(1)}, u32[]{:S(2)}, u32[]{:S(2)}) collective-permute-start(bf16[128,1024]{1,0:T(8,128)(2,1)} %param.6), channel_id=1, source_target_pairs={{0,8},{1,17},{2,10},{3,19},{4,12},{5,21},{6,14},{7,23},{8,0},{9,25... | collective-permute-start | bytes 786440 | tf_op jit(solution)/shard_map/ppermute | solution.py:32
  3.6 1.5 %collective-permute-start.1 = (bf16[128,1024]{1,0:T(8,128)(2,1)}, bf16[128,1024]{1,0:T(8,128)(2,1)S(1)}, u32[]{:S(2)}, u32[]{:S(2)}) collective-permute-start(bf16[128,1024]{1,0:T(8,128)(2,1)} %param.6), channel_id=1, source_target_pairs={{0,16},{1,9},{2,18},{3,11},{4,20},{5,13},{6,22},{7,15},{8,24},{9,1... | collective-permute-start | bytes 786440 | tf_op jit(solution)/shard_map/ppermute | solution.py:32
  5.2 1.6 %collective-permute-start.4 = (bf16[128,1024]{1,0:T(8,128)(2,1)}, bf16[128,1024]{1,0:T(8,128)(2,1)S(1)}, u32[]{:S(2)}, u32[]{:S(2)}) collective-permute-start(bf16[128,1024]{1,0:T(8,128)(2,1)} %param.6), channel_id=1, source_target_pairs={{0,2},{1,3},{2,4},{3,5},{4,6},{5,7},{6,0},{7,1},{8,10},{9,11},{10,... | collective-permute-start | bytes 786440 | tf_op jit(solution)/shard_map/ppermute | solution.py:32
  6.7 2.2 %collective-permute-start.5 = (bf16[128,1024]{1,0:T(8,128)(2,1)}, bf16[128,1024]{1,0:T(8,128)(2,1)S(1)}, u32[]{:S(2)}, u32[]{:S(2)}) collective-permute-start(bf16[128,1024]{1,0:T(8,128)(2,1)} %param.6), channel_id=1, source_target_pairs={{0,6},{1,7},{2,0},{3,1},{4,2},{5,3},{6,4},{7,5},{8,14},{9,15},{10,... | collective-permute-start | bytes 786440 | tf_op jit(solution)/shard_map/ppermute | solution.py:32
  9.0 1.1 multiply_reduce_fusion
  10.1 0.7 pad_maximum_fusion
  10.8 0.6 broadcast_in_dim.11
  11.4 3.3 %all-to-all-start = ((f32[8,1,1152]{2,1,0:T(1,128)}), f32[8,1,1152]{2,1,0:T(1,128)S(1)}, u32[]{:S(2)}, u32[]{:S(2)}) async-start(f32[8,1,1152]{2,1,0:T(1,128)} %broadcast_in_dim.11), calls=%async_computation | async-start | bytes 73728 | tf_op jit(solution)/shard_map/all_to_all | solution.py:79
  15.0 0.7 convert_bitcast_fusion
  15.9 5.3 %all-to-all-done = f32[8,1,1152]{2,1,0:T(1,128)S(1)} async-done(((f32[8,1,1152]{2,1,0:T(1,128)}), f32[8,1,1152]{2,1,0:T(1,128)S(1)}, u32[]{:S(2)}, u32[]{:S(2)}) %all-to-all-start) | async-done | bytes 36896 | tf_op jit(solution)/shard_map/all_to_all | solution.py:79
  21.2 0.6 broadcast_in_dim.12
  21.8 3.2 %all-to-all-start.1 = ((f32[4,2,128]{2,1,0:T(2,128)}), f32[4,2,128]{2,1,0:T(2,128)S(1)}, u32[]{:S(2)}, u32[]{:S(2)}) async-start(f32[4,2,128]{2,1,0:T(2,128)} %broadcast_in_dim.12), calls=%async_computation.1 | async-start | bytes 8192 | tf_op jit(solution)/shard_map/all_to_all | solution.py:79
  25.1 2.0 %collective-permute-start.2 = (bf16[128,1024]{1,0:T(8,128)(2,1)S(1)}, bf16[128,1024]{1,0:T(8,128)(2,1)S(1)}, u32[]{:S(2)}, u32[]{:S(2)}) collective-permute-start(bf16[128,1024]{1,0:T(8,128)(2,1)S(1)} %collective-permute-done), channel_id=1, source_target_pairs={{0,16},{1,9},{2,18},{3,11},{4,20},{5,13},{6,22},{7,15},{8,24},{9,1... | collective-permute-start | bytes 786440 | tf_op jit(solution)/shard_map/ppermute | solution.py:32
  27.2 4.4 %collective-permute-done.2 = bf16[128,1024]{1,0:T(8,128)(2,1)S(1)} collective-permute-done((bf16[128,1024]{1,0:T(8,128)(2,1)S(1)}, bf16[128,1024]{1,0:T(8,128)(2,1)S(1)}, u32[]{:S(2)}, u32[]{:S(2)}) %collective-permute-start.2) | collective-permute-done | bytes 262176 | tf_op jit(solution)/shard_map/ppermute | solution.py:32
  31.8 0.3 broadcast_in_dim.13
  32.0 0.7 copy-done.4
  32.7 0.8 constant_dynamic-update-slice_fusion.11
  33.5 0.8 constant_dynamic-update-slice_fusion.10
  34.2 1.8 %collective-permute-start.6 = (bf16[256,1024]{1,0:T(8,128)(2,1)}, bf16[256,1024]{1,0:T(8,128)(2,1)}, u32[]{:S(2)}, u32[]{:S(2)}) collective-permute-start(bf16[256,1024]{1,0:T(8,128)(2,1)} %get-tuple-element.18), channel_id=1, source_target_pairs={{0,8},{1,17},{2,10},{3,19},{4,12},{5,21},{6,14},{7,23},{8,0},{9,25... | collective-permute-start | bytes 1572872 | tf_op jit(solution)/shard_map/ppermute | solution.py:32
  36.0 1.5 %collective-permute-start.7 = (bf16[256,1024]{1,0:T(8,128)(2,1)}, bf16[256,1024]{1,0:T(8,128)(2,1)S(1)}, u32[]{:S(2)}, u32[]{:S(2)}) collective-permute-start(bf16[256,1024]{1,0:T(8,128)(2,1)} %get-tuple-element.18), channel_id=1, source_target_pairs={{0,16},{1,9},{2,18},{3,11},{4,20},{5,13},{6,22},{7,15},{8,24},{9,1... | collective-permute-start | bytes 1572872 | tf_op jit(solution)/shard_map/ppermute | solution.py:32
  37.6 0.6 collective-permute-start.8
  38.1 3.2 %fusion.7 = f32[512,1152]{1,0:T(8,128)S(1)} fusion(bf16[8192,1152]{1,0:T(8,128)(2,1)} %param.8, s32[]{:T(128)S(6)} %select_n.220, bf16[512,1024]{1,0:T(8,128)(2,1)S(1)} %constant_dynamic-update-slice_fusion.6, f32[1024]{0:T(1024)S(1)} %bitcast.57, f32[512]{0:T(512)S(1)} %bitcast.60), kind=kOutput, calls=%fused_computation.16 | convolution fusion | flops 1210056704 | bytes 5773316 | tf_op jit(solution)/shard_map/dot_general | solution.py:141
  41.4 6.8 %collective-permute-done.6 = bf16[256,1024]{1,0:T(8,128)(2,1)} collective-permute-done((bf16[256,1024]{1,0:T(8,128)(2,1)}, bf16[256,1024]{1,0:T(8,128)(2,1)}, u32[]{:S(2)}, u32[]{:S(2)}) %collective-permute-start.6) | collective-permute-done | bytes 524320 | tf_op jit(solution)/shard_map/ppermute | solution.py:32
  48.2 1.0 slice_dynamic-update-slice_fusion.5
  49.2 5.0 %convolution_add_fusion.6 = f32[512,1152]{1,0:T(8,128)} fusion(f32[512,1152]{1,0:T(8,128)S(1)} %fusion.7, bf16[8192,1152]{1,0:T(8,128)(2,1)} %param.8, s32[]{:T(128)S(6)} %select_n.223, bf16[512,1024]{1,0:T(8,128)(2,1)} %collective-permute-done.3, f32[1024]{0:T(1024)S(1)} %bitcast.56, f32[512]{0:T(512)S(1)} %bitcast.61), kind=kOutput, calls=%fused_computation.6 | convolution fusion | flops 1210646528 | bytes 8132612 | tf_op jit(solution)/shard_map/dot_general | solution.py:141
  54.2 2.5 %collective-permute-start.9 = (bf16[256,1024]{1,0:T(8,128)(2,1)}, bf16[256,1024]{1,0:T(8,128)(2,1)S(1)}, u32[]{:S(2)}, u32[]{:S(2)}) collective-permute-start(bf16[256,1024]{1,0:T(8,128)(2,1)} %collective-permute-done.6), channel_id=1, source_target_pairs={{0,16},{1,9},{2,18},{3,11},{4,20},{5,13},{6,22},{7,15},{8,24},{9,1... | collective-permute-start | bytes 1572872 | tf_op jit(solution)/shard_map/ppermute | solution.py:32
  56.7 1.0 slice_dynamic-update-slice_fusion.4
  57.8 6.3 %collective-permute-done.9 = bf16[256,1024]{1,0:T(8,128)(2,1)S(1)} collective-permute-done((bf16[256,1024]{1,0:T(8,128)(2,1)}, bf16[256,1024]{1,0:T(8,128)(2,1)S(1)}, u32[]{:S(2)}, u32[]{:S(2)}) %collective-permute-start.9) | collective-permute-done | bytes 524320 | tf_op jit(solution)/shard_map/ppermute | solution.py:32
  64.3 1.8 %collective-permute-start.11 = (bf16[128,1024]{1,0:T(8,128)(2,1)}, bf16[128,1024]{1,0:T(8,128)(2,1)S(1)}, u32[]{:S(2)}, u32[]{:S(2)}) collective-permute-start(bf16[128,1024]{1,0:T(8,128)(2,1)} %collective-permute-done.8), channel_id=1, source_target_pairs={{0,8},{1,17},{2,10},{3,19},{4,12},{5,21},{6,14},{7,23},{8,0},{9,25... | collective-permute-start | bytes 786440 | tf_op jit(solution)/shard_map/ppermute | solution.py:32
  66.1 2.0 %collective-permute-start.12 = (bf16[128,1024]{1,0:T(8,128)(2,1)}, bf16[128,1024]{1,0:T(8,128)(2,1)S(1)}, u32[]{:S(2)}, u32[]{:S(2)}) collective-permute-start(bf16[128,1024]{1,0:T(8,128)(2,1)} %collective-permute-done.8), channel_id=1, source_target_pairs={{0,16},{1,9},{2,18},{3,11},{4,20},{5,13},{6,22},{7,15},{8,24},{9,1... | collective-permute-start | bytes 786440 | tf_op jit(solution)/shard_map/ppermute | solution.py:32
  68.1 4.3 %collective-permute-done.11 = bf16[128,1024]{1,0:T(8,128)(2,1)S(1)} collective-permute-done((bf16[128,1024]{1,0:T(8,128)(2,1)}, bf16[128,1024]{1,0:T(8,128)(2,1)S(1)}, u32[]{:S(2)}, u32[]{:S(2)}) %collective-permute-start.11) | collective-permute-done | bytes 262176 | tf_op jit(solution)/shard_map/ppermute | solution.py:32
  72.4 1.0 collective-permute-done.12
  73.5 1.8 %collective-permute-start.13 = (bf16[128,1024]{1,0:T(8,128)(2,1)S(1)}, bf16[128,1024]{1,0:T(8,128)(2,1)S(1)}, u32[]{:S(2)}, u32[]{:S(2)}) collective-permute-start(bf16[128,1024]{1,0:T(8,128)(2,1)S(1)} %collective-permute-done.11), channel_id=1, source_target_pairs={{0,16},{1,9},{2,18},{3,11},{4,20},{5,13},{6,22},{7,15},{8,24},{9,1... | collective-permute-start | bytes 786440 | tf_op jit(solution)/shard_map/ppermute | solution.py:32
  75.2 0.1 broadcast.56.clone.1
  75.4 1.0 constant_dynamic-update-slice_fusion.3
  76.4 3.4 %collective-permute-done.13 = bf16[128,1024]{1,0:T(8,128)(2,1)S(1)} collective-permute-done((bf16[128,1024]{1,0:T(8,128)(2,1)S(1)}, bf16[128,1024]{1,0:T(8,128)(2,1)S(1)}, u32[]{:S(2)}, u32[]{:S(2)}) %collective-permute-start.13) | collective-permute-done | bytes 262176 | tf_op jit(solution)/shard_map/ppermute | solution.py:32
  79.9 3.2 %convolution_add_fusion.5 = f32[512,1152]{1,0:T(8,128)S(1)} fusion(f32[512,1152]{1,0:T(8,128)S(1)} %copy-done.6, bf16[8192,1152]{1,0:T(8,128)(2,1)} %param.8, s32[]{:T(128)S(6)} %select_n.234, bf16[1024,1024]{1,0:T(8,128)(2,1)S(1)} %slice_dynamic-update-slice_fusion, f32[1024]{0:T(1024)S(1)} %bitcast.55, f32[512]{0:T(512)S(1)} %bitcast.62), kind=kOutput, calls=%fused_computation.5 | convolution fusion | flops 1210646528 | bytes 8132612 | tf_op jit(solution)/shard_map/dot_general | solution.py:141
  83.2 3.6 %convolution_add_fusion.4 = f32[512,1152]{1,0:T(8,128)S(1)} fusion(f32[512,1152]{1,0:T(8,128)S(1)} %convolution_add_fusion.5, bf16[8192,1152]{1,0:T(8,128)(2,1)} %param.8, s32[]{:T(128)S(6)} %select_n.236, bf16[1024,1024]{1,0:T(8,128)(2,1)} %collective-permute-done.10, f32[1024]{0:T(1024)S(1)} %bitcast.54, f32[512]{0:T(512)S(1)} %bitcast.63), kind=kOutput, calls=%fused_computation.4 | convolution fusion | flops 1210646528 | bytes 8132612 | tf_op jit(solution)/shard_map/dot_general | solution.py:141
  86.8 3.2 %convolution_add_fusion.3 = f32[512,1152]{1,0:T(8,128)S(1)} fusion(f32[512,1152]{1,0:T(8,128)S(1)} %convolution_add_fusion.4, bf16[8192,1152]{1,0:T(8,128)(2,1)} %param.8, s32[]{:T(128)S(6)} %select_n.239, bf16[1024,1024]{1,0:T(8,128)(2,1)S(1)} %slice_dynamic-update-slice_fusion, f32[1024]{0:T(1024)S(1)} %bitcast.53, f32[512]{0:T(512)S(1)} %bitcast.64), kind=kOutput, calls=%fused_computation.3 | convolution fusion | flops 1210646528 | bytes 8132612 | tf_op jit(solution)/shard_map/dot_general | solution.py:141
  90.0 3.6 %convolution_add_fusion.2 = f32[512,1152]{1,0:T(8,128)S(1)} fusion(f32[512,1152]{1,0:T(8,128)S(1)} %convolution_add_fusion.3, bf16[8192,1152]{1,0:T(8,128)(2,1)} %param.8, s32[]{:T(128)S(6)} %select_n.241, bf16[1024,1024]{1,0:T(8,128)(2,1)} %collective-permute-done.10, f32[1024]{0:T(1024)S(1)} %bitcast.52, f32[512]{0:T(512)S(1)} %bitcast.65), kind=kOutput, calls=%fused_computation.2 | convolution fusion | flops 1210646528 | bytes 8132612 | tf_op jit(solution)/shard_map/dot_general | solution.py:141
  93.6 3.3 %convolution_add_fusion.1 = f32[512,1152]{1,0:T(8,128)S(1)} fusion(f32[512,1152]{1,0:T(8,128)S(1)} %convolution_add_fusion.2, bf16[8192,1152]{1,0:T(8,128)(2,1)} %param.8, s32[]{:T(128)S(6)} %select_n.244, bf16[512,1024]{1,0:T(8,128)(2,1)S(1)} %constant_dynamic-update-slice_fusion, f32[1024]{0:T(1024)S(1)} %bitcast.51, f32[512]{0:T(512)S(1)} %bitcast.66), kind=kOutput, calls=%fused_computation.1 | convolution fusion | flops 1210646528 | bytes 8132612 | tf_op jit(solution)/shard_map/dot_general | solution.py:141
  96.9 3.4 %fusion.39 = (f32[512]{0:T(512)S(1)}, f32[512,1152]{1,0:T(8,128)S(1)}) fusion(f32[512,1152]{1,0:T(8,128)S(1)} %convolution_add_fusion.1, bf16[8192,1152]{1,0:T(8,128)(2,1)} %param.8, s32[]{:T(128)S(6)} %select_n.246, bf16[512,1024]{1,0:T(8,128)(2,1)S(1)} %collective-permute-done.14, f32[1024]{0:T(1024)S(1)} %bitcast.50, f32[512]{0:T(512)S(1)} %bitcast.67), kind=kOutput, calls=%fused_computation.98 | convolution fusion | flops 1211235840 | bytes 8134660 | tf_op jit(solution)/shard_map/dot_general | solution.py:141
  100.2 0.7 exponential_reduce_fusion
  100.9 8.7 %all_to_all.24 = f32[4,3,128]{2,1,0:T(4,128)S(1)} all-to-all(f32[4,3,128]{2,1,0:T(4,128)S(1)} %pad_maximum_fusion.1), channel_id=1, replica_groups=mesh['dp'=4,'tensor'=8] {'dp'}, dimensions={0} | all-to-all | bytes 12288 | tf_op jit(solution)/shard_map/all_to_all | solution.py:152
  109.8 0.6 broadcast_in_dim.15
  110.4 3.3 %all-to-all-start.3 = ((f32[8,3,128]{2,1,0:T(4,128)}), f32[8,3,128]{2,1,0:T(4,128)S(1)}, u32[]{:S(2)}, u32[]{:S(2)}) async-start(f32[8,3,128]{2,1,0:T(4,128)} %broadcast_in_dim.15), calls=%async_computation.3 | async-start | bytes 32768 | tf_op jit(solution)/shard_map/all_to_all | solution.py:79
  114.3 4.9 %all-to-all-done.3 = f32[8,3,128]{2,1,0:T(4,128)S(1)} async-done(((f32[8,3,128]{2,1,0:T(4,128)}), f32[8,3,128]{2,1,0:T(4,128)S(1)}, u32[]{:S(2)}, u32[]{:S(2)}) %all-to-all-start.3) | async-done | bytes 12320 | tf_op jit(solution)/shard_map/all_to_all | solution.py:79
  119.3 0.5 compare_select_fusion
  (56 shorter events, 0.9 us)
Async XLA Ops:
  0.6 15.2 %copy-start = (bf16[128,1024]{1,0:T(8,128)(2,1)S(1)}, bf16[128,1024]{1,0:T(8,128)(2,1)}, u32[]{:S(2)}) copy-start(bf16[128,1024]{1,0:T(8,128)(2,1)} %param.6) | copy-start | bytes 786436
  0.6 24.4 %collective-permute-start = (bf16[128,1024]{1,0:T(8,128)(2,1)}, bf16[128,1024]{1,0:T(8,128)(2,1)S(1)}, u32[]{:S(2)}, u32[]{:S(2)}) collective-permute-start(bf16[128,1024]{1,0:T(8,128)(2,1)} %param.6), channel_id=1, source_target_pairs={{0,8},{1,17},{2,10},{3,19},{4,12},{5,21},{6,14},{7,23},{8,0},{9,25... | collective-permute-start | bytes 786440 | tf_op jit(solution)/shard_map/ppermute | solution.py:32
  3.6 21.4 %collective-permute-start.1 = (bf16[128,1024]{1,0:T(8,128)(2,1)}, bf16[128,1024]{1,0:T(8,128)(2,1)S(1)}, u32[]{:S(2)}, u32[]{:S(2)}) collective-permute-start(bf16[128,1024]{1,0:T(8,128)(2,1)} %param.6), channel_id=1, source_target_pairs={{0,16},{1,9},{2,18},{3,11},{4,20},{5,13},{6,22},{7,15},{8,24},{9,1... | collective-permute-start | bytes 786440 | tf_op jit(solution)/shard_map/ppermute | solution.py:32
  5.2 21.9 %collective-permute-start.4 = (bf16[128,1024]{1,0:T(8,128)(2,1)}, bf16[128,1024]{1,0:T(8,128)(2,1)S(1)}, u32[]{:S(2)}, u32[]{:S(2)}) collective-permute-start(bf16[128,1024]{1,0:T(8,128)(2,1)} %param.6), channel_id=1, source_target_pairs={{0,2},{1,3},{2,4},{3,5},{4,6},{5,7},{6,0},{7,1},{8,10},{9,11},{10,... | collective-permute-start | bytes 786440 | tf_op jit(solution)/shard_map/ppermute | solution.py:32
  6.7 20.4 %collective-permute-start.5 = (bf16[128,1024]{1,0:T(8,128)(2,1)}, bf16[128,1024]{1,0:T(8,128)(2,1)S(1)}, u32[]{:S(2)}, u32[]{:S(2)}) collective-permute-start(bf16[128,1024]{1,0:T(8,128)(2,1)} %param.6), channel_id=1, source_target_pairs={{0,6},{1,7},{2,0},{3,1},{4,2},{5,3},{6,4},{7,5},{8,14},{9,15},{10,... | collective-permute-start | bytes 786440 | tf_op jit(solution)/shard_map/ppermute | solution.py:32
  11.4 9.7 %all-to-all-start = ((f32[8,1,1152]{2,1,0:T(1,128)}), f32[8,1,1152]{2,1,0:T(1,128)S(1)}, u32[]{:S(2)}, u32[]{:S(2)}) async-start(f32[8,1,1152]{2,1,0:T(1,128)} %broadcast_in_dim.11), calls=%async_computation | async-start | bytes 73728 | tf_op jit(solution)/shard_map/all_to_all | solution.py:79
  21.8 14.2 %all-to-all-start.1 = ((f32[4,2,128]{2,1,0:T(2,128)}), f32[4,2,128]{2,1,0:T(2,128)S(1)}, u32[]{:S(2)}, u32[]{:S(2)}) async-start(f32[4,2,128]{2,1,0:T(2,128)} %broadcast_in_dim.12), calls=%async_computation.1 | async-start | bytes 8192 | tf_op jit(solution)/shard_map/all_to_all | solution.py:79
  25.1 6.5 %collective-permute-start.2 = (bf16[128,1024]{1,0:T(8,128)(2,1)S(1)}, bf16[128,1024]{1,0:T(8,128)(2,1)S(1)}, u32[]{:S(2)}, u32[]{:S(2)}) collective-permute-start(bf16[128,1024]{1,0:T(8,128)(2,1)S(1)} %collective-permute-done), channel_id=1, source_target_pairs={{0,16},{1,9},{2,18},{3,11},{4,20},{5,13},{6,22},{7,15},{8,24},{9,1... | collective-permute-start | bytes 786440 | tf_op jit(solution)/shard_map/ppermute | solution.py:32
  27.1 4.6 %copy-start.3 = (bf16[128,1024]{1,0:T(8,128)(2,1)}, bf16[128,1024]{1,0:T(8,128)(2,1)S(1)}, u32[]{:S(2)}) copy-start(bf16[128,1024]{1,0:T(8,128)(2,1)S(1)} %collective-permute-done.4) | copy-start | bytes 786436
  27.1 4.5 %copy-start.1 = (bf16[128,1024]{1,0:T(8,128)(2,1)}, bf16[128,1024]{1,0:T(8,128)(2,1)S(1)}, u32[]{:S(2)}) copy-start(bf16[128,1024]{1,0:T(8,128)(2,1)S(1)} %collective-permute-done.5) | copy-start | bytes 786436
  31.7 17.5 %collective-permute-start.3 = (bf16[512,1024]{1,0:T(8,128)(2,1)S(1)}, bf16[512,1024]{1,0:T(8,128)(2,1)}, u32[]{:S(2)}, u32[]{:S(2)}) collective-permute-start(bf16[512,1024]{1,0:T(8,128)(2,1)S(1)} %constant_dynamic-update-slice_fusion.6), channel_id=1, source_target_pairs={{0,1},{1,0},{2,3},{3,2},{4,5},{5,4},{6,7},{7,6},{8,9},{9,8},{10,11... | collective-permute-start | bytes 3145736 | tf_op jit(solution)/shard_map/ppermute | solution.py:32
  31.8 1.0 copy-start.4
  31.8 1.7 %copy-start.2 = (bf16[128,1024]{1,0:T(8,128)(2,1)S(1)}, bf16[128,1024]{1,0:T(8,128)(2,1)}, u32[]{:S(2)}) copy-start(bf16[128,1024]{1,0:T(8,128)(2,1)} %copy-done.1) | copy-start | bytes 786436
  34.2 14.0 %collective-permute-start.6 = (bf16[256,1024]{1,0:T(8,128)(2,1)}, bf16[256,1024]{1,0:T(8,128)(2,1)}, u32[]{:S(2)}, u32[]{:S(2)}) collective-permute-start(bf16[256,1024]{1,0:T(8,128)(2,1)} %get-tuple-element.18), channel_id=1, source_target_pairs={{0,8},{1,17},{2,10},{3,19},{4,12},{5,21},{6,14},{7,23},{8,0},{9,25... | collective-permute-start | bytes 1572872 | tf_op jit(solution)/shard_map/ppermute | solution.py:32
  36.0 18.2 %collective-permute-start.7 = (bf16[256,1024]{1,0:T(8,128)(2,1)}, bf16[256,1024]{1,0:T(8,128)(2,1)S(1)}, u32[]{:S(2)}, u32[]{:S(2)}) collective-permute-start(bf16[256,1024]{1,0:T(8,128)(2,1)} %get-tuple-element.18), channel_id=1, source_target_pairs={{0,16},{1,9},{2,18},{3,11},{4,20},{5,13},{6,22},{7,15},{8,24},{9,1... | collective-permute-start | bytes 1572872 | tf_op jit(solution)/shard_map/ppermute | solution.py:32
  37.6 16.6 %collective-permute-start.8 = (bf16[128,1024]{1,0:T(8,128)(2,1)S(1)}, bf16[128,1024]{1,0:T(8,128)(2,1)}, u32[]{:S(2)}, u32[]{:S(2)}) collective-permute-start(bf16[128,1024]{1,0:T(8,128)(2,1)S(1)} %copy-done), channel_id=1, source_target_pairs={{0,4},{1,5},{2,6},{3,7},{4,0},{5,1},{6,2},{7,3},{8,12},{9,13},{10,... | collective-permute-start | bytes 786440 | tf_op jit(solution)/shard_map/ppermute | solution.py:32
  54.2 9.9 %collective-permute-start.9 = (bf16[256,1024]{1,0:T(8,128)(2,1)}, bf16[256,1024]{1,0:T(8,128)(2,1)S(1)}, u32[]{:S(2)}, u32[]{:S(2)}) collective-permute-start(bf16[256,1024]{1,0:T(8,128)(2,1)} %collective-permute-done.6), channel_id=1, source_target_pairs={{0,16},{1,9},{2,18},{3,11},{4,20},{5,13},{6,22},{7,15},{8,24},{9,1... | collective-permute-start | bytes 1572872 | tf_op jit(solution)/shard_map/ppermute | solution.py:32
  64.2 19.0 %collective-permute-start.10 = (bf16[1024,1024]{1,0:T(8,128)(2,1)S(1)}, bf16[1024,1024]{1,0:T(8,128)(2,1)}, u32[]{:S(2)}, u32[]{:S(2)}) collective-permute-start(bf16[1024,1024]{1,0:T(8,128)(2,1)S(1)} %slice_dynamic-update-slice_fusion), channel_id=1, source_target_pairs={{0,1},{1,0},{2,3},{3,2},{4,5},{5,4},{6,7},{7,6},{8,9},{9,8},{10,11... | collective-permute-start | bytes 6291464 | tf_op jit(solution)/shard_map/ppermute | solution.py:32
  64.3 8.2 %collective-permute-start.11 = (bf16[128,1024]{1,0:T(8,128)(2,1)}, bf16[128,1024]{1,0:T(8,128)(2,1)S(1)}, u32[]{:S(2)}, u32[]{:S(2)}) collective-permute-start(bf16[128,1024]{1,0:T(8,128)(2,1)} %collective-permute-done.8), channel_id=1, source_target_pairs={{0,8},{1,17},{2,10},{3,19},{4,12},{5,21},{6,14},{7,23},{8,0},{9,25... | collective-permute-start | bytes 786440 | tf_op jit(solution)/shard_map/ppermute | solution.py:32
  66.1 7.4 %collective-permute-start.12 = (bf16[128,1024]{1,0:T(8,128)(2,1)}, bf16[128,1024]{1,0:T(8,128)(2,1)S(1)}, u32[]{:S(2)}, u32[]{:S(2)}) collective-permute-start(bf16[128,1024]{1,0:T(8,128)(2,1)} %collective-permute-done.8), channel_id=1, source_target_pairs={{0,16},{1,9},{2,18},{3,11},{4,20},{5,13},{6,22},{7,15},{8,24},{9,1... | collective-permute-start | bytes 786440 | tf_op jit(solution)/shard_map/ppermute | solution.py:32
  68.1 11.8 %copy-start.6 = (f32[512,1152]{1,0:T(8,128)S(1)}, f32[512,1152]{1,0:T(8,128)}, u32[]{:S(2)}) copy-start(f32[512,1152]{1,0:T(8,128)} %convolution_add_fusion.6) | copy-start | bytes 7077892
  73.5 6.4 %collective-permute-start.13 = (bf16[128,1024]{1,0:T(8,128)(2,1)S(1)}, bf16[128,1024]{1,0:T(8,128)(2,1)S(1)}, u32[]{:S(2)}, u32[]{:S(2)}) collective-permute-start(bf16[128,1024]{1,0:T(8,128)(2,1)S(1)} %collective-permute-done.11), channel_id=1, source_target_pairs={{0,16},{1,9},{2,18},{3,11},{4,20},{5,13},{6,22},{7,15},{8,24},{9,1... | collective-permute-start | bytes 786440 | tf_op jit(solution)/shard_map/ppermute | solution.py:32
  79.9 17.0 %collective-permute-start.14 = (bf16[512,1024]{1,0:T(8,128)(2,1)S(1)}, bf16[512,1024]{1,0:T(8,128)(2,1)S(1)}, u32[]{:S(2)}, u32[]{:S(2)}) collective-permute-start(bf16[512,1024]{1,0:T(8,128)(2,1)S(1)} %constant_dynamic-update-slice_fusion), channel_id=1, source_target_pairs={{0,1},{1,0},{2,3},{3,2},{4,5},{5,4},{6,7},{7,6},{8,9},{9,8},{10,11... | collective-permute-start | bytes 3145736 | tf_op jit(solution)/shard_map/ppermute | solution.py:32
  100.2 19.1 %copy-start.5 = (f32[128]{0:T(128)S(1)}, f32[128]{0:T(128)}, u32[]{:S(2)}) copy-start(f32[128]{0:T(128)} %param.10) | copy-start | bytes 1540
  110.4 8.9 %all-to-all-start.3 = ((f32[8,3,128]{2,1,0:T(4,128)}), f32[8,3,128]{2,1,0:T(4,128)S(1)}, u32[]{:S(2)}, u32[]{:S(2)}) async-start(f32[8,3,128]{2,1,0:T(4,128)} %broadcast_in_dim.15), calls=%async_computation.3 | async-start | bytes 32768 | tf_op jit(solution)/shard_map/all_to_all | solution.py:79
where the time goes:
time: 121 us; the launch traced here: 120 us
  waiting for transfers between devices  36.6 us (30%)
  starting transfers between devices  32.5 us (27%)
  matrix products  28.5 us (24%)
  blocking collectives  8.74 us (7%)
  local copies, waits for them, and re-layouts  7.78 us (6%)
  other arithmetic  3.88 us (3%)
  between operations  1.92 us (2%)
    dot_general x8, matrix products, body(): product = jnp.dot(normed, weights, preferred_element_type=jnp.float32)  28.5 us
    ppermute x15, waiting for transfers between devices, permute(): return lax.ppermute(a, ('dp', 'tensor'), perm)  26.3 us
    ppermute x15, starting transfers between devices, permute(): return lax.ppermute(a, ('dp', 'tensor'), perm)  22.6 us
    all_to_all x3, waiting for transfers between devices, exchange(): return lax.all_to_all(copies, axis, 0, 0, tiled=True)  10.2 us
    all_to_all x3, starting transfers between devices, exchange(): return lax.all_to_all(copies, axis, 0, 0, tiled=True)  9.9 us
    all_to_all x1, blocking collectives, body(): stats = jnp.stack(merge(lax.all_to_all(stats, 'dp', 0, 0, tiled=True)))  8.74 us
    dynamic_update_slice x14, local copies, waits for them, and re-layouts, body(): lax.dynamic_update_slice_in_dim(block, piece, (j * n_dp + owner) * tok, 0)  3.2 us
  transfers between devices with their start and end apart: 18, of which 8 were waited for; matrix products, arithmetic and copies ran while one was open for 28% of the time, Pallas kernels for 0%

commit v1 on v0

v1 whole, which is shorter than its diff:
```python
import functools

import jax
import jax.numpy as jnp
from jax import lax
from jax.experimental import pallas as pl
from jax.experimental.pallas import tpu as pltpu
from jax.sharding import PartitionSpec as P

D = 8192
CORES = 2
X_ONLY, Y_ONLY = (0, 1), (1, 0)
VMEM_LIMIT = 24 * 1024 * 1024
SMALL_LIMIT = 6 * 1024 * 1024
TILES = (256, 384)


class Grid:
    def __init__(self, n_dp, n_t):
        self.n_t = n_t
        self.cols = 2
        self.rows = n_dp // self.cols
        self.depth = n_t // CORES
        self.square = self.rows == self.cols
        self.first = (X_ONLY, Y_ONLY) if self.square else (X_ONLY, X_ONLY)
        self.second = (Y_ONLY, X_ONLY) if self.square else (Y_ONLY, Y_ONLY)
        self.spots = [(j, i) for j in range(self.rows) for i in range(self.cols)]

    def permute(self, a, place):
        perm = []
        for y in range(self.rows):
            for x in range(self.cols):
                for z in range(self.depth):
                    for c in range(CORES):
                        src = (y * self.cols + x) * self.n_t + z * CORES + c
                        v, u, w, d = place(y, x, z, c)
                        dst = (v % self.rows * self.cols + u % self.cols) * self.n_t
                        perm.append((src, dst + w % self.depth * CORES + d % CORES))
        return lax.ppermute(a, ("dp", "tensor"), perm)

    def plane(self, a, ways, step):
        def place(y, x, z, c):
            return y + ways[c][0] * step, x + ways[c][1] * step, z, c

        return self.permute(a, place)

    def along(self, a, step):
        return self.permute(a, lambda y, x, z, c: (y, x, z + step, c))

    def sibling(self, a):
        return self.permute(a, lambda y, x, z, c: (y, x, z, c + 1))

    def reach(self, a):
        got = {(0, 0): a}
        for i in range(1, self.cols):
            got[0, i] = self.plane(a, self.first, i)
        for j in range(1, self.rows):
            got[j, 0] = self.plane(a, self.second, j)
        return got

    def fill(self, got, *late):
        late = (*late, *got.values())
        for j in range(1, self.rows):
            for i in range(1, self.cols):
                got[j, i] = self.plane(after(got[0, i], *late), self.second, j)
        return [got[s] for s in self.spots]

    def owners(self, y, x, c):
        ways = [(self.first[k], self.second[k]) for k in range(CORES)]
        out = []
        for j, i in self.spots:
            at = [
                (y - f[0] * i - s[0] * j) % self.rows * self.cols + (x - f[1] * i - s[1] * j) % self.cols
                for f, s in ways
            ]
            out.append(jnp.where(c == 0, at[0], at[1]))
        return out

    def sibling_spot(self, k):
        j, i = self.spots[k]
        return self.spots.index((i, j)) if self.square else k


def far(a):
    return pltpu.with_memory_space_constraint(a, pltpu.HBM)


def after(a, *others):
    return lax.optimization_barrier((a, *others))[0] if others else a


def diagonal(size):
    row = lax.broadcasted_iota(jnp.int32, (size, size), 0)
    return row == lax.broadcasted_iota(jnp.int32, (size, size), 1)


def to_column(row):
    return jnp.sum(jnp.where(diagonal(row.shape[1]), row, 0.0), axis=1, keepdims=True)


def to_row(column):
    return jnp.sum(jnp.where(diagonal(column.shape[0]), column, 0.0), axis=0, keepdims=True)


def column_tiles(vocab):
    cuts = [0]
    for width in TILES:
        if cuts[-1] + width < vocab:
            cuts.append(cuts[-1] + width)
    return list(zip(cuts, [*cuts[1:], vocab], strict=True))


def layer_kernel(n, n_t, place, layer, first, last, *refs):
    refs = list(refs)
    start_ref, fine_ref = refs.pop(0), refs.pop(0)
    blocks = [refs.pop(0) for _ in range(CORES * n)]
    head_ref = refs.pop(0)
    acc_ref = None if first else refs.pop(0)
    out_ref, raw, rows, weights, raw_sem, head_sem = refs[:6]
    acc = refs[6] if last else out_ref
    feat = raw.shape[2]
    tok = raw.shape[1] // n
    vocab = weights.shape[1]
    z_from, c_me, base = start_ref[0], start_ref[1], start_ref[2]
    owners = [start_ref[3 + k] for k in range(n)]

    offset = pl.multiple_of(z_from * (CORES * feat), CORES * feat)
    tiles = column_tiles(vocab)
    head_copies = [
        pltpu.make_async_copy(
            head_ref.at[pl.ds(offset, CORES * feat), pl.ds(lo, hi - lo)],
            weights.at[:, pl.ds(lo, hi - lo)],
            head_sem.at[i],
        )
        for i, (lo, hi) in enumerate(tiles)
    ]
    block_copies = []
    for c in range(CORES):
        for k in range(n):
            spot = place[k] if c else k
            block_copies.append(
                pltpu.make_async_copy(
                    blocks[c * n + k].at[pl.ds(layer * tok, tok)],
                    raw.at[c, pl.ds(spot * tok, tok)],
                    raw_sem.at[c * n + k],
                )
            )
    head_copies[0].start()
    for copy in block_copies:
        copy.start()
    for copy in head_copies[1:]:
        copy.start()

    def peer_rows(k):
        return pl.ds(pl.multiple_of(owners[k] * n_t, n_t), n_t)

    scales = []
    for k in range(n):
        sums = jnp.sum(fine_ref[peer_rows(k), feat : feat + tok], axis=0, keepdims=True)
        scales.append(to_column(lax.rsqrt(sums / D + 1e-06)))
    for c in range(CORES):
        core = 1 - c_me if c else c_me
        gain = fine_ref[pl.ds(z_from * CORES + core, 1), :feat]
        columns = pl.ds(pl.multiple_of(core * feat, feat), feat)
        for k in range(n):
            block_copies[c * n + k].wait()
        for k in range(n):
            here = slice(k * tok, (k + 1) * tok)
            part = raw[c, here, :].astype(jnp.float32) * scales[k] * gain
            rows[here, columns] = part.astype(jnp.bfloat16)
    for copy, (lo, hi) in zip(head_copies, tiles, strict=True):
        copy.wait()
        product = jnp.dot(rows[...], weights[:, lo:hi], preferred_element_type=jnp.float32)
        acc[:, lo:hi] = product if first else acc_ref[:, lo:hi] + product
    if not last:
        return
    for b in range(n):
        logits = acc[b * tok : (b + 1) * tok, :]
        top = jnp.max(logits, axis=1, keepdims=True)
        total = jnp.sum(jnp.exp(logits - top), axis=1, keepdims=True)
        entry = lax.broadcasted_iota(jnp.int32, logits.shape, 1) + base
        target = fine_ref[peer_rows(b), feat + tok : feat + 2 * tok][0:1, :]
        target = to_column(target).astype(jnp.int32)
        pick = jnp.sum(jnp.where(entry == target, logits, 0.0), axis=1, keepdims=True)
        for peer in range(n_t):
            out_ref[owners[b], peer, 0:1, :] = to_row(top)
            out_ref[owners[b], peer, 1:2, :] = to_row(total)
            out_ref[owners[b], peer, 2:3, :] = to_row(pick)


def layer_product(tok, n_t, starts, fine, blocks, layer, place, head, acc, last):
    n = len(place)
    feat = blocks[0].shape[1]
    vocab = head.shape[1]
    vmem, whole = pl.BlockSpec(memory_space=pltpu.VMEM), pl.BlockSpec(memory_space=pl.ANY)
    first = acc is None
    logits = jax.ShapeDtypeStruct((n * tok, vocab), jnp.float32)
    operands = [starts, fine, *blocks, far(head)] + ([] if first else [acc])
    specs = [pl.BlockSpec(memory_space=pltpu.SMEM), vmem] + [whole] * (len(blocks) + 1) + [vmem] * (not first)
    scratch = [
        pltpu.VMEM((CORES, n * tok, feat), jnp.bfloat16),
        pltpu.VMEM((n * tok, CORES * feat), jnp.bfloat16),
        pltpu.VMEM((CORES * feat, vocab), jnp.bfloat16),
        pltpu.SemaphoreType.DMA((CORES * n,)),
        pltpu.SemaphoreType.DMA((len(column_tiles(vocab)),)),
    ]
    if last:
        scratch.append(pltpu.VMEM(logits.shape, jnp.float32))
    work = 2 * n * tok * CORES * feat * vocab
    return pl.pallas_call(
        functools.partial(layer_kernel, n, n_t, place, layer, first, last),
        out_shape=jax.ShapeDtypeStruct((n, n_t, 3, tok), jnp.float32) if last else logits,
        in_specs=specs,
        out_specs=vmem,
        scratch_shapes=scratch,
        compiler_params=pltpu.CompilerParams(vmem_limit_bytes=VMEM_LIMIT),
        cost_estimate=pl.CostEstimate(
            flops=work, bytes_accessed=2 * CORES * feat * vocab, transcendentals=0
        ),
    )(*operands)


def squares_kernel(hidden_ref, gain_ref, target_ref, out_ref, raw, gain, target, sems):
    pairs = ((hidden_ref, raw), (gain_ref, gain), (target_ref, target))
    copies = [pltpu.make_async_copy(a, b, sems.at[i]) for i, (a, b) in enumerate(pairs)]
    for copy in copies:
        copy.start()
    for copy in copies:
        copy.wait()
    tok, feat = raw.shape
    values = raw[...].astype(jnp.float32)
    sums = to_row(jnp.sum(values * values, axis=1, keepdims=True))
    peers = out_ref.shape[0]
    out_ref[:, :feat] = jnp.broadcast_to(gain[...], (peers, feat))
    out_ref[:, feat : feat + tok] = jnp.broadcast_to(sums, (peers, tok))
    out_ref[:, feat + tok :] = jnp.broadcast_to(target[...].astype(jnp.float32), (peers, tok))


def squares(hidden, gain, targets, peers):
    tok, feat = hidden.shape
    return pl.pallas_call(
        squares_kernel,
        out_shape=jax.ShapeDtypeStruct((peers, feat + 2 * tok), jnp.float32),
        in_specs=[pl.BlockSpec(memory_space=pltpu.HBM)] * 3,
        out_specs=pl.BlockSpec(memory_space=pltpu.VMEM),
        scratch_shapes=[
            pltpu.VMEM(hidden.shape, hidden.dtype),
            pltpu.VMEM(gain.shape, gain.dtype),
            pltpu.VMEM(targets.shape, targets.dtype),
            pltpu.SemaphoreType.DMA((3,)),
        ],
        compiler_params=pltpu.CompilerParams(vmem_limit_bytes=SMALL_LIMIT),
    )(far(hidden), far(gain), far(targets))


def body(hidden, norm_gain, head, targets, old_logprob, lengths):
    n_dp, n_t = lax.axis_size("dp"), lax.axis_size("tensor")
    grid = Grid(n_dp, n_t)
    depth = grid.depth
    tok, feat = hidden.shape
    plane, tensor = lax.axis_index("dp"), lax.axis_index("tensor")
    z_me, c_me = tensor // CORES, tensor % CORES
    owners = grid.owners(plane // grid.cols, plane % grid.cols, c_me)
    groups = [[0]] + [[d, depth - d] for d in range(1, (depth + 1) // 2)] + [[depth // 2]]
    place = [grid.sibling_spot(k) for k in range(n_dp)]

    layers = {0: hidden}
    before = []
    for group in groups[1:]:
        for dz in group:
            layers[dz] = grid.along(after(hidden, *before), dz)
        before = [layers[dz] for dz in group]
    reached = [grid.reach(hidden)]
    for group in groups[1:]:
        sources = [layers[dz] for dz in group]
        sources[0] = after(sources[0], *reached[-1].values())
        joined = jnp.concatenate(sources) if len(sources) > 1 else sources[0]
        reached.append(grid.reach(joined))

    packed = squares(hidden, norm_gain[None, :], targets[None, :], n_dp * n_t)
    fine = lax.all_to_all(packed, ("dp", "tensor"), 0, 0, tiled=True)

    vocab_cols = head.shape[1]
    vocab_start = lax.axis_index(("dp", "tensor")) * vocab_cols
    acc = None
    for at, group in enumerate(groups):
        final = at == len(groups) - 1
        held = [] if final or not at else [layers[dz] for dz in groups[at + 1]]
        spread = grid.fill(dict(reached[at]), *([acc] if at == 1 else []), *held)
        blocks = spread + [grid.sibling(a) for a in spread]
        following = [] if final or not at else list(reached[at + 1].values())
        for layer, dz in enumerate(group):
            starts = jnp.stack([(z_me - dz) % depth, c_me, vocab_start] + owners)
            if layer == len(group) - 1:
                starts = after(starts, *following)
            last = final and layer == len(group) - 1
            acc = layer_product(tok, n_t, starts, fine, blocks, layer, place, head, acc, last)

    parts = lax.all_to_all(acc.reshape(n_dp * n_t, 3, tok), ("dp", "tensor"), 0, 0, tiled=True)
    top = jnp.max(parts[:, 0], axis=0)
    total = jnp.sum(parts[:, 1] * jnp.exp(parts[:, 0] - top[None, :]), axis=0)
    picked = jnp.sum(parts[:, 2], axis=0)

    seq_count = lengths.shape[0]
    position = jnp.arange(tok // seq_count, dtype=jnp.int32)
    live = (position[None, :] < lengths[:, None]).reshape(-1).astype(jnp.float32)
    logprob = picked - top - jnp.log(total)
    return (live * logprob, live * (logprob - old_logprob))


def solution(mesh):
    in_specs = (
        P("dp", "tensor"),
        P("tensor"),
        P(None, ("dp", "tensor")),
        P("dp"),
        P("dp"),
        P("dp"),
    )
    out_specs = (P("dp"), P("dp"))
    return jax.shard_map(body, mesh=mesh, in_specs=in_specs, out_specs=out_specs, check_vma=False)
```

time: 121 us -> 97.4 us (0.80)
  Pallas kernels: 0 us -> 29.7 us
  matrix products: 28.5 us -> 0 us
  waiting for transfers between devices: 36.6 us -> 26.9 us
  blocking collectives: 8.74 us -> 0 us
  starting transfers between devices: 32.5 us -> 28.2 us
  other arithmetic: 3.88 us -> 0.63 us
  local copies, waits for them, and re-layouts: 7.78 us -> 10 us
    pallas_call x0 -> x5, Pallas kernels: none -> 29.7 us  [the longest x4 28.5 us: layer_product(): pl.pallas_call(functools.partial(layer_kernel, n, n_t, place, layer, firs...]
    dot_general x8 -> x0, matrix products: 28.5 us -> none  [body(): product = jnp.dot(normed, weights, preferred_element_type=jnp.float32)]
    all_to_all x1 -> x0, blocking collectives: 8.74 us -> none  [body(): stats = jnp.stack(merge(lax.all_to_all(stats, 'dp', 0, 0, tiled=True)))]
    unnamed x16 -> x34, local copies, waits for them, and re-layouts: 1.46 us -> 8.8 us
    ppermute x15 -> x24, waiting for transfers between devices: 26.3 us -> 20.1 us  [permute(): return lax.ppermute(a, ('dp', 'tensor'), perm)]
    all_to_all x3 -> x2, waiting for transfers between devices: 10.2 us -> 6.74 us  [the longest x1 6.74 us: body(): lax.all_to_all(acc.reshape(n_dp * n_t, 3, tok), ('dp', 'tensor'), 0, 0, t...]
    dynamic_update_slice x14 -> x0, local copies, waits for them, and re-layouts: 3.2 us -> none  [body(): lax.dynamic_update_slice_in_dim(block, piece, (j * n_dp + owner) * tok, 0)]
    all_to_all x3 -> x2, starting transfers between devices: 9.9 us -> 7.69 us  [the longest x1 5.11 us: body(): lax.all_to_all(acc.reshape(n_dp * n_t, 3, tok), ('dp', 'tensor'), 0, 0, t...]
  transfers between devices with their start and end apart: 18 -> 26, of which waited for: 8 -> 7; matrix products, arithmetic and copies ran while one was open for 28% -> 1% of each run, Pallas kernels for 0% -> 22%
where the time goes in v1:
time: 97.4 us; the launch traced here: 96.9 us
  Pallas kernels  29.7 us (30%)
  starting transfers between devices  28.2 us (29%)
  waiting for transfers between devices  26.9 us (28%)
  local copies, waits for them, and re-layouts  10 us (10%)
  between operations  1.56 us (2%)
    pallas_call x4, Pallas kernels, layer_product(): pl.pallas_call(functools.partial(layer_kernel, n, n_t, place, layer, firs...  28.5 us
    ppermute x24, starting transfers between devices, permute(): return lax.ppermute(a, ('dp', 'tensor'), perm)  20.5 us
    ppermute x24, waiting for transfers between devices, permute(): return lax.ppermute(a, ('dp', 'tensor'), perm)  20.1 us
    unnamed x34, local copies, waits for them, and re-layouts  8.8 us
    all_to_all x1, waiting for transfers between devices, body(): lax.all_to_all(acc.reshape(n_dp * n_t, 3, tok), ('dp', 'tensor'), 0, 0, t...  6.74 us
    all_to_all x1, starting transfers between devices, body(): lax.all_to_all(acc.reshape(n_dp * n_t, 3, tok), ('dp', 'tensor'), 0, 0, t...  5.11 us
    all_to_all x1, starting transfers between devices, body(): fine = lax.all_to_all(packed, ('dp', 'tensor'), 0, 0, tiled=True)  2.58 us
  transfers between devices with their start and end apart: 26, of which 7 were waited for; matrix products, arithmetic and copies ran while one was open for 1% of the time, Pallas kernels for 22%

profile of v1, /device:TPU:0, one launch (start us, length us, event | category | flops | bytes accessed | tf_op | source)
XLA Modules:
  0.0 96.9 jit_solution(8150384644257783821)
XLA Ops:
  0.6 3.0 %collective-permute-start.3 = (bf16[128,1024]{1,0:T(8,128)(2,1)}, bf16[128,1024]{1,0:T(8,128)(2,1)S(1)}, u32[]{:S(2)}, u32[]{:S(2)}) collective-permute-start(bf16[128,1024]{1,0:T(8,128)(2,1)} %refs_2_.1), channel_id=1, source_target_pairs={{0,8},{1,17},{2,10},{3,19},{4,12},{5,21},{6,14},{7,23},{8,0},{9,25... | collective-permute-start | bytes 786440 | tf_op jit(solution)/shard_map/ppermute | solution.py:39
  3.6 1.5 %collective-permute-start.4 = (bf16[128,1024]{1,0:T(8,128)(2,1)}, bf16[128,1024]{1,0:T(8,128)(2,1)S(1)}, u32[]{:S(2)}, u32[]{:S(2)}) collective-permute-start(bf16[128,1024]{1,0:T(8,128)(2,1)} %refs_2_.1), channel_id=1, source_target_pairs={{0,16},{1,9},{2,18},{3,11},{4,20},{5,13},{6,22},{7,15},{8,24},{9,1... | collective-permute-start | bytes 786440 | tf_op jit(solution)/shard_map/ppermute | solution.py:39
  5.2 1.6 %collective-permute-start = (bf16[128,1024]{1,0:T(8,128)(2,1)}, bf16[128,1024]{1,0:T(8,128)(2,1)S(1)}, u32[]{:S(2)}, u32[]{:S(2)}) collective-permute-start(bf16[128,1024]{1,0:T(8,128)(2,1)} %refs_2_.1), channel_id=1, source_target_pairs={{0,2},{1,3},{2,4},{3,5},{4,6},{5,7},{6,0},{7,1},{8,10},{9,11},{10,... | collective-permute-start | bytes 786440 | tf_op jit(solution)/shard_map/ppermute | solution.py:39
  6.7 2.2 %collective-permute-start.1 = (bf16[128,1024]{1,0:T(8,128)(2,1)}, bf16[128,1024]{1,0:T(8,128)(2,1)S(1)}, u32[]{:S(2)}, u32[]{:S(2)}) collective-permute-start(bf16[128,1024]{1,0:T(8,128)(2,1)} %refs_2_.1), channel_id=1, source_target_pairs={{0,6},{1,7},{2,0},{3,1},{4,2},{5,3},{6,4},{7,5},{8,14},{9,15},{10,... | collective-permute-start | bytes 786440 | tf_op jit(solution)/shard_map/ppermute | solution.py:39
  9.0 1.1 %shard_map.77 = f32[32,1280]{1,0:T(8,128)S(1)} custom-call(bf16[128,1024]{1,0:T(8,128)(2,1)} %refs_2_.1, f32[1,1024]{1,0:T(1,128)} %bitcast.31, s32[1,128]{1,0:T(1,128)} %bitcast.32), custom_call_target="tpu_custom_call" | custom-call | tf_op jit(solution)/shard_map/pallas_call | solution.py:241
  10.2 0.8 copy.9
  11.0 2.6 %all-to-all-start = ((f32[32,1,1280]{2,1,0:T(1,128)}), f32[32,1,1280]{2,1,0:T(1,128)S(1)}, u32[]{:S(2)}, u32[]{:S(2)}) async-start(f32[32,1,1280]{2,1,0:T(1,128)} %copy.9), calls=%async_computation | async-start | bytes 327680 | tf_op jit(solution)/shard_map/all_to_all | solution.py:281
  13.6 1.7 %collective-permute-start.14 = (bf16[128,1024]{1,0:T(8,128)(2,1)S(1)}, bf16[128,1024]{1,0:T(8,128)(2,1)S(1)}, u32[]{:S(2)}, u32[]{:S(2)}) collective-permute-start(bf16[128,1024]{1,0:T(8,128)(2,1)S(1)} %collective-permute-done.3.refs_3_), channel_id=1, source_target_pairs={{0,16},{1,9},{2,18},{3,11},{4,20},{5,13},{6,22},{7,15},{8,24},{9,1... | collective-permute-start | bytes 786440 | tf_op jit(solution)/shard_map/ppermute | solution.py:39
  15.3 1.1 %collective-permute-done = bf16[128,1024]{1,0:T(8,128)(2,1)S(1)} collective-permute-done((bf16[128,1024]{1,0:T(8,128)(2,1)}, bf16[128,1024]{1,0:T(8,128)(2,1)S(1)}, u32[]{:S(2)}, u32[]{:S(2)}) %collective-permute-start) | collective-permute-done | bytes 262176 | tf_op jit(solution)/shard_map/ppermute | solution.py:39
  16.5 4.0 %collective-permute-done.1 = bf16[128,1024]{1,0:T(8,128)(2,1)S(1)} collective-permute-done((bf16[128,1024]{1,0:T(8,128)(2,1)}, bf16[128,1024]{1,0:T(8,128)(2,1)S(1)}, u32[]{:S(2)}, u32[]{:S(2)}) %collective-permute-start.1) | collective-permute-done | bytes 262176 | tf_op jit(solution)/shard_map/ppermute | solution.py:39
  20.5 0.5 collective-permute-start.5
  20.9 0.4 collective-permute-start.6
  21.4 0.5 collective-permute-start.18
  21.9 0.7 copy-done.9
  22.6 2.7 %collective-permute-start.2 = (bf16[128,1024]{1,0:T(8,128)(2,1)}, bf16[128,1024]{1,0:T(8,128)(2,1)}, u32[]{:S(2)}, u32[]{:S(2)}) collective-permute-start(bf16[128,1024]{1,0:T(8,128)(2,1)} %refs_2_.1), channel_id=1, source_target_pairs={{0,4},{1,5},{2,6},{3,7},{4,0},{5,1},{6,2},{7,3},{8,12},{9,13},{10,... | collective-permute-start | bytes 786440 | tf_op jit(solution)/shard_map/ppermute | solution.py:39
  25.2 0.1 stack.71.refs_0_
  25.4 0.7 copy-done.11
  26.1 0.7 copy-done.13
  26.8 0.9 copy-done.2
  27.8 0.9 copy-done.4
  28.7 0.9 copy-done.6
  29.7 0.9 copy-done.8
  30.6 0.9 copy-done.10
  31.6 0.9 copy-done.12
  32.5 0.9 copy-done.14
  33.5 5.1 %shard_map.78.refs_11_ = f32[512,1152]{1,0:T(8,128)S(1)} custom-call(s32[7]{0:T(128)S(1)} %stack.71.refs_0_, f32[32,1280]{1,0:T(8,128)S(1)} %bitcast.23, bf16[128,1024]{1,0:T(8,128)(2,1)S(1)} %copy-done, bf16[128,1024]{1,0:T(8,128)(2,1)S(1)} %copy-done.2, bf16[128,1024]{1,0:T(8,128)(2,1)S(1)} %copy-done.4, bf16[128,1024]{1,0:T(8,128)(2,1)S(1)} %copy-done.8, ...), custom_call_target="tpu_custom_call" | custom-call | flops 2415919104 | bytes 4718592 | tf_op jit(solution)/shard_map/pallas_call | solution.py:210
  38.6 1.7 %collective-permute-start.19 = (bf16[256,1024]{1,0:T(8,128)(2,1)}, bf16[256,1024]{1,0:T(8,128)(2,1)}, u32[]{:S(2)}, u32[]{:S(2)}) collective-permute-start(bf16[256,1024]{1,0:T(8,128)(2,1)} %collective-permute-done.5.refs_3_), channel_id=1, source_target_pairs={{0,16},{1,9},{2,18},{3,11},{4,20},{5,13},{6,22},{7,15},{8,24},{9,1... | collective-permute-start | bytes 1572872 | tf_op jit(solution)/shard_map/ppermute | solution.py:39
  40.3 1.9 %collective-permute-start.7 = (bf16[128,1024]{1,0:T(8,128)(2,1)}, bf16[128,1024]{1,0:T(8,128)(2,1)S(1)}, u32[]{:S(2)}, u32[]{:S(2)}) collective-permute-start(bf16[128,1024]{1,0:T(8,128)(2,1)} %collective-permute-done.2.refs_2_), channel_id=1, source_target_pairs={{0,8},{1,17},{2,10},{3,19},{4,12},{5,21},{6,14},{7,23},{8,0},{9,25... | collective-permute-start | bytes 786440 | tf_op jit(solution)/shard_map/ppermute | solution.py:39
  42.2 0.3 collective-permute-start.8
  42.5 0.2 collective-permute-start.21
  42.7 7.1 %collective-permute-done.7.refs_3_ = bf16[128,1024]{1,0:T(8,128)(2,1)S(1)} collective-permute-done((bf16[128,1024]{1,0:T(8,128)(2,1)}, bf16[128,1024]{1,0:T(8,128)(2,1)S(1)}, u32[]{:S(2)}, u32[]{:S(2)}) %collective-permute-start.7) | collective-permute-done | bytes 262176 | tf_op jit(solution)/shard_map/ppermute | solution.py:39
  49.8 1.2 %collective-permute-done.19.refs_5_ = bf16[256,1024]{1,0:T(8,128)(2,1)} collective-permute-done((bf16[256,1024]{1,0:T(8,128)(2,1)}, bf16[256,1024]{1,0:T(8,128)(2,1)}, u32[]{:S(2)}, u32[]{:S(2)}) %collective-permute-start.19) | collective-permute-done | bytes 524320 | tf_op jit(solution)/shard_map/ppermute | solution.py:39
  50.9 2.8 %collective-permute-done.8.refs_4_ = bf16[128,1024]{1,0:T(8,128)(2,1)} collective-permute-done((bf16[128,1024]{1,0:T(8,128)(2,1)}, bf16[128,1024]{1,0:T(8,128)(2,1)}, u32[]{:S(2)}, u32[]{:S(2)}) %collective-permute-start.8) | collective-permute-done | bytes 262176 | tf_op jit(solution)/shard_map/ppermute | solution.py:39
  53.8 1.7 %collective-permute-start.9 = (bf16[128,1024]{1,0:T(8,128)(2,1)S(1)}, bf16[128,1024]{1,0:T(8,128)(2,1)}, u32[]{:S(2)}, u32[]{:S(2)}) collective-permute-start(bf16[128,1024]{1,0:T(8,128)(2,1)S(1)} %collective-permute-done.7.refs_3_), channel_id=1, source_target_pairs={{0,16},{1,9},{2,18},{3,11},{4,20},{5,13},{6,22},{7,15},{8,24},{9,1... | collective-permute-start | bytes 786440 | tf_op jit(solution)/shard_map/ppermute | solution.py:39
  55.4 0.1 stack.73.refs_0_
  55.5 0.1 stack.69.refs_0_
  55.6 0.1 stack.67.refs_0_
  55.7 0.1 collective-permute-start.10
  55.7 0.5 collective-permute-start.11
  56.2 0.1 collective-permute-start.12
  56.3 3.9 %collective-permute-done.9.refs_5_ = bf16[128,1024]{1,0:T(8,128)(2,1)} collective-permute-done((bf16[128,1024]{1,0:T(8,128)(2,1)S(1)}, bf16[128,1024]{1,0:T(8,128)(2,1)}, u32[]{:S(2)}, u32[]{:S(2)}) %collective-permute-start.9) | collective-permute-done | bytes 262176 | tf_op jit(solution)/shard_map/ppermute | solution.py:39
  60.2 7.4 %shard_map.79.refs_11_ = f32[512,1152]{1,0:T(8,128)S(1)} custom-call(s32[7]{0:T(128)S(1)} %stack.73.refs_0_, f32[32,1280]{1,0:T(8,128)S(1)} %bitcast.24, bf16[256,1024]{1,0:T(8,128)(2,1)S(1)} %constant_dynamic-update-slice_fusion.refs_2_, bf16[256,1024]{1,0:T(8,128)(2,1)} %collective-permute-done.5.refs_3_, ...), custom_call_target="tpu_custom_call" | custom-call | flops 2415919104 | bytes 4718592 | tf_op jit(solution)/shard_map/pallas_call | solution.py:210
  67.6 8.0 %shard_map.80.refs_11_ = f32[512,1152]{1,0:T(8,128)S(1)} custom-call(s32[7]{0:T(128)S(1)} %stack.69.refs_0_, f32[32,1280]{1,0:T(8,128)S(1)} %bitcast.25, bf16[256,1024]{1,0:T(8,128)(2,1)S(1)} %constant_dynamic-update-slice_fusion.refs_2_, bf16[256,1024]{1,0:T(8,128)(2,1)} %collective-permute-done.5.refs_3_, ...), custom_call_target="tpu_custom_call" | custom-call | flops 2415919104 | bytes 4718592 | tf_op jit(solution)/shard_map/pallas_call | solution.py:210
  75.7 8.1 %shard_map.81 = f32[4,8,3,128]{3,2,1,0:T(4,128)} custom-call(s32[7]{0:T(128)S(1)} %stack.67.refs_0_, f32[32,1280]{1,0:T(8,128)S(1)} %bitcast.26, bf16[128,1024]{1,0:T(8,128)(2,1)} %collective-permute-done.2.refs_2_, bf16[128,1024]{1,0:T(8,128)(2,1)S(1)} %collective-permute-done.7.refs_3_, bf16[128,1024]{1,0:T(8,128)(2,1)} %collective-permute-done.8.refs_4_, ...), custom_call_target="tpu_custom_call" | custom-call | flops 2415919104 | bytes 4718592 | tf_op jit(solution)/shard_map/pallas_call | solution.py:210
  83.8 5.1 %all-to-all-start.1 = ((f32[32,3,128]{2,1,0:T(4,128)}), f32[32,3,128]{2,1,0:T(4,128)S(1)}, u32[]{:S(2)}, u32[]{:S(2)}) async-start(f32[32,3,128]{2,1,0:T(4,128)} %bitcast.14), calls=%async_computation.1 | async-start | bytes 131072 | tf_op jit(solution)/shard_map/all_to_all | solution.py:299
  89.5 6.7 %all-to-all-done.1 = f32[32,3,128]{2,1,0:T(4,128)S(1)} async-done(((f32[32,3,128]{2,1,0:T(4,128)}), f32[32,3,128]{2,1,0:T(4,128)S(1)}, u32[]{:S(2)}, u32[]{:S(2)}) %all-to-all-start.1) | async-done | bytes 49184 | tf_op jit(solution)/shard_map/all_to_all | solution.py:299
  96.3 0.1 slice_reduce_fusion
  96.4 0.5 compare_select_fusion
  (53 shorter events, 0.2 us)
Async XLA Ops:
  0.6 26.2 %copy-start = (bf16[128,1024]{1,0:T(8,128)(2,1)S(1)}, bf16[128,1024]{1,0:T(8,128)(2,1)}, u32[]{:S(2)}) copy-start(bf16[128,1024]{1,0:T(8,128)(2,1)} %refs_2_.1) | copy-start | bytes 786436
  0.6 12.9 %collective-permute-start.3 = (bf16[128,1024]{1,0:T(8,128)(2,1)}, bf16[128,1024]{1,0:T(8,128)(2,1)S(1)}, u32[]{:S(2)}, u32[]{:S(2)}) collective-permute-start(bf16[128,1024]{1,0:T(8,128)(2,1)} %refs_2_.1), channel_id=1, source_target_pairs={{0,8},{1,17},{2,10},{3,19},{4,12},{5,21},{6,14},{7,23},{8,0},{9,25... | collective-permute-start | bytes 786440 | tf_op jit(solution)/shard_map/ppermute | solution.py:39
  3.6 10.0 %collective-permute-start.4 = (bf16[128,1024]{1,0:T(8,128)(2,1)}, bf16[128,1024]{1,0:T(8,128)(2,1)S(1)}, u32[]{:S(2)}, u32[]{:S(2)}) collective-permute-start(bf16[128,1024]{1,0:T(8,128)(2,1)} %refs_2_.1), channel_id=1, source_target_pairs={{0,16},{1,9},{2,18},{3,11},{4,20},{5,13},{6,22},{7,15},{8,24},{9,1... | collective-permute-start | bytes 786440 | tf_op jit(solution)/shard_map/ppermute | solution.py:39
  5.2 11.3 %collective-permute-start = (bf16[128,1024]{1,0:T(8,128)(2,1)}, bf16[128,1024]{1,0:T(8,128)(2,1)S(1)}, u32[]{:S(2)}, u32[]{:S(2)}) collective-permute-start(bf16[128,1024]{1,0:T(8,128)(2,1)} %refs_2_.1), channel_id=1, source_target_pairs={{0,2},{1,3},{2,4},{3,5},{4,6},{5,7},{6,0},{7,1},{8,10},{9,11},{10,... | collective-permute-start | bytes 786440 | tf_op jit(solution)/shard_map/ppermute | solution.py:39
  6.7 13.7 %collective-permute-start.1 = (bf16[128,1024]{1,0:T(8,128)(2,1)}, bf16[128,1024]{1,0:T(8,128)(2,1)S(1)}, u32[]{:S(2)}, u32[]{:S(2)}) collective-permute-start(bf16[128,1024]{1,0:T(8,128)(2,1)} %refs_2_.1), channel_id=1, source_target_pairs={{0,6},{1,7},{2,0},{3,1},{4,2},{5,3},{6,4},{7,5},{8,14},{9,15},{10,... | collective-permute-start | bytes 786440 | tf_op jit(solution)/shard_map/ppermute | solution.py:39
  9.0 12.4 %collective-permute-start.15 = (bf16[128,1024]{1,0:T(8,128)(2,1)}, bf16[128,1024]{1,0:T(8,128)(2,1)S(1)}, u32[]{:S(2)}, u32[]{:S(2)}) collective-permute-start(bf16[128,1024]{1,0:T(8,128)(2,1)} %refs_2_.1), channel_id=1, source_target_pairs={{0,1},{1,0},{2,3},{3,2},{4,5},{5,4},{6,7},{7,6},{8,9},{9,8},{10,11... | collective-permute-start | bytes 786440 | tf_op jit(solution)/shard_map/ppermute | solution.py:39
  11.0 14.3 %all-to-all-start = ((f32[32,1,1280]{2,1,0:T(1,128)}), f32[32,1,1280]{2,1,0:T(1,128)S(1)}, u32[]{:S(2)}, u32[]{:S(2)}) async-start(f32[32,1,1280]{2,1,0:T(1,128)} %copy.9), calls=%async_computation | async-start | bytes 327680 | tf_op jit(solution)/shard_map/all_to_all | solution.py:281
  13.6 12.5 %copy-start.1 = (bf16[128,1024]{1,0:T(8,128)(2,1)}, bf16[128,1024]{1,0:T(8,128)(2,1)S(1)}, u32[]{:S(2)}) copy-start(bf16[128,1024]{1,0:T(8,128)(2,1)S(1)} %collective-permute-done.3.refs_3_) | copy-start | bytes 786436
  13.6 12.5 %copy-start.3 = (bf16[128,1024]{1,0:T(8,128)(2,1)}, bf16[128,1024]{1,0:T(8,128)(2,1)S(1)}, u32[]{:S(2)}) copy-start(bf16[128,1024]{1,0:T(8,128)(2,1)S(1)} %collective-permute-done.4.refs_4_) | copy-start | bytes 786436
  13.6 7.7 %collective-permute-start.14 = (bf16[128,1024]{1,0:T(8,128)(2,1)S(1)}, bf16[128,1024]{1,0:T(8,128)(2,1)S(1)}, u32[]{:S(2)}, u32[]{:S(2)}) collective-permute-start(bf16[128,1024]{1,0:T(8,128)(2,1)S(1)} %collective-permute-done.3.refs_3_), channel_id=1, source_target_pairs={{0,16},{1,9},{2,18},{3,11},{4,20},{5,13},{6,22},{7,15},{8,24},{9,1... | collective-permute-start | bytes 786440 | tf_op jit(solution)/shard_map/ppermute | solution.py:39
  16.5 5.4 %collective-permute-start.16 = (bf16[128,1024]{1,0:T(8,128)(2,1)S(1)}, bf16[128,1024]{1,0:T(8,128)(2,1)S(1)}, u32[]{:S(2)}, u32[]{:S(2)}) collective-permute-start(bf16[128,1024]{1,0:T(8,128)(2,1)S(1)} %collective-permute-done.3.refs_3_), channel_id=1, source_target_pairs={{0,1},{1,0},{2,3},{3,2},{4,5},{5,4},{6,7},{7,6},{8,9},{9,8},{10,11... | collective-permute-start | bytes 786440 | tf_op jit(solution)/shard_map/ppermute | solution.py:39
  20.5 18.1 %collective-permute-start.5 = (bf16[256,1024]{1,0:T(8,128)(2,1)S(1)}, bf16[256,1024]{1,0:T(8,128)(2,1)}, u32[]{:S(2)}, u32[]{:S(2)}) collective-permute-start(bf16[256,1024]{1,0:T(8,128)(2,1)S(1)} %constant_dynamic-update-slice_fusion.refs_2_), channel_id=1, source_target_pairs={{0,8},{1,17},{2,10},{3,19},{4,12},{5,21},{6,14},{7,23},{8,0},{9,25... | collective-permute-start | bytes 1572872 | tf_op jit(solution)/shard_map/ppermute | solution.py:39
  20.9 17.6 %collective-permute-start.6 = (bf16[256,1024]{1,0:T(8,128)(2,1)S(1)}, bf16[256,1024]{1,0:T(8,128)(2,1)}, u32[]{:S(2)}, u32[]{:S(2)}) collective-permute-start(bf16[256,1024]{1,0:T(8,128)(2,1)S(1)} %constant_dynamic-update-slice_fusion.refs_2_), channel_id=1, source_target_pairs={{0,16},{1,9},{2,18},{3,11},{4,20},{5,13},{6,22},{7,15},{8,24},{9,1... | collective-permute-start | bytes 1572872 | tf_op jit(solution)/shard_map/ppermute | solution.py:39
  21.3 4.7 %copy-start.5 = (bf16[128,1024]{1,0:T(8,128)(2,1)}, bf16[128,1024]{1,0:T(8,128)(2,1)S(1)}, u32[]{:S(2)}) copy-start(bf16[128,1024]{1,0:T(8,128)(2,1)S(1)} %collective-permute-done.15.refs_6_) | copy-start | bytes 786436
  21.4 4.0 %collective-permute-start.17 = (bf16[128,1024]{1,0:T(8,128)(2,1)S(1)}, bf16[128,1024]{1,0:T(8,128)(2,1)S(1)}, u32[]{:S(2)}, u32[]{:S(2)}) collective-permute-start(bf16[128,1024]{1,0:T(8,128)(2,1)S(1)} %collective-permute-done.4.refs_4_), channel_id=1, source_target_pairs={{0,1},{1,0},{2,3},{3,2},{4,5},{5,4},{6,7},{7,6},{8,9},{9,8},{10,11... | collective-permute-start | bytes 786440 | tf_op jit(solution)/shard_map/ppermute | solution.py:39
  21.4 4.7 %copy-start.7 = (bf16[128,1024]{1,0:T(8,128)(2,1)}, bf16[128,1024]{1,0:T(8,128)(2,1)S(1)}, u32[]{:S(2)}) copy-start(bf16[128,1024]{1,0:T(8,128)(2,1)S(1)} %collective-permute-done.14.refs_5_) | copy-start | bytes 786436
  21.4 4.7 %collective-permute-start.18 = (bf16[128,1024]{1,0:T(8,128)(2,1)S(1)}, bf16[128,1024]{1,0:T(8,128)(2,1)S(1)}, u32[]{:S(2)}, u32[]{:S(2)}) collective-permute-start(bf16[128,1024]{1,0:T(8,128)(2,1)S(1)} %collective-permute-done.14.refs_5_), channel_id=1, source_target_pairs={{0,1},{1,0},{2,3},{3,2},{4,5},{5,4},{6,7},{7,6},{8,9},{9,8},{10,11... | collective-permute-start | bytes 786440 | tf_op jit(solution)/shard_map/ppermute | solution.py:39
  21.9 0.7 copy-start.9
  22.6 16.0 %collective-permute-start.2 = (bf16[128,1024]{1,0:T(8,128)(2,1)}, bf16[128,1024]{1,0:T(8,128)(2,1)}, u32[]{:S(2)}, u32[]{:S(2)}) collective-permute-start(bf16[128,1024]{1,0:T(8,128)(2,1)} %refs_2_.1), channel_id=1, source_target_pairs={{0,4},{1,5},{2,6},{3,7},{4,0},{5,1},{6,2},{7,3},{8,12},{9,13},{10,... | collective-permute-start | bytes 786440 | tf_op jit(solution)/shard_map/ppermute | solution.py:39
  25.4 0.7 copy-start.11
  26.1 0.7 copy-start.13
  26.8 1.0 copy-start.2
  27.8 0.9 copy-start.4
  28.7 0.9 copy-start.6
  29.7 0.9 copy-start.8
  30.6 0.9 copy-start.10
  31.6 0.9 copy-start.12
  32.5 0.9 copy-start.14
  38.6 12.4 %collective-permute-start.19 = (bf16[256,1024]{1,0:T(8,128)(2,1)}, bf16[256,1024]{1,0:T(8,128)(2,1)}, u32[]{:S(2)}, u32[]{:S(2)}) collective-permute-start(bf16[256,1024]{1,0:T(8,128)(2,1)} %collective-permute-done.5.refs_3_), channel_id=1, source_target_pairs={{0,16},{1,9},{2,18},{3,11},{4,20},{5,13},{6,22},{7,15},{8,24},{9,1... | collective-permute-start | bytes 1572872 | tf_op jit(solution)/shard_map/ppermute | solution.py:39
  40.3 9.5 %collective-permute-start.7 = (bf16[128,1024]{1,0:T(8,128)(2,1)}, bf16[128,1024]{1,0:T(8,128)(2,1)S(1)}, u32[]{:S(2)}, u32[]{:S(2)}) collective-permute-start(bf16[128,1024]{1,0:T(8,128)(2,1)} %collective-permute-done.2.refs_2_), channel_id=1, source_target_pairs={{0,8},{1,17},{2,10},{3,19},{4,12},{5,21},{6,14},{7,23},{8,0},{9,25... | collective-permute-start | bytes 786440 | tf_op jit(solution)/shard_map/ppermute | solution.py:39
  42.2 13.5 %collective-permute-start.20 = (bf16[256,1024]{1,0:T(8,128)(2,1)S(1)}, bf16[256,1024]{1,0:T(8,128)(2,1)}, u32[]{:S(2)}, u32[]{:S(2)}) collective-permute-start(bf16[256,1024]{1,0:T(8,128)(2,1)S(1)} %constant_dynamic-update-slice_fusion.refs_2_), channel_id=1, source_target_pairs={{0,1},{1,0},{2,3},{3,2},{4,5},{5,4},{6,7},{7,6},{8,9},{9,8},{10,11... | collective-permute-start | bytes 1572872 | tf_op jit(solution)/shard_map/ppermute | solution.py:39
  42.2 11.6 %collective-permute-start.8 = (bf16[128,1024]{1,0:T(8,128)(2,1)}, bf16[128,1024]{1,0:T(8,128)(2,1)}, u32[]{:S(2)}, u32[]{:S(2)}) collective-permute-start(bf16[128,1024]{1,0:T(8,128)(2,1)} %collective-permute-done.2.refs_2_), channel_id=1, source_target_pairs={{0,16},{1,9},{2,18},{3,11},{4,20},{5,13},{6,22},{7,15},{8,24},{9,1... | collective-permute-start | bytes 786440 | tf_op jit(solution)/shard_map/ppermute | solution.py:39
  42.5 13.2 %collective-permute-start.21 = (bf16[256,1024]{1,0:T(8,128)(2,1)}, bf16[256,1024]{1,0:T(8,128)(2,1)}, u32[]{:S(2)}, u32[]{:S(2)}) collective-permute-start(bf16[256,1024]{1,0:T(8,128)(2,1)} %collective-permute-done.5.refs_3_), channel_id=1, source_target_pairs={{0,1},{1,0},{2,3},{3,2},{4,5},{5,4},{6,7},{7,6},{8,9},{9,8},{10,11... | collective-permute-start | bytes 1572872 | tf_op jit(solution)/shard_map/ppermute | solution.py:39
  49.7 6.5 %collective-permute-start.22 = (bf16[256,1024]{1,0:T(8,128)(2,1)}, bf16[256,1024]{1,0:T(8,128)(2,1)}, u32[]{:S(2)}, u32[]{:S(2)}) collective-permute-start(bf16[256,1024]{1,0:T(8,128)(2,1)} %collective-permute-done.6.refs_4_), channel_id=1, source_target_pairs={{0,1},{1,0},{2,3},{3,2},{4,5},{5,4},{6,7},{7,6},{8,9},{9,8},{10,11... | collective-permute-start | bytes 1572872 | tf_op jit(solution)/shard_map/ppermute | solution.py:39
  50.9 9.3 %collective-permute-start.23 = (bf16[256,1024]{1,0:T(8,128)(2,1)}, bf16[256,1024]{1,0:T(8,128)(2,1)}, u32[]{:S(2)}, u32[]{:S(2)}) collective-permute-start(bf16[256,1024]{1,0:T(8,128)(2,1)} %collective-permute-done.19.refs_5_), channel_id=1, source_target_pairs={{0,1},{1,0},{2,3},{3,2},{4,5},{5,4},{6,7},{7,6},{8,9},{9,8},{10,11... | collective-permute-start | bytes 1572872 | tf_op jit(solution)/shard_map/ppermute | solution.py:39
  53.8 6.5 %collective-permute-start.9 = (bf16[128,1024]{1,0:T(8,128)(2,1)S(1)}, bf16[128,1024]{1,0:T(8,128)(2,1)}, u32[]{:S(2)}, u32[]{:S(2)}) collective-permute-start(bf16[128,1024]{1,0:T(8,128)(2,1)S(1)} %collective-permute-done.7.refs_3_), channel_id=1, source_target_pairs={{0,16},{1,9},{2,18},{3,11},{4,20},{5,13},{6,22},{7,15},{8,24},{9,1... | collective-permute-start | bytes 786440 | tf_op jit(solution)/shard_map/ppermute | solution.py:39
  55.7 20.0 %collective-permute-start.10 = (bf16[128,1024]{1,0:T(8,128)(2,1)}, bf16[128,1024]{1,0:T(8,128)(2,1)S(1)}, u32[]{:S(2)}, u32[]{:S(2)}) collective-permute-start(bf16[128,1024]{1,0:T(8,128)(2,1)} %collective-permute-done.2.refs_2_), channel_id=1, source_target_pairs={{0,1},{1,0},{2,3},{3,2},{4,5},{5,4},{6,7},{7,6},{8,9},{9,8},{10,11... | collective-permute-start | bytes 786440 | tf_op jit(solution)/shard_map/ppermute | solution.py:39
  55.7 20.0 %collective-permute-start.11 = (bf16[128,1024]{1,0:T(8,128)(2,1)S(1)}, bf16[128,1024]{1,0:T(8,128)(2,1)S(1)}, u32[]{:S(2)}, u32[]{:S(2)}) collective-permute-start(bf16[128,1024]{1,0:T(8,128)(2,1)S(1)} %collective-permute-done.7.refs_3_), channel_id=1, source_target_pairs={{0,1},{1,0},{2,3},{3,2},{4,5},{5,4},{6,7},{7,6},{8,9},{9,8},{10,11... | collective-permute-start | bytes 786440 | tf_op jit(solution)/shard_map/ppermute | solution.py:39
  56.2 19.5 %collective-permute-start.12 = (bf16[128,1024]{1,0:T(8,128)(2,1)}, bf16[128,1024]{1,0:T(8,128)(2,1)S(1)}, u32[]{:S(2)}, u32[]{:S(2)}) collective-permute-start(bf16[128,1024]{1,0:T(8,128)(2,1)} %collective-permute-done.8.refs_4_), channel_id=1, source_target_pairs={{0,1},{1,0},{2,3},{3,2},{4,5},{5,4},{6,7},{7,6},{8,9},{9,8},{10,11... | collective-permute-start | bytes 786440 | tf_op jit(solution)/shard_map/ppermute | solution.py:39
  60.2 15.5 %collective-permute-start.13 = (bf16[128,1024]{1,0:T(8,128)(2,1)}, bf16[128,1024]{1,0:T(8,128)(2,1)S(1)}, u32[]{:S(2)}, u32[]{:S(2)}) collective-permute-start(bf16[128,1024]{1,0:T(8,128)(2,1)} %collective-permute-done.9.refs_5_), channel_id=1, source_target_pairs={{0,1},{1,0},{2,3},{3,2},{4,5},{5,4},{6,7},{7,6},{8,9},{9,8},{10,11... | collective-permute-start | bytes 786440 | tf_op jit(solution)/shard_map/ppermute | solution.py:39
  75.7 20.7 %copy-start.15 = (f32[128]{0:T(128)S(1)}, f32[128]{0:T(128)}, u32[]{:S(2)}) copy-start(f32[128]{0:T(128)} %param.10) | copy-start | bytes 1540
  83.8 12.5 %all-to-all-start.1 = ((f32[32,3,128]{2,1,0:T(4,128)}), f32[32,3,128]{2,1,0:T(4,128)S(1)}, u32[]{:S(2)}, u32[]{:S(2)}) async-start(f32[32,3,128]{2,1,0:T(4,128)} %bitcast.14), calls=%async_computation.1 | async-start | bytes 131072 | tf_op jit(solution)/shard_map/all_to_all | solution.py:299

commit v2 on v1

--- a/solution.py
+++ b/solution.py
@@ -10,7 +10,7 @@
 D = 8192
 CORES = 2
 X_ONLY, Y_ONLY = (0, 1), (1, 0)
-VMEM_LIMIT = 24 * 1024 * 1024
+VMEM_LIMIT = 30 * 1024 * 1024
 SMALL_LIMIT = 6 * 1024 * 1024
 TILES = (256, 384)
 
@@ -110,68 +110,88 @@
     return list(zip(cuts, [*cuts[1:], vocab], strict=True))
 
 
-def layer_kernel(n, n_t, place, layer, first, last, *refs):
+def group_kernel(n, n_t, place, size, first, last, *refs):
     refs = list(refs)
     start_ref, fine_ref = refs.pop(0), refs.pop(0)
     blocks = [refs.pop(0) for _ in range(CORES * n)]
     head_ref = refs.pop(0)
     acc_ref = None if first else refs.pop(0)
-    out_ref, raw, rows, weights, raw_sem, head_sem = refs[:6]
-    acc = refs[6] if last else out_ref
-    feat = raw.shape[2]
-    tok = raw.shape[1] // n
-    vocab = weights.shape[1]
-    z_from, c_me, base = start_ref[0], start_ref[1], start_ref[2]
-    owners = [start_ref[3 + k] for k in range(n)]
-
-    offset = pl.multiple_of(z_from * (CORES * feat), CORES * feat)
+    out_ref, raw, rows, weights, acc, fine, raw_sem, head_sem, acc_sem, fine_sem = refs
+    feat = raw.shape[3]
+    tok = raw.shape[2] // n
+    vocab = weights.shape[2]
     tiles = column_tiles(vocab)
-    head_copies = [
-        pltpu.make_async_copy(
-            head_ref.at[pl.ds(offset, CORES * feat), pl.ds(lo, hi - lo)],
-            weights.at[:, pl.ds(lo, hi - lo)],
-            head_sem.at[i],
+    c_me, base = start_ref[size], start_ref[size + 1]
+    owners = [start_ref[size + 2 + k] for k in range(n)]
+
+    fine_copy = pltpu.make_async_copy(fine_ref, fine, fine_sem)
+    fine_copy.start()
+    head_copies, block_copies = [], []
+    for j in range(size):
+        offset = pl.multiple_of(start_ref[j] * (CORES * feat), CORES * feat)
+        head_copies.append(
+            [
+                pltpu.make_async_copy(
+                    head_ref.at[pl.ds(offset, CORES * feat), pl.ds(lo, hi - lo)],
+                    weights.at[j, :, pl.ds(lo, hi - lo)],
+                    head_sem.at[j, i],
+                )
+                for i, (lo, hi) in enumerate(tiles)
+            ]
         )
-        for i, (lo, hi) in enumerate(tiles)
-    ]
-    block_copies = []
-    for c in range(CORES):
-        for k in range(n):
-            spot = place[k] if c else k
-            block_copies.append(
+        block_copies.append(
+            [
                 pltpu.make_async_copy(
-                    blocks[c * n + k].at[pl.ds(layer * tok, tok)],
-                    raw.at[c, pl.ds(spot * tok, tok)],
-                    raw_sem.at[c * n + k],
+                    blocks[c * n + k].at[pl.ds(j * tok, tok)],
+                    raw.at[j, c, pl.ds((place[k] if c else k) * tok, tok)],
+                    raw_sem.at[j, c * n + k],
                 )
-            )
-    head_copies[0].start()
-    for copy in block_copies:
-        copy.start()
-    for copy in head_copies[1:]:
-        copy.start()
-
-    def peer_rows(k):
-        return pl.ds(pl.multiple_of(owners[k] * n_t, n_t), n_t)
-
+                for c in range(CORES)
+                for k in range(n)
+            ]
+        )
+        head_copies[j][0].start()
+        for copy in block_copies[j]:
+            copy.start()
+        for copy in head_copies[j][1:]:
+            copy.start()
+        if j == 0 and not first:
+            acc_copy = pltpu.make_async_copy(acc_ref, acc, acc_sem.at[len(tiles)])
+            acc_copy.start()
+
+    def peers(k):
+        return pl.ds(owners[k] * n_t, n_t)
+
+    fine_copy.wait()
     scales = []
     for k in range(n):
-        sums = jnp.sum(fine_ref[peer_rows(k), feat : feat + tok], axis=0, keepdims=True)
+        sums = jnp.sum(fine[peers(k), :, feat : feat + tok], axis=0)
         scales.append(to_column(lax.rsqrt(sums / D + 1e-06)))
-    for c in range(CORES):
-        core = 1 - c_me if c else c_me
-        gain = fine_ref[pl.ds(z_from * CORES + core, 1), :feat]
-        columns = pl.ds(pl.multiple_of(core * feat, feat), feat)
-        for k in range(n):
-            block_copies[c * n + k].wait()
-        for k in range(n):
-            here = slice(k * tok, (k + 1) * tok)
-            part = raw[c, here, :].astype(jnp.float32) * scales[k] * gain
-            rows[here, columns] = part.astype(jnp.bfloat16)
-    for copy, (lo, hi) in zip(head_copies, tiles, strict=True):
+    out_copies = []
+    for j in range(size):
+        for c in range(CORES):
+            core = 1 - c_me if c else c_me
+            gain = fine[start_ref[j] * CORES + core, :, :feat]
+            columns = pl.ds(pl.multiple_of(core * feat, feat), feat)
+            for k in range(n):
+                block_copies[j][c * n + k].wait()
+            for k in range(n):
+                here = slice(k * tok, (k + 1) * tok)
+                part = raw[j, c, here, :].astype(jnp.float32) * scales[k] * gain
+                rows[here, columns] = part.astype(jnp.bfloat16)
+        for i, (lo, hi) in enumerate(tiles):
+            head_copies[j][i].wait()
+            product = jnp.dot(rows[...], weights[j, :, lo:hi], preferred_element_type=jnp.float32)
+            if j == 0 and i == 0 and not first:
+                acc_copy.wait()
+            acc[:, lo:hi] = product if first and j == 0 else acc[:, lo:hi] + product
+            if j == size - 1 and not last:
+                here = pl.ds(lo, hi - lo)
+                copy = pltpu.make_async_copy(acc.at[:, here], out_ref.at[:, here], acc_sem.at[i])
+                copy.start()
+                out_copies.append(copy)
+    for copy in out_copies:
         copy.wait()
-        product = jnp.dot(rows[...], weights[:, lo:hi], preferred_element_type=jnp.float32)
-        acc[:, lo:hi] = product if first else acc_ref[:, lo:hi] + product
     if not last:
         return
     for b in range(n):
@@ -179,7 +199,7 @@
         top = jnp.max(logits, axis=1, keepdims=True)
         total = jnp.sum(jnp.exp(logits - top), axis=1, keepdims=True)
         entry = lax.broadcasted_iota(jnp.int32, logits.shape, 1) + base
-        target = fine_ref[peer_rows(b), feat + tok : feat + 2 * tok][0:1, :]
+        target = fine[owners[b] * n_t, :, feat + tok : feat + 2 * tok]
         target = to_column(target).astype(jnp.int32)
         pick = jnp.sum(jnp.where(entry == target, logits, 0.0), axis=1, keepdims=True)
         for peer in range(n_t):
@@ -188,7 +208,7 @@
             out_ref[owners[b], peer, 2:3, :] = to_row(pick)
 
 
-def layer_product(tok, n_t, starts, fine, blocks, layer, place, head, acc, last):
+def group_product(tok, n_t, starts, size, fine, blocks, place, head, acc, last):
     n = len(place)
     feat = blocks[0].shape[1]
     vocab = head.shape[1]
@@ -196,26 +216,29 @@
     first = acc is None
     logits = jax.ShapeDtypeStruct((n * tok, vocab), jnp.float32)
     operands = [starts, fine, *blocks, far(head)] + ([] if first else [acc])
-    specs = [pl.BlockSpec(memory_space=pltpu.SMEM), vmem] + [whole] * (len(blocks) + 1) + [vmem] * (not first)
+    specs = [pl.BlockSpec(memory_space=pltpu.SMEM)] + [whole] * (len(operands) - 1)
+    tiles = len(column_tiles(vocab))
     scratch = [
-        pltpu.VMEM((CORES, n * tok, feat), jnp.bfloat16),
+        pltpu.VMEM((size, CORES, n * tok, feat), jnp.bfloat16),
         pltpu.VMEM((n * tok, CORES * feat), jnp.bfloat16),
-        pltpu.VMEM((CORES * feat, vocab), jnp.bfloat16),
-        pltpu.SemaphoreType.DMA((CORES * n,)),
-        pltpu.SemaphoreType.DMA((len(column_tiles(vocab)),)),
+        pltpu.VMEM((size, CORES * feat, vocab), jnp.bfloat16),
+        pltpu.VMEM(logits.shape, jnp.float32),
+        pltpu.VMEM(fine.shape, fine.dtype),
+        pltpu.SemaphoreType.DMA((size, CORES * n)),
+        pltpu.SemaphoreType.DMA((size, tiles)),
+        pltpu.SemaphoreType.DMA((tiles + 1,)),
+        pltpu.SemaphoreType.DMA,
     ]
-    if last:
-        scratch.append(pltpu.VMEM(logits.shape, jnp.float32))
-    work = 2 * n * tok * CORES * feat * vocab
+    work = 2 * n * tok * CORES * feat * vocab * size
     return pl.pallas_call(
-        functools.partial(layer_kernel, n, n_t, place, layer, first, last),
+        functools.partial(group_kernel, n, n_t, place, size, first, last),
         out_shape=jax.ShapeDtypeStruct((n, n_t, 3, tok), jnp.float32) if last else logits,
         in_specs=specs,
-        out_specs=vmem,
+        out_specs=vmem if last else whole,
         scratch_shapes=scratch,
         compiler_params=pltpu.CompilerParams(vmem_limit_bytes=VMEM_LIMIT),
         cost_estimate=pl.CostEstimate(
-            flops=work, bytes_accessed=2 * CORES * feat * vocab, transcendentals=0
+            flops=work, bytes_accessed=2 * CORES * feat * vocab * size, transcendentals=0
         ),
     )(*operands)
 
@@ -231,16 +254,17 @@
     values = raw[...].astype(jnp.float32)
     sums = to_row(jnp.sum(values * values, axis=1, keepdims=True))
     peers = out_ref.shape[0]
-    out_ref[:, :feat] = jnp.broadcast_to(gain[...], (peers, feat))
-    out_ref[:, feat : feat + tok] = jnp.broadcast_to(sums, (peers, tok))
-    out_ref[:, feat + tok :] = jnp.broadcast_to(target[...].astype(jnp.float32), (peers, tok))
+    for peer in range(peers):
+        out_ref[peer, :, :feat] = gain[...]
+        out_ref[peer, :, feat : feat + tok] = sums
+        out_ref[peer, :, feat + tok :] = target[...].astype(jnp.float32)
 
 
 def squares(hidden, gain, targets, peers):
     tok, feat = hidden.shape
     return pl.pallas_call(
         squares_kernel,
-        out_shape=jax.ShapeDtypeStruct((peers, feat + 2 * tok), jnp.float32),
+        out_shape=jax.ShapeDtypeStruct((peers, 1, feat + 2 * tok), jnp.float32),
         in_specs=[pl.BlockSpec(memory_space=pltpu.HBM)] * 3,
         out_specs=pl.BlockSpec(memory_space=pltpu.VMEM),
         scratch_shapes=[
@@ -285,16 +309,19 @@
     acc = None
     for at, group in enumerate(groups):
         final = at == len(groups) - 1
-        held = [] if final or not at else [layers[dz] for dz in groups[at + 1]]
+        middle = at and not final
+        own = grid.sibling(reached[at][0, 0])
+        held = [layers[dz] for dz in groups[at + 1]] + [own] if middle else []
         spread = grid.fill(dict(reached[at]), *([acc] if at == 1 else []), *held)
-        blocks = spread + [grid.sibling(a) for a in spread]
-        following = [] if final or not at else list(reached[at + 1].values())
-        for layer, dz in enumerate(group):
-            starts = jnp.stack([(z_me - dz) % depth, c_me, vocab_start] + owners)
-            if layer == len(group) - 1:
-                starts = after(starts, *following)
-            last = final and layer == len(group) - 1
-            acc = layer_product(tok, n_t, starts, fine, blocks, layer, place, head, acc, last)
+        others = [own] + [grid.sibling(after(a, spread[-1]) if middle else a) for a in spread[1:-1]]
+        others.append(grid.sibling(after(spread[-1], acc) if final else spread[-1]))
+        blocks = spread + others
+        if not at:
+            blocks = [far(a) for a in blocks]
+        starts = jnp.stack([(z_me - dz) % depth for dz in group] + [c_me, vocab_start] + owners)
+        if middle:
+            starts = after(starts, *reached[at + 1].values())
+        acc = group_product(tok, n_t, starts, len(group), fine, blocks, place, head, acc, final)
 
     parts = lax.all_to_all(acc.reshape(n_dp * n_t, 3, tok), ("dp", "tensor"), 0, 0, tiled=True)
     top = jnp.max(parts[:, 0], axis=0)

time: 97.4 us -> 98 us (level)
  local copies, waits for them, and re-layouts: 10 us -> 3.4 us
  waiting for transfers between devices: 26.9 us -> 31.3 us
  starting transfers between devices: 28.2 us -> 31.5 us
    unnamed x34 -> x19, local copies, waits for them, and re-layouts: 8.8 us -> 3.13 us
    all_to_all x1, starting transfers between devices: 2.58 us -> 5.79 us  [body(): fine = lax.all_to_all(packed, ('dp', 'tensor'), 0, 0, tiled=True)]
    ppermute x24, waiting for transfers between devices: 20.1 us -> 23 us  [permute(): return lax.ppermute(a, ('dp', 'tensor'), perm)]
    ppermute x24, starting transfers between devices: 20.5 us -> 22.1 us  [permute(): return lax.ppermute(a, ('dp', 'tensor'), perm)]
    all_to_all x1, waiting for transfers between devices: 0.01 us -> 1.51 us  [body(): fine = lax.all_to_all(packed, ('dp', 'tensor'), 0, 0, tiled=True)]
    all_to_all x1, starting transfers between devices: 5.11 us -> 3.64 us  [body(): lax.all_to_all(acc.reshape(n_dp * n_t, 3, tok), ('dp', 'tensor'), 0, 0, t...]
    pallas_call x5 -> x4, Pallas kernels: 29.7 us -> 29.5 us  [the longest x3 27.7 us: group_product(): pl.pallas_call(functools.partial(group_kernel, n, n_t, place, size, first...]
  transfers between devices with their start and end apart: 26 -> 26, of which waited for: 7 -> 7; matrix products, arithmetic and copies ran while one was open for 1% -> 0% of each run, Pallas kernels for 22% -> 22%
where the time goes in v2:
time: 98 us; the launch traced here: 97.8 us
  starting transfers between devices  31.5 us (32%)
  waiting for transfers between devices  31.3 us (32%)
  Pallas kernels  29.5 us (30%)
  local copies, waits for them, and re-layouts  3.4 us (3%)
  between operations  1.46 us (1%)
    pallas_call x3, Pallas kernels, group_product(): pl.pallas_call(functools.partial(group_kernel, n, n_t, place, size, first...  27.7 us
    ppermute x24, waiting for transfers between devices, permute(): return lax.ppermute(a, ('dp', 'tensor'), perm)  23 us
    ppermute x24, starting transfers between devices, permute(): return lax.ppermute(a, ('dp', 'tensor'), perm)  22.1 us
    all_to_all x1, waiting for transfers between devices, body(): lax.all_to_all(acc.reshape(n_dp * n_t, 3, tok), ('dp', 'tensor'), 0, 0, t...  6.74 us
    all_to_all x1, starting transfers between devices, body(): fine = lax.all_to_all(packed, ('dp', 'tensor'), 0, 0, tiled=True)  5.79 us
    all_to_all x1, starting transfers between devices, body(): lax.all_to_all(acc.reshape(n_dp * n_t, 3, tok), ('dp', 'tensor'), 0, 0, t...  3.64 us
    unnamed x19, local copies, waits for them, and re-layouts  3.13 us
  transfers between devices with their start and end apart: 26, of which 7 were waited for; matrix products, arithmetic and copies ran while one was open for 0% of the time, Pallas kernels for 22%

profile of v2, /device:TPU:0, one launch (start us, length us, event | category | flops | bytes accessed | tf_op | source)
XLA Modules:
  0.0 97.8 jit_solution(1938551062658545563)
XLA Ops:
  0.6 3.0 %collective-permute-start.3 = (bf16[128,1024]{1,0:T(8,128)(2,1)}, bf16[128,1024]{1,0:T(8,128)(2,1)S(1)}, u32[]{:S(2)}, u32[]{:S(2)}) collective-permute-start(bf16[128,1024]{1,0:T(8,128)(2,1)} %refs_2_.1), channel_id=1, source_target_pairs={{0,8},{1,17},{2,10},{3,19},{4,12},{5,21},{6,14},{7,23},{8,0},{9,25... | collective-permute-start | bytes 786440 | tf_op jit(solution)/shard_map/ppermute | solution.py:39
  3.6 1.5 %collective-permute-start.4 = (bf16[128,1024]{1,0:T(8,128)(2,1)}, bf16[128,1024]{1,0:T(8,128)(2,1)S(1)}, u32[]{:S(2)}, u32[]{:S(2)}) collective-permute-start(bf16[128,1024]{1,0:T(8,128)(2,1)} %refs_2_.1), channel_id=1, source_target_pairs={{0,16},{1,9},{2,18},{3,11},{4,20},{5,13},{6,22},{7,15},{8,24},{9,1... | collective-permute-start | bytes 786440 | tf_op jit(solution)/shard_map/ppermute | solution.py:39
  5.2 1.6 %collective-permute-start = (bf16[128,1024]{1,0:T(8,128)(2,1)}, bf16[128,1024]{1,0:T(8,128)(2,1)S(1)}, u32[]{:S(2)}, u32[]{:S(2)}) collective-permute-start(bf16[128,1024]{1,0:T(8,128)(2,1)} %refs_2_.1), channel_id=1, source_target_pairs={{0,2},{1,3},{2,4},{3,5},{4,6},{5,7},{6,0},{7,1},{8,10},{9,11},{10,... | collective-permute-start | bytes 786440 | tf_op jit(solution)/shard_map/ppermute | solution.py:39
  6.7 2.2 %collective-permute-start.1 = (bf16[128,1024]{1,0:T(8,128)(2,1)}, bf16[128,1024]{1,0:T(8,128)(2,1)S(1)}, u32[]{:S(2)}, u32[]{:S(2)}) collective-permute-start(bf16[128,1024]{1,0:T(8,128)(2,1)} %refs_2_.1), channel_id=1, source_target_pairs={{0,6},{1,7},{2,0},{3,1},{4,2},{5,3},{6,4},{7,5},{8,14},{9,15},{10,... | collective-permute-start | bytes 786440 | tf_op jit(solution)/shard_map/ppermute | solution.py:39
  9.0 0.0 collective-permute-start.14
  9.0 1.6 %collective-permute-done.3.refs_3_ = bf16[128,1024]{1,0:T(8,128)(2,1)S(1)} collective-permute-done((bf16[128,1024]{1,0:T(8,128)(2,1)}, bf16[128,1024]{1,0:T(8,128)(2,1)S(1)}, u32[]{:S(2)}, u32[]{:S(2)}) %collective-permute-start.3) | collective-permute-done | bytes 262176 | tf_op jit(solution)/shard_map/ppermute | solution.py:39
  10.5 1.5 %collective-permute-start.13 = (bf16[128,1024]{1,0:T(8,128)(2,1)S(1)}, bf16[128,1024]{1,0:T(8,128)(2,1)S(1)}, u32[]{:S(2)}, u32[]{:S(2)}) collective-permute-start(bf16[128,1024]{1,0:T(8,128)(2,1)S(1)} %collective-permute-done.3.refs_3_), channel_id=1, source_target_pairs={{0,16},{1,9},{2,18},{3,11},{4,20},{5,13},{6,22},{7,15},{8,24},{9,1... | collective-permute-start | bytes 786440 | tf_op jit(solution)/shard_map/ppermute | solution.py:39
  12.1 1.8 %shard_map.77 = f32[32,1,1280]{2,1,0:T(1,128)} custom-call(bf16[128,1024]{1,0:T(8,128)(2,1)} %refs_2_.1, f32[1,1024]{1,0:T(1,128)} %bitcast.22, s32[1,128]{1,0:T(1,128)} %bitcast.23), custom_call_target="tpu_custom_call" | custom-call | tf_op jit(solution)/shard_map/pallas_call | solution.py:265
  13.9 5.8 %all-to-all-start = ((f32[32,1,1280]{2,1,0:T(1,128)}), f32[32,1,1280]{2,1,0:T(1,128)S(1)}, u32[]{:S(2)}, u32[]{:S(2)}) async-start(f32[32,1,1280]{2,1,0:T(1,128)} %shard_map.77), calls=%async_computation | async-start | bytes 327680 | tf_op jit(solution)/shard_map/all_to_all | solution.py:305
  19.7 0.3 collective-permute-start.15
  20.0 0.3 collective-permute-start.16
  20.3 0.0 collective-permute-done.1
  20.3 1.8 %collective-permute-start.5 = (bf16[256,1024]{1,0:T(8,128)(2,1)S(1)}, bf16[256,1024]{1,0:T(8,128)(2,1)}, u32[]{:S(2)}, u32[]{:S(2)}) collective-permute-start(bf16[256,1024]{1,0:T(8,128)(2,1)S(1)} %constant_dynamic-update-slice_fusion.refs_2_), channel_id=1, source_target_pairs={{0,8},{1,17},{2,10},{3,19},{4,12},{5,21},{6,14},{7,23},{8,0},{9,25... | collective-permute-start | bytes 1572872 | tf_op jit(solution)/shard_map/ppermute | solution.py:39
  22.1 0.0 collective-permute-done.14.refs_6_
  22.1 1.5 %collective-permute-start.6 = (bf16[256,1024]{1,0:T(8,128)(2,1)S(1)}, bf16[256,1024]{1,0:T(8,128)(2,1)}, u32[]{:S(2)}, u32[]{:S(2)}) collective-permute-start(bf16[256,1024]{1,0:T(8,128)(2,1)S(1)} %constant_dynamic-update-slice_fusion.refs_2_), channel_id=1, source_target_pairs={{0,16},{1,9},{2,18},{3,11},{4,20},{5,13},{6,22},{7,15},{8,24},{9,1... | collective-permute-start | bytes 1572872 | tf_op jit(solution)/shard_map/ppermute | solution.py:39
  23.6 0.0 collective-permute-done.15.refs_7_
  23.6 0.5 collective-permute-start.17
  24.1 0.0 collective-permute-done.16.refs_8_
  24.1 2.4 %collective-permute-start.2 = (bf16[128,1024]{1,0:T(8,128)(2,1)}, bf16[128,1024]{1,0:T(8,128)(2,1)S(1)}, u32[]{:S(2)}, u32[]{:S(2)}) collective-permute-start(bf16[128,1024]{1,0:T(8,128)(2,1)} %refs_2_.1), channel_id=1, source_target_pairs={{0,4},{1,5},{2,6},{3,7},{4,0},{5,1},{6,2},{7,3},{8,12},{9,13},{10,... | collective-permute-start | bytes 786440 | tf_op jit(solution)/shard_map/ppermute | solution.py:39
  26.5 0.1 stack.63.refs_0_
  26.6 1.5 %all-to-all-done.refs_1_ = f32[32,1,1280]{2,1,0:T(1,128)S(1)} async-done(((f32[32,1,1280]{2,1,0:T(1,128)}), f32[32,1,1280]{2,1,0:T(1,128)S(1)}, u32[]{:S(2)}, u32[]{:S(2)}) %all-to-all-start) | async-done | bytes 163872 | tf_op jit(solution)/shard_map/all_to_all | solution.py:305
  28.2 0.0 collective-permute-done.17.refs_9_
  28.2 6.8 %shard_map.78.refs_11_ = f32[512,1152]{1,0:T(8,128)S(1)} custom-call(s32[7]{0:T(128)S(1)} %stack.63.refs_0_, f32[32,1,1280]{2,1,0:T(1,128)S(1)} %all-to-all-done.refs_1_, bf16[128,1024]{1,0:T(8,128)(2,1)} %refs_2_.1, bf16[128,1024]{1,0:T(8,128)(2,1)} %copy-done.2, bf16[128,1024]{1,0:T(8,128)(2,1)} %copy-done.3, bf16[128,1024]{1,0:T(8,128)(2,1)} %copy-done.5, ...), custom_call_target="tpu_custom_call" | custom-call | flops 2415919104 | bytes 4718592 | tf_op jit(solution)/shard_map/pallas_call | solution.py:233
  35.0 4.1 %collective-permute-done.2.refs_2_ = bf16[128,1024]{1,0:T(8,128)(2,1)S(1)} collective-permute-done((bf16[128,1024]{1,0:T(8,128)(2,1)}, bf16[128,1024]{1,0:T(8,128)(2,1)S(1)}, u32[]{:S(2)}, u32[]{:S(2)}) %collective-permute-start.2) | collective-permute-done | bytes 262176 | tf_op jit(solution)/shard_map/ppermute | solution.py:39
  39.2 0.6 collective-permute-start.19
  39.8 8.9 %collective-permute-done.19.refs_5_ = bf16[256,1024]{1,0:T(8,128)(2,1)} collective-permute-done((bf16[256,1024]{1,0:T(8,128)(2,1)}, bf16[256,1024]{1,0:T(8,128)(2,1)}, u32[]{:S(2)}, u32[]{:S(2)}) %collective-permute-start.19) | collective-permute-done | bytes 524320 | tf_op jit(solution)/shard_map/ppermute | solution.py:39
  48.7 0.1 collective-permute-start.21
  48.8 0.4 collective-permute-start.20
  49.2 0.1 collective-permute-start.22
  49.3 1.4 %collective-permute-start.7 = (bf16[128,1024]{1,0:T(8,128)(2,1)S(1)}, bf16[128,1024]{1,0:T(8,128)(2,1)}, u32[]{:S(2)}, u32[]{:S(2)}) collective-permute-start(bf16[128,1024]{1,0:T(8,128)(2,1)S(1)} %collective-permute-done.2.refs_2_), channel_id=1, source_target_pairs={{0,8},{1,17},{2,10},{3,19},{4,12},{5,21},{6,14},{7,23},{8,0},{9,25... | collective-permute-start | bytes 786440 | tf_op jit(solution)/shard_map/ppermute | solution.py:39
  50.8 0.6 collective-permute-start.8
  51.3 0.1 stack.61.refs_0_
  51.4 6.9 %collective-permute-done.7.refs_3_ = bf16[128,1024]{1,0:T(8,128)(2,1)} collective-permute-done((bf16[128,1024]{1,0:T(8,128)(2,1)S(1)}, bf16[128,1024]{1,0:T(8,128)(2,1)}, u32[]{:S(2)}, u32[]{:S(2)}) %collective-permute-start.7) | collective-permute-done | bytes 262176 | tf_op jit(solution)/shard_map/ppermute | solution.py:39
  58.3 0.0 collective-permute-start.10
  58.3 1.5 %collective-permute-start.9 = (bf16[128,1024]{1,0:T(8,128)(2,1)}, bf16[128,1024]{1,0:T(8,128)(2,1)}, u32[]{:S(2)}, u32[]{:S(2)}) collective-permute-start(bf16[128,1024]{1,0:T(8,128)(2,1)} %collective-permute-done.7.refs_3_), channel_id=1, source_target_pairs={{0,16},{1,9},{2,18},{3,11},{4,20},{5,13},{6,22},{7,15},{8,24},{9,1... | collective-permute-start | bytes 786440 | tf_op jit(solution)/shard_map/ppermute | solution.py:39
  59.8 0.2 collective-permute-start.11
  60.0 0.3 collective-permute-start.12
  60.3 12.5 %shard_map.79.refs_11_ = f32[512,1152]{1,0:T(8,128)S(1)} custom-call(s32[8]{0:T(128)S(1)} %stack.61.refs_0_, f32[32,1,1280]{2,1,0:T(1,128)S(1)} %all-to-all-done.refs_1_, bf16[256,1024]{1,0:T(8,128)(2,1)S(1)} %constant_dynamic-update-slice_fusion.refs_2_, bf16[256,1024]{1,0:T(8,128)(2,1)} %collective-permute-done.5.refs_3_, ...), custom_call_target="tpu_custom_call" | custom-call | flops 4831838208 | bytes 9437184 | tf_op jit(solution)/shard_map/pallas_call | solution.py:233
  72.9 1.4 %copy-done = f32[512,1152]{1,0:T(8,128)} copy-done((f32[512,1152]{1,0:T(8,128)}, f32[512,1152]{1,0:T(8,128)S(1)}, u32[]{:S(2)}) %copy-start) | copy-done | bytes 2359320
  74.3 0.2 collective-permute-start.23
  74.5 0.1 stack.58.refs_0_
  74.6 1.5 %collective-permute-done.23.refs_9_ = bf16[128,1024]{1,0:T(8,128)(2,1)S(1)} collective-permute-done((bf16[128,1024]{1,0:T(8,128)(2,1)}, bf16[128,1024]{1,0:T(8,128)(2,1)S(1)}, u32[]{:S(2)}, u32[]{:S(2)}) %collective-permute-start.23) | collective-permute-done | bytes 262176 | tf_op jit(solution)/shard_map/ppermute | solution.py:39
  76.1 1.7 %copy-done.1 = f32[512,1152]{1,0:T(8,128)S(1)} copy-done((f32[512,1152]{1,0:T(8,128)S(1)}, f32[512,1152]{1,0:T(8,128)}, u32[]{:S(2)}) %copy-start.1) | copy-done | bytes 2359320
  77.7 8.3 %shard_map.80 = f32[4,8,3,128]{3,2,1,0:T(4,128)} custom-call(s32[7]{0:T(128)S(1)} %stack.58.refs_0_, f32[32,1,1280]{2,1,0:T(1,128)S(1)} %all-to-all-done.refs_1_, bf16[128,1024]{1,0:T(8,128)(2,1)S(1)} %collective-permute-done.2.refs_2_, bf16[128,1024]{1,0:T(8,128)(2,1)} %collective-permute-done.7.refs_3_, bf16[128,1024]{1,0:T(8,128)(2,1)} %collective-permute-done.8.refs_4_, ...), custom_call_target="tpu_custom_call" | custom-call | flops 2415919104 | bytes 4718592 | tf_op jit(solution)/shard_map/pallas_call | solution.py:233
  86.1 3.6 %all-to-all-start.1 = ((f32[32,3,128]{2,1,0:T(4,128)}), f32[32,3,128]{2,1,0:T(4,128)S(1)}, u32[]{:S(2)}, u32[]{:S(2)}) async-start(f32[32,3,128]{2,1,0:T(4,128)} %bitcast.13), calls=%async_computation.1 | async-start | bytes 131072 | tf_op jit(solution)/shard_map/all_to_all | solution.py:326
  90.4 6.7 %all-to-all-done.1 = f32[32,3,128]{2,1,0:T(4,128)S(1)} async-done(((f32[32,3,128]{2,1,0:T(4,128)}), f32[32,3,128]{2,1,0:T(4,128)S(1)}, u32[]{:S(2)}, u32[]{:S(2)}) %all-to-all-start.1) | async-done | bytes 49184 | tf_op jit(solution)/shard_map/all_to_all | solution.py:326
  97.1 0.1 slice_reduce_fusion
  97.2 0.5 compare_select_fusion
  (35 shorter events, 0.2 us)
Async XLA Ops:
  0.6 9.9 %collective-permute-start.3 = (bf16[128,1024]{1,0:T(8,128)(2,1)}, bf16[128,1024]{1,0:T(8,128)(2,1)S(1)}, u32[]{:S(2)}, u32[]{:S(2)}) collective-permute-start(bf16[128,1024]{1,0:T(8,128)(2,1)} %refs_2_.1), channel_id=1, source_target_pairs={{0,8},{1,17},{2,10},{3,19},{4,12},{5,21},{6,14},{7,23},{8,0},{9,25... | collective-permute-start | bytes 786440 | tf_op jit(solution)/shard_map/ppermute | solution.py:39
  3.6 6.9 %collective-permute-start.4 = (bf16[128,1024]{1,0:T(8,128)(2,1)}, bf16[128,1024]{1,0:T(8,128)(2,1)S(1)}, u32[]{:S(2)}, u32[]{:S(2)}) collective-permute-start(bf16[128,1024]{1,0:T(8,128)(2,1)} %refs_2_.1), channel_id=1, source_target_pairs={{0,16},{1,9},{2,18},{3,11},{4,20},{5,13},{6,22},{7,15},{8,24},{9,1... | collective-permute-start | bytes 786440 | tf_op jit(solution)/shard_map/ppermute | solution.py:39
  5.2 14.5 %collective-permute-start = (bf16[128,1024]{1,0:T(8,128)(2,1)}, bf16[128,1024]{1,0:T(8,128)(2,1)S(1)}, u32[]{:S(2)}, u32[]{:S(2)}) collective-permute-start(bf16[128,1024]{1,0:T(8,128)(2,1)} %refs_2_.1), channel_id=1, source_target_pairs={{0,2},{1,3},{2,4},{3,5},{4,6},{5,7},{6,0},{7,1},{8,10},{9,11},{10,... | collective-permute-start | bytes 786440 | tf_op jit(solution)/shard_map/ppermute | solution.py:39
  6.7 13.5 %collective-permute-start.1 = (bf16[128,1024]{1,0:T(8,128)(2,1)}, bf16[128,1024]{1,0:T(8,128)(2,1)S(1)}, u32[]{:S(2)}, u32[]{:S(2)}) collective-permute-start(bf16[128,1024]{1,0:T(8,128)(2,1)} %refs_2_.1), channel_id=1, source_target_pairs={{0,6},{1,7},{2,0},{3,1},{4,2},{5,3},{6,4},{7,5},{8,14},{9,15},{10,... | collective-permute-start | bytes 786440 | tf_op jit(solution)/shard_map/ppermute | solution.py:39
  9.0 13.2 %collective-permute-start.14 = (bf16[128,1024]{1,0:T(8,128)(2,1)}, bf16[128,1024]{1,0:T(8,128)(2,1)S(1)}, u32[]{:S(2)}, u32[]{:S(2)}) collective-permute-start(bf16[128,1024]{1,0:T(8,128)(2,1)} %refs_2_.1), channel_id=1, source_target_pairs={{0,1},{1,0},{2,3},{3,2},{4,5},{5,4},{6,7},{7,6},{8,9},{9,8},{10,11... | collective-permute-start | bytes 786440 | tf_op jit(solution)/shard_map/ppermute | solution.py:39
  10.5 17.6 %copy-start.2 = (bf16[128,1024]{1,0:T(8,128)(2,1)}, bf16[128,1024]{1,0:T(8,128)(2,1)S(1)}, u32[]{:S(2)}) copy-start(bf16[128,1024]{1,0:T(8,128)(2,1)S(1)} %collective-permute-done.3.refs_3_) | copy-start | bytes 786436
  10.5 17.6 %copy-start.3 = (bf16[128,1024]{1,0:T(8,128)(2,1)}, bf16[128,1024]{1,0:T(8,128)(2,1)S(1)}, u32[]{:S(2)}) copy-start(bf16[128,1024]{1,0:T(8,128)(2,1)S(1)} %collective-permute-done.4.refs_4_) | copy-start | bytes 786436
  10.5 13.1 %collective-permute-start.13 = (bf16[128,1024]{1,0:T(8,128)(2,1)S(1)}, bf16[128,1024]{1,0:T(8,128)(2,1)S(1)}, u32[]{:S(2)}, u32[]{:S(2)}) collective-permute-start(bf16[128,1024]{1,0:T(8,128)(2,1)S(1)} %collective-permute-done.3.refs_3_), channel_id=1, source_target_pairs={{0,16},{1,9},{2,18},{3,11},{4,20},{5,13},{6,22},{7,15},{8,24},{9,1... | collective-permute-start | bytes 786440 | tf_op jit(solution)/shard_map/ppermute | solution.py:39
  13.9 14.3 %all-to-all-start = ((f32[32,1,1280]{2,1,0:T(1,128)}), f32[32,1,1280]{2,1,0:T(1,128)S(1)}, u32[]{:S(2)}, u32[]{:S(2)}) async-start(f32[32,1,1280]{2,1,0:T(1,128)} %shard_map.77), calls=%async_computation | async-start | bytes 327680 | tf_op jit(solution)/shard_map/all_to_all | solution.py:305
  19.7 4.0 %collective-permute-start.15 = (bf16[128,1024]{1,0:T(8,128)(2,1)S(1)}, bf16[128,1024]{1,0:T(8,128)(2,1)S(1)}, u32[]{:S(2)}, u32[]{:S(2)}) collective-permute-start(bf16[128,1024]{1,0:T(8,128)(2,1)S(1)} %collective-permute-done.3.refs_3_), channel_id=1, source_target_pairs={{0,1},{1,0},{2,3},{3,2},{4,5},{5,4},{6,7},{7,6},{8,9},{9,8},{10,11... | collective-permute-start | bytes 786440 | tf_op jit(solution)/shard_map/ppermute | solution.py:39
  20.0 4.1 %collective-permute-start.16 = (bf16[128,1024]{1,0:T(8,128)(2,1)S(1)}, bf16[128,1024]{1,0:T(8,128)(2,1)S(1)}, u32[]{:S(2)}, u32[]{:S(2)}) collective-permute-start(bf16[128,1024]{1,0:T(8,128)(2,1)S(1)} %collective-permute-done.4.refs_4_), channel_id=1, source_target_pairs={{0,1},{1,0},{2,3},{3,2},{4,5},{5,4},{6,7},{7,6},{8,9},{9,8},{10,11... | collective-permute-start | bytes 786440 | tf_op jit(solution)/shard_map/ppermute | solution.py:39
  20.3 18.9 %collective-permute-start.5 = (bf16[256,1024]{1,0:T(8,128)(2,1)S(1)}, bf16[256,1024]{1,0:T(8,128)(2,1)}, u32[]{:S(2)}, u32[]{:S(2)}) collective-permute-start(bf16[256,1024]{1,0:T(8,128)(2,1)S(1)} %constant_dynamic-update-slice_fusion.refs_2_), channel_id=1, source_target_pairs={{0,8},{1,17},{2,10},{3,19},{4,12},{5,21},{6,14},{7,23},{8,0},{9,25... | collective-permute-start | bytes 1572872 | tf_op jit(solution)/shard_map/ppermute | solution.py:39
  22.1 6.0 %copy-start.4 = (bf16[128,1024]{1,0:T(8,128)(2,1)}, bf16[128,1024]{1,0:T(8,128)(2,1)S(1)}, u32[]{:S(2)}) copy-start(bf16[128,1024]{1,0:T(8,128)(2,1)S(1)} %collective-permute-done.14.refs_6_) | copy-start | bytes 786436
  22.1 17.0 %collective-permute-start.6 = (bf16[256,1024]{1,0:T(8,128)(2,1)S(1)}, bf16[256,1024]{1,0:T(8,128)(2,1)}, u32[]{:S(2)}, u32[]{:S(2)}) collective-permute-start(bf16[256,1024]{1,0:T(8,128)(2,1)S(1)} %constant_dynamic-update-slice_fusion.refs_2_), channel_id=1, source_target_pairs={{0,16},{1,9},{2,18},{3,11},{4,20},{5,13},{6,22},{7,15},{8,24},{9,1... | collective-permute-start | bytes 1572872 | tf_op jit(solution)/shard_map/ppermute | solution.py:39
  23.6 4.5 %copy-start.5 = (bf16[128,1024]{1,0:T(8,128)(2,1)}, bf16[128,1024]{1,0:T(8,128)(2,1)S(1)}, u32[]{:S(2)}) copy-start(bf16[128,1024]{1,0:T(8,128)(2,1)S(1)} %collective-permute-done.13.refs_5_) | copy-start | bytes 786436
  23.6 15.6 %collective-permute-start.18 = (bf16[256,1024]{1,0:T(8,128)(2,1)S(1)}, bf16[256,1024]{1,0:T(8,128)(2,1)}, u32[]{:S(2)}, u32[]{:S(2)}) collective-permute-start(bf16[256,1024]{1,0:T(8,128)(2,1)S(1)} %constant_dynamic-update-slice_fusion.refs_2_), channel_id=1, source_target_pairs={{0,1},{1,0},{2,3},{3,2},{4,5},{5,4},{6,7},{7,6},{8,9},{9,8},{10,11... | collective-permute-start | bytes 1572872 | tf_op jit(solution)/shard_map/ppermute | solution.py:39
  23.6 4.5 %copy-start.6 = (bf16[128,1024]{1,0:T(8,128)(2,1)}, bf16[128,1024]{1,0:T(8,128)(2,1)S(1)}, u32[]{:S(2)}) copy-start(bf16[128,1024]{1,0:T(8,128)(2,1)S(1)} %collective-permute-done.15.refs_7_) | copy-start | bytes 786436
  23.6 4.5 %collective-permute-start.17 = (bf16[128,1024]{1,0:T(8,128)(2,1)S(1)}, bf16[128,1024]{1,0:T(8,128)(2,1)}, u32[]{:S(2)}, u32[]{:S(2)}) collective-permute-start(bf16[128,1024]{1,0:T(8,128)(2,1)S(1)} %collective-permute-done.13.refs_5_), channel_id=1, source_target_pairs={{0,1},{1,0},{2,3},{3,2},{4,5},{5,4},{6,7},{7,6},{8,9},{9,8},{10,11... | collective-permute-start | bytes 786440 | tf_op jit(solution)/shard_map/ppermute | solution.py:39
  24.1 4.0 %copy-start.7 = (bf16[128,1024]{1,0:T(8,128)(2,1)}, bf16[128,1024]{1,0:T(8,128)(2,1)S(1)}, u32[]{:S(2)}) copy-start(bf16[128,1024]{1,0:T(8,128)(2,1)S(1)} %collective-permute-done.16.refs_8_) | copy-start | bytes 786436
  24.1 15.0 %collective-permute-start.2 = (bf16[128,1024]{1,0:T(8,128)(2,1)}, bf16[128,1024]{1,0:T(8,128)(2,1)S(1)}, u32[]{:S(2)}, u32[]{:S(2)}) collective-permute-start(bf16[128,1024]{1,0:T(8,128)(2,1)} %refs_2_.1), channel_id=1, source_target_pairs={{0,4},{1,5},{2,6},{3,7},{4,0},{5,1},{6,2},{7,3},{8,12},{9,13},{10,... | collective-permute-start | bytes 786440 | tf_op jit(solution)/shard_map/ppermute | solution.py:39
  39.2 9.6 %collective-permute-start.19 = (bf16[256,1024]{1,0:T(8,128)(2,1)}, bf16[256,1024]{1,0:T(8,128)(2,1)}, u32[]{:S(2)}, u32[]{:S(2)}) collective-permute-start(bf16[256,1024]{1,0:T(8,128)(2,1)} %collective-permute-done.5.refs_3_), channel_id=1, source_target_pairs={{0,16},{1,9},{2,18},{3,11},{4,20},{5,13},{6,22},{7,15},{8,24},{9,1... | collective-permute-start | bytes 1572872 | tf_op jit(solution)/shard_map/ppermute | solution.py:39
  48.7 11.1 %collective-permute-start.21 = (bf16[256,1024]{1,0:T(8,128)(2,1)}, bf16[256,1024]{1,0:T(8,128)(2,1)}, u32[]{:S(2)}, u32[]{:S(2)}) collective-permute-start(bf16[256,1024]{1,0:T(8,128)(2,1)} %collective-permute-done.6.refs_4_), channel_id=1, source_target_pairs={{0,1},{1,0},{2,3},{3,2},{4,5},{5,4},{6,7},{7,6},{8,9},{9,8},{10,11... | collective-permute-start | bytes 1572872 | tf_op jit(solution)/shard_map/ppermute | solution.py:39
  48.8 11.2 %collective-permute-start.20 = (bf16[256,1024]{1,0:T(8,128)(2,1)}, bf16[256,1024]{1,0:T(8,128)(2,1)}, u32[]{:S(2)}, u32[]{:S(2)}) collective-permute-start(bf16[256,1024]{1,0:T(8,128)(2,1)} %collective-permute-done.5.refs_3_), channel_id=1, source_target_pairs={{0,1},{1,0},{2,3},{3,2},{4,5},{5,4},{6,7},{7,6},{8,9},{9,8},{10,11... | collective-permute-start | bytes 1572872 | tf_op jit(solution)/shard_map/ppermute | solution.py:39
  49.2 11.1 %collective-permute-start.22 = (bf16[256,1024]{1,0:T(8,128)(2,1)}, bf16[256,1024]{1,0:T(8,128)(2,1)}, u32[]{:S(2)}, u32[]{:S(2)}) collective-permute-start(bf16[256,1024]{1,0:T(8,128)(2,1)} %collective-permute-done.19.refs_5_), channel_id=1, source_target_pairs={{0,1},{1,0},{2,3},{3,2},{4,5},{5,4},{6,7},{7,6},{8,9},{9,8},{10,11... | collective-permute-start | bytes 1572872 | tf_op jit(solution)/shard_map/ppermute | solution.py:39
  49.3 9.0 %collective-permute-start.7 = (bf16[128,1024]{1,0:T(8,128)(2,1)S(1)}, bf16[128,1024]{1,0:T(8,128)(2,1)}, u32[]{:S(2)}, u32[]{:S(2)}) collective-permute-start(bf16[128,1024]{1,0:T(8,128)(2,1)S(1)} %collective-permute-done.2.refs_2_), channel_id=1, source_target_pairs={{0,8},{1,17},{2,10},{3,19},{4,12},{5,21},{6,14},{7,23},{8,0},{9,25... | collective-permute-start | bytes 786440 | tf_op jit(solution)/shard_map/ppermute | solution.py:39
  50.8 7.5 %collective-permute-start.8 = (bf16[128,1024]{1,0:T(8,128)(2,1)S(1)}, bf16[128,1024]{1,0:T(8,128)(2,1)}, u32[]{:S(2)}, u32[]{:S(2)}) collective-permute-start(bf16[128,1024]{1,0:T(8,128)(2,1)S(1)} %collective-permute-done.2.refs_2_), channel_id=1, source_target_pairs={{0,16},{1,9},{2,18},{3,11},{4,20},{5,13},{6,22},{7,15},{8,24},{9,1... | collective-permute-start | bytes 786440 | tf_op jit(solution)/shard_map/ppermute | solution.py:39
  58.3 16.3 %collective-permute-start.10 = (bf16[128,1024]{1,0:T(8,128)(2,1)S(1)}, bf16[128,1024]{1,0:T(8,128)(2,1)}, u32[]{:S(2)}, u32[]{:S(2)}) collective-permute-start(bf16[128,1024]{1,0:T(8,128)(2,1)S(1)} %collective-permute-done.2.refs_2_), channel_id=1, source_target_pairs={{0,1},{1,0},{2,3},{3,2},{4,5},{5,4},{6,7},{7,6},{8,9},{9,8},{10,11... | collective-permute-start | bytes 786440 | tf_op jit(solution)/shard_map/ppermute | solution.py:39
  58.3 16.0 %collective-permute-start.9 = (bf16[128,1024]{1,0:T(8,128)(2,1)}, bf16[128,1024]{1,0:T(8,128)(2,1)}, u32[]{:S(2)}, u32[]{:S(2)}) collective-permute-start(bf16[128,1024]{1,0:T(8,128)(2,1)} %collective-permute-done.7.refs_3_), channel_id=1, source_target_pairs={{0,16},{1,9},{2,18},{3,11},{4,20},{5,13},{6,22},{7,15},{8,24},{9,1... | collective-permute-start | bytes 786440 | tf_op jit(solution)/shard_map/ppermute | solution.py:39
  59.8 14.8 %collective-permute-start.11 = (bf16[128,1024]{1,0:T(8,128)(2,1)}, bf16[128,1024]{1,0:T(8,128)(2,1)}, u32[]{:S(2)}, u32[]{:S(2)}) collective-permute-start(bf16[128,1024]{1,0:T(8,128)(2,1)} %collective-permute-done.7.refs_3_), channel_id=1, source_target_pairs={{0,1},{1,0},{2,3},{3,2},{4,5},{5,4},{6,7},{7,6},{8,9},{9,8},{10,11... | collective-permute-start | bytes 786440 | tf_op jit(solution)/shard_map/ppermute | solution.py:39
  60.0 14.6 %collective-permute-start.12 = (bf16[128,1024]{1,0:T(8,128)(2,1)}, bf16[128,1024]{1,0:T(8,128)(2,1)}, u32[]{:S(2)}, u32[]{:S(2)}) collective-permute-start(bf16[128,1024]{1,0:T(8,128)(2,1)} %collective-permute-done.8.refs_4_), channel_id=1, source_target_pairs={{0,1},{1,0},{2,3},{3,2},{4,5},{5,4},{6,7},{7,6},{8,9},{9,8},{10,11... | collective-permute-start | bytes 786440 | tf_op jit(solution)/shard_map/ppermute | solution.py:39
  72.9 1.4 %copy-start = (f32[512,1152]{1,0:T(8,128)}, f32[512,1152]{1,0:T(8,128)S(1)}, u32[]{:S(2)}) copy-start(f32[512,1152]{1,0:T(8,128)S(1)} %shard_map.79.refs_11_) | copy-start | bytes 7077892
  74.3 1.7 %collective-permute-start.23 = (bf16[128,1024]{1,0:T(8,128)(2,1)}, bf16[128,1024]{1,0:T(8,128)(2,1)S(1)}, u32[]{:S(2)}, u32[]{:S(2)}) collective-permute-start(bf16[128,1024]{1,0:T(8,128)(2,1)} %collective-permute-done.9.refs_5_), channel_id=1, source_target_pairs={{0,1},{1,0},{2,3},{3,2},{4,5},{5,4},{6,7},{7,6},{8,9},{9,8},{10,11... | collective-permute-start | bytes 786440 | tf_op jit(solution)/shard_map/ppermute | solution.py:39
  74.5 22.7 %copy-start.8 = (f32[128]{0:T(128)S(1)}, f32[128]{0:T(128)}, u32[]{:S(2)}) copy-start(f32[128]{0:T(128)} %param.10) | copy-start | bytes 1540
  76.1 1.7 %copy-start.1 = (f32[512,1152]{1,0:T(8,128)S(1)}, f32[512,1152]{1,0:T(8,128)}, u32[]{:S(2)}) copy-start(f32[512,1152]{1,0:T(8,128)} %copy-done) | copy-start | bytes 7077892
  86.1 11.0 %all-to-all-start.1 = ((f32[32,3,128]{2,1,0:T(4,128)}), f32[32,3,128]{2,1,0:T(4,128)S(1)}, u32[]{:S(2)}, u32[]{:S(2)}) async-start(f32[32,3,128]{2,1,0:T(4,128)} %bitcast.13), calls=%async_computation.1 | async-start | bytes 131072 | tf_op jit(solution)/shard_map/all_to_all | solution.py:326

commit v3 on v2

--- a/solution.py
+++ b/solution.py
@@ -125,7 +125,6 @@
     owners = [start_ref[size + 2 + k] for k in range(n)]
 
     fine_copy = pltpu.make_async_copy(fine_ref, fine, fine_sem)
-    fine_copy.start()
     head_copies, block_copies = [], []
     for j in range(size):
         offset = pl.multiple_of(start_ref[j] * (CORES * feat), CORES * feat)
@@ -150,14 +149,20 @@
                 for k in range(n)
             ]
         )
-        head_copies[j][0].start()
-        for copy in block_copies[j]:
+    stages = []
+    for j in range(size):
+        stages.append([*block_copies[j], head_copies[j][0]])
+        stages += [[copy] for copy in head_copies[j][1:]]
+    stages[0].insert(0, fine_copy)
+    if not first:
+        acc_copy = pltpu.make_async_copy(acc_ref, acc, acc_sem.at[len(tiles)])
+        stages[1].append(acc_copy)
+
+    def advance():
+        for copy in stages.pop(0) if stages else ():
             copy.start()
-        for copy in head_copies[j][1:]:
-            copy.start()
-        if j == 0 and not first:
-            acc_copy = pltpu.make_async_copy(acc_ref, acc, acc_sem.at[len(tiles)])
-            acc_copy.start()
+
+    advance()
 
     def peers(k):
         return pl.ds(owners[k] * n_t, n_t)
@@ -175,12 +180,16 @@
             columns = pl.ds(pl.multiple_of(core * feat, feat), feat)
             for k in range(n):
                 block_copies[j][c * n + k].wait()
+            if j == 0 and c == CORES - 1:
+                advance()
             for k in range(n):
                 here = slice(k * tok, (k + 1) * tok)
                 part = raw[j, c, here, :].astype(jnp.float32) * scales[k] * gain
                 rows[here, columns] = part.astype(jnp.bfloat16)
         for i, (lo, hi) in enumerate(tiles):
             head_copies[j][i].wait()
+            if i or j:
+                advance()
             product = jnp.dot(rows[...], weights[j, :, lo:hi], preferred_element_type=jnp.float32)
             if j == 0 and i == 0 and not first:
                 acc_copy.wait()
@@ -215,7 +224,7 @@
     vmem, whole = pl.BlockSpec(memory_space=pltpu.VMEM), pl.BlockSpec(memory_space=pl.ANY)
     first = acc is None
     logits = jax.ShapeDtypeStruct((n * tok, vocab), jnp.float32)
-    operands = [starts, fine, *blocks, far(head)] + ([] if first else [acc])
+    operands = [starts, fine, *blocks, far(head)] + ([] if first else [far(acc)])
     specs = [pl.BlockSpec(memory_space=pltpu.SMEM)] + [whole] * (len(operands) - 1)
     tiles = len(column_tiles(vocab))
     scratch = [
@@ -232,7 +241,7 @@
     work = 2 * n * tok * CORES * feat * vocab * size
     return pl.pallas_call(
         functools.partial(group_kernel, n, n_t, place, size, first, last),
-        out_shape=jax.ShapeDtypeStruct((n, n_t, 3, tok), jnp.float32) if last else logits,
+        out_shape=jax.ShapeDtypeStruct((n, n_t, 3, tok), jnp.float32) if last else pltpu.HBM(logits.shape, logits.dtype),
         in_specs=specs,
         out_specs=vmem if last else whole,
         scratch_shapes=scratch,
@@ -289,12 +298,12 @@
     place = [grid.sibling_spot(k) for k in range(n_dp)]
 
     layers = {0: hidden}
+    reached = [grid.reach(hidden)]
     before = []
     for group in groups[1:]:
         for dz in group:
             layers[dz] = grid.along(after(hidden, *before), dz)
-        before = [layers[dz] for dz in group]
-    reached = [grid.reach(hidden)]
+        before = list(reached[0].values()) if len(before) == 0 else [layers[dz] for dz in group]
     for group in groups[1:]:
         sources = [layers[dz] for dz in group]
         sources[0] = after(sources[0], *reached[-1].values())
@@ -313,14 +322,15 @@
         own = grid.sibling(reached[at][0, 0])
         held = [layers[dz] for dz in groups[at + 1]] + [own] if middle else []
         spread = grid.fill(dict(reached[at]), *([acc] if at == 1 else []), *held)
-        others = [own] + [grid.sibling(after(a, spread[-1]) if middle else a) for a in spread[1:-1]]
-        others.append(grid.sibling(after(spread[-1], acc) if final else spread[-1]))
+        following = list(reached[at + 1].values()) if middle else []
+        others = [own] + [grid.sibling(after(a, *following)) for a in spread[1:-1]]
+        others.append(grid.sibling(after(spread[-1], *([acc] if final else following))))
         blocks = spread + others
         if not at:
             blocks = [far(a) for a in blocks]
         starts = jnp.stack([(z_me - dz) % depth for dz in group] + [c_me, vocab_start] + owners)
         if middle:
-            starts = after(starts, *reached[at + 1].values())
+            starts = after(starts, *following)
         acc = group_product(tok, n_t, starts, len(group), fine, blocks, place, head, acc, final)
 
     parts = lax.all_to_all(acc.reshape(n_dp * n_t, 3, tok), ("dp", "tensor"), 0, 0, tiled=True)

time: 98 us -> 95.8 us (0.978)
  waiting for transfers between devices: 31.3 us -> 27.7 us
  Pallas kernels: 29.5 us -> 31.8 us
  local copies, waits for them, and re-layouts: 3.4 us -> 1.47 us
    ppermute x24, waiting for transfers between devices: 23 us -> 19.6 us  [permute(): return lax.ppermute(a, ('dp', 'tensor'), perm)]
    pallas_call x3, Pallas kernels: 27.7 us -> 30 us  [group_product(): pl.pallas_call(functools.partial(group_kernel, n, n_t, place, size, first...]
    unnamed x19 -> x17, local copies, waits for them, and re-layouts: 3.13 us -> 1.2 us
  transfers between devices with their start and end apart: 26 -> 26, of which waited for: 7 -> 10; matrix products, arithmetic and copies ran while one was open for 0% -> 0% of each run, Pallas kernels for 22% -> 24%
where the time goes in v3:
time: 95.8 us; the launch traced here: 95.4 us
  starting transfers between devices  32.4 us (34%)
  Pallas kernels  31.8 us (33%)
  waiting for transfers between devices  27.7 us (29%)
  local copies, waits for them, and re-layouts  1.47 us (2%)
  between operations  1.43 us (1%)
    pallas_call x3, Pallas kernels, group_product(): pl.pallas_call(functools.partial(group_kernel, n, n_t, place, size, first...  30 us
    ppermute x24, starting transfers between devices, permute(): return lax.ppermute(a, ('dp', 'tensor'), perm)  22 us
    ppermute x24, waiting for transfers between devices, permute(): return lax.ppermute(a, ('dp', 'tensor'), perm)  19.6 us
    all_to_all x1, waiting for transfers between devices, body(): lax.all_to_all(acc.reshape(n_dp * n_t, 3, tok), ('dp', 'tensor'), 0, 0, t...  6.74 us
    all_to_all x1, starting transfers between devices, body(): fine = lax.all_to_all(packed, ('dp', 'tensor'), 0, 0, tiled=True)  5.79 us
    all_to_all x1, starting transfers between devices, body(): lax.all_to_all(acc.reshape(n_dp * n_t, 3, tok), ('dp', 'tensor'), 0, 0, t...  4.61 us
  transfers between devices with their start and end apart: 26, of which 10 were waited for; matrix products, arithmetic and copies ran while one was open for 0% of the time, Pallas kernels for 24%

profile of v3, /device:TPU:0, one launch (start us, length us, event | category | flops | bytes accessed | tf_op | source)
XLA Modules:
  0.0 95.4 jit_solution(2317401854295787488)
XLA Ops:
  0.6 3.0 %collective-permute-start = (bf16[128,1024]{1,0:T(8,128)(2,1)}, bf16[128,1024]{1,0:T(8,128)(2,1)S(1)}, u32[]{:S(2)}, u32[]{:S(2)}) collective-permute-start(bf16[128,1024]{1,0:T(8,128)(2,1)} %refs_2_.1), channel_id=1, source_target_pairs={{0,8},{1,17},{2,10},{3,19},{4,12},{5,21},{6,14},{7,23},{8,0},{9,25... | collective-permute-start | bytes 786440 | tf_op jit(solution)/shard_map/ppermute | solution.py:39
  3.6 1.5 %collective-permute-start.1 = (bf16[128,1024]{1,0:T(8,128)(2,1)}, bf16[128,1024]{1,0:T(8,128)(2,1)S(1)}, u32[]{:S(2)}, u32[]{:S(2)}) collective-permute-start(bf16[128,1024]{1,0:T(8,128)(2,1)} %refs_2_.1), channel_id=1, source_target_pairs={{0,16},{1,9},{2,18},{3,11},{4,20},{5,13},{6,22},{7,15},{8,24},{9,1... | collective-permute-start | bytes 786440 | tf_op jit(solution)/shard_map/ppermute | solution.py:39
  5.2 1.6 %collective-permute-start.3 = (bf16[128,1024]{1,0:T(8,128)(2,1)}, bf16[128,1024]{1,0:T(8,128)(2,1)S(1)}, u32[]{:S(2)}, u32[]{:S(2)}) collective-permute-start(bf16[128,1024]{1,0:T(8,128)(2,1)} %refs_2_.1), channel_id=1, source_target_pairs={{0,2},{1,3},{2,4},{3,5},{4,6},{5,7},{6,0},{7,1},{8,10},{9,11},{10,... | collective-permute-start | bytes 786440 | tf_op jit(solution)/shard_map/ppermute | solution.py:39
  6.7 2.2 %collective-permute-start.4 = (bf16[128,1024]{1,0:T(8,128)(2,1)}, bf16[128,1024]{1,0:T(8,128)(2,1)S(1)}, u32[]{:S(2)}, u32[]{:S(2)}) collective-permute-start(bf16[128,1024]{1,0:T(8,128)(2,1)} %refs_2_.1), channel_id=1, source_target_pairs={{0,6},{1,7},{2,0},{3,1},{4,2},{5,3},{6,4},{7,5},{8,14},{9,15},{10,... | collective-permute-start | bytes 786440 | tf_op jit(solution)/shard_map/ppermute | solution.py:39
  9.0 0.0 collective-permute-start.14
  9.0 1.6 %collective-permute-done.refs_3_ = bf16[128,1024]{1,0:T(8,128)(2,1)S(1)} collective-permute-done((bf16[128,1024]{1,0:T(8,128)(2,1)}, bf16[128,1024]{1,0:T(8,128)(2,1)S(1)}, u32[]{:S(2)}, u32[]{:S(2)}) %collective-permute-start) | collective-permute-done | bytes 262176 | tf_op jit(solution)/shard_map/ppermute | solution.py:39
  10.5 1.5 %collective-permute-start.13 = (bf16[128,1024]{1,0:T(8,128)(2,1)S(1)}, bf16[128,1024]{1,0:T(8,128)(2,1)}, u32[]{:S(2)}, u32[]{:S(2)}) collective-permute-start(bf16[128,1024]{1,0:T(8,128)(2,1)S(1)} %collective-permute-done.refs_3_), channel_id=1, source_target_pairs={{0,16},{1,9},{2,18},{3,11},{4,20},{5,13},{6,22},{7,15},{8,24},{9,1... | collective-permute-start | bytes 786440 | tf_op jit(solution)/shard_map/ppermute | solution.py:39
  12.1 1.8 %shard_map.77 = f32[32,1,1280]{2,1,0:T(1,128)} custom-call(bf16[128,1024]{1,0:T(8,128)(2,1)} %refs_2_.1, f32[1,1024]{1,0:T(1,128)} %bitcast.22, s32[1,128]{1,0:T(1,128)} %bitcast.23), custom_call_target="tpu_custom_call" | custom-call | tf_op jit(solution)/shard_map/pallas_call | solution.py:274
  13.9 5.8 %all-to-all-start = ((f32[32,1,1280]{2,1,0:T(1,128)}), f32[32,1,1280]{2,1,0:T(1,128)S(1)}, u32[]{:S(2)}, u32[]{:S(2)}) async-start(f32[32,1,1280]{2,1,0:T(1,128)} %shard_map.77), calls=%async_computation | async-start | bytes 327680 | tf_op jit(solution)/shard_map/all_to_all | solution.py:314
  19.7 0.0 collective-permute-done.3
  19.7 0.3 collective-permute-start.15
  20.0 0.3 collective-permute-start.16
  20.3 0.0 collective-permute-done.4
  20.3 1.8 %collective-permute-start.5 = (bf16[256,1024]{1,0:T(8,128)(2,1)S(1)}, bf16[256,1024]{1,0:T(8,128)(2,1)S(1)}, u32[]{:S(2)}, u32[]{:S(2)}) collective-permute-start(bf16[256,1024]{1,0:T(8,128)(2,1)S(1)} %constant_dynamic-update-slice_fusion.refs_2_), channel_id=1, source_target_pairs={{0,8},{1,17},{2,10},{3,19},{4,12},{5,21},{6,14},{7,23},{8,0},{9,25... | collective-permute-start | bytes 1572872 | tf_op jit(solution)/shard_map/ppermute | solution.py:39
  22.1 1.5 %collective-permute-start.6 = (bf16[256,1024]{1,0:T(8,128)(2,1)S(1)}, bf16[256,1024]{1,0:T(8,128)(2,1)S(1)}, u32[]{:S(2)}, u32[]{:S(2)}) collective-permute-start(bf16[256,1024]{1,0:T(8,128)(2,1)S(1)} %constant_dynamic-update-slice_fusion.refs_2_), channel_id=1, source_target_pairs={{0,16},{1,9},{2,18},{3,11},{4,20},{5,13},{6,22},{7,15},{8,24},{9,1... | collective-permute-start | bytes 1572872 | tf_op jit(solution)/shard_map/ppermute | solution.py:39
  23.6 0.0 collective-permute-done.13.refs_5_
  23.6 0.5 collective-permute-start.17
  24.1 0.2 copy-done.5
  24.3 2.4 %collective-permute-start.2 = (bf16[128,1024]{1,0:T(8,128)(2,1)}, bf16[128,1024]{1,0:T(8,128)(2,1)S(1)}, u32[]{:S(2)}, u32[]{:S(2)}) collective-permute-start(bf16[128,1024]{1,0:T(8,128)(2,1)} %refs_2_.1), channel_id=1, source_target_pairs={{0,4},{1,5},{2,6},{3,7},{4,0},{5,1},{6,2},{7,3},{8,12},{9,13},{10,... | collective-permute-start | bytes 786440 | tf_op jit(solution)/shard_map/ppermute | solution.py:39
  26.7 0.1 stack.63.refs_0_
  26.8 1.3 %all-to-all-done.refs_1_ = f32[32,1,1280]{2,1,0:T(1,128)S(1)} async-done(((f32[32,1,1280]{2,1,0:T(1,128)}), f32[32,1,1280]{2,1,0:T(1,128)S(1)}, u32[]{:S(2)}, u32[]{:S(2)}) %all-to-all-start) | async-done | bytes 163872 | tf_op jit(solution)/shard_map/all_to_all | solution.py:314
  28.1 7.7 %shard_map.78.refs_11_ = f32[512,1152]{1,0:T(8,128)} custom-call(s32[7]{0:T(128)S(1)} %stack.63.refs_0_, f32[32,1,1280]{2,1,0:T(1,128)S(1)} %all-to-all-done.refs_1_, bf16[128,1024]{1,0:T(8,128)(2,1)} %refs_2_.1, bf16[128,1024]{1,0:T(8,128)(2,1)} %copy-done.2, bf16[128,1024]{1,0:T(8,128)(2,1)} %copy-done.3, ...), custom_call_target="tpu_custom_call" | custom-call | flops 2415919104 | bytes 4718592 | tf_op jit(solution)/shard_map/pallas_call | solution.py:242
  35.9 3.9 %collective-permute-done.2.refs_2_ = bf16[128,1024]{1,0:T(8,128)(2,1)S(1)} collective-permute-done((bf16[128,1024]{1,0:T(8,128)(2,1)}, bf16[128,1024]{1,0:T(8,128)(2,1)S(1)}, u32[]{:S(2)}, u32[]{:S(2)}) %collective-permute-start.2) | collective-permute-done | bytes 262176 | tf_op jit(solution)/shard_map/ppermute | solution.py:39
  39.8 0.6 collective-permute-start.19
  40.4 0.8 collective-permute-start.7
  41.2 1.2 %collective-permute-start.8 = (bf16[128,1024]{1,0:T(8,128)(2,1)S(1)}, bf16[128,1024]{1,0:T(8,128)(2,1)}, u32[]{:S(2)}, u32[]{:S(2)}) collective-permute-start(bf16[128,1024]{1,0:T(8,128)(2,1)S(1)} %collective-permute-done.2.refs_2_), channel_id=1, source_target_pairs={{0,16},{1,9},{2,18},{3,11},{4,20},{5,13},{6,22},{7,15},{8,24},{9,1... | collective-permute-start | bytes 786440 | tf_op jit(solution)/shard_map/ppermute | solution.py:39
  42.5 7.3 %collective-permute-done.7.refs_3_ = bf16[128,1024]{1,0:T(8,128)(2,1)} collective-permute-done((bf16[128,1024]{1,0:T(8,128)(2,1)S(1)}, bf16[128,1024]{1,0:T(8,128)(2,1)}, u32[]{:S(2)}, u32[]{:S(2)}) %collective-permute-start.7) | collective-permute-done | bytes 262176 | tf_op jit(solution)/shard_map/ppermute | solution.py:39
  49.8 4.0 %collective-permute-done.8.refs_4_ = bf16[128,1024]{1,0:T(8,128)(2,1)} collective-permute-done((bf16[128,1024]{1,0:T(8,128)(2,1)S(1)}, bf16[128,1024]{1,0:T(8,128)(2,1)}, u32[]{:S(2)}, u32[]{:S(2)}) %collective-permute-start.8) | collective-permute-done | bytes 262176 | tf_op jit(solution)/shard_map/ppermute | solution.py:39
  53.8 0.5 collective-permute-start.20
  54.3 0.0 collective-permute-start.22
  54.3 0.1 stack.61.refs_0_
  54.4 0.5 collective-permute-start.10
  54.9 1.1 %collective-permute-start.9 = (bf16[128,1024]{1,0:T(8,128)(2,1)}, bf16[128,1024]{1,0:T(8,128)(2,1)}, u32[]{:S(2)}, u32[]{:S(2)}) collective-permute-start(bf16[128,1024]{1,0:T(8,128)(2,1)} %collective-permute-done.7.refs_3_), channel_id=1, source_target_pairs={{0,16},{1,9},{2,18},{3,11},{4,20},{5,13},{6,22},{7,15},{8,24},{9,1... | collective-permute-start | bytes 786440 | tf_op jit(solution)/shard_map/ppermute | solution.py:39
  56.0 0.4 collective-permute-done.21.refs_8_
  56.4 0.1 collective-permute-start.11
  56.6 0.1 collective-permute-done.20.refs_7_
  56.6 0.3 collective-permute-start.12
  57.0 0.8 collective-permute-done.22.refs_9_
  57.7 13.5 %shard_map.79.refs_11_ = f32[512,1152]{1,0:T(8,128)} custom-call(s32[8]{0:T(128)S(1)} %stack.61.refs_0_, f32[32,1,1280]{2,1,0:T(1,128)S(1)} %all-to-all-done.refs_1_, bf16[256,1024]{1,0:T(8,128)(2,1)S(1)} %constant_dynamic-update-slice_fusion.refs_2_, bf16[256,1024]{1,0:T(8,128)(2,1)S(1)} %collective-permute-done.5.refs_3_, ...), custom_call_target="tpu_custom_call" | custom-call | flops 4831838208 | bytes 9437184 | tf_op jit(solution)/shard_map/pallas_call | solution.py:242
  71.2 0.2 collective-permute-start.23
  71.4 0.1 stack.58.refs_0_
  71.5 1.5 %collective-permute-done.23.refs_9_ = bf16[128,1024]{1,0:T(8,128)(2,1)S(1)} collective-permute-done((bf16[128,1024]{1,0:T(8,128)(2,1)}, bf16[128,1024]{1,0:T(8,128)(2,1)S(1)}, u32[]{:S(2)}, u32[]{:S(2)}) %collective-permute-start.23) | collective-permute-done | bytes 262176 | tf_op jit(solution)/shard_map/ppermute | solution.py:39
  73.0 0.9 copy-done.1
  74.0 8.8 %shard_map.80 = f32[4,8,3,128]{3,2,1,0:T(4,128)} custom-call(s32[7]{0:T(128)S(1)} %stack.58.refs_0_, f32[32,1,1280]{2,1,0:T(1,128)S(1)} %all-to-all-done.refs_1_, bf16[128,1024]{1,0:T(8,128)(2,1)S(1)} %copy-done.1, bf16[128,1024]{1,0:T(8,128)(2,1)} %collective-permute-done.7.refs_3_, bf16[128,1024]{1,0:T(8,128)(2,1)} %collective-permute-done.8.refs_4_, ...), custom_call_target="tpu_custom_call" | custom-call | flops 2415919104 | bytes 4718592 | tf_op jit(solution)/shard_map/pallas_call | solution.py:242
  82.7 4.6 %all-to-all-start.1 = ((f32[32,3,128]{2,1,0:T(4,128)}), f32[32,3,128]{2,1,0:T(4,128)S(1)}, u32[]{:S(2)}, u32[]{:S(2)}) async-start(f32[32,3,128]{2,1,0:T(4,128)} %bitcast.13), calls=%async_computation.1 | async-start | bytes 131072 | tf_op jit(solution)/shard_map/all_to_all | solution.py:336
  88.0 6.7 %all-to-all-done.1 = f32[32,3,128]{2,1,0:T(4,128)S(1)} async-done(((f32[32,3,128]{2,1,0:T(4,128)}), f32[32,3,128]{2,1,0:T(4,128)S(1)}, u32[]{:S(2)}, u32[]{:S(2)}) %all-to-all-start.1) | async-done | bytes 49184 | tf_op jit(solution)/shard_map/all_to_all | solution.py:336
  94.8 0.1 slice_reduce_fusion
  94.9 0.5 compare_select_fusion
  (33 shorter events, 0.2 us)
Async XLA Ops:
  0.6 9.9 %collective-permute-start = (bf16[128,1024]{1,0:T(8,128)(2,1)}, bf16[128,1024]{1,0:T(8,128)(2,1)S(1)}, u32[]{:S(2)}, u32[]{:S(2)}) collective-permute-start(bf16[128,1024]{1,0:T(8,128)(2,1)} %refs_2_.1), channel_id=1, source_target_pairs={{0,8},{1,17},{2,10},{3,19},{4,12},{5,21},{6,14},{7,23},{8,0},{9,25... | collective-permute-start | bytes 786440 | tf_op jit(solution)/shard_map/ppermute | solution.py:39
  3.6 6.9 %collective-permute-start.1 = (bf16[128,1024]{1,0:T(8,128)(2,1)}, bf16[128,1024]{1,0:T(8,128)(2,1)S(1)}, u32[]{:S(2)}, u32[]{:S(2)}) collective-permute-start(bf16[128,1024]{1,0:T(8,128)(2,1)} %refs_2_.1), channel_id=1, source_target_pairs={{0,16},{1,9},{2,18},{3,11},{4,20},{5,13},{6,22},{7,15},{8,24},{9,1... | collective-permute-start | bytes 786440 | tf_op jit(solution)/shard_map/ppermute | solution.py:39
  5.2 14.5 %collective-permute-start.3 = (bf16[128,1024]{1,0:T(8,128)(2,1)}, bf16[128,1024]{1,0:T(8,128)(2,1)S(1)}, u32[]{:S(2)}, u32[]{:S(2)}) collective-permute-start(bf16[128,1024]{1,0:T(8,128)(2,1)} %refs_2_.1), channel_id=1, source_target_pairs={{0,2},{1,3},{2,4},{3,5},{4,6},{5,7},{6,0},{7,1},{8,10},{9,11},{10,... | collective-permute-start | bytes 786440 | tf_op jit(solution)/shard_map/ppermute | solution.py:39
  6.7 13.5 %collective-permute-start.4 = (bf16[128,1024]{1,0:T(8,128)(2,1)}, bf16[128,1024]{1,0:T(8,128)(2,1)S(1)}, u32[]{:S(2)}, u32[]{:S(2)}) collective-permute-start(bf16[128,1024]{1,0:T(8,128)(2,1)} %refs_2_.1), channel_id=1, source_target_pairs={{0,6},{1,7},{2,0},{3,1},{4,2},{5,3},{6,4},{7,5},{8,14},{9,15},{10,... | collective-permute-start | bytes 786440 | tf_op jit(solution)/shard_map/ppermute | solution.py:39
  9.0 13.2 %collective-permute-start.14 = (bf16[128,1024]{1,0:T(8,128)(2,1)}, bf16[128,1024]{1,0:T(8,128)(2,1)S(1)}, u32[]{:S(2)}, u32[]{:S(2)}) collective-permute-start(bf16[128,1024]{1,0:T(8,128)(2,1)} %refs_2_.1), channel_id=1, source_target_pairs={{0,1},{1,0},{2,3},{3,2},{4,5},{5,4},{6,7},{7,6},{8,9},{9,8},{10,11... | collective-permute-start | bytes 786440 | tf_op jit(solution)/shard_map/ppermute | solution.py:39
  10.5 17.6 %copy-start.2 = (bf16[128,1024]{1,0:T(8,128)(2,1)}, bf16[128,1024]{1,0:T(8,128)(2,1)S(1)}, u32[]{:S(2)}) copy-start(bf16[128,1024]{1,0:T(8,128)(2,1)S(1)} %collective-permute-done.refs_3_) | copy-start | bytes 786436
  10.5 17.6 %copy-start.3 = (bf16[128,1024]{1,0:T(8,128)(2,1)}, bf16[128,1024]{1,0:T(8,128)(2,1)S(1)}, u32[]{:S(2)}) copy-start(bf16[128,1024]{1,0:T(8,128)(2,1)S(1)} %collective-permute-done.1.refs_4_) | copy-start | bytes 786436
  10.5 13.1 %collective-permute-start.13 = (bf16[128,1024]{1,0:T(8,128)(2,1)S(1)}, bf16[128,1024]{1,0:T(8,128)(2,1)}, u32[]{:S(2)}, u32[]{:S(2)}) collective-permute-start(bf16[128,1024]{1,0:T(8,128)(2,1)S(1)} %collective-permute-done.refs_3_), channel_id=1, source_target_pairs={{0,16},{1,9},{2,18},{3,11},{4,20},{5,13},{6,22},{7,15},{8,24},{9,1... | collective-permute-start | bytes 786440 | tf_op jit(solution)/shard_map/ppermute | solution.py:39
  13.9 14.3 %all-to-all-start = ((f32[32,1,1280]{2,1,0:T(1,128)}), f32[32,1,1280]{2,1,0:T(1,128)S(1)}, u32[]{:S(2)}, u32[]{:S(2)}) async-start(f32[32,1,1280]{2,1,0:T(1,128)} %shard_map.77), calls=%async_computation | async-start | bytes 327680 | tf_op jit(solution)/shard_map/all_to_all | solution.py:314
  19.7 3.9 %collective-permute-start.15 = (bf16[128,1024]{1,0:T(8,128)(2,1)S(1)}, bf16[128,1024]{1,0:T(8,128)(2,1)S(1)}, u32[]{:S(2)}, u32[]{:S(2)}) collective-permute-start(bf16[128,1024]{1,0:T(8,128)(2,1)S(1)} %collective-permute-done.refs_3_), channel_id=1, source_target_pairs={{0,1},{1,0},{2,3},{3,2},{4,5},{5,4},{6,7},{7,6},{8,9},{9,8},{10,11... | collective-permute-start | bytes 786440 | tf_op jit(solution)/shard_map/ppermute | solution.py:39
  20.0 4.1 %collective-permute-start.16 = (bf16[128,1024]{1,0:T(8,128)(2,1)S(1)}, bf16[128,1024]{1,0:T(8,128)(2,1)S(1)}, u32[]{:S(2)}, u32[]{:S(2)}) collective-permute-start(bf16[128,1024]{1,0:T(8,128)(2,1)S(1)} %collective-permute-done.1.refs_4_), channel_id=1, source_target_pairs={{0,1},{1,0},{2,3},{3,2},{4,5},{5,4},{6,7},{7,6},{8,9},{9,8},{10,11... | collective-permute-start | bytes 786440 | tf_op jit(solution)/shard_map/ppermute | solution.py:39
  20.3 19.5 %collective-permute-start.5 = (bf16[256,1024]{1,0:T(8,128)(2,1)S(1)}, bf16[256,1024]{1,0:T(8,128)(2,1)S(1)}, u32[]{:S(2)}, u32[]{:S(2)}) collective-permute-start(bf16[256,1024]{1,0:T(8,128)(2,1)S(1)} %constant_dynamic-update-slice_fusion.refs_2_), channel_id=1, source_target_pairs={{0,8},{1,17},{2,10},{3,19},{4,12},{5,21},{6,14},{7,23},{8,0},{9,25... | collective-permute-start | bytes 1572872 | tf_op jit(solution)/shard_map/ppermute | solution.py:39
  22.1 2.0 %copy-start.4 = (bf16[128,1024]{1,0:T(8,128)(2,1)}, bf16[128,1024]{1,0:T(8,128)(2,1)S(1)}, u32[]{:S(2)}) copy-start(bf16[128,1024]{1,0:T(8,128)(2,1)S(1)} %collective-permute-done.14.refs_6_) | copy-start | bytes 786436
  22.1 17.7 %collective-permute-start.6 = (bf16[256,1024]{1,0:T(8,128)(2,1)S(1)}, bf16[256,1024]{1,0:T(8,128)(2,1)S(1)}, u32[]{:S(2)}, u32[]{:S(2)}) collective-permute-start(bf16[256,1024]{1,0:T(8,128)(2,1)S(1)} %constant_dynamic-update-slice_fusion.refs_2_), channel_id=1, source_target_pairs={{0,16},{1,9},{2,18},{3,11},{4,20},{5,13},{6,22},{7,15},{8,24},{9,1... | collective-permute-start | bytes 1572872 | tf_op jit(solution)/shard_map/ppermute | solution.py:39
  23.6 16.2 %collective-permute-start.18 = (bf16[256,1024]{1,0:T(8,128)(2,1)S(1)}, bf16[256,1024]{1,0:T(8,128)(2,1)S(1)}, u32[]{:S(2)}, u32[]{:S(2)}) collective-permute-start(bf16[256,1024]{1,0:T(8,128)(2,1)S(1)} %constant_dynamic-update-slice_fusion.refs_2_), channel_id=1, source_target_pairs={{0,1},{1,0},{2,3},{3,2},{4,5},{5,4},{6,7},{7,6},{8,9},{9,8},{10,11... | collective-permute-start | bytes 1572872 | tf_op jit(solution)/shard_map/ppermute | solution.py:39
  23.6 0.7 copy-start.5
  23.6 4.5 %collective-permute-start.17 = (bf16[128,1024]{1,0:T(8,128)(2,1)}, bf16[128,1024]{1,0:T(8,128)(2,1)}, u32[]{:S(2)}, u32[]{:S(2)}) collective-permute-start(bf16[128,1024]{1,0:T(8,128)(2,1)} %collective-permute-done.13.refs_5_), channel_id=1, source_target_pairs={{0,1},{1,0},{2,3},{3,2},{4,5},{5,4},{6,7},{7,6},{8,9},{9,8},{10,11... | collective-permute-start | bytes 786440 | tf_op jit(solution)/shard_map/ppermute | solution.py:39
  24.3 2.4 %copy-start.6 = (bf16[128,1024]{1,0:T(8,128)(2,1)}, bf16[128,1024]{1,0:T(8,128)(2,1)S(1)}, u32[]{:S(2)}) copy-start(bf16[128,1024]{1,0:T(8,128)(2,1)S(1)} %collective-permute-done.16.refs_8_) | copy-start | bytes 786436
  24.3 15.4 %collective-permute-start.2 = (bf16[128,1024]{1,0:T(8,128)(2,1)}, bf16[128,1024]{1,0:T(8,128)(2,1)S(1)}, u32[]{:S(2)}, u32[]{:S(2)}) collective-permute-start(bf16[128,1024]{1,0:T(8,128)(2,1)} %refs_2_.1), channel_id=1, source_target_pairs={{0,4},{1,5},{2,6},{3,7},{4,0},{5,1},{6,2},{7,3},{8,12},{9,13},{10,... | collective-permute-start | bytes 786440 | tf_op jit(solution)/shard_map/ppermute | solution.py:39
  39.8 10.0 %copy-start = (bf16[128,1024]{1,0:T(8,128)(2,1)}, bf16[128,1024]{1,0:T(8,128)(2,1)S(1)}, u32[]{:S(2)}) copy-start(bf16[128,1024]{1,0:T(8,128)(2,1)S(1)} %collective-permute-done.2.refs_2_) | copy-start | bytes 786436
  39.8 14.5 %collective-permute-start.19 = (bf16[256,1024]{1,0:T(8,128)(2,1)S(1)}, bf16[256,1024]{1,0:T(8,128)(2,1)S(1)}, u32[]{:S(2)}, u32[]{:S(2)}) collective-permute-start(bf16[256,1024]{1,0:T(8,128)(2,1)S(1)} %collective-permute-done.5.refs_3_), channel_id=1, source_target_pairs={{0,16},{1,9},{2,18},{3,11},{4,20},{5,13},{6,22},{7,15},{8,24},{9,1... | collective-permute-start | bytes 1572872 | tf_op jit(solution)/shard_map/ppermute | solution.py:39
  40.4 9.4 %collective-permute-start.7 = (bf16[128,1024]{1,0:T(8,128)(2,1)S(1)}, bf16[128,1024]{1,0:T(8,128)(2,1)}, u32[]{:S(2)}, u32[]{:S(2)}) collective-permute-start(bf16[128,1024]{1,0:T(8,128)(2,1)S(1)} %collective-permute-done.2.refs_2_), channel_id=1, source_target_pairs={{0,8},{1,17},{2,10},{3,19},{4,12},{5,21},{6,14},{7,23},{8,0},{9,25... | collective-permute-start | bytes 786440 | tf_op jit(solution)/shard_map/ppermute | solution.py:39
  41.2 12.6 %collective-permute-start.8 = (bf16[128,1024]{1,0:T(8,128)(2,1)S(1)}, bf16[128,1024]{1,0:T(8,128)(2,1)}, u32[]{:S(2)}, u32[]{:S(2)}) collective-permute-start(bf16[128,1024]{1,0:T(8,128)(2,1)S(1)} %collective-permute-done.2.refs_2_), channel_id=1, source_target_pairs={{0,16},{1,9},{2,18},{3,11},{4,20},{5,13},{6,22},{7,15},{8,24},{9,1... | collective-permute-start | bytes 786440 | tf_op jit(solution)/shard_map/ppermute | solution.py:39
  53.8 2.6 %collective-permute-start.21 = (bf16[256,1024]{1,0:T(8,128)(2,1)S(1)}, bf16[256,1024]{1,0:T(8,128)(2,1)S(1)}, u32[]{:S(2)}, u32[]{:S(2)}) collective-permute-start(bf16[256,1024]{1,0:T(8,128)(2,1)S(1)} %collective-permute-done.6.refs_4_), channel_id=1, source_target_pairs={{0,1},{1,0},{2,3},{3,2},{4,5},{5,4},{6,7},{7,6},{8,9},{9,8},{10,11... | collective-permute-start | bytes 1572872 | tf_op jit(solution)/shard_map/ppermute | solution.py:39
  53.8 2.8 %collective-permute-start.20 = (bf16[256,1024]{1,0:T(8,128)(2,1)S(1)}, bf16[256,1024]{1,0:T(8,128)(2,1)}, u32[]{:S(2)}, u32[]{:S(2)}) collective-permute-start(bf16[256,1024]{1,0:T(8,128)(2,1)S(1)} %collective-permute-done.5.refs_3_), channel_id=1, source_target_pairs={{0,1},{1,0},{2,3},{3,2},{4,5},{5,4},{6,7},{7,6},{8,9},{9,8},{10,11... | collective-permute-start | bytes 1572872 | tf_op jit(solution)/shard_map/ppermute | solution.py:39
  54.3 3.4 %collective-permute-start.22 = (bf16[256,1024]{1,0:T(8,128)(2,1)S(1)}, bf16[256,1024]{1,0:T(8,128)(2,1)}, u32[]{:S(2)}, u32[]{:S(2)}) collective-permute-start(bf16[256,1024]{1,0:T(8,128)(2,1)S(1)} %collective-permute-done.19.refs_5_), channel_id=1, source_target_pairs={{0,1},{1,0},{2,3},{3,2},{4,5},{5,4},{6,7},{7,6},{8,9},{9,8},{10,11... | collective-permute-start | bytes 1572872 | tf_op jit(solution)/shard_map/ppermute | solution.py:39
  54.4 17.1 %collective-permute-start.10 = (bf16[128,1024]{1,0:T(8,128)(2,1)}, bf16[128,1024]{1,0:T(8,128)(2,1)}, u32[]{:S(2)}, u32[]{:S(2)}) collective-permute-start(bf16[128,1024]{1,0:T(8,128)(2,1)} %copy-done), channel_id=1, source_target_pairs={{0,1},{1,0},{2,3},{3,2},{4,5},{5,4},{6,7},{7,6},{8,9},{9,8},{10,11... | collective-permute-start | bytes 786440 | tf_op jit(solution)/shard_map/ppermute | solution.py:39
  54.9 16.3 %collective-permute-start.9 = (bf16[128,1024]{1,0:T(8,128)(2,1)}, bf16[128,1024]{1,0:T(8,128)(2,1)}, u32[]{:S(2)}, u32[]{:S(2)}) collective-permute-start(bf16[128,1024]{1,0:T(8,128)(2,1)} %collective-permute-done.7.refs_3_), channel_id=1, source_target_pairs={{0,16},{1,9},{2,18},{3,11},{4,20},{5,13},{6,22},{7,15},{8,24},{9,1... | collective-permute-start | bytes 786440 | tf_op jit(solution)/shard_map/ppermute | solution.py:39
  56.4 15.1 %collective-permute-start.11 = (bf16[128,1024]{1,0:T(8,128)(2,1)}, bf16[128,1024]{1,0:T(8,128)(2,1)}, u32[]{:S(2)}, u32[]{:S(2)}) collective-permute-start(bf16[128,1024]{1,0:T(8,128)(2,1)} %collective-permute-done.7.refs_3_), channel_id=1, source_target_pairs={{0,1},{1,0},{2,3},{3,2},{4,5},{5,4},{6,7},{7,6},{8,9},{9,8},{10,11... | collective-permute-start | bytes 786440 | tf_op jit(solution)/shard_map/ppermute | solution.py:39
  56.6 14.9 %collective-permute-start.12 = (bf16[128,1024]{1,0:T(8,128)(2,1)}, bf16[128,1024]{1,0:T(8,128)(2,1)}, u32[]{:S(2)}, u32[]{:S(2)}) collective-permute-start(bf16[128,1024]{1,0:T(8,128)(2,1)} %collective-permute-done.8.refs_4_), channel_id=1, source_target_pairs={{0,1},{1,0},{2,3},{3,2},{4,5},{5,4},{6,7},{7,6},{8,9},{9,8},{10,11... | collective-permute-start | bytes 786440 | tf_op jit(solution)/shard_map/ppermute | solution.py:39
  71.2 1.8 %collective-permute-start.23 = (bf16[128,1024]{1,0:T(8,128)(2,1)}, bf16[128,1024]{1,0:T(8,128)(2,1)S(1)}, u32[]{:S(2)}, u32[]{:S(2)}) collective-permute-start(bf16[128,1024]{1,0:T(8,128)(2,1)} %collective-permute-done.9.refs_5_), channel_id=1, source_target_pairs={{0,1},{1,0},{2,3},{3,2},{4,5},{5,4},{6,7},{7,6},{8,9},{9,8},{10,11... | collective-permute-start | bytes 786440 | tf_op jit(solution)/shard_map/ppermute | solution.py:39
  71.4 23.5 %copy-start.7 = (f32[128]{0:T(128)S(1)}, f32[128]{0:T(128)}, u32[]{:S(2)}) copy-start(f32[128]{0:T(128)} %param.10) | copy-start | bytes 1540
  73.0 1.0 copy-start.1
  82.7 12.0 %all-to-all-start.1 = ((f32[32,3,128]{2,1,0:T(4,128)}), f32[32,3,128]{2,1,0:T(4,128)S(1)}, u32[]{:S(2)}, u32[]{:S(2)}) async-start(f32[32,3,128]{2,1,0:T(4,128)} %bitcast.13), calls=%async_computation.1 | async-start | bytes 131072 | tf_op jit(solution)/shard_map/all_to_all | solution.py:336

commit v4 on v1

v4 whole, which is shorter than its diff:
```python
import functools

import jax
import jax.numpy as jnp
from jax import lax
from jax.experimental import pallas as pl
from jax.experimental.pallas import tpu as pltpu
from jax.sharding import PartitionSpec as P

D = 8192
CORES = 2
X_ONLY, Y_ONLY = (0, 1), (1, 0)
VMEM_LIMIT = 16 * 1024 * 1024
SMALL_LIMIT = 6 * 1024 * 1024


class Grid:
    def __init__(self, n_dp, n_t):
        self.n_t = n_t
        self.cols = 2
        self.rows = n_dp // self.cols
        self.depth = n_t // CORES
        self.square = self.rows == self.cols
        self.first = (X_ONLY, Y_ONLY) if self.square else (X_ONLY, X_ONLY)
        self.second = (Y_ONLY, X_ONLY) if self.square else (Y_ONLY, Y_ONLY)
        self.spots = [(j, i) for j in range(self.rows) for i in range(self.cols)]

    def permute(self, a, place):
        perm = []
        for y in range(self.rows):
            for x in range(self.cols):
                for z in range(self.depth):
                    for c in range(CORES):
                        src = (y * self.cols + x) * self.n_t + z * CORES + c
                        v, u, w, d = place(y, x, z, c)
                        dst = (v % self.rows * self.cols + u % self.cols) * self.n_t
                        perm.append((src, dst + w % self.depth * CORES + d % CORES))
        return lax.ppermute(a, ("dp", "tensor"), perm)

    def plane(self, a, ways, step):
        def place(y, x, z, c):
            return y + ways[c][0] * step, x + ways[c][1] * step, z, c

        return self.permute(a, place)

    def along(self, a, step):
        return self.permute(a, lambda y, x, z, c: (y, x, z + step, c))

    def sibling(self, a):
        return self.permute(a, lambda y, x, z, c: (y, x, z, c + 1))

    def reach(self, a):
        got = {(0, 0): a}
        for i in range(1, self.cols):
            got[0, i] = self.plane(a, self.first, i)
        for j in range(1, self.rows):
            got[j, 0] = self.plane(a, self.second, j)
        return got

    def fill(self, got, *late):
        late = (*late, *got.values())
        for j in range(1, self.rows):
            for i in range(1, self.cols):
                got[j, i] = self.plane(after(got[0, i], *late), self.second, j)
        return [got[s] for s in self.spots]

    def owners(self, y, x, c):
        ways = [(self.first[k], self.second[k]) for k in range(CORES)]
        out = []
        for j, i in self.spots:
            at = [
                (y - f[0] * i - s[0] * j) % self.rows * self.cols + (x - f[1] * i - s[1] * j) % self.cols
                for f, s in ways
            ]
            out.append(jnp.where(c == 0, at[0], at[1]))
        return out

    def sibling_spot(self, k):
        j, i = self.spots[k]
        return self.spots.index((i, j)) if self.square else k


def far(a):
    return pltpu.with_memory_space_constraint(a, pltpu.HBM)


def after(a, *others):
    return lax.optimization_barrier((a, *others))[0] if others else a


def diagonal(size):
    row = lax.broadcasted_iota(jnp.int32, (size, size), 0)
    return row == lax.broadcasted_iota(jnp.int32, (size, size), 1)


def to_column(row):
    return jnp.sum(jnp.where(diagonal(row.shape[1]), row, 0.0), axis=1, keepdims=True)


def to_row(column):
    return jnp.sum(jnp.where(diagonal(column.shape[0]), column, 0.0), axis=0, keepdims=True)


def load_kernel(offsets, start_ref, head_ref, out_ref, sems):
    size, deep = out_ref.shape[:2]
    copies = []
    for j in range(size):
        rows = pl.ds(pl.multiple_of(start_ref[offsets[j]] * deep, deep), deep)
        copies.append(pltpu.make_async_copy(head_ref.at[rows], out_ref.at[j], sems.at[j]))
        copies[-1].start()
    for copy in copies:
        copy.wait()


def loaded(starts, offsets, head, deep):
    return pl.pallas_call(
        functools.partial(load_kernel, offsets),
        out_shape=pltpu.VMEM((len(offsets), deep, head.shape[1]), head.dtype),
        in_specs=[pl.BlockSpec(memory_space=pltpu.SMEM), pl.BlockSpec(memory_space=pl.ANY)],
        out_specs=pl.BlockSpec(memory_space=pltpu.VMEM),
        scratch_shapes=[pltpu.SemaphoreType.DMA((len(offsets),))],
        compiler_params=pltpu.CompilerParams(vmem_limit_bytes=SMALL_LIMIT),
    )(starts, far(head))


def join_kernel(*refs):
    tok = refs[0].shape[0]
    for j, ref in enumerate(refs[:-1]):
        refs[-1][j * tok : (j + 1) * tok, :] = ref[...]


def joined(blocks):
    tok, feat = blocks[0].shape
    vmem = pl.BlockSpec(memory_space=pltpu.VMEM)
    return pl.pallas_call(
        join_kernel,
        out_shape=jax.ShapeDtypeStruct((len(blocks) * tok, feat), blocks[0].dtype),
        in_specs=[vmem] * len(blocks),
        out_specs=vmem,
        compiler_params=pltpu.CompilerParams(vmem_limit_bytes=SMALL_LIMIT),
    )(*blocks)


def group_kernel(n, n_t, place, offsets, first, last, *refs):
    refs = list(refs)
    start_ref, fine = refs.pop(0), refs.pop(0)
    blocks = [refs.pop(0) for _ in range(CORES * n)]
    weights = refs.pop(0)
    acc_ref = None if first else refs.pop(0)
    out_ref, rows = refs[:2]
    acc = refs[2] if last else out_ref
    feat = blocks[0].shape[1]
    tok = rows.shape[0] // n
    c_me, base = start_ref[0], start_ref[1]
    owners = [start_ref[2 + k] for k in range(n)]
    scales = []
    for k in range(n):
        sums = jnp.sum(fine[pl.ds(owners[k] * n_t, n_t), :, feat : feat + tok], axis=0)
        scales.append(to_column(lax.rsqrt(sums / D + 1e-06)))
    for j, offset in enumerate(offsets):
        for c in range(CORES):
            core = 1 - c_me if c else c_me
            gain = fine[start_ref[offset] * CORES + core, :, :feat]
            columns = pl.ds(pl.multiple_of(core * feat, feat), feat)
            for k in range(n):
                spot = place[k] if c else k
                part = blocks[c * n + k][j * tok : (j + 1) * tok, :].astype(jnp.float32)
                part = part * scales[spot] * gain
                rows[spot * tok : (spot + 1) * tok, columns] = part.astype(jnp.bfloat16)
        product = jnp.dot(rows[...], weights[j], preferred_element_type=jnp.float32)
        if j:
            acc[...] += product
        else:
            acc[...] = product if first else acc_ref[...] + product
    if not last:
        return
    for b in range(n):
        logits = acc[b * tok : (b + 1) * tok, :]
        top = jnp.max(logits, axis=1, keepdims=True)
        total = jnp.sum(jnp.exp(logits - top), axis=1, keepdims=True)
        entry = lax.broadcasted_iota(jnp.int32, logits.shape, 1) + base
        target = fine[owners[b] * n_t, :, feat + tok : feat + 2 * tok]
        target = to_column(target).astype(jnp.int32)
        pick = jnp.sum(jnp.where(entry == target, logits, 0.0), axis=1, keepdims=True)
        for peer in range(n_t):
            out_ref[owners[b], peer, 0:1, :] = to_row(top)
            out_ref[owners[b], peer, 1:2, :] = to_row(total)
            out_ref[owners[b], peer, 2:3, :] = to_row(pick)


def group_product(tok, n_t, starts, offsets, fine, blocks, place, weights, acc, last):
    n = len(place)
    feat = blocks[0].shape[1]
    size, deep, vocab = weights.shape
    vmem = pl.BlockSpec(memory_space=pltpu.VMEM)
    first = acc is None
    logits = jax.ShapeDtypeStruct((n * tok, vocab), jnp.float32)
    operands = [starts, fine, *blocks, weights] + ([] if first else [acc])
    scratch = [pltpu.VMEM((n * tok, deep), jnp.bfloat16)]
    if last:
        scratch.append(pltpu.VMEM(logits.shape, jnp.float32))
    return pl.pallas_call(
        functools.partial(group_kernel, n, n_t, place, offsets, first, last),
        out_shape=jax.ShapeDtypeStruct((n, n_t, 3, tok), jnp.float32) if last else logits,
        in_specs=[pl.BlockSpec(memory_space=pltpu.SMEM)] + [vmem] * (len(operands) - 1),
        out_specs=vmem,
        scratch_shapes=scratch,
        compiler_params=pltpu.CompilerParams(vmem_limit_bytes=VMEM_LIMIT),
        cost_estimate=pl.CostEstimate(
            flops=2 * n * tok * deep * vocab * size, bytes_accessed=2 * deep * vocab * size, transcendentals=0
        ),
    )(*operands)


def squares_kernel(hidden_ref, gain_ref, target_ref, out_ref, raw, gain, target, sems):
    pairs = ((hidden_ref, raw), (gain_ref, gain), (target_ref, target))
    copies = [pltpu.make_async_copy(a, b, sems.at[i]) for i, (a, b) in enumerate(pairs)]
    for copy in copies:
        copy.start()
    for copy in copies:
        copy.wait()
    tok, feat = raw.shape
    values = raw[...].astype(jnp.float32)
    sums = to_row(jnp.sum(values * values, axis=1, keepdims=True))
    peers = out_ref.shape[0]
    for peer in range(peers):
        out_ref[peer, :, :feat] = gain[...]
        out_ref[peer, :, feat : feat + tok] = sums
        out_ref[peer, :, feat + tok :] = target[...].astype(jnp.float32)


def squares(hidden, gain, targets, peers):
    tok, feat = hidden.shape
    return pl.pallas_call(
        squares_kernel,
        out_shape=jax.ShapeDtypeStruct((peers, 1, feat + 2 * tok), jnp.float32),
        in_specs=[pl.BlockSpec(memory_space=pltpu.HBM)] * 3,
        out_specs=pl.BlockSpec(memory_space=pltpu.VMEM),
        scratch_shapes=[
            pltpu.VMEM(hidden.shape, hidden.dtype),
            pltpu.VMEM(gain.shape, gain.dtype),
            pltpu.VMEM(targets.shape, targets.dtype),
            pltpu.SemaphoreType.DMA((3,)),
        ],
        compiler_params=pltpu.CompilerParams(vmem_limit_bytes=SMALL_LIMIT),
    )(far(hidden), far(gain), far(targets))


def body(hidden, norm_gain, head, targets, old_logprob, lengths):
    n_dp, n_t = lax.axis_size("dp"), lax.axis_size("tensor")
    grid = Grid(n_dp, n_t)
    depth = grid.depth
    tok, feat = hidden.shape
    plane, tensor = lax.axis_index("dp"), lax.axis_index("tensor")
    z_me, c_me = tensor // CORES, tensor % CORES
    owners = grid.owners(plane // grid.cols, plane % grid.cols, c_me)
    groups = [[0]] + [[d, depth - d] for d in range(1, (depth + 1) // 2)] + [[depth // 2]]
    place = [grid.sibling_spot(k) for k in range(n_dp)]

    layers = {0: hidden}
    reached = [grid.reach(hidden)]
    before = []
    for group in groups[1:]:
        for dz in group:
            layers[dz] = grid.along(after(hidden, *before), dz)
        before = list(reached[0].values()) if len(before) == 0 else [layers[dz] for dz in group]
    for group in groups[1:]:
        sources = [layers[dz] for dz in group]
        sources[0] = after(sources[0], *reached[-1].values())
        reached.append(grid.reach(joined(sources) if len(sources) > 1 else sources[0]))

    vocab_cols = head.shape[1]
    vocab_start = lax.axis_index(("dp", "tensor")) * vocab_cols
    starts = jnp.stack([c_me, vocab_start] + owners + [(z_me - dz) % depth for dz in range(depth)])
    packed = squares(after(hidden, starts), norm_gain[None, :], targets[None, :], n_dp * n_t)
    fine = lax.all_to_all(packed, ("dp", "tensor"), 0, 0, tiled=True)

    acc, deep = None, CORES * feat
    for at, group in enumerate(groups):
        final = at == len(groups) - 1
        middle = at and not final
        offsets = [2 + n_dp + dz for dz in group]
        own = grid.sibling(reached[at][0, 0])
        held = [layers[dz] for dz in groups[at + 1]] + [own] if middle else []
        spread = grid.fill(dict(reached[at]), *([acc] if at == 1 else []), *held)
        if at == 0:
            weights = [loaded(starts, offsets, after(head, packed), deep)]
        elif at == 1:
            for later in groups[1:]:
                ready = after(head, acc, *(layers[dz] for dz in groups[2]))
                weights.append(loaded(starts, [2 + n_dp + dz for dz in later], ready, deep))
        following = [*reached[at + 1].values(), *weights[1:3]] if middle else []
        others = [own] + [grid.sibling(after(a, *following)) for a in spread[1:-1]]
        others.append(grid.sibling(after(spread[-1], *([acc] if final else following))))
        blocks = spread + others
        acc = group_product(tok, n_t, starts, offsets, fine, blocks, place, weights[at], acc, final)

    parts = lax.all_to_all(acc.reshape(n_dp * n_t, 3, tok), ("dp", "tensor"), 0, 0, tiled=True)
    top = jnp.max(parts[:, 0], axis=0)
    total = jnp.sum(parts[:, 1] * jnp.exp(parts[:, 0] - top[None, :]), axis=0)
    picked = jnp.sum(parts[:, 2], axis=0)

    seq_count = lengths.shape[0]
    position = jnp.arange(tok // seq_count, dtype=jnp.int32)
    live = (position[None, :] < lengths[:, None]).reshape(-1).astype(jnp.float32)
    logprob = picked - top - jnp.log(total)
    return (live * logprob, live * (logprob - old_logprob))


def solution(mesh):
    in_specs = (
        P("dp", "tensor"),
        P("tensor"),
        P(None, ("dp", "tensor")),
        P("dp"),
        P("dp"),
        P("dp"),
    )
    out_specs = (P("dp"), P("dp"))
    return jax.shard_map(body, mesh=mesh, in_specs=in_specs, out_specs=out_specs, check_vma=False)
```

time: 97.4 us -> 85.6 us (0.88)
  waiting for transfers between devices: 26.9 us -> 16.1 us
  local copies, waits for them, and re-layouts: 10 us -> 6.2 us
  starting transfers between devices: 28.2 us -> 30.6 us
    ppermute x24, waiting for transfers between devices: 20.1 us -> 9.33 us  [permute(): return lax.ppermute(a, ('dp', 'tensor'), perm)]
    unnamed x34 -> x12, local copies, waits for them, and re-layouts: 8.8 us -> 6.12 us
    all_to_all x1, starting transfers between devices: 2.58 us -> 5.05 us  [body(): fine = lax.all_to_all(packed, ('dp', 'tensor'), 0, 0, tiled=True)]
    all_to_all x1, starting transfers between devices: 5.11 us -> 3.92 us  [body(): lax.all_to_all(acc.reshape(n_dp * n_t, 3, tok), ('dp', 'tensor'), 0, 0, t...]
    ppermute x24, starting transfers between devices: 20.5 us -> 21.6 us  [permute(): return lax.ppermute(a, ('dp', 'tensor'), perm)]
    pallas_call x5 -> x8, Pallas kernels: 29.7 us -> 30.2 us  [the longest x3 18.3 us: group_product(): pl.pallas_call(functools.partial(group_kernel, n, n_t, place, offsets, fi...]
  transfers between devices with their start and end apart: 26 -> 26, of which waited for: 7 -> 9; matrix products, arithmetic and copies ran while one was open for 1% -> 0% of each run, Pallas kernels for 22% -> 29%
where the time goes in v4:
time: 85.6 us; the launch traced here: 85.2 us
  starting transfers between devices  30.6 us (36%)
  Pallas kernels  30.2 us (35%)
  waiting for transfers between devices  16.1 us (19%)
  local copies, waits for them, and re-layouts  6.2 us (7%)
  between operations  1.46 us (2%)
    ppermute x24, starting transfers between devices, permute(): return lax.ppermute(a, ('dp', 'tensor'), perm)  21.6 us
    pallas_call x3, Pallas kernels, group_product(): pl.pallas_call(functools.partial(group_kernel, n, n_t, place, offsets, fi...  18.3 us
    pallas_call x3, Pallas kernels, loaded(): pl.pallas_call(functools.partial(load_kernel, offsets), out_shape=pltpu.V...  10.1 us
    ppermute x24, waiting for transfers between devices, permute(): return lax.ppermute(a, ('dp', 'tensor'), perm)  9.33 us
    all_to_all x1, waiting for transfers between devices, body(): lax.all_to_all(acc.reshape(n_dp * n_t, 3, tok), ('dp', 'tensor'), 0, 0, t...  6.74 us
    unnamed x12, local copies, waits for them, and re-layouts  6.12 us
    all_to_all x1, starting transfers between devices, body(): fine = lax.all_to_all(packed, ('dp', 'tensor'), 0, 0, tiled=True)  5.05 us
    all_to_all x1, starting transfers between devices, body(): lax.all_to_all(acc.reshape(n_dp * n_t, 3, tok), ('dp', 'tensor'), 0, 0, t...  3.92 us
  transfers between devices with their start and end apart: 26, of which 9 were waited for; matrix products, arithmetic and copies ran while one was open for 0% of the time, Pallas kernels for 29%

profile of v4, /device:TPU:0, one launch (start us, length us, event | category | flops | bytes accessed | tf_op | source)
XLA Modules:
  0.0 85.2 jit_solution(11357203713284198875)
XLA Ops:
  0.6 3.0 %collective-permute-start = (bf16[128,1024]{1,0:T(8,128)(2,1)}, bf16[128,1024]{1,0:T(8,128)(2,1)S(1)}, u32[]{:S(2)}, u32[]{:S(2)}) collective-permute-start(bf16[128,1024]{1,0:T(8,128)(2,1)} %refs_2_.1), channel_id=1, source_target_pairs={{0,8},{1,17},{2,10},{3,19},{4,12},{5,21},{6,14},{7,23},{8,0},{9,25... | collective-permute-start | bytes 786440 | tf_op jit(solution)/shard_map/ppermute | solution.py:38
  3.6 1.5 %collective-permute-start.1 = (bf16[128,1024]{1,0:T(8,128)(2,1)}, bf16[128,1024]{1,0:T(8,128)(2,1)S(1)}, u32[]{:S(2)}, u32[]{:S(2)}) collective-permute-start(bf16[128,1024]{1,0:T(8,128)(2,1)} %refs_2_.1), channel_id=1, source_target_pairs={{0,16},{1,9},{2,18},{3,11},{4,20},{5,13},{6,22},{7,15},{8,24},{9,1... | collective-permute-start | bytes 786440 | tf_op jit(solution)/shard_map/ppermute | solution.py:38
  5.2 1.6 %collective-permute-start.3 = (bf16[128,1024]{1,0:T(8,128)(2,1)}, bf16[128,1024]{1,0:T(8,128)(2,1)S(1)}, u32[]{:S(2)}, u32[]{:S(2)}) collective-permute-start(bf16[128,1024]{1,0:T(8,128)(2,1)} %refs_2_.1), channel_id=1, source_target_pairs={{0,2},{1,3},{2,4},{3,5},{4,6},{5,7},{6,0},{7,1},{8,10},{9,11},{10,... | collective-permute-start | bytes 786440 | tf_op jit(solution)/shard_map/ppermute | solution.py:38
  6.7 2.2 %collective-permute-start.4 = (bf16[128,1024]{1,0:T(8,128)(2,1)}, bf16[128,1024]{1,0:T(8,128)(2,1)S(1)}, u32[]{:S(2)}, u32[]{:S(2)}) collective-permute-start(bf16[128,1024]{1,0:T(8,128)(2,1)} %refs_2_.1), channel_id=1, source_target_pairs={{0,6},{1,7},{2,0},{3,1},{4,2},{5,3},{6,4},{7,5},{8,14},{9,15},{10,... | collective-permute-start | bytes 786440 | tf_op jit(solution)/shard_map/ppermute | solution.py:38
  9.0 1.6 %collective-permute-done.refs_3_ = bf16[128,1024]{1,0:T(8,128)(2,1)S(1)} collective-permute-done((bf16[128,1024]{1,0:T(8,128)(2,1)}, bf16[128,1024]{1,0:T(8,128)(2,1)S(1)}, u32[]{:S(2)}, u32[]{:S(2)}) %collective-permute-start) | collective-permute-done | bytes 262176 | tf_op jit(solution)/shard_map/ppermute | solution.py:38
  10.5 1.5 %collective-permute-start.13 = (bf16[128,1024]{1,0:T(8,128)(2,1)S(1)}, bf16[128,1024]{1,0:T(8,128)(2,1)}, u32[]{:S(2)}, u32[]{:S(2)}) collective-permute-start(bf16[128,1024]{1,0:T(8,128)(2,1)S(1)} %collective-permute-done.refs_3_), channel_id=1, source_target_pairs={{0,16},{1,9},{2,18},{3,11},{4,20},{5,13},{6,22},{7,15},{8,24},{9,1... | collective-permute-start | bytes 786440 | tf_op jit(solution)/shard_map/ppermute | solution.py:38
  12.0 0.9 %collective-permute-start.15 = (bf16[128,1024]{1,0:T(8,128)(2,1)S(1)}, bf16[128,1024]{1,0:T(8,128)(2,1)}, u32[]{:S(2)}, u32[]{:S(2)}) collective-permute-start(bf16[128,1024]{1,0:T(8,128)(2,1)S(1)} %collective-permute-done.refs_3_), channel_id=1, source_target_pairs={{0,1},{1,0},{2,3},{3,2},{4,5},{5,4},{6,7},{7,6},{8,9},{9,8},{10,11... | collective-permute-start | bytes 786440 | tf_op jit(solution)/shard_map/ppermute | solution.py:38
  12.9 0.1 stack.43.start_ref.refs_0_
  12.9 1.8 %shard_map.77 = f32[32,1,1280]{2,1,0:T(1,128)} custom-call(bf16[128,1024]{1,0:T(8,128)(2,1)} %refs_2_.1, f32[1,1024]{1,0:T(1,128)} %bitcast.22, s32[1,128]{1,0:T(1,128)} %bitcast.23), custom_call_target="tpu_custom_call" | custom-call | tf_op jit(solution)/shard_map/pallas_call | solution.py:234
  14.7 5.0 %all-to-all-start = ((f32[32,1,1280]{2,1,0:T(1,128)}), f32[32,1,1280]{2,1,0:T(1,128)S(1)}, u32[]{:S(2)}, u32[]{:S(2)}) async-start(f32[32,1,1280]{2,1,0:T(1,128)} %shard_map.77), calls=%async_computation | async-start | bytes 327680 | tf_op jit(solution)/shard_map/all_to_all | solution.py:276
  19.8 0.3 collective-permute-start.16
  20.1 0.2 collective-permute-done.4.refs_1_
  20.4 0.0 copy-start.2
  20.4 1.5 %collective-permute-start.5 = (bf16[256,1024]{1,0:T(8,128)(2,1)S(1)}, bf16[256,1024]{1,0:T(8,128)(2,1)S(1)}, u32[]{:S(2)}, u32[]{:S(2)}) collective-permute-start(bf16[256,1024]{1,0:T(8,128)(2,1)S(1)} %shard_map.78.refs_2_), channel_id=1, source_target_pairs={{0,8},{1,17},{2,10},{3,19},{4,12},{5,21},{6,14},{7,23},{8,0},{9,25... | collective-permute-start | bytes 1572872 | tf_op jit(solution)/shard_map/ppermute | solution.py:38
  21.9 1.5 %collective-permute-start.6 = (bf16[256,1024]{1,0:T(8,128)(2,1)S(1)}, bf16[256,1024]{1,0:T(8,128)(2,1)S(1)}, u32[]{:S(2)}, u32[]{:S(2)}) collective-permute-start(bf16[256,1024]{1,0:T(8,128)(2,1)S(1)} %shard_map.78.refs_2_), channel_id=1, source_target_pairs={{0,16},{1,9},{2,18},{3,11},{4,20},{5,13},{6,22},{7,15},{8,24},{9,1... | collective-permute-start | bytes 1572872 | tf_op jit(solution)/shard_map/ppermute | solution.py:38
  23.4 0.5 collective-permute-start.17
  23.9 0.7 copy-done.3
  24.6 2.4 %collective-permute-start.2 = (bf16[128,1024]{1,0:T(8,128)(2,1)}, bf16[128,1024]{1,0:T(8,128)(2,1)}, u32[]{:S(2)}, u32[]{:S(2)}) collective-permute-start(bf16[128,1024]{1,0:T(8,128)(2,1)} %refs_2_.1), channel_id=1, source_target_pairs={{0,4},{1,5},{2,6},{3,7},{4,0},{5,1},{6,2},{7,3},{8,12},{9,13},{10,... | collective-permute-start | bytes 786440 | tf_op jit(solution)/shard_map/ppermute | solution.py:38
  27.0 2.9 %shard_map.79.refs_10_ = bf16[1,2048,1152]{2,1,0:T(8,128)(2,1)S(1)} custom-call(s32[10]{0:T(128)S(1)} %stack.43.start_ref.refs_0_, bf16[8192,1152]{1,0:T(8,128)(2,1)} %head_ref.2), custom_call_target="tpu_custom_call" | custom-call | tf_op jit(solution)/shard_map/pallas_call | solution.py:116
  29.9 2.1 %copy-done = bf16[1,2048,1152]{2,1,0:T(8,128)(2,1)} copy-done((bf16[1,2048,1152]{2,1,0:T(8,128)(2,1)}, bf16[1,2048,1152]{2,1,0:T(8,128)(2,1)S(1)}, u32[]{:S(2)}) %copy-start) | copy-done | bytes 4718616
  32.0 2.3 %copy-done.1 = bf16[1,2048,1152]{2,1,0:T(8,128)(2,1)S(1)} copy-done((bf16[1,2048,1152]{2,1,0:T(8,128)(2,1)S(1)}, bf16[1,2048,1152]{2,1,0:T(8,128)(2,1)}, u32[]{:S(2)}) %copy-start.1) | copy-done | bytes 4718616
  34.4 0.9 %copy-done.4 = bf16[128,1024]{1,0:T(8,128)(2,1)S(1)} copy-done((bf16[128,1024]{1,0:T(8,128)(2,1)S(1)}, bf16[128,1024]{1,0:T(8,128)(2,1)}, u32[]{:S(2)}) %copy-start.4) | copy-done | bytes 262168
  35.3 4.8 %shard_map.80.refs_11_ = f32[512,1152]{1,0:T(8,128)S(1)} custom-call(s32[10]{0:T(128)S(1)} %stack.43.start_ref.refs_0_, f32[32,1,1280]{2,1,0:T(1,128)S(1)} %all-to-all-done.refs_1_, bf16[128,1024]{1,0:T(8,128)(2,1)S(1)} %copy-done.2, bf16[128,1024]{1,0:T(8,128)(2,1)S(1)} %collective-permute-done.refs_3_, ...), custom_call_target="tpu_custom_call" | custom-call | flops 2415919104 | bytes 4718592 | tf_op jit(solution)/shard_map/pallas_call | solution.py:202
  40.1 0.6 collective-permute-start.19
  40.7 0.7 collective-permute-start.7
  41.4 1.4 %collective-permute-start.8 = (bf16[128,1024]{1,0:T(8,128)(2,1)}, bf16[128,1024]{1,0:T(8,128)(2,1)S(1)}, u32[]{:S(2)}, u32[]{:S(2)}) collective-permute-start(bf16[128,1024]{1,0:T(8,128)(2,1)} %collective-permute-done.2.refs_2_), channel_id=1, source_target_pairs={{0,16},{1,9},{2,18},{3,11},{4,20},{5,13},{6,22},{7,15},{8,24},{9,1... | collective-permute-start | bytes 786440 | tf_op jit(solution)/shard_map/ppermute | solution.py:38
  42.8 4.3 %shard_map.81.refs_10_ = bf16[2,2048,1152]{2,1,0:T(8,128)(2,1)S(1)} custom-call(s32[10]{0:T(128)S(1)} %stack.43.start_ref.refs_0_, bf16[8192,1152]{1,0:T(8,128)(2,1)} %head_ref.2), custom_call_target="tpu_custom_call" | custom-call | tf_op jit(solution)/shard_map/pallas_call | solution.py:116
  47.1 2.9 %shard_map.82.refs_10_ = bf16[1,2048,1152]{2,1,0:T(8,128)(2,1)S(1)} custom-call(s32[10]{0:T(128)S(1)} %stack.43.start_ref.refs_0_, bf16[8192,1152]{1,0:T(8,128)(2,1)} %head_ref.2), custom_call_target="tpu_custom_call" | custom-call | tf_op jit(solution)/shard_map/pallas_call | solution.py:116
  50.0 0.2 collective-permute-done.7.refs_3_
  50.2 4.1 %collective-permute-done.8.refs_4_ = bf16[128,1024]{1,0:T(8,128)(2,1)S(1)} collective-permute-done((bf16[128,1024]{1,0:T(8,128)(2,1)}, bf16[128,1024]{1,0:T(8,128)(2,1)S(1)}, u32[]{:S(2)}, u32[]{:S(2)}) %collective-permute-start.8) | collective-permute-done | bytes 262176 | tf_op jit(solution)/shard_map/ppermute | solution.py:38
  54.3 0.5 collective-permute-start.20
  54.8 0.0 collective-permute-start.22
  54.8 0.5 collective-permute-start.10
  55.3 0.6 collective-permute-start.9
  56.0 0.2 collective-permute-done.21.refs_8_
  56.2 0.1 collective-permute-start.11
  56.4 1.0 %collective-permute-done.20.refs_7_ = bf16[256,1024]{1,0:T(8,128)(2,1)S(1)} collective-permute-done((bf16[256,1024]{1,0:T(8,128)(2,1)S(1)}, bf16[256,1024]{1,0:T(8,128)(2,1)S(1)}, u32[]{:S(2)}, u32[]{:S(2)}) %collective-permute-start.20) | collective-permute-done | bytes 524320 | tf_op jit(solution)/shard_map/ppermute | solution.py:38
  57.3 0.1 collective-permute-start.12
  57.5 0.6 collective-permute-done.22.refs_9_
  58.1 7.6 %shard_map.83.refs_11_ = f32[512,1152]{1,0:T(8,128)S(1)} custom-call(s32[10]{0:T(128)S(1)} %stack.43.start_ref.refs_0_, f32[32,1,1280]{2,1,0:T(1,128)S(1)} %all-to-all-done.refs_1_, bf16[256,1024]{1,0:T(8,128)(2,1)S(1)} %shard_map.78.refs_2_, bf16[256,1024]{1,0:T(8,128)(2,1)S(1)} %collective-permute-done.5.refs_3_, ...), custom_call_target="tpu_custom_call" | custom-call | flops 4831838208 | bytes 9437184 | tf_op jit(solution)/shard_map/pallas_call | solution.py:202
  65.7 0.0 copy-start.5
  65.7 0.2 collective-permute-start.23
  65.9 1.4 %collective-permute-done.23.refs_9_ = bf16[128,1024]{1,0:T(8,128)(2,1)S(1)} collective-permute-done((bf16[128,1024]{1,0:T(8,128)(2,1)S(1)}, bf16[128,1024]{1,0:T(8,128)(2,1)S(1)}, u32[]{:S(2)}, u32[]{:S(2)}) %collective-permute-start.23) | collective-permute-done | bytes 262176 | tf_op jit(solution)/shard_map/ppermute | solution.py:38
  67.3 5.9 %shard_map.84 = f32[4,8,3,128]{3,2,1,0:T(4,128)} custom-call(s32[10]{0:T(128)S(1)} %stack.43.start_ref.refs_0_, f32[32,1,1280]{2,1,0:T(1,128)S(1)} %all-to-all-done.refs_1_, bf16[128,1024]{1,0:T(8,128)(2,1)} %collective-permute-done.2.refs_2_, bf16[128,1024]{1,0:T(8,128)(2,1)S(1)} %collective-permute-done.7.refs_3_, ...), custom_call_target="tpu_custom_call" | custom-call | flops 2415919104 | bytes 4718592 | tf_op jit(solution)/shard_map/pallas_call | solution.py:202
  73.2 3.9 %all-to-all-start.1 = ((f32[32,3,128]{2,1,0:T(4,128)}), f32[32,3,128]{2,1,0:T(4,128)S(1)}, u32[]{:S(2)}, u32[]{:S(2)}) async-start(f32[32,3,128]{2,1,0:T(4,128)} %bitcast.13), calls=%async_computation.1 | async-start | bytes 131072 | tf_op jit(solution)/shard_map/all_to_all | solution.py:298
  77.8 6.7 %all-to-all-done.1 = f32[32,3,128]{2,1,0:T(4,128)S(1)} async-done(((f32[32,3,128]{2,1,0:T(4,128)}), f32[32,3,128]{2,1,0:T(4,128)S(1)}, u32[]{:S(2)}, u32[]{:S(2)}) %all-to-all-start.1) | async-done | bytes 49184 | tf_op jit(solution)/shard_map/all_to_all | solution.py:298
  84.5 0.1 slice_reduce_fusion
  84.6 0.5 compare_select_fusion
  (29 shorter events, 0.1 us)
Async XLA Ops:
  0.6 9.9 %collective-permute-start = (bf16[128,1024]{1,0:T(8,128)(2,1)}, bf16[128,1024]{1,0:T(8,128)(2,1)S(1)}, u32[]{:S(2)}, u32[]{:S(2)}) collective-permute-start(bf16[128,1024]{1,0:T(8,128)(2,1)} %refs_2_.1), channel_id=1, source_target_pairs={{0,8},{1,17},{2,10},{3,19},{4,12},{5,21},{6,14},{7,23},{8,0},{9,25... | collective-permute-start | bytes 786440 | tf_op jit(solution)/shard_map/ppermute | solution.py:38
  3.6 6.9 %collective-permute-start.1 = (bf16[128,1024]{1,0:T(8,128)(2,1)}, bf16[128,1024]{1,0:T(8,128)(2,1)S(1)}, u32[]{:S(2)}, u32[]{:S(2)}) collective-permute-start(bf16[128,1024]{1,0:T(8,128)(2,1)} %refs_2_.1), channel_id=1, source_target_pairs={{0,16},{1,9},{2,18},{3,11},{4,20},{5,13},{6,22},{7,15},{8,24},{9,1... | collective-permute-start | bytes 786440 | tf_op jit(solution)/shard_map/ppermute | solution.py:38
  5.2 14.6 %collective-permute-start.3 = (bf16[128,1024]{1,0:T(8,128)(2,1)}, bf16[128,1024]{1,0:T(8,128)(2,1)S(1)}, u32[]{:S(2)}, u32[]{:S(2)}) collective-permute-start(bf16[128,1024]{1,0:T(8,128)(2,1)} %refs_2_.1), channel_id=1, source_target_pairs={{0,2},{1,3},{2,4},{3,5},{4,6},{5,7},{6,0},{7,1},{8,10},{9,11},{10,... | collective-permute-start | bytes 786440 | tf_op jit(solution)/shard_map/ppermute | solution.py:38
  6.7 15.2 %collective-permute-start.14 = (bf16[128,1024]{1,0:T(8,128)(2,1)}, bf16[128,1024]{1,0:T(8,128)(2,1)S(1)}, u32[]{:S(2)}, u32[]{:S(2)}) collective-permute-start(bf16[128,1024]{1,0:T(8,128)(2,1)} %refs_2_.1), channel_id=1, source_target_pairs={{0,1},{1,0},{2,3},{3,2},{4,5},{5,4},{6,7},{7,6},{8,9},{9,8},{10,11... | collective-permute-start | bytes 786440 | tf_op jit(solution)/shard_map/ppermute | solution.py:38
  6.7 13.6 %collective-permute-start.4 = (bf16[128,1024]{1,0:T(8,128)(2,1)}, bf16[128,1024]{1,0:T(8,128)(2,1)S(1)}, u32[]{:S(2)}, u32[]{:S(2)}) collective-permute-start(bf16[128,1024]{1,0:T(8,128)(2,1)} %refs_2_.1), channel_id=1, source_target_pairs={{0,6},{1,7},{2,0},{3,1},{4,2},{5,3},{6,4},{7,5},{8,14},{9,15},{10,... | collective-permute-start | bytes 786440 | tf_op jit(solution)/shard_map/ppermute | solution.py:38
  10.5 12.8 %collective-permute-start.13 = (bf16[128,1024]{1,0:T(8,128)(2,1)S(1)}, bf16[128,1024]{1,0:T(8,128)(2,1)}, u32[]{:S(2)}, u32[]{:S(2)}) collective-permute-start(bf16[128,1024]{1,0:T(8,128)(2,1)S(1)} %collective-permute-done.refs_3_), channel_id=1, source_target_pairs={{0,16},{1,9},{2,18},{3,11},{4,20},{5,13},{6,22},{7,15},{8,24},{9,1... | collective-permute-start | bytes 786440 | tf_op jit(solution)/shard_map/ppermute | solution.py:38
  12.0 11.4 %collective-permute-start.15 = (bf16[128,1024]{1,0:T(8,128)(2,1)S(1)}, bf16[128,1024]{1,0:T(8,128)(2,1)}, u32[]{:S(2)}, u32[]{:S(2)}) collective-permute-start(bf16[128,1024]{1,0:T(8,128)(2,1)S(1)} %collective-permute-done.refs_3_), channel_id=1, source_target_pairs={{0,1},{1,0},{2,3},{3,2},{4,5},{5,4},{6,7},{7,6},{8,9},{9,8},{10,11... | collective-permute-start | bytes 786440 | tf_op jit(solution)/shard_map/ppermute | solution.py:38
  14.7 17.3 %all-to-all-start = ((f32[32,1,1280]{2,1,0:T(1,128)}), f32[32,1,1280]{2,1,0:T(1,128)S(1)}, u32[]{:S(2)}, u32[]{:S(2)}) async-start(f32[32,1,1280]{2,1,0:T(1,128)} %shard_map.77), calls=%async_computation | async-start | bytes 327680 | tf_op jit(solution)/shard_map/all_to_all | solution.py:276
  19.8 4.1 %collective-permute-start.16 = (bf16[128,1024]{1,0:T(8,128)(2,1)S(1)}, bf16[128,1024]{1,0:T(8,128)(2,1)S(1)}, u32[]{:S(2)}, u32[]{:S(2)}) collective-permute-start(bf16[128,1024]{1,0:T(8,128)(2,1)S(1)} %collective-permute-done.1.refs_4_), channel_id=1, source_target_pairs={{0,1},{1,0},{2,3},{3,2},{4,5},{5,4},{6,7},{7,6},{8,9},{9,8},{10,11... | collective-permute-start | bytes 786440 | tf_op jit(solution)/shard_map/ppermute | solution.py:38
  20.4 11.6 %copy-start.2 = (bf16[128,1024]{1,0:T(8,128)(2,1)S(1)}, bf16[128,1024]{1,0:T(8,128)(2,1)}, u32[]{:S(2)}) copy-start(bf16[128,1024]{1,0:T(8,128)(2,1)} %refs_2_.1) | copy-start | bytes 786436
  20.4 19.7 %collective-permute-start.5 = (bf16[256,1024]{1,0:T(8,128)(2,1)S(1)}, bf16[256,1024]{1,0:T(8,128)(2,1)S(1)}, u32[]{:S(2)}, u32[]{:S(2)}) collective-permute-start(bf16[256,1024]{1,0:T(8,128)(2,1)S(1)} %shard_map.78.refs_2_), channel_id=1, source_target_pairs={{0,8},{1,17},{2,10},{3,19},{4,12},{5,21},{6,14},{7,23},{8,0},{9,25... | collective-permute-start | bytes 1572872 | tf_op jit(solution)/shard_map/ppermute | solution.py:38
  21.9 18.2 %collective-permute-start.6 = (bf16[256,1024]{1,0:T(8,128)(2,1)S(1)}, bf16[256,1024]{1,0:T(8,128)(2,1)S(1)}, u32[]{:S(2)}, u32[]{:S(2)}) collective-permute-start(bf16[256,1024]{1,0:T(8,128)(2,1)S(1)} %shard_map.78.refs_2_), channel_id=1, source_target_pairs={{0,16},{1,9},{2,18},{3,11},{4,20},{5,13},{6,22},{7,15},{8,24},{9,1... | collective-permute-start | bytes 1572872 | tf_op jit(solution)/shard_map/ppermute | solution.py:38
  23.4 16.8 %collective-permute-start.18 = (bf16[256,1024]{1,0:T(8,128)(2,1)S(1)}, bf16[256,1024]{1,0:T(8,128)(2,1)S(1)}, u32[]{:S(2)}, u32[]{:S(2)}) collective-permute-start(bf16[256,1024]{1,0:T(8,128)(2,1)S(1)} %shard_map.78.refs_2_), channel_id=1, source_target_pairs={{0,1},{1,0},{2,3},{3,2},{4,5},{5,4},{6,7},{7,6},{8,9},{9,8},{10,11... | collective-permute-start | bytes 1572872 | tf_op jit(solution)/shard_map/ppermute | solution.py:38
  23.4 8.6 %collective-permute-start.17 = (bf16[128,1024]{1,0:T(8,128)(2,1)}, bf16[128,1024]{1,0:T(8,128)(2,1)}, u32[]{:S(2)}, u32[]{:S(2)}) collective-permute-start(bf16[128,1024]{1,0:T(8,128)(2,1)} %collective-permute-done.13.refs_5_), channel_id=1, source_target_pairs={{0,1},{1,0},{2,3},{3,2},{4,5},{5,4},{6,7},{7,6},{8,9},{9,8},{10,11... | collective-permute-start | bytes 786440 | tf_op jit(solution)/shard_map/ppermute | solution.py:38
  23.9 0.7 copy-start.3
  24.6 15.5 %collective-permute-start.2 = (bf16[128,1024]{1,0:T(8,128)(2,1)}, bf16[128,1024]{1,0:T(8,128)(2,1)}, u32[]{:S(2)}, u32[]{:S(2)}) collective-permute-start(bf16[128,1024]{1,0:T(8,128)(2,1)} %refs_2_.1), channel_id=1, source_target_pairs={{0,4},{1,5},{2,6},{3,7},{4,0},{5,1},{6,2},{7,3},{8,12},{9,13},{10,... | collective-permute-start | bytes 786440 | tf_op jit(solution)/shard_map/ppermute | solution.py:38
  29.9 2.1 %copy-start = (bf16[1,2048,1152]{2,1,0:T(8,128)(2,1)}, bf16[1,2048,1152]{2,1,0:T(8,128)(2,1)S(1)}, u32[]{:S(2)}) copy-start(bf16[1,2048,1152]{2,1,0:T(8,128)(2,1)S(1)} %shard_map.79.refs_10_) | copy-start | bytes 14155780
  32.0 2.3 %copy-start.1 = (bf16[1,2048,1152]{2,1,0:T(8,128)(2,1)S(1)}, bf16[1,2048,1152]{2,1,0:T(8,128)(2,1)}, u32[]{:S(2)}) copy-start(bf16[1,2048,1152]{2,1,0:T(8,128)(2,1)} %copy-done) | copy-start | bytes 14155780
  34.4 0.9 %copy-start.4 = (bf16[128,1024]{1,0:T(8,128)(2,1)S(1)}, bf16[128,1024]{1,0:T(8,128)(2,1)}, u32[]{:S(2)}) copy-start(bf16[128,1024]{1,0:T(8,128)(2,1)} %copy-done.3) | copy-start | bytes 786436
  40.1 14.7 %collective-permute-start.19 = (bf16[256,1024]{1,0:T(8,128)(2,1)S(1)}, bf16[256,1024]{1,0:T(8,128)(2,1)S(1)}, u32[]{:S(2)}, u32[]{:S(2)}) collective-permute-start(bf16[256,1024]{1,0:T(8,128)(2,1)S(1)} %collective-permute-done.5.refs_3_), channel_id=1, source_target_pairs={{0,16},{1,9},{2,18},{3,11},{4,20},{5,13},{6,22},{7,15},{8,24},{9,1... | collective-permute-start | bytes 1572872 | tf_op jit(solution)/shard_map/ppermute | solution.py:38
  40.7 9.5 %collective-permute-start.7 = (bf16[128,1024]{1,0:T(8,128)(2,1)}, bf16[128,1024]{1,0:T(8,128)(2,1)S(1)}, u32[]{:S(2)}, u32[]{:S(2)}) collective-permute-start(bf16[128,1024]{1,0:T(8,128)(2,1)} %collective-permute-done.2.refs_2_), channel_id=1, source_target_pairs={{0,8},{1,17},{2,10},{3,19},{4,12},{5,21},{6,14},{7,23},{8,0},{9,25... | collective-permute-start | bytes 786440 | tf_op jit(solution)/shard_map/ppermute | solution.py:38
  41.4 12.9 %collective-permute-start.8 = (bf16[128,1024]{1,0:T(8,128)(2,1)}, bf16[128,1024]{1,0:T(8,128)(2,1)S(1)}, u32[]{:S(2)}, u32[]{:S(2)}) collective-permute-start(bf16[128,1024]{1,0:T(8,128)(2,1)} %collective-permute-done.2.refs_2_), channel_id=1, source_target_pairs={{0,16},{1,9},{2,18},{3,11},{4,20},{5,13},{6,22},{7,15},{8,24},{9,1... | collective-permute-start | bytes 786440 | tf_op jit(solution)/shard_map/ppermute | solution.py:38
  54.3 1.9 %collective-permute-start.21 = (bf16[256,1024]{1,0:T(8,128)(2,1)S(1)}, bf16[256,1024]{1,0:T(8,128)(2,1)S(1)}, u32[]{:S(2)}, u32[]{:S(2)}) collective-permute-start(bf16[256,1024]{1,0:T(8,128)(2,1)S(1)} %collective-permute-done.6.refs_4_), channel_id=1, source_target_pairs={{0,1},{1,0},{2,3},{3,2},{4,5},{5,4},{6,7},{7,6},{8,9},{9,8},{10,11... | collective-permute-start | bytes 1572872 | tf_op jit(solution)/shard_map/ppermute | solution.py:38
  54.3 3.0 %collective-permute-start.20 = (bf16[256,1024]{1,0:T(8,128)(2,1)S(1)}, bf16[256,1024]{1,0:T(8,128)(2,1)S(1)}, u32[]{:S(2)}, u32[]{:S(2)}) collective-permute-start(bf16[256,1024]{1,0:T(8,128)(2,1)S(1)} %collective-permute-done.5.refs_3_), channel_id=1, source_target_pairs={{0,1},{1,0},{2,3},{3,2},{4,5},{5,4},{6,7},{7,6},{8,9},{9,8},{10,11... | collective-permute-start | bytes 1572872 | tf_op jit(solution)/shard_map/ppermute | solution.py:38
  54.8 3.3 %collective-permute-start.22 = (bf16[256,1024]{1,0:T(8,128)(2,1)S(1)}, bf16[256,1024]{1,0:T(8,128)(2,1)S(1)}, u32[]{:S(2)}, u32[]{:S(2)}) collective-permute-start(bf16[256,1024]{1,0:T(8,128)(2,1)S(1)} %collective-permute-done.19.refs_5_), channel_id=1, source_target_pairs={{0,1},{1,0},{2,3},{3,2},{4,5},{5,4},{6,7},{7,6},{8,9},{9,8},{10,11... | collective-permute-start | bytes 1572872 | tf_op jit(solution)/shard_map/ppermute | solution.py:38
  54.8 11.1 %collective-permute-start.10 = (bf16[128,1024]{1,0:T(8,128)(2,1)}, bf16[128,1024]{1,0:T(8,128)(2,1)S(1)}, u32[]{:S(2)}, u32[]{:S(2)}) collective-permute-start(bf16[128,1024]{1,0:T(8,128)(2,1)} %collective-permute-done.2.refs_2_), channel_id=1, source_target_pairs={{0,1},{1,0},{2,3},{3,2},{4,5},{5,4},{6,7},{7,6},{8,9},{9,8},{10,11... | collective-permute-start | bytes 786440 | tf_op jit(solution)/shard_map/ppermute | solution.py:38
  55.3 10.4 %collective-permute-start.9 = (bf16[128,1024]{1,0:T(8,128)(2,1)S(1)}, bf16[128,1024]{1,0:T(8,128)(2,1)S(1)}, u32[]{:S(2)}, u32[]{:S(2)}) collective-permute-start(bf16[128,1024]{1,0:T(8,128)(2,1)S(1)} %collective-permute-done.7.refs_3_), channel_id=1, source_target_pairs={{0,16},{1,9},{2,18},{3,11},{4,20},{5,13},{6,22},{7,15},{8,24},{9,1... | collective-permute-start | bytes 786440 | tf_op jit(solution)/shard_map/ppermute | solution.py:38
  56.2 9.7 %collective-permute-start.11 = (bf16[128,1024]{1,0:T(8,128)(2,1)S(1)}, bf16[128,1024]{1,0:T(8,128)(2,1)S(1)}, u32[]{:S(2)}, u32[]{:S(2)}) collective-permute-start(bf16[128,1024]{1,0:T(8,128)(2,1)S(1)} %collective-permute-done.7.refs_3_), channel_id=1, source_target_pairs={{0,1},{1,0},{2,3},{3,2},{4,5},{5,4},{6,7},{7,6},{8,9},{9,8},{10,11... | collective-permute-start | bytes 786440 | tf_op jit(solution)/shard_map/ppermute | solution.py:38
  57.3 8.6 %collective-permute-start.12 = (bf16[128,1024]{1,0:T(8,128)(2,1)S(1)}, bf16[128,1024]{1,0:T(8,128)(2,1)S(1)}, u32[]{:S(2)}, u32[]{:S(2)}) collective-permute-start(bf16[128,1024]{1,0:T(8,128)(2,1)S(1)} %collective-permute-done.8.refs_4_), channel_id=1, source_target_pairs={{0,1},{1,0},{2,3},{3,2},{4,5},{5,4},{6,7},{7,6},{8,9},{9,8},{10,11... | collective-permute-start | bytes 786440 | tf_op jit(solution)/shard_map/ppermute | solution.py:38
  65.7 19.0 %copy-start.5 = (f32[128]{0:T(128)S(1)}, f32[128]{0:T(128)}, u32[]{:S(2)}) copy-start(f32[128]{0:T(128)} %param.10) | copy-start | bytes 1540
  65.7 1.6 %collective-permute-start.23 = (bf16[128,1024]{1,0:T(8,128)(2,1)S(1)}, bf16[128,1024]{1,0:T(8,128)(2,1)S(1)}, u32[]{:S(2)}, u32[]{:S(2)}) collective-permute-start(bf16[128,1024]{1,0:T(8,128)(2,1)S(1)} %collective-permute-done.9.refs_5_), channel_id=1, source_target_pairs={{0,1},{1,0},{2,3},{3,2},{4,5},{5,4},{6,7},{7,6},{8,9},{9,8},{10,11... | collective-permute-start | bytes 786440 | tf_op jit(solution)/shard_map/ppermute | solution.py:38
  73.2 11.3 %all-to-all-start.1 = ((f32[32,3,128]{2,1,0:T(4,128)}), f32[32,3,128]{2,1,0:T(4,128)S(1)}, u32[]{:S(2)}, u32[]{:S(2)}) async-start(f32[32,3,128]{2,1,0:T(4,128)} %bitcast.13), calls=%async_computation.1 | async-start | bytes 131072 | tf_op jit(solution)/shard_map/all_to_all | solution.py:298

commit v5 on v4

--- a/solution.py
+++ b/solution.py
@@ -120,6 +120,7 @@
         out_specs=pl.BlockSpec(memory_space=pltpu.VMEM),
         scratch_shapes=[pltpu.SemaphoreType.DMA((len(offsets),))],
         compiler_params=pltpu.CompilerParams(vmem_limit_bytes=SMALL_LIMIT),
+        cost_estimate=pl.CostEstimate(flops=0, bytes_accessed=0, transcendentals=0),
     )(starts, far(head))
 
 
@@ -141,7 +142,7 @@
     )(*blocks)
 
 
-def group_kernel(n, n_t, place, offsets, first, last, *refs):
+def layer_kernel(n, n_t, place, layer, offset, first, last, *refs):
     refs = list(refs)
     start_ref, fine = refs.pop(0), refs.pop(0)
     blocks = [refs.pop(0) for _ in range(CORES * n)]
@@ -157,21 +158,17 @@
     for k in range(n):
         sums = jnp.sum(fine[pl.ds(owners[k] * n_t, n_t), :, feat : feat + tok], axis=0)
         scales.append(to_column(lax.rsqrt(sums / D + 1e-06)))
-    for j, offset in enumerate(offsets):
-        for c in range(CORES):
-            core = 1 - c_me if c else c_me
-            gain = fine[start_ref[offset] * CORES + core, :, :feat]
-            columns = pl.ds(pl.multiple_of(core * feat, feat), feat)
-            for k in range(n):
-                spot = place[k] if c else k
-                part = blocks[c * n + k][j * tok : (j + 1) * tok, :].astype(jnp.float32)
-                part = part * scales[spot] * gain
-                rows[spot * tok : (spot + 1) * tok, columns] = part.astype(jnp.bfloat16)
-        product = jnp.dot(rows[...], weights[j], preferred_element_type=jnp.float32)
-        if j:
-            acc[...] += product
-        else:
-            acc[...] = product if first else acc_ref[...] + product
+    for c in range(CORES):
+        core = 1 - c_me if c else c_me
+        gain = fine[start_ref[offset] * CORES + core, :, :feat]
+        columns = pl.ds(pl.multiple_of(core * feat, feat), feat)
+        for k in range(n):
+            spot = place[k] if c else k
+            part = blocks[c * n + k][layer * tok : (layer + 1) * tok, :].astype(jnp.float32)
+            part = part * scales[spot] * gain
+            rows[spot * tok : (spot + 1) * tok, columns] = part.astype(jnp.bfloat16)
+    product = jnp.dot(rows[...], weights[layer], preferred_element_type=jnp.float32)
+    acc[...] = product if first else acc_ref[...] + product
     if not last:
         return
     for b in range(n):
@@ -188,10 +185,10 @@
             out_ref[owners[b], peer, 2:3, :] = to_row(pick)
 
 
-def group_product(tok, n_t, starts, offsets, fine, blocks, place, weights, acc, last):
+def layer_product(tok, n_t, starts, layer, offset, fine, blocks, place, weights, acc, last):
     n = len(place)
     feat = blocks[0].shape[1]
-    size, deep, vocab = weights.shape
+    deep, vocab = weights.shape[1:]
     vmem = pl.BlockSpec(memory_space=pltpu.VMEM)
     first = acc is None
     logits = jax.ShapeDtypeStruct((n * tok, vocab), jnp.float32)
@@ -200,14 +197,14 @@
     if last:
         scratch.append(pltpu.VMEM(logits.shape, jnp.float32))
     return pl.pallas_call(
-        functools.partial(group_kernel, n, n_t, place, offsets, first, last),
+        functools.partial(layer_kernel, n, n_t, place, layer, offset, first, last),
         out_shape=jax.ShapeDtypeStruct((n, n_t, 3, tok), jnp.float32) if last else logits,
         in_specs=[pl.BlockSpec(memory_space=pltpu.SMEM)] + [vmem] * (len(operands) - 1),
         out_specs=vmem,
         scratch_shapes=scratch,
         compiler_params=pltpu.CompilerParams(vmem_limit_bytes=VMEM_LIMIT),
         cost_estimate=pl.CostEstimate(
-            flops=2 * n * tok * deep * vocab * size, bytes_accessed=2 * deep * vocab * size, transcendentals=0
+            flops=0, bytes_accessed=0, transcendentals=0
         ),
     )(*operands)
 
@@ -264,16 +261,15 @@
         for dz in group:
             layers[dz] = grid.along(after(hidden, *before), dz)
         before = list(reached[0].values()) if len(before) == 0 else [layers[dz] for dz in group]
-    for group in groups[1:]:
-        sources = [layers[dz] for dz in group]
-        sources[0] = after(sources[0], *reached[-1].values())
-        reached.append(grid.reach(joined(sources) if len(sources) > 1 else sources[0]))
-
     vocab_cols = head.shape[1]
     vocab_start = lax.axis_index(("dp", "tensor")) * vocab_cols
     starts = jnp.stack([c_me, vocab_start] + owners + [(z_me - dz) % depth for dz in range(depth)])
     packed = squares(after(hidden, starts), norm_gain[None, :], targets[None, :], n_dp * n_t)
     fine = lax.all_to_all(packed, ("dp", "tensor"), 0, 0, tiled=True)
+    for group in groups[1:]:
+        sources = [layers[dz] for dz in group]
+        sources[0] = after(sources[0], packed, *reached[-1].values())
+        reached.append(grid.reach(joined(sources) if len(sources) > 1 else sources[0]))
 
     acc, deep = None, CORES * feat
     for at, group in enumerate(groups):
@@ -284,16 +280,21 @@
         held = [layers[dz] for dz in groups[at + 1]] + [own] if middle else []
         spread = grid.fill(dict(reached[at]), *([acc] if at == 1 else []), *held)
         if at == 0:
-            weights = [loaded(starts, offsets, after(head, packed), deep)]
+            weights = [loaded(starts, offsets, after(head, fine), deep)]
         elif at == 1:
             for later in groups[1:]:
                 ready = after(head, acc, *(layers[dz] for dz in groups[2]))
                 weights.append(loaded(starts, [2 + n_dp + dz for dz in later], ready, deep))
-        following = [*reached[at + 1].values(), *weights[1:3]] if middle else []
-        others = [own] + [grid.sibling(after(a, *following)) for a in spread[1:-1]]
-        others.append(grid.sibling(after(spread[-1], *([acc] if final else following))))
+        ready = weights[1:3] if middle else []
+        others = [own] + [grid.sibling(after(a, *ready)) for a in spread[1:-1]]
+        others.append(grid.sibling(after(spread[-1], *([acc] if final else ready))))
         blocks = spread + others
-        acc = group_product(tok, n_t, starts, offsets, fine, blocks, place, weights[at], acc, final)
+        for layer, offset in enumerate(offsets):
+            done = layer == len(offsets) - 1
+            if middle and done:
+                blocks[0] = after(blocks[0], *reached[at + 1].values())
+            last = final and done
+            acc = layer_product(tok, n_t, starts, layer, offset, fine, blocks, place, weights[at], acc, last)
 
     parts = lax.all_to_all(acc.reshape(n_dp * n_t, 3, tok), ("dp", "tensor"), 0, 0, tiled=True)
     top = jnp.max(parts[:, 0], axis=0)

time: 85.6 us -> 93.8 us (1.096)
  waiting for transfers between devices: 16.1 us -> 28.7 us
  local copies, waits for them, and re-layouts: 6.2 us -> 0.1 us
    all_to_all x1, waiting for transfers between devices: 0.01 us -> 7.85 us  [body(): fine = lax.all_to_all(packed, ('dp', 'tensor'), 0, 0, tiled=True)]
    unnamed x12 -> x4, local copies, waits for them, and re-layouts: 6.12 us -> 0.01 us
    ppermute x24, waiting for transfers between devices: 9.33 us -> 14.1 us  [permute(): return lax.ppermute(a, ('dp', 'tensor'), perm)]
    ppermute x24, starting transfers between devices: 21.6 us -> 22.6 us  [permute(): return lax.ppermute(a, ('dp', 'tensor'), perm)]
    pallas_call x3 -> x4, Pallas kernels: 18.3 us -> 19.2 us  [layer_product(): pl.pallas_call(functools.partial(layer_kernel, n, n_t, place, layer, offs...]
  transfers between devices with their start and end apart: 26 -> 26, of which waited for: 9 -> 8; matrix products, arithmetic and copies ran while one was open for 0% -> 0% of each run, Pallas kernels for 29% -> 27%
where the time goes in v5:
time: 93.8 us; the launch traced here: 93.4 us
  starting transfers between devices  31.4 us (33%)
  Pallas kernels  31.1 us (33%)
  waiting for transfers between devices  28.7 us (31%)
  between operations  1.42 us (2%)
    ppermute x24, starting transfers between devices, permute(): return lax.ppermute(a, ('dp', 'tensor'), perm)  22.6 us
    pallas_call x4, Pallas kernels, layer_product(): pl.pallas_call(functools.partial(layer_kernel, n, n_t, place, layer, offs...  19.2 us
    ppermute x24, waiting for transfers between devices, permute(): return lax.ppermute(a, ('dp', 'tensor'), perm)  14.1 us
    pallas_call x3, Pallas kernels, loaded(): pl.pallas_call(functools.partial(load_kernel, offsets), out_shape=pltpu.V...  10.1 us
    all_to_all x1, waiting for transfers between devices, body(): fine = lax.all_to_all(packed, ('dp', 'tensor'), 0, 0, tiled=True)  7.85 us
    all_to_all x1, waiting for transfers between devices, body(): lax.all_to_all(acc.reshape(n_dp * n_t, 3, tok), ('dp', 'tensor'), 0, 0, t...  6.74 us
    all_to_all x1, starting transfers between devices, body(): fine = lax.all_to_all(packed, ('dp', 'tensor'), 0, 0, tiled=True)  4.47 us
    all_to_all x1, starting transfers between devices, body(): lax.all_to_all(acc.reshape(n_dp * n_t, 3, tok), ('dp', 'tensor'), 0, 0, t...  4.33 us
  transfers between devices with their start and end apart: 26, of which 8 were waited for; matrix products, arithmetic and copies ran while one was open for 0% of the time, Pallas kernels for 27%

profile of v5, /device:TPU:0, one launch (start us, length us, event | category | flops | bytes accessed | tf_op | source)
XLA Modules:
  0.0 93.4 jit_solution(5826013073698668215)
XLA Ops:
  0.6 3.0 %collective-permute-start = (bf16[128,1024]{1,0:T(8,128)(2,1)}, bf16[128,1024]{1,0:T(8,128)(2,1)S(1)}, u32[]{:S(2)}, u32[]{:S(2)}) collective-permute-start(bf16[128,1024]{1,0:T(8,128)(2,1)} %refs_2_.1), channel_id=1, source_target_pairs={{0,8},{1,17},{2,10},{3,19},{4,12},{5,21},{6,14},{7,23},{8,0},{9,25... | collective-permute-start | bytes 786440 | tf_op jit(solution)/shard_map/ppermute | solution.py:38
  3.6 1.5 %collective-permute-start.1 = (bf16[128,1024]{1,0:T(8,128)(2,1)}, bf16[128,1024]{1,0:T(8,128)(2,1)S(1)}, u32[]{:S(2)}, u32[]{:S(2)}) collective-permute-start(bf16[128,1024]{1,0:T(8,128)(2,1)} %refs_2_.1), channel_id=1, source_target_pairs={{0,16},{1,9},{2,18},{3,11},{4,20},{5,13},{6,22},{7,15},{8,24},{9,1... | collective-permute-start | bytes 786440 | tf_op jit(solution)/shard_map/ppermute | solution.py:38
  5.2 1.6 %collective-permute-start.3 = (bf16[128,1024]{1,0:T(8,128)(2,1)}, bf16[128,1024]{1,0:T(8,128)(2,1)S(1)}, u32[]{:S(2)}, u32[]{:S(2)}) collective-permute-start(bf16[128,1024]{1,0:T(8,128)(2,1)} %refs_2_.1), channel_id=1, source_target_pairs={{0,2},{1,3},{2,4},{3,5},{4,6},{5,7},{6,0},{7,1},{8,10},{9,11},{10,... | collective-permute-start | bytes 786440 | tf_op jit(solution)/shard_map/ppermute | solution.py:38
  6.7 0.0 collective-permute-start.14
  6.7 2.2 %collective-permute-start.4 = (bf16[128,1024]{1,0:T(8,128)(2,1)}, bf16[128,1024]{1,0:T(8,128)(2,1)S(1)}, u32[]{:S(2)}, u32[]{:S(2)}) collective-permute-start(bf16[128,1024]{1,0:T(8,128)(2,1)} %refs_2_.1), channel_id=1, source_target_pairs={{0,6},{1,7},{2,0},{3,1},{4,2},{5,3},{6,4},{7,5},{8,14},{9,15},{10,... | collective-permute-start | bytes 786440 | tf_op jit(solution)/shard_map/ppermute | solution.py:38
  9.0 1.6 %collective-permute-done.refs_3_ = bf16[128,1024]{1,0:T(8,128)(2,1)S(1)} collective-permute-done((bf16[128,1024]{1,0:T(8,128)(2,1)}, bf16[128,1024]{1,0:T(8,128)(2,1)S(1)}, u32[]{:S(2)}, u32[]{:S(2)}) %collective-permute-start) | collective-permute-done | bytes 262176 | tf_op jit(solution)/shard_map/ppermute | solution.py:38
  10.5 1.5 %collective-permute-start.13 = (bf16[128,1024]{1,0:T(8,128)(2,1)S(1)}, bf16[128,1024]{1,0:T(8,128)(2,1)}, u32[]{:S(2)}, u32[]{:S(2)}) collective-permute-start(bf16[128,1024]{1,0:T(8,128)(2,1)S(1)} %collective-permute-done.refs_3_), channel_id=1, source_target_pairs={{0,16},{1,9},{2,18},{3,11},{4,20},{5,13},{6,22},{7,15},{8,24},{9,1... | collective-permute-start | bytes 786440 | tf_op jit(solution)/shard_map/ppermute | solution.py:38
  12.0 0.1 stack.43.start_ref.refs_0_
  12.1 1.8 %shard_map.77 = f32[32,1,1280]{2,1,0:T(1,128)} custom-call(bf16[128,1024]{1,0:T(8,128)(2,1)} %refs_2_.1, f32[1,1024]{1,0:T(1,128)} %bitcast.22, s32[1,128]{1,0:T(1,128)} %bitcast.23), custom_call_target="tpu_custom_call" | custom-call | tf_op jit(solution)/shard_map/pallas_call | solution.py:231
  13.9 2.6 %collective-permute-done.3.refs_0_ = bf16[128,1024]{1,0:T(8,128)(2,1)S(1)} collective-permute-done((bf16[128,1024]{1,0:T(8,128)(2,1)}, bf16[128,1024]{1,0:T(8,128)(2,1)S(1)}, u32[]{:S(2)}, u32[]{:S(2)}) %collective-permute-start.3) | collective-permute-done | bytes 262176 | tf_op jit(solution)/shard_map/ppermute | solution.py:38
  16.5 0.5 collective-permute-start.16
  17.0 3.4 %collective-permute-done.4.refs_1_ = bf16[128,1024]{1,0:T(8,128)(2,1)S(1)} collective-permute-done((bf16[128,1024]{1,0:T(8,128)(2,1)}, bf16[128,1024]{1,0:T(8,128)(2,1)S(1)}, u32[]{:S(2)}, u32[]{:S(2)}) %collective-permute-start.4) | collective-permute-done | bytes 262176 | tf_op jit(solution)/shard_map/ppermute | solution.py:38
  20.4 0.1 collective-permute-start.18
  20.5 0.5 collective-permute-start.5
  21.1 0.5 collective-permute-start.6
  21.6 4.5 %all-to-all-start = ((f32[32,1,1280]{2,1,0:T(1,128)}), f32[32,1,1280]{2,1,0:T(1,128)S(1)}, u32[]{:S(2)}, u32[]{:S(2)}) async-start(f32[32,1,1280]{2,1,0:T(1,128)} %shard_map.77), calls=%async_computation | async-start | bytes 327680 | tf_op jit(solution)/shard_map/all_to_all | solution.py:268
  26.1 0.0 copy-start
  26.1 0.3 collective-permute-start.17
  26.4 0.0 collective-permute-done.16.refs_8_
  26.4 2.6 %collective-permute-start.2 = (bf16[128,1024]{1,0:T(8,128)(2,1)}, bf16[128,1024]{1,0:T(8,128)(2,1)}, u32[]{:S(2)}, u32[]{:S(2)}) collective-permute-start(bf16[128,1024]{1,0:T(8,128)(2,1)} %refs_2_.1), channel_id=1, source_target_pairs={{0,4},{1,5},{2,6},{3,7},{4,0},{5,1},{6,2},{7,3},{8,12},{9,13},{10,... | collective-permute-start | bytes 786440 | tf_op jit(solution)/shard_map/ppermute | solution.py:38
  29.0 7.8 %all-to-all-done.refs_1_ = f32[32,1,1280]{2,1,0:T(1,128)S(1)} async-done(((f32[32,1,1280]{2,1,0:T(1,128)}), f32[32,1,1280]{2,1,0:T(1,128)S(1)}, u32[]{:S(2)}, u32[]{:S(2)}) %all-to-all-start) | async-done | bytes 163872 | tf_op jit(solution)/shard_map/all_to_all | solution.py:268
  36.9 2.9 %shard_map.79.refs_10_ = bf16[1,2048,1152]{2,1,0:T(8,128)(2,1)S(1)} custom-call(s32[10]{0:T(128)S(1)} %stack.43.start_ref.refs_0_, bf16[8192,1152]{1,0:T(8,128)(2,1)} %head_ref.2), custom_call_target="tpu_custom_call" | custom-call | tf_op jit(solution)/shard_map/pallas_call | solution.py:116
  39.8 0.0 collective-permute-done.17.refs_9_
  39.8 4.9 %shard_map.80.refs_11_ = f32[512,1152]{1,0:T(8,128)S(1)} custom-call(s32[10]{0:T(128)S(1)} %stack.43.start_ref.refs_0_, f32[32,1,1280]{2,1,0:T(1,128)S(1)} %all-to-all-done.refs_1_, bf16[128,1024]{1,0:T(8,128)(2,1)S(1)} %copy-done, bf16[128,1024]{1,0:T(8,128)(2,1)S(1)} %collective-permute-done.refs_3_, bf16[128,1024]{1,0:T(8,128)(2,1)S(1)} %collective-permute-done.1.refs_4_, ...), custom_call_target="tpu_custom_call" | custom-call | tf_op jit(solution)/shard_map/pallas_call | solution.py:199
  44.7 0.0 collective-permute-done.2.refs_2_
  44.7 1.5 %collective-permute-start.19 = (bf16[256,1024]{1,0:T(8,128)(2,1)S(1)}, bf16[256,1024]{1,0:T(8,128)(2,1)S(1)}, u32[]{:S(2)}, u32[]{:S(2)}) collective-permute-start(bf16[256,1024]{1,0:T(8,128)(2,1)S(1)} %collective-permute-done.5.refs_3_), channel_id=1, source_target_pairs={{0,16},{1,9},{2,18},{3,11},{4,20},{5,13},{6,22},{7,15},{8,24},{9,1... | collective-permute-start | bytes 1572872 | tf_op jit(solution)/shard_map/ppermute | solution.py:38
  46.3 4.3 %shard_map.81.refs_10_ = bf16[2,2048,1152]{2,1,0:T(8,128)(2,1)S(1)} custom-call(s32[10]{0:T(128)S(1)} %stack.43.start_ref.refs_0_, bf16[8192,1152]{1,0:T(8,128)(2,1)} %head_ref.2), custom_call_target="tpu_custom_call" | custom-call | tf_op jit(solution)/shard_map/pallas_call | solution.py:116
  50.6 2.9 %shard_map.82.refs_10_ = bf16[1,2048,1152]{2,1,0:T(8,128)(2,1)S(1)} custom-call(s32[10]{0:T(128)S(1)} %stack.43.start_ref.refs_0_, bf16[8192,1152]{1,0:T(8,128)(2,1)} %head_ref.2), custom_call_target="tpu_custom_call" | custom-call | tf_op jit(solution)/shard_map/pallas_call | solution.py:116
  53.5 1.5 %collective-permute-start.7 = (bf16[128,1024]{1,0:T(8,128)(2,1)}, bf16[128,1024]{1,0:T(8,128)(2,1)S(1)}, u32[]{:S(2)}, u32[]{:S(2)}) collective-permute-start(bf16[128,1024]{1,0:T(8,128)(2,1)} %collective-permute-done.2.refs_2_), channel_id=1, source_target_pairs={{0,8},{1,17},{2,10},{3,19},{4,12},{5,21},{6,14},{7,23},{8,0},{9,25... | collective-permute-start | bytes 786440 | tf_op jit(solution)/shard_map/ppermute | solution.py:38
  55.0 0.5 collective-permute-start.8
  55.6 2.5 %collective-permute-start.21 = (bf16[256,1024]{1,0:T(8,128)(2,1)S(1)}, bf16[256,1024]{1,0:T(8,128)(2,1)S(1)}, u32[]{:S(2)}, u32[]{:S(2)}) collective-permute-start(bf16[256,1024]{1,0:T(8,128)(2,1)S(1)} %collective-permute-done.6.refs_4_), channel_id=1, source_target_pairs={{0,1},{1,0},{2,3},{3,2},{4,5},{5,4},{6,7},{7,6},{8,9},{9,8},{10,11... | collective-permute-start | bytes 1572872 | tf_op jit(solution)/shard_map/ppermute | solution.py:38
  58.1 0.5 collective-permute-start.22
  58.6 2.0 %collective-permute-done.7.refs_3_ = bf16[128,1024]{1,0:T(8,128)(2,1)S(1)} collective-permute-done((bf16[128,1024]{1,0:T(8,128)(2,1)}, bf16[128,1024]{1,0:T(8,128)(2,1)S(1)}, u32[]{:S(2)}, u32[]{:S(2)}) %collective-permute-start.7) | collective-permute-done | bytes 262176 | tf_op jit(solution)/shard_map/ppermute | solution.py:38
  60.6 3.4 %collective-permute-done.8.refs_4_ = bf16[128,1024]{1,0:T(8,128)(2,1)S(1)} collective-permute-done((bf16[128,1024]{1,0:T(8,128)(2,1)}, bf16[128,1024]{1,0:T(8,128)(2,1)S(1)}, u32[]{:S(2)}, u32[]{:S(2)}) %collective-permute-start.8) | collective-permute-done | bytes 262176 | tf_op jit(solution)/shard_map/ppermute | solution.py:38
  63.9 0.5 collective-permute-start.9
  64.4 0.1 collective-permute-start.10
  64.5 0.4 collective-permute-start.11
  65.0 0.1 collective-permute-start.12
  65.0 4.2 %shard_map.83.refs_11_ = f32[512,1152]{1,0:T(8,128)S(1)} custom-call(s32[10]{0:T(128)S(1)} %stack.43.start_ref.refs_0_, f32[32,1,1280]{2,1,0:T(1,128)S(1)} %all-to-all-done.refs_1_, bf16[256,1024]{1,0:T(8,128)(2,1)S(1)} %shard_map.78.refs_2_, bf16[256,1024]{1,0:T(8,128)(2,1)S(1)} %collective-permute-done.5.refs_3_, ...), custom_call_target="tpu_custom_call" | custom-call | tf_op jit(solution)/shard_map/pallas_call | solution.py:199
  69.2 4.2 %shard_map.84.refs_11_ = f32[512,1152]{1,0:T(8,128)S(1)} custom-call(s32[10]{0:T(128)S(1)} %stack.43.start_ref.refs_0_, f32[32,1,1280]{2,1,0:T(1,128)S(1)} %all-to-all-done.refs_1_, bf16[256,1024]{1,0:T(8,128)(2,1)S(1)} %shard_map.78.refs_2_, bf16[256,1024]{1,0:T(8,128)(2,1)S(1)} %collective-permute-done.5.refs_3_, ...), custom_call_target="tpu_custom_call" | custom-call | tf_op jit(solution)/shard_map/pallas_call | solution.py:199
  73.4 0.0 copy-start.1
  73.5 0.5 collective-permute-start.23
  74.0 1.1 %collective-permute-done.23.refs_9_ = bf16[128,1024]{1,0:T(8,128)(2,1)S(1)} collective-permute-done((bf16[128,1024]{1,0:T(8,128)(2,1)S(1)}, bf16[128,1024]{1,0:T(8,128)(2,1)S(1)}, u32[]{:S(2)}, u32[]{:S(2)}) %collective-permute-start.23) | collective-permute-done | bytes 262176 | tf_op jit(solution)/shard_map/ppermute | solution.py:38
  75.1 5.9 %shard_map.85 = f32[4,8,3,128]{3,2,1,0:T(4,128)} custom-call(s32[10]{0:T(128)S(1)} %stack.43.start_ref.refs_0_, f32[32,1,1280]{2,1,0:T(1,128)S(1)} %all-to-all-done.refs_1_, bf16[128,1024]{1,0:T(8,128)(2,1)} %collective-permute-done.2.refs_2_, bf16[128,1024]{1,0:T(8,128)(2,1)S(1)} %collective-permute-done.7.refs_3_, ...), custom_call_target="tpu_custom_call" | custom-call | tf_op jit(solution)/shard_map/pallas_call | solution.py:199
  81.0 4.3 %all-to-all-start.1 = ((f32[32,3,128]{2,1,0:T(4,128)}), f32[32,3,128]{2,1,0:T(4,128)S(1)}, u32[]{:S(2)}, u32[]{:S(2)}) async-start(f32[32,3,128]{2,1,0:T(4,128)} %bitcast.13), calls=%async_computation.1 | async-start | bytes 131072 | tf_op jit(solution)/shard_map/all_to_all | solution.py:299
  86.0 6.7 %all-to-all-done.1 = f32[32,3,128]{2,1,0:T(4,128)S(1)} async-done(((f32[32,3,128]{2,1,0:T(4,128)}), f32[32,3,128]{2,1,0:T(4,128)S(1)}, u32[]{:S(2)}, u32[]{:S(2)}) %all-to-all-start.1) | async-done | bytes 49184 | tf_op jit(solution)/shard_map/all_to_all | solution.py:299
  92.8 0.1 slice_reduce_fusion
  92.9 0.5 compare_select_fusion
  (22 shorter events, 0.1 us)
Async XLA Ops:
  0.6 9.9 %collective-permute-start = (bf16[128,1024]{1,0:T(8,128)(2,1)}, bf16[128,1024]{1,0:T(8,128)(2,1)S(1)}, u32[]{:S(2)}, u32[]{:S(2)}) collective-permute-start(bf16[128,1024]{1,0:T(8,128)(2,1)} %refs_2_.1), channel_id=1, source_target_pairs={{0,8},{1,17},{2,10},{3,19},{4,12},{5,21},{6,14},{7,23},{8,0},{9,25... | collective-permute-start | bytes 786440 | tf_op jit(solution)/shard_map/ppermute | solution.py:38
  3.6 6.9 %collective-permute-start.1 = (bf16[128,1024]{1,0:T(8,128)(2,1)}, bf16[128,1024]{1,0:T(8,128)(2,1)S(1)}, u32[]{:S(2)}, u32[]{:S(2)}) collective-permute-start(bf16[128,1024]{1,0:T(8,128)(2,1)} %refs_2_.1), channel_id=1, source_target_pairs={{0,16},{1,9},{2,18},{3,11},{4,20},{5,13},{6,22},{7,15},{8,24},{9,1... | collective-permute-start | bytes 786440 | tf_op jit(solution)/shard_map/ppermute | solution.py:38
  5.2 11.3 %collective-permute-start.3 = (bf16[128,1024]{1,0:T(8,128)(2,1)}, bf16[128,1024]{1,0:T(8,128)(2,1)S(1)}, u32[]{:S(2)}, u32[]{:S(2)}) collective-permute-start(bf16[128,1024]{1,0:T(8,128)(2,1)} %refs_2_.1), channel_id=1, source_target_pairs={{0,2},{1,3},{2,4},{3,5},{4,6},{5,7},{6,0},{7,1},{8,10},{9,11},{10,... | collective-permute-start | bytes 786440 | tf_op jit(solution)/shard_map/ppermute | solution.py:38
  6.7 13.8 %collective-permute-start.14 = (bf16[128,1024]{1,0:T(8,128)(2,1)}, bf16[128,1024]{1,0:T(8,128)(2,1)S(1)}, u32[]{:S(2)}, u32[]{:S(2)}) collective-permute-start(bf16[128,1024]{1,0:T(8,128)(2,1)} %refs_2_.1), channel_id=1, source_target_pairs={{0,1},{1,0},{2,3},{3,2},{4,5},{5,4},{6,7},{7,6},{8,9},{9,8},{10,11... | collective-permute-start | bytes 786440 | tf_op jit(solution)/shard_map/ppermute | solution.py:38
  6.7 13.6 %collective-permute-start.4 = (bf16[128,1024]{1,0:T(8,128)(2,1)}, bf16[128,1024]{1,0:T(8,128)(2,1)S(1)}, u32[]{:S(2)}, u32[]{:S(2)}) collective-permute-start(bf16[128,1024]{1,0:T(8,128)(2,1)} %refs_2_.1), channel_id=1, source_target_pairs={{0,6},{1,7},{2,0},{3,1},{4,2},{5,3},{6,4},{7,5},{8,14},{9,15},{10,... | collective-permute-start | bytes 786440 | tf_op jit(solution)/shard_map/ppermute | solution.py:38
  10.5 10.5 %collective-permute-start.13 = (bf16[128,1024]{1,0:T(8,128)(2,1)S(1)}, bf16[128,1024]{1,0:T(8,128)(2,1)}, u32[]{:S(2)}, u32[]{:S(2)}) collective-permute-start(bf16[128,1024]{1,0:T(8,128)(2,1)S(1)} %collective-permute-done.refs_3_), channel_id=1, source_target_pairs={{0,16},{1,9},{2,18},{3,11},{4,20},{5,13},{6,22},{7,15},{8,24},{9,1... | collective-permute-start | bytes 786440 | tf_op jit(solution)/shard_map/ppermute | solution.py:38
  16.5 9.6 %collective-permute-start.15 = (bf16[128,1024]{1,0:T(8,128)(2,1)S(1)}, bf16[128,1024]{1,0:T(8,128)(2,1)}, u32[]{:S(2)}, u32[]{:S(2)}) collective-permute-start(bf16[128,1024]{1,0:T(8,128)(2,1)S(1)} %collective-permute-done.refs_3_), channel_id=1, source_target_pairs={{0,1},{1,0},{2,3},{3,2},{4,5},{5,4},{6,7},{7,6},{8,9},{9,8},{10,11... | collective-permute-start | bytes 786440 | tf_op jit(solution)/shard_map/ppermute | solution.py:38
  16.5 10.0 %collective-permute-start.16 = (bf16[128,1024]{1,0:T(8,128)(2,1)S(1)}, bf16[128,1024]{1,0:T(8,128)(2,1)}, u32[]{:S(2)}, u32[]{:S(2)}) collective-permute-start(bf16[128,1024]{1,0:T(8,128)(2,1)S(1)} %collective-permute-done.1.refs_4_), channel_id=1, source_target_pairs={{0,1},{1,0},{2,3},{3,2},{4,5},{5,4},{6,7},{7,6},{8,9},{9,8},{10,11... | collective-permute-start | bytes 786440 | tf_op jit(solution)/shard_map/ppermute | solution.py:38
  20.4 24.3 %collective-permute-start.18 = (bf16[256,1024]{1,0:T(8,128)(2,1)S(1)}, bf16[256,1024]{1,0:T(8,128)(2,1)S(1)}, u32[]{:S(2)}, u32[]{:S(2)}) collective-permute-start(bf16[256,1024]{1,0:T(8,128)(2,1)S(1)} %shard_map.78.refs_2_), channel_id=1, source_target_pairs={{0,1},{1,0},{2,3},{3,2},{4,5},{5,4},{6,7},{7,6},{8,9},{9,8},{10,11... | collective-permute-start | bytes 1572872 | tf_op jit(solution)/shard_map/ppermute | solution.py:38
  20.5 24.2 %collective-permute-start.5 = (bf16[256,1024]{1,0:T(8,128)(2,1)S(1)}, bf16[256,1024]{1,0:T(8,128)(2,1)S(1)}, u32[]{:S(2)}, u32[]{:S(2)}) collective-permute-start(bf16[256,1024]{1,0:T(8,128)(2,1)S(1)} %shard_map.78.refs_2_), channel_id=1, source_target_pairs={{0,8},{1,17},{2,10},{3,19},{4,12},{5,21},{6,14},{7,23},{8,0},{9,25... | collective-permute-start | bytes 1572872 | tf_op jit(solution)/shard_map/ppermute | solution.py:38
  21.1 23.6 %collective-permute-start.6 = (bf16[256,1024]{1,0:T(8,128)(2,1)S(1)}, bf16[256,1024]{1,0:T(8,128)(2,1)S(1)}, u32[]{:S(2)}, u32[]{:S(2)}) collective-permute-start(bf16[256,1024]{1,0:T(8,128)(2,1)S(1)} %shard_map.78.refs_2_), channel_id=1, source_target_pairs={{0,16},{1,9},{2,18},{3,11},{4,20},{5,13},{6,22},{7,15},{8,24},{9,1... | collective-permute-start | bytes 1572872 | tf_op jit(solution)/shard_map/ppermute | solution.py:38
  21.6 15.3 %all-to-all-start = ((f32[32,1,1280]{2,1,0:T(1,128)}), f32[32,1,1280]{2,1,0:T(1,128)S(1)}, u32[]{:S(2)}, u32[]{:S(2)}) async-start(f32[32,1,1280]{2,1,0:T(1,128)} %shard_map.77), calls=%async_computation | async-start | bytes 327680 | tf_op jit(solution)/shard_map/all_to_all | solution.py:268
  26.1 13.7 %copy-start = (bf16[128,1024]{1,0:T(8,128)(2,1)S(1)}, bf16[128,1024]{1,0:T(8,128)(2,1)}, u32[]{:S(2)}) copy-start(bf16[128,1024]{1,0:T(8,128)(2,1)} %refs_2_.1) | copy-start | bytes 786436
  26.1 13.7 %collective-permute-start.17 = (bf16[128,1024]{1,0:T(8,128)(2,1)}, bf16[128,1024]{1,0:T(8,128)(2,1)}, u32[]{:S(2)}, u32[]{:S(2)}) collective-permute-start(bf16[128,1024]{1,0:T(8,128)(2,1)} %collective-permute-done.13.refs_5_), channel_id=1, source_target_pairs={{0,1},{1,0},{2,3},{3,2},{4,5},{5,4},{6,7},{7,6},{8,9},{9,8},{10,11... | collective-permute-start | bytes 786440 | tf_op jit(solution)/shard_map/ppermute | solution.py:38
  26.4 18.3 %collective-permute-start.2 = (bf16[128,1024]{1,0:T(8,128)(2,1)}, bf16[128,1024]{1,0:T(8,128)(2,1)}, u32[]{:S(2)}, u32[]{:S(2)}) collective-permute-start(bf16[128,1024]{1,0:T(8,128)(2,1)} %refs_2_.1), channel_id=1, source_target_pairs={{0,4},{1,5},{2,6},{3,7},{4,0},{5,1},{6,2},{7,3},{8,12},{9,13},{10,... | collective-permute-start | bytes 786440 | tf_op jit(solution)/shard_map/ppermute | solution.py:38
  44.7 13.4 %collective-permute-start.19 = (bf16[256,1024]{1,0:T(8,128)(2,1)S(1)}, bf16[256,1024]{1,0:T(8,128)(2,1)S(1)}, u32[]{:S(2)}, u32[]{:S(2)}) collective-permute-start(bf16[256,1024]{1,0:T(8,128)(2,1)S(1)} %collective-permute-done.5.refs_3_), channel_id=1, source_target_pairs={{0,16},{1,9},{2,18},{3,11},{4,20},{5,13},{6,22},{7,15},{8,24},{9,1... | collective-permute-start | bytes 1572872 | tf_op jit(solution)/shard_map/ppermute | solution.py:38
  53.5 7.1 %collective-permute-start.7 = (bf16[128,1024]{1,0:T(8,128)(2,1)}, bf16[128,1024]{1,0:T(8,128)(2,1)S(1)}, u32[]{:S(2)}, u32[]{:S(2)}) collective-permute-start(bf16[128,1024]{1,0:T(8,128)(2,1)} %collective-permute-done.2.refs_2_), channel_id=1, source_target_pairs={{0,8},{1,17},{2,10},{3,19},{4,12},{5,21},{6,14},{7,23},{8,0},{9,25... | collective-permute-start | bytes 786440 | tf_op jit(solution)/shard_map/ppermute | solution.py:38
  55.0 8.9 %collective-permute-start.8 = (bf16[128,1024]{1,0:T(8,128)(2,1)}, bf16[128,1024]{1,0:T(8,128)(2,1)S(1)}, u32[]{:S(2)}, u32[]{:S(2)}) collective-permute-start(bf16[128,1024]{1,0:T(8,128)(2,1)} %collective-permute-done.2.refs_2_), channel_id=1, source_target_pairs={{0,16},{1,9},{2,18},{3,11},{4,20},{5,13},{6,22},{7,15},{8,24},{9,1... | collective-permute-start | bytes 786440 | tf_op jit(solution)/shard_map/ppermute | solution.py:38
  55.6 9.0 %collective-permute-start.21 = (bf16[256,1024]{1,0:T(8,128)(2,1)S(1)}, bf16[256,1024]{1,0:T(8,128)(2,1)S(1)}, u32[]{:S(2)}, u32[]{:S(2)}) collective-permute-start(bf16[256,1024]{1,0:T(8,128)(2,1)S(1)} %collective-permute-done.6.refs_4_), channel_id=1, source_target_pairs={{0,1},{1,0},{2,3},{3,2},{4,5},{5,4},{6,7},{7,6},{8,9},{9,8},{10,11... | collective-permute-start | bytes 1572872 | tf_op jit(solution)/shard_map/ppermute | solution.py:38
  58.1 6.9 %collective-permute-start.20 = (bf16[256,1024]{1,0:T(8,128)(2,1)S(1)}, bf16[256,1024]{1,0:T(8,128)(2,1)S(1)}, u32[]{:S(2)}, u32[]{:S(2)}) collective-permute-start(bf16[256,1024]{1,0:T(8,128)(2,1)S(1)} %collective-permute-done.5.refs_3_), channel_id=1, source_target_pairs={{0,1},{1,0},{2,3},{3,2},{4,5},{5,4},{6,7},{7,6},{8,9},{9,8},{10,11... | collective-permute-start | bytes 1572872 | tf_op jit(solution)/shard_map/ppermute | solution.py:38
  58.1 7.0 %collective-permute-start.22 = (bf16[256,1024]{1,0:T(8,128)(2,1)S(1)}, bf16[256,1024]{1,0:T(8,128)(2,1)S(1)}, u32[]{:S(2)}, u32[]{:S(2)}) collective-permute-start(bf16[256,1024]{1,0:T(8,128)(2,1)S(1)} %collective-permute-done.19.refs_5_), channel_id=1, source_target_pairs={{0,1},{1,0},{2,3},{3,2},{4,5},{5,4},{6,7},{7,6},{8,9},{9,8},{10,11... | collective-permute-start | bytes 1572872 | tf_op jit(solution)/shard_map/ppermute | solution.py:38
  63.9 9.5 %collective-permute-start.9 = (bf16[128,1024]{1,0:T(8,128)(2,1)S(1)}, bf16[128,1024]{1,0:T(8,128)(2,1)S(1)}, u32[]{:S(2)}, u32[]{:S(2)}) collective-permute-start(bf16[128,1024]{1,0:T(8,128)(2,1)S(1)} %collective-permute-done.7.refs_3_), channel_id=1, source_target_pairs={{0,16},{1,9},{2,18},{3,11},{4,20},{5,13},{6,22},{7,15},{8,24},{9,1... | collective-permute-start | bytes 786440 | tf_op jit(solution)/shard_map/ppermute | solution.py:38
  64.4 9.5 %collective-permute-start.10 = (bf16[128,1024]{1,0:T(8,128)(2,1)}, bf16[128,1024]{1,0:T(8,128)(2,1)S(1)}, u32[]{:S(2)}, u32[]{:S(2)}) collective-permute-start(bf16[128,1024]{1,0:T(8,128)(2,1)} %collective-permute-done.2.refs_2_), channel_id=1, source_target_pairs={{0,1},{1,0},{2,3},{3,2},{4,5},{5,4},{6,7},{7,6},{8,9},{9,8},{10,11... | collective-permute-start | bytes 786440 | tf_op jit(solution)/shard_map/ppermute | solution.py:38
  64.5 9.4 %collective-permute-start.11 = (bf16[128,1024]{1,0:T(8,128)(2,1)S(1)}, bf16[128,1024]{1,0:T(8,128)(2,1)S(1)}, u32[]{:S(2)}, u32[]{:S(2)}) collective-permute-start(bf16[128,1024]{1,0:T(8,128)(2,1)S(1)} %collective-permute-done.7.refs_3_), channel_id=1, source_target_pairs={{0,1},{1,0},{2,3},{3,2},{4,5},{5,4},{6,7},{7,6},{8,9},{9,8},{10,11... | collective-permute-start | bytes 786440 | tf_op jit(solution)/shard_map/ppermute | solution.py:38
  65.0 9.0 %collective-permute-start.12 = (bf16[128,1024]{1,0:T(8,128)(2,1)S(1)}, bf16[128,1024]{1,0:T(8,128)(2,1)S(1)}, u32[]{:S(2)}, u32[]{:S(2)}) collective-permute-start(bf16[128,1024]{1,0:T(8,128)(2,1)S(1)} %collective-permute-done.8.refs_4_), channel_id=1, source_target_pairs={{0,1},{1,0},{2,3},{3,2},{4,5},{5,4},{6,7},{7,6},{8,9},{9,8},{10,11... | collective-permute-start | bytes 786440 | tf_op jit(solution)/shard_map/ppermute | solution.py:38
  73.4 19.4 %copy-start.1 = (f32[128]{0:T(128)S(1)}, f32[128]{0:T(128)}, u32[]{:S(2)}) copy-start(f32[128]{0:T(128)} %param.10) | copy-start | bytes 1540
  73.5 1.7 %collective-permute-start.23 = (bf16[128,1024]{1,0:T(8,128)(2,1)S(1)}, bf16[128,1024]{1,0:T(8,128)(2,1)S(1)}, u32[]{:S(2)}, u32[]{:S(2)}) collective-permute-start(bf16[128,1024]{1,0:T(8,128)(2,1)S(1)} %collective-permute-done.9.refs_5_), channel_id=1, source_target_pairs={{0,1},{1,0},{2,3},{3,2},{4,5},{5,4},{6,7},{7,6},{8,9},{9,8},{10,11... | collective-permute-start | bytes 786440 | tf_op jit(solution)/shard_map/ppermute | solution.py:38
  81.0 11.7 %all-to-all-start.1 = ((f32[32,3,128]{2,1,0:T(4,128)}), f32[32,3,128]{2,1,0:T(4,128)S(1)}, u32[]{:S(2)}, u32[]{:S(2)}) async-start(f32[32,3,128]{2,1,0:T(4,128)} %bitcast.13), calls=%async_computation.1 | async-start | bytes 131072 | tf_op jit(solution)/shard_map/all_to_all | solution.py:299

commit v6 on v5

--- a/solution.py
+++ b/solution.py
@@ -120,7 +120,6 @@
         out_specs=pl.BlockSpec(memory_space=pltpu.VMEM),
         scratch_shapes=[pltpu.SemaphoreType.DMA((len(offsets),))],
         compiler_params=pltpu.CompilerParams(vmem_limit_bytes=SMALL_LIMIT),
-        cost_estimate=pl.CostEstimate(flops=0, bytes_accessed=0, transcendentals=0),
     )(starts, far(head))
 
 
@@ -142,16 +141,22 @@
     )(*blocks)
 
 
-def layer_kernel(n, n_t, place, layer, offset, first, last, *refs):
+def layer_kernel(n, n_t, place, layer, offset, own, first, last, *refs):
     refs = list(refs)
     start_ref, fine = refs.pop(0), refs.pop(0)
     blocks = [refs.pop(0) for _ in range(CORES * n)]
     weights = refs.pop(0)
     acc_ref = None if first else refs.pop(0)
-    out_ref, rows = refs[:2]
-    acc = refs[2] if last else out_ref
+    out_ref, rows = refs.pop(0), refs.pop(0)
+    acc = refs.pop(0) if last else out_ref
     feat = blocks[0].shape[1]
     tok = rows.shape[0] // n
+    if own:
+        deep = rows.shape[1]
+        source = weights.at[pl.ds(pl.multiple_of(start_ref[offset] * deep, deep), deep)]
+        copy = pltpu.make_async_copy(source, refs[0].at[layer], refs[1])
+        copy.start()
+        weights = refs[0]
     c_me, base = start_ref[0], start_ref[1]
     owners = [start_ref[2 + k] for k in range(n)]
     scales = []
@@ -167,6 +172,8 @@
             part = blocks[c * n + k][layer * tok : (layer + 1) * tok, :].astype(jnp.float32)
             part = part * scales[spot] * gain
             rows[spot * tok : (spot + 1) * tok, columns] = part.astype(jnp.bfloat16)
+    if own:
+        copy.wait()
     product = jnp.dot(rows[...], weights[layer], preferred_element_type=jnp.float32)
     acc[...] = product if first else acc_ref[...] + product
     if not last:
@@ -188,23 +195,28 @@
 def layer_product(tok, n_t, starts, layer, offset, fine, blocks, place, weights, acc, last):
     n = len(place)
     feat = blocks[0].shape[1]
-    deep, vocab = weights.shape[1:]
+    own = weights.ndim == 2
+    deep, vocab = CORES * feat, weights.shape[-1]
     vmem = pl.BlockSpec(memory_space=pltpu.VMEM)
     first = acc is None
     logits = jax.ShapeDtypeStruct((n * tok, vocab), jnp.float32)
-    operands = [starts, fine, *blocks, weights] + ([] if first else [acc])
+    operands = [starts, fine, *blocks, far(weights) if own else weights] + ([] if first else [acc])
+    specs = [pl.BlockSpec(memory_space=pltpu.SMEM)] + [vmem] * (len(operands) - 1)
     scratch = [pltpu.VMEM((n * tok, deep), jnp.bfloat16)]
     if last:
         scratch.append(pltpu.VMEM(logits.shape, jnp.float32))
+    if own:
+        specs[2 + len(blocks)] = pl.BlockSpec(memory_space=pl.ANY)
+        scratch += [pltpu.VMEM((1, deep, vocab), weights.dtype), pltpu.SemaphoreType.DMA]
     return pl.pallas_call(
-        functools.partial(layer_kernel, n, n_t, place, layer, offset, first, last),
+        functools.partial(layer_kernel, n, n_t, place, layer, offset, own, first, last),
         out_shape=jax.ShapeDtypeStruct((n, n_t, 3, tok), jnp.float32) if last else logits,
-        in_specs=[pl.BlockSpec(memory_space=pltpu.SMEM)] + [vmem] * (len(operands) - 1),
+        in_specs=specs,
         out_specs=vmem,
         scratch_shapes=scratch,
         compiler_params=pltpu.CompilerParams(vmem_limit_bytes=VMEM_LIMIT),
         cost_estimate=pl.CostEstimate(
-            flops=0, bytes_accessed=0, transcendentals=0
+            flops=2 * n * tok * deep * vocab, bytes_accessed=2 * deep * vocab, transcendentals=0
         ),
     )(*operands)
 
@@ -261,15 +273,16 @@
         for dz in group:
             layers[dz] = grid.along(after(hidden, *before), dz)
         before = list(reached[0].values()) if len(before) == 0 else [layers[dz] for dz in group]
+    for group in groups[1:]:
+        sources = [layers[dz] for dz in group]
+        sources[0] = after(sources[0], *reached[-1].values())
+        reached.append(grid.reach(joined(sources) if len(sources) > 1 else sources[0]))
+
     vocab_cols = head.shape[1]
     vocab_start = lax.axis_index(("dp", "tensor")) * vocab_cols
     starts = jnp.stack([c_me, vocab_start] + owners + [(z_me - dz) % depth for dz in range(depth)])
     packed = squares(after(hidden, starts), norm_gain[None, :], targets[None, :], n_dp * n_t)
     fine = lax.all_to_all(packed, ("dp", "tensor"), 0, 0, tiled=True)
-    for group in groups[1:]:
-        sources = [layers[dz] for dz in group]
-        sources[0] = after(sources[0], packed, *reached[-1].values())
-        reached.append(grid.reach(joined(sources) if len(sources) > 1 else sources[0]))
 
     acc, deep = None, CORES * feat
     for at, group in enumerate(groups):
@@ -280,14 +293,14 @@
         held = [layers[dz] for dz in groups[at + 1]] + [own] if middle else []
         spread = grid.fill(dict(reached[at]), *([acc] if at == 1 else []), *held)
         if at == 0:
-            weights = [loaded(starts, offsets, after(head, fine), deep)]
+            weights = [head]
         elif at == 1:
             for later in groups[1:]:
                 ready = after(head, acc, *(layers[dz] for dz in groups[2]))
                 weights.append(loaded(starts, [2 + n_dp + dz for dz in later], ready, deep))
-        ready = weights[1:3] if middle else []
-        others = [own] + [grid.sibling(after(a, *ready)) for a in spread[1:-1]]
-        others.append(grid.sibling(after(spread[-1], *([acc] if final else ready))))
+        following = [*reached[at + 1].values(), *weights[1:3]] if middle else []
+        others = [own] + [grid.sibling(after(a, *following)) for a in spread[1:-1]]
+        others.append(grid.sibling(after(spread[-1], *([acc] if final else following))))
         blocks = spread + others
         for layer, offset in enumerate(offsets):
             done = layer == len(offsets) - 1

time: 93.8 us -> 86.4 us (0.921)
  waiting for transfers between devices: 28.7 us -> 18.8 us
  local copies, waits for them, and re-layouts: 0.1 us -> 2.7 us
  Pallas kernels: 31.1 us -> 30 us
  starting transfers between devices: 31.4 us -> 32.5 us
    all_to_all x1, waiting for transfers between devices: 7.85 us -> 1.27 us  [body(): fine = lax.all_to_all(packed, ('dp', 'tensor'), 0, 0, tiled=True)]
    ppermute x24, waiting for transfers between devices: 14.1 us -> 10.7 us  [permute(): return lax.ppermute(a, ('dp', 'tensor'), perm)]
    pallas_call x3 -> x2, Pallas kernels: 10.1 us -> 7.23 us  [loaded(): pl.pallas_call(functools.partial(load_kernel, offsets), out_shape=pltpu.V...]
    unnamed x4 -> x8, local copies, waits for them, and re-layouts: 0.01 us -> 2.62 us
    pallas_call x4, Pallas kernels: 19.2 us -> 21 us  [layer_product(): pl.pallas_call(functools.partial(layer_kernel, n, n_t, place, layer, offs...]
  transfers between devices with their start and end apart: 26 -> 26, of which waited for: 8 -> 10; matrix products, arithmetic and copies ran while one was open for 0% -> 0% of each run, Pallas kernels for 27% -> 28%
where the time goes in v6:
time: 86.4 us; the launch traced here: 86 us
  starting transfers between devices  32.5 us (38%)
  Pallas kernels  30 us (35%)
  waiting for transfers between devices  18.8 us (22%)
  local copies, waits for them, and re-layouts  2.7 us (3%)
  between operations  1.4 us (2%)
    ppermute x24, starting transfers between devices, permute(): return lax.ppermute(a, ('dp', 'tensor'), perm)  22.5 us
    pallas_call x4, Pallas kernels, layer_product(): pl.pallas_call(functools.partial(layer_kernel, n, n_t, place, layer, offs...  21 us
    ppermute x24, waiting for transfers between devices, permute(): return lax.ppermute(a, ('dp', 'tensor'), perm)  10.7 us
    pallas_call x2, Pallas kernels, loaded(): pl.pallas_call(functools.partial(load_kernel, offsets), out_shape=pltpu.V...  7.23 us
    all_to_all x1, waiting for transfers between devices, body(): lax.all_to_all(acc.reshape(n_dp * n_t, 3, tok), ('dp', 'tensor'), 0, 0, t...  6.74 us
    all_to_all x1, starting transfers between devices, body(): fine = lax.all_to_all(packed, ('dp', 'tensor'), 0, 0, tiled=True)  5.05 us
    all_to_all x1, starting transfers between devices, body(): lax.all_to_all(acc.reshape(n_dp * n_t, 3, tok), ('dp', 'tensor'), 0, 0, t...  4.89 us
    unnamed x8, local copies, waits for them, and re-layouts  2.62 us
  transfers between devices with their start and end apart: 26, of which 10 were waited for; matrix products, arithmetic and copies ran while one was open for 0% of the time, Pallas kernels for 28%

profile of v6, /device:TPU:0, one launch (start us, length us, event | category | flops | bytes accessed | tf_op | source)
XLA Modules:
  0.0 86.0 jit_solution(14558075040810503198)
XLA Ops:
  0.6 3.0 %collective-permute-start = (bf16[128,1024]{1,0:T(8,128)(2,1)}, bf16[128,1024]{1,0:T(8,128)(2,1)S(1)}, u32[]{:S(2)}, u32[]{:S(2)}) collective-permute-start(bf16[128,1024]{1,0:T(8,128)(2,1)} %refs_2_.1), channel_id=1, source_target_pairs={{0,8},{1,17},{2,10},{3,19},{4,12},{5,21},{6,14},{7,23},{8,0},{9,25... | collective-permute-start | bytes 786440 | tf_op jit(solution)/shard_map/ppermute | solution.py:38
  3.6 1.5 %collective-permute-start.1 = (bf16[128,1024]{1,0:T(8,128)(2,1)}, bf16[128,1024]{1,0:T(8,128)(2,1)S(1)}, u32[]{:S(2)}, u32[]{:S(2)}) collective-permute-start(bf16[128,1024]{1,0:T(8,128)(2,1)} %refs_2_.1), channel_id=1, source_target_pairs={{0,16},{1,9},{2,18},{3,11},{4,20},{5,13},{6,22},{7,15},{8,24},{9,1... | collective-permute-start | bytes 786440 | tf_op jit(solution)/shard_map/ppermute | solution.py:38
  5.2 1.6 %collective-permute-start.3 = (bf16[128,1024]{1,0:T(8,128)(2,1)}, bf16[128,1024]{1,0:T(8,128)(2,1)S(1)}, u32[]{:S(2)}, u32[]{:S(2)}) collective-permute-start(bf16[128,1024]{1,0:T(8,128)(2,1)} %refs_2_.1), channel_id=1, source_target_pairs={{0,2},{1,3},{2,4},{3,5},{4,6},{5,7},{6,0},{7,1},{8,10},{9,11},{10,... | collective-permute-start | bytes 786440 | tf_op jit(solution)/shard_map/ppermute | solution.py:38
  6.7 0.0 collective-permute-start.14
  6.7 2.2 %collective-permute-start.4 = (bf16[128,1024]{1,0:T(8,128)(2,1)}, bf16[128,1024]{1,0:T(8,128)(2,1)S(1)}, u32[]{:S(2)}, u32[]{:S(2)}) collective-permute-start(bf16[128,1024]{1,0:T(8,128)(2,1)} %refs_2_.1), channel_id=1, source_target_pairs={{0,6},{1,7},{2,0},{3,1},{4,2},{5,3},{6,4},{7,5},{8,14},{9,15},{10,... | collective-permute-start | bytes 786440 | tf_op jit(solution)/shard_map/ppermute | solution.py:38
  9.0 1.6 %collective-permute-done.refs_3_ = bf16[128,1024]{1,0:T(8,128)(2,1)S(1)} collective-permute-done((bf16[128,1024]{1,0:T(8,128)(2,1)}, bf16[128,1024]{1,0:T(8,128)(2,1)S(1)}, u32[]{:S(2)}, u32[]{:S(2)}) %collective-permute-start) | collective-permute-done | bytes 262176 | tf_op jit(solution)/shard_map/ppermute | solution.py:38
  10.5 1.5 %collective-permute-start.13 = (bf16[128,1024]{1,0:T(8,128)(2,1)S(1)}, bf16[128,1024]{1,0:T(8,128)(2,1)S(1)}, u32[]{:S(2)}, u32[]{:S(2)}) collective-permute-start(bf16[128,1024]{1,0:T(8,128)(2,1)S(1)} %collective-permute-done.refs_3_), channel_id=1, source_target_pairs={{0,16},{1,9},{2,18},{3,11},{4,20},{5,13},{6,22},{7,15},{8,24},{9,1... | collective-permute-start | bytes 786440 | tf_op jit(solution)/shard_map/ppermute | solution.py:38
  12.0 0.9 collective-permute-start.15
  12.9 0.1 stack.43.refs_0_.start_ref
  12.9 1.8 %shard_map.77 = f32[32,1,1280]{2,1,0:T(1,128)} custom-call(bf16[128,1024]{1,0:T(8,128)(2,1)} %refs_2_.1, f32[1,1024]{1,0:T(1,128)} %bitcast.22, s32[1,128]{1,0:T(1,128)} %bitcast.23), custom_call_target="tpu_custom_call" | custom-call | tf_op jit(solution)/shard_map/pallas_call | solution.py:243
  14.7 5.0 %all-to-all-start = ((f32[32,1,1280]{2,1,0:T(1,128)}), f32[32,1,1280]{2,1,0:T(1,128)S(1)}, u32[]{:S(2)}, u32[]{:S(2)}) async-start(f32[32,1,1280]{2,1,0:T(1,128)} %shard_map.77), calls=%async_computation | async-start | bytes 327680 | tf_op jit(solution)/shard_map/all_to_all | solution.py:285
  19.8 0.0 collective-permute-done.3.refs_0_
  19.8 0.3 collective-permute-start.16
  20.1 0.2 collective-permute-done.4.refs_1_
  20.4 1.5 %collective-permute-start.5 = (bf16[256,1024]{1,0:T(8,128)(2,1)S(1)}, bf16[256,1024]{1,0:T(8,128)(2,1)S(1)}, u32[]{:S(2)}, u32[]{:S(2)}) collective-permute-start(bf16[256,1024]{1,0:T(8,128)(2,1)S(1)} %shard_map.78.refs_2_), channel_id=1, source_target_pairs={{0,8},{1,17},{2,10},{3,19},{4,12},{5,21},{6,14},{7,23},{8,0},{9,25... | collective-permute-start | bytes 1572872 | tf_op jit(solution)/shard_map/ppermute | solution.py:38
  21.9 1.5 %collective-permute-start.6 = (bf16[256,1024]{1,0:T(8,128)(2,1)S(1)}, bf16[256,1024]{1,0:T(8,128)(2,1)S(1)}, u32[]{:S(2)}, u32[]{:S(2)}) collective-permute-start(bf16[256,1024]{1,0:T(8,128)(2,1)S(1)} %shard_map.78.refs_2_), channel_id=1, source_target_pairs={{0,16},{1,9},{2,18},{3,11},{4,20},{5,13},{6,22},{7,15},{8,24},{9,1... | collective-permute-start | bytes 1572872 | tf_op jit(solution)/shard_map/ppermute | solution.py:38
  23.4 0.5 collective-permute-start.17
  23.9 0.7 copy-done.1
  24.6 2.4 %collective-permute-start.2 = (bf16[128,1024]{1,0:T(8,128)(2,1)}, bf16[128,1024]{1,0:T(8,128)(2,1)}, u32[]{:S(2)}, u32[]{:S(2)}) collective-permute-start(bf16[128,1024]{1,0:T(8,128)(2,1)} %refs_2_.1), channel_id=1, source_target_pairs={{0,4},{1,5},{2,6},{3,7},{4,0},{5,1},{6,2},{7,3},{8,12},{9,13},{10,... | collective-permute-start | bytes 786440 | tf_op jit(solution)/shard_map/ppermute | solution.py:38
  27.0 1.3 %all-to-all-done.refs_1_ = f32[32,1,1280]{2,1,0:T(1,128)S(1)} async-done(((f32[32,1,1280]{2,1,0:T(1,128)}), f32[32,1,1280]{2,1,0:T(1,128)S(1)}, u32[]{:S(2)}, u32[]{:S(2)}) %all-to-all-start) | async-done | bytes 163872 | tf_op jit(solution)/shard_map/all_to_all | solution.py:285
  28.3 0.9 %copy-done = bf16[128,1024]{1,0:T(8,128)(2,1)S(1)} copy-done((bf16[128,1024]{1,0:T(8,128)(2,1)S(1)}, bf16[128,1024]{1,0:T(8,128)(2,1)}, u32[]{:S(2)}) %copy-start) | copy-done | bytes 262168
  29.2 0.9 %copy-done.2 = bf16[128,1024]{1,0:T(8,128)(2,1)S(1)} copy-done((bf16[128,1024]{1,0:T(8,128)(2,1)S(1)}, bf16[128,1024]{1,0:T(8,128)(2,1)}, u32[]{:S(2)}) %copy-start.2) | copy-done | bytes 262168
  30.2 6.7 %shard_map.79.refs_11_ = f32[512,1152]{1,0:T(8,128)S(1)} custom-call(s32[10]{0:T(128)S(1)} %stack.43.refs_0_.start_ref, f32[32,1,1280]{2,1,0:T(1,128)S(1)} %all-to-all-done.refs_1_, bf16[128,1024]{1,0:T(8,128)(2,1)S(1)} %copy-done, bf16[128,1024]{1,0:T(8,128)(2,1)S(1)} %collective-permute-done.refs_3_, bf16[128,1024]{1,0:T(8,128)(2,1)S(1)} %collective-permute-done.1.refs_4_, ...), custom_call_target="tpu_custom_call" | custom-call | flops 2415919104 | bytes 4718592 | tf_op jit(solution)/shard_map/pallas_call | solution.py:211
  36.9 2.8 %collective-permute-done.2.refs_2_ = bf16[128,1024]{1,0:T(8,128)(2,1)} collective-permute-done((bf16[128,1024]{1,0:T(8,128)(2,1)}, bf16[128,1024]{1,0:T(8,128)(2,1)}, u32[]{:S(2)}, u32[]{:S(2)}) %collective-permute-start.2) | collective-permute-done | bytes 262176 | tf_op jit(solution)/shard_map/ppermute | solution.py:38
  39.7 0.6 collective-permute-start.19
  40.4 1.1 %collective-permute-start.7 = (bf16[128,1024]{1,0:T(8,128)(2,1)}, bf16[128,1024]{1,0:T(8,128)(2,1)S(1)}, u32[]{:S(2)}, u32[]{:S(2)}) collective-permute-start(bf16[128,1024]{1,0:T(8,128)(2,1)} %collective-permute-done.2.refs_2_), channel_id=1, source_target_pairs={{0,8},{1,17},{2,10},{3,19},{4,12},{5,21},{6,14},{7,23},{8,0},{9,25... | collective-permute-start | bytes 786440 | tf_op jit(solution)/shard_map/ppermute | solution.py:38
  41.5 0.9 %collective-permute-start.8 = (bf16[128,1024]{1,0:T(8,128)(2,1)}, bf16[128,1024]{1,0:T(8,128)(2,1)S(1)}, u32[]{:S(2)}, u32[]{:S(2)}) collective-permute-start(bf16[128,1024]{1,0:T(8,128)(2,1)} %collective-permute-done.2.refs_2_), channel_id=1, source_target_pairs={{0,16},{1,9},{2,18},{3,11},{4,20},{5,13},{6,22},{7,15},{8,24},{9,1... | collective-permute-start | bytes 786440 | tf_op jit(solution)/shard_map/ppermute | solution.py:38
  42.4 4.3 %shard_map.80.refs_10_ = bf16[2,2048,1152]{2,1,0:T(8,128)(2,1)S(1)} custom-call(s32[10]{0:T(128)S(1)} %stack.43.refs_0_.start_ref, bf16[8192,1152]{1,0:T(8,128)(2,1)} %head_ref.1), custom_call_target="tpu_custom_call" | custom-call | tf_op jit(solution)/shard_map/pallas_call | solution.py:116
  46.7 2.9 %shard_map.81.refs_10_ = bf16[1,2048,1152]{2,1,0:T(8,128)(2,1)S(1)} custom-call(s32[10]{0:T(128)S(1)} %stack.43.refs_0_.start_ref, bf16[8192,1152]{1,0:T(8,128)(2,1)} %head_ref.1), custom_call_target="tpu_custom_call" | custom-call | tf_op jit(solution)/shard_map/pallas_call | solution.py:116
  49.6 0.2 collective-permute-done.7.refs_3_
  49.8 3.5 %collective-permute-done.8.refs_4_ = bf16[128,1024]{1,0:T(8,128)(2,1)S(1)} collective-permute-done((bf16[128,1024]{1,0:T(8,128)(2,1)}, bf16[128,1024]{1,0:T(8,128)(2,1)S(1)}, u32[]{:S(2)}, u32[]{:S(2)}) %collective-permute-start.8) | collective-permute-done | bytes 262176 | tf_op jit(solution)/shard_map/ppermute | solution.py:38
  53.3 0.5 collective-permute-start.20
  53.9 0.0 collective-permute-start.22
  53.9 0.5 collective-permute-start.10
  54.4 1.6 %collective-permute-start.9 = (bf16[128,1024]{1,0:T(8,128)(2,1)S(1)}, bf16[128,1024]{1,0:T(8,128)(2,1)S(1)}, u32[]{:S(2)}, u32[]{:S(2)}) collective-permute-start(bf16[128,1024]{1,0:T(8,128)(2,1)S(1)} %collective-permute-done.7.refs_3_), channel_id=1, source_target_pairs={{0,16},{1,9},{2,18},{3,11},{4,20},{5,13},{6,22},{7,15},{8,24},{9,1... | collective-permute-start | bytes 786440 | tf_op jit(solution)/shard_map/ppermute | solution.py:38
  56.0 0.4 collective-permute-done.20.refs_7_
  56.4 0.1 collective-permute-start.12
  56.5 0.6 collective-permute-done.22.refs_9_
  57.1 4.2 %shard_map.82.refs_11_ = f32[512,1152]{1,0:T(8,128)S(1)} custom-call(s32[10]{0:T(128)S(1)} %stack.43.refs_0_.start_ref, f32[32,1,1280]{2,1,0:T(1,128)S(1)} %all-to-all-done.refs_1_, bf16[256,1024]{1,0:T(8,128)(2,1)S(1)} %shard_map.78.refs_2_, bf16[256,1024]{1,0:T(8,128)(2,1)S(1)} %collective-permute-done.5.refs_3_, ...), custom_call_target="tpu_custom_call" | custom-call | flops 2415919104 | bytes 4718592 | tf_op jit(solution)/shard_map/pallas_call | solution.py:211
  61.3 4.2 %shard_map.83.refs_11_ = f32[512,1152]{1,0:T(8,128)S(1)} custom-call(s32[10]{0:T(128)S(1)} %stack.43.refs_0_.start_ref, f32[32,1,1280]{2,1,0:T(1,128)S(1)} %all-to-all-done.refs_1_, bf16[256,1024]{1,0:T(8,128)(2,1)S(1)} %shard_map.78.refs_2_, bf16[256,1024]{1,0:T(8,128)(2,1)S(1)} %collective-permute-done.5.refs_3_, ...), custom_call_target="tpu_custom_call" | custom-call | flops 2415919104 | bytes 4718592 | tf_op jit(solution)/shard_map/pallas_call | solution.py:211
  65.5 0.0 copy-start.3
  65.5 0.2 collective-permute-start.23
  65.8 1.4 %collective-permute-done.23.refs_9_ = bf16[128,1024]{1,0:T(8,128)(2,1)S(1)} collective-permute-done((bf16[128,1024]{1,0:T(8,128)(2,1)S(1)}, bf16[128,1024]{1,0:T(8,128)(2,1)S(1)}, u32[]{:S(2)}, u32[]{:S(2)}) %collective-permute-start.23) | collective-permute-done | bytes 262176 | tf_op jit(solution)/shard_map/ppermute | solution.py:38
  67.1 5.9 %shard_map.84 = f32[4,8,3,128]{3,2,1,0:T(4,128)} custom-call(s32[10]{0:T(128)S(1)} %stack.43.refs_0_.start_ref, f32[32,1,1280]{2,1,0:T(1,128)S(1)} %all-to-all-done.refs_1_, bf16[128,1024]{1,0:T(8,128)(2,1)} %collective-permute-done.2.refs_2_, bf16[128,1024]{1,0:T(8,128)(2,1)S(1)} %collective-permute-done.7.refs_3_, ...), custom_call_target="tpu_custom_call" | custom-call | flops 2415919104 | bytes 4718592 | tf_op jit(solution)/shard_map/pallas_call | solution.py:211
  73.1 4.9 %all-to-all-start.1 = ((f32[32,3,128]{2,1,0:T(4,128)}), f32[32,3,128]{2,1,0:T(4,128)S(1)}, u32[]{:S(2)}, u32[]{:S(2)}) async-start(f32[32,3,128]{2,1,0:T(4,128)} %bitcast.13), calls=%async_computation.1 | async-start | bytes 131072 | tf_op jit(solution)/shard_map/all_to_all | solution.py:312
  78.6 6.7 %all-to-all-done.1 = f32[32,3,128]{2,1,0:T(4,128)S(1)} async-done(((f32[32,3,128]{2,1,0:T(4,128)}), f32[32,3,128]{2,1,0:T(4,128)S(1)}, u32[]{:S(2)}, u32[]{:S(2)}) %all-to-all-start.1) | async-done | bytes 49184 | tf_op jit(solution)/shard_map/all_to_all | solution.py:312
  85.3 0.1 slice_reduce_fusion
  85.5 0.5 compare_select_fusion
  (25 shorter events, 0.1 us)
Async XLA Ops:
  0.6 9.9 %collective-permute-start = (bf16[128,1024]{1,0:T(8,128)(2,1)}, bf16[128,1024]{1,0:T(8,128)(2,1)S(1)}, u32[]{:S(2)}, u32[]{:S(2)}) collective-permute-start(bf16[128,1024]{1,0:T(8,128)(2,1)} %refs_2_.1), channel_id=1, source_target_pairs={{0,8},{1,17},{2,10},{3,19},{4,12},{5,21},{6,14},{7,23},{8,0},{9,25... | collective-permute-start | bytes 786440 | tf_op jit(solution)/shard_map/ppermute | solution.py:38
  3.6 6.9 %collective-permute-start.1 = (bf16[128,1024]{1,0:T(8,128)(2,1)}, bf16[128,1024]{1,0:T(8,128)(2,1)S(1)}, u32[]{:S(2)}, u32[]{:S(2)}) collective-permute-start(bf16[128,1024]{1,0:T(8,128)(2,1)} %refs_2_.1), channel_id=1, source_target_pairs={{0,16},{1,9},{2,18},{3,11},{4,20},{5,13},{6,22},{7,15},{8,24},{9,1... | collective-permute-start | bytes 786440 | tf_op jit(solution)/shard_map/ppermute | solution.py:38
  5.2 14.6 %collective-permute-start.3 = (bf16[128,1024]{1,0:T(8,128)(2,1)}, bf16[128,1024]{1,0:T(8,128)(2,1)S(1)}, u32[]{:S(2)}, u32[]{:S(2)}) collective-permute-start(bf16[128,1024]{1,0:T(8,128)(2,1)} %refs_2_.1), channel_id=1, source_target_pairs={{0,2},{1,3},{2,4},{3,5},{4,6},{5,7},{6,0},{7,1},{8,10},{9,11},{10,... | collective-permute-start | bytes 786440 | tf_op jit(solution)/shard_map/ppermute | solution.py:38
  6.7 15.2 %collective-permute-start.14 = (bf16[128,1024]{1,0:T(8,128)(2,1)}, bf16[128,1024]{1,0:T(8,128)(2,1)S(1)}, u32[]{:S(2)}, u32[]{:S(2)}) collective-permute-start(bf16[128,1024]{1,0:T(8,128)(2,1)} %refs_2_.1), channel_id=1, source_target_pairs={{0,1},{1,0},{2,3},{3,2},{4,5},{5,4},{6,7},{7,6},{8,9},{9,8},{10,11... | collective-permute-start | bytes 786440 | tf_op jit(solution)/shard_map/ppermute | solution.py:38
  6.7 13.6 %collective-permute-start.4 = (bf16[128,1024]{1,0:T(8,128)(2,1)}, bf16[128,1024]{1,0:T(8,128)(2,1)S(1)}, u32[]{:S(2)}, u32[]{:S(2)}) collective-permute-start(bf16[128,1024]{1,0:T(8,128)(2,1)} %refs_2_.1), channel_id=1, source_target_pairs={{0,6},{1,7},{2,0},{3,1},{4,2},{5,3},{6,4},{7,5},{8,14},{9,15},{10,... | collective-permute-start | bytes 786440 | tf_op jit(solution)/shard_map/ppermute | solution.py:38
  10.5 12.8 %collective-permute-start.13 = (bf16[128,1024]{1,0:T(8,128)(2,1)S(1)}, bf16[128,1024]{1,0:T(8,128)(2,1)S(1)}, u32[]{:S(2)}, u32[]{:S(2)}) collective-permute-start(bf16[128,1024]{1,0:T(8,128)(2,1)S(1)} %collective-permute-done.refs_3_), channel_id=1, source_target_pairs={{0,16},{1,9},{2,18},{3,11},{4,20},{5,13},{6,22},{7,15},{8,24},{9,1... | collective-permute-start | bytes 786440 | tf_op jit(solution)/shard_map/ppermute | solution.py:38
  12.0 11.4 %collective-permute-start.15 = (bf16[128,1024]{1,0:T(8,128)(2,1)S(1)}, bf16[128,1024]{1,0:T(8,128)(2,1)}, u32[]{:S(2)}, u32[]{:S(2)}) collective-permute-start(bf16[128,1024]{1,0:T(8,128)(2,1)S(1)} %collective-permute-done.refs_3_), channel_id=1, source_target_pairs={{0,1},{1,0},{2,3},{3,2},{4,5},{5,4},{6,7},{7,6},{8,9},{9,8},{10,11... | collective-permute-start | bytes 786440 | tf_op jit(solution)/shard_map/ppermute | solution.py:38
  14.7 13.5 %all-to-all-start = ((f32[32,1,1280]{2,1,0:T(1,128)}), f32[32,1,1280]{2,1,0:T(1,128)S(1)}, u32[]{:S(2)}, u32[]{:S(2)}) async-start(f32[32,1,1280]{2,1,0:T(1,128)} %shard_map.77), calls=%async_computation | async-start | bytes 327680 | tf_op jit(solution)/shard_map/all_to_all | solution.py:285
  19.8 4.1 %collective-permute-start.16 = (bf16[128,1024]{1,0:T(8,128)(2,1)S(1)}, bf16[128,1024]{1,0:T(8,128)(2,1)S(1)}, u32[]{:S(2)}, u32[]{:S(2)}) collective-permute-start(bf16[128,1024]{1,0:T(8,128)(2,1)S(1)} %collective-permute-done.1.refs_4_), channel_id=1, source_target_pairs={{0,1},{1,0},{2,3},{3,2},{4,5},{5,4},{6,7},{7,6},{8,9},{9,8},{10,11... | collective-permute-start | bytes 786440 | tf_op jit(solution)/shard_map/ppermute | solution.py:38
  20.4 19.3 %collective-permute-start.5 = (bf16[256,1024]{1,0:T(8,128)(2,1)S(1)}, bf16[256,1024]{1,0:T(8,128)(2,1)S(1)}, u32[]{:S(2)}, u32[]{:S(2)}) collective-permute-start(bf16[256,1024]{1,0:T(8,128)(2,1)S(1)} %shard_map.78.refs_2_), channel_id=1, source_target_pairs={{0,8},{1,17},{2,10},{3,19},{4,12},{5,21},{6,14},{7,23},{8,0},{9,25... | collective-permute-start | bytes 1572872 | tf_op jit(solution)/shard_map/ppermute | solution.py:38
  21.9 17.8 %collective-permute-start.6 = (bf16[256,1024]{1,0:T(8,128)(2,1)S(1)}, bf16[256,1024]{1,0:T(8,128)(2,1)S(1)}, u32[]{:S(2)}, u32[]{:S(2)}) collective-permute-start(bf16[256,1024]{1,0:T(8,128)(2,1)S(1)} %shard_map.78.refs_2_), channel_id=1, source_target_pairs={{0,16},{1,9},{2,18},{3,11},{4,20},{5,13},{6,22},{7,15},{8,24},{9,1... | collective-permute-start | bytes 1572872 | tf_op jit(solution)/shard_map/ppermute | solution.py:38
  23.4 16.4 %collective-permute-start.18 = (bf16[256,1024]{1,0:T(8,128)(2,1)S(1)}, bf16[256,1024]{1,0:T(8,128)(2,1)S(1)}, u32[]{:S(2)}, u32[]{:S(2)}) collective-permute-start(bf16[256,1024]{1,0:T(8,128)(2,1)S(1)} %shard_map.78.refs_2_), channel_id=1, source_target_pairs={{0,1},{1,0},{2,3},{3,2},{4,5},{5,4},{6,7},{7,6},{8,9},{9,8},{10,11... | collective-permute-start | bytes 1572872 | tf_op jit(solution)/shard_map/ppermute | solution.py:38
  23.4 4.9 %collective-permute-start.17 = (bf16[128,1024]{1,0:T(8,128)(2,1)S(1)}, bf16[128,1024]{1,0:T(8,128)(2,1)}, u32[]{:S(2)}, u32[]{:S(2)}) collective-permute-start(bf16[128,1024]{1,0:T(8,128)(2,1)S(1)} %collective-permute-done.13.refs_5_), channel_id=1, source_target_pairs={{0,1},{1,0},{2,3},{3,2},{4,5},{5,4},{6,7},{7,6},{8,9},{9,8},{10,11... | collective-permute-start | bytes 786440 | tf_op jit(solution)/shard_map/ppermute | solution.py:38
  23.9 0.7 copy-start.1
  24.6 15.1 %collective-permute-start.2 = (bf16[128,1024]{1,0:T(8,128)(2,1)}, bf16[128,1024]{1,0:T(8,128)(2,1)}, u32[]{:S(2)}, u32[]{:S(2)}) collective-permute-start(bf16[128,1024]{1,0:T(8,128)(2,1)} %refs_2_.1), channel_id=1, source_target_pairs={{0,4},{1,5},{2,6},{3,7},{4,0},{5,1},{6,2},{7,3},{8,12},{9,13},{10,... | collective-permute-start | bytes 786440 | tf_op jit(solution)/shard_map/ppermute | solution.py:38
  28.3 1.0 %copy-start = (bf16[128,1024]{1,0:T(8,128)(2,1)S(1)}, bf16[128,1024]{1,0:T(8,128)(2,1)}, u32[]{:S(2)}) copy-start(bf16[128,1024]{1,0:T(8,128)(2,1)} %refs_2_.1) | copy-start | bytes 786436
  29.2 0.9 %copy-start.2 = (bf16[128,1024]{1,0:T(8,128)(2,1)S(1)}, bf16[128,1024]{1,0:T(8,128)(2,1)}, u32[]{:S(2)}) copy-start(bf16[128,1024]{1,0:T(8,128)(2,1)} %copy-done.1) | copy-start | bytes 786436
  39.7 14.1 %collective-permute-start.19 = (bf16[256,1024]{1,0:T(8,128)(2,1)S(1)}, bf16[256,1024]{1,0:T(8,128)(2,1)S(1)}, u32[]{:S(2)}, u32[]{:S(2)}) collective-permute-start(bf16[256,1024]{1,0:T(8,128)(2,1)S(1)} %collective-permute-done.5.refs_3_), channel_id=1, source_target_pairs={{0,16},{1,9},{2,18},{3,11},{4,20},{5,13},{6,22},{7,15},{8,24},{9,1... | collective-permute-start | bytes 1572872 | tf_op jit(solution)/shard_map/ppermute | solution.py:38
  40.4 9.5 %collective-permute-start.7 = (bf16[128,1024]{1,0:T(8,128)(2,1)}, bf16[128,1024]{1,0:T(8,128)(2,1)S(1)}, u32[]{:S(2)}, u32[]{:S(2)}) collective-permute-start(bf16[128,1024]{1,0:T(8,128)(2,1)} %collective-permute-done.2.refs_2_), channel_id=1, source_target_pairs={{0,8},{1,17},{2,10},{3,19},{4,12},{5,21},{6,14},{7,23},{8,0},{9,25... | collective-permute-start | bytes 786440 | tf_op jit(solution)/shard_map/ppermute | solution.py:38
  41.5 11.9 %collective-permute-start.8 = (bf16[128,1024]{1,0:T(8,128)(2,1)}, bf16[128,1024]{1,0:T(8,128)(2,1)S(1)}, u32[]{:S(2)}, u32[]{:S(2)}) collective-permute-start(bf16[128,1024]{1,0:T(8,128)(2,1)} %collective-permute-done.2.refs_2_), channel_id=1, source_target_pairs={{0,16},{1,9},{2,18},{3,11},{4,20},{5,13},{6,22},{7,15},{8,24},{9,1... | collective-permute-start | bytes 786440 | tf_op jit(solution)/shard_map/ppermute | solution.py:38
  53.3 2.7 %collective-permute-start.21 = (bf16[256,1024]{1,0:T(8,128)(2,1)S(1)}, bf16[256,1024]{1,0:T(8,128)(2,1)S(1)}, u32[]{:S(2)}, u32[]{:S(2)}) collective-permute-start(bf16[256,1024]{1,0:T(8,128)(2,1)S(1)} %collective-permute-done.6.refs_4_), channel_id=1, source_target_pairs={{0,1},{1,0},{2,3},{3,2},{4,5},{5,4},{6,7},{7,6},{8,9},{9,8},{10,11... | collective-permute-start | bytes 1572872 | tf_op jit(solution)/shard_map/ppermute | solution.py:38
  53.3 3.0 %collective-permute-start.20 = (bf16[256,1024]{1,0:T(8,128)(2,1)S(1)}, bf16[256,1024]{1,0:T(8,128)(2,1)S(1)}, u32[]{:S(2)}, u32[]{:S(2)}) collective-permute-start(bf16[256,1024]{1,0:T(8,128)(2,1)S(1)} %collective-permute-done.5.refs_3_), channel_id=1, source_target_pairs={{0,1},{1,0},{2,3},{3,2},{4,5},{5,4},{6,7},{7,6},{8,9},{9,8},{10,11... | collective-permute-start | bytes 1572872 | tf_op jit(solution)/shard_map/ppermute | solution.py:38
  53.9 3.3 %collective-permute-start.22 = (bf16[256,1024]{1,0:T(8,128)(2,1)S(1)}, bf16[256,1024]{1,0:T(8,128)(2,1)S(1)}, u32[]{:S(2)}, u32[]{:S(2)}) collective-permute-start(bf16[256,1024]{1,0:T(8,128)(2,1)S(1)} %collective-permute-done.19.refs_5_), channel_id=1, source_target_pairs={{0,1},{1,0},{2,3},{3,2},{4,5},{5,4},{6,7},{7,6},{8,9},{9,8},{10,11... | collective-permute-start | bytes 1572872 | tf_op jit(solution)/shard_map/ppermute | solution.py:38
  53.9 11.9 %collective-permute-start.10 = (bf16[128,1024]{1,0:T(8,128)(2,1)}, bf16[128,1024]{1,0:T(8,128)(2,1)S(1)}, u32[]{:S(2)}, u32[]{:S(2)}) collective-permute-start(bf16[128,1024]{1,0:T(8,128)(2,1)} %collective-permute-done.2.refs_2_), channel_id=1, source_target_pairs={{0,1},{1,0},{2,3},{3,2},{4,5},{5,4},{6,7},{7,6},{8,9},{9,8},{10,11... | collective-permute-start | bytes 786440 | tf_op jit(solution)/shard_map/ppermute | solution.py:38
  54.4 11.2 %collective-permute-start.9 = (bf16[128,1024]{1,0:T(8,128)(2,1)S(1)}, bf16[128,1024]{1,0:T(8,128)(2,1)S(1)}, u32[]{:S(2)}, u32[]{:S(2)}) collective-permute-start(bf16[128,1024]{1,0:T(8,128)(2,1)S(1)} %collective-permute-done.7.refs_3_), channel_id=1, source_target_pairs={{0,16},{1,9},{2,18},{3,11},{4,20},{5,13},{6,22},{7,15},{8,24},{9,1... | collective-permute-start | bytes 786440 | tf_op jit(solution)/shard_map/ppermute | solution.py:38
  56.0 9.8 %collective-permute-start.11 = (bf16[128,1024]{1,0:T(8,128)(2,1)S(1)}, bf16[128,1024]{1,0:T(8,128)(2,1)S(1)}, u32[]{:S(2)}, u32[]{:S(2)}) collective-permute-start(bf16[128,1024]{1,0:T(8,128)(2,1)S(1)} %collective-permute-done.7.refs_3_), channel_id=1, source_target_pairs={{0,1},{1,0},{2,3},{3,2},{4,5},{5,4},{6,7},{7,6},{8,9},{9,8},{10,11... | collective-permute-start | bytes 786440 | tf_op jit(solution)/shard_map/ppermute | solution.py:38
  56.4 9.4 %collective-permute-start.12 = (bf16[128,1024]{1,0:T(8,128)(2,1)S(1)}, bf16[128,1024]{1,0:T(8,128)(2,1)S(1)}, u32[]{:S(2)}, u32[]{:S(2)}) collective-permute-start(bf16[128,1024]{1,0:T(8,128)(2,1)S(1)} %collective-permute-done.8.refs_4_), channel_id=1, source_target_pairs={{0,1},{1,0},{2,3},{3,2},{4,5},{5,4},{6,7},{7,6},{8,9},{9,8},{10,11... | collective-permute-start | bytes 786440 | tf_op jit(solution)/shard_map/ppermute | solution.py:38
  65.5 19.9 %copy-start.3 = (f32[128]{0:T(128)S(1)}, f32[128]{0:T(128)}, u32[]{:S(2)}) copy-start(f32[128]{0:T(128)} %param.10) | copy-start | bytes 1540
  65.5 1.6 %collective-permute-start.23 = (bf16[128,1024]{1,0:T(8,128)(2,1)S(1)}, bf16[128,1024]{1,0:T(8,128)(2,1)S(1)}, u32[]{:S(2)}, u32[]{:S(2)}) collective-permute-start(bf16[128,1024]{1,0:T(8,128)(2,1)S(1)} %collective-permute-done.9.refs_5_), channel_id=1, source_target_pairs={{0,1},{1,0},{2,3},{3,2},{4,5},{5,4},{6,7},{7,6},{8,9},{9,8},{10,11... | collective-permute-start | bytes 786440 | tf_op jit(solution)/shard_map/ppermute | solution.py:38
  73.1 12.3 %all-to-all-start.1 = ((f32[32,3,128]{2,1,0:T(4,128)}), f32[32,3,128]{2,1,0:T(4,128)S(1)}, u32[]{:S(2)}, u32[]{:S(2)}) async-start(f32[32,3,128]{2,1,0:T(4,128)} %bitcast.13), calls=%async_computation.1 | async-start | bytes 131072 | tf_op jit(solution)/shard_map/all_to_all | solution.py:312

commit v7 on v6

--- a/solution.py
+++ b/solution.py
@@ -263,19 +263,19 @@
     plane, tensor = lax.axis_index("dp"), lax.axis_index("tensor")
     z_me, c_me = tensor // CORES, tensor % CORES
     owners = grid.owners(plane // grid.cols, plane % grid.cols, c_me)
-    groups = [[0]] + [[d, depth - d] for d in range(1, (depth + 1) // 2)] + [[depth // 2]]
+    rest = [depth - 1, *range(2, depth - 1)]
+    groups = [[0], [1]] + [rest[k : k + 2] for k in range(0, len(rest), 2)]
     place = [grid.sibling_spot(k) for k in range(n_dp)]
 
     layers = {0: hidden}
     reached = [grid.reach(hidden)]
-    before = []
-    for group in groups[1:]:
+    for at, group in enumerate(groups[1:], 1):
         for dz in group:
+            before = [layers[d] for d in groups[at - 1]] if at > 1 else []
             layers[dz] = grid.along(after(hidden, *before), dz)
-        before = list(reached[0].values()) if len(before) == 0 else [layers[dz] for dz in group]
     for group in groups[1:]:
         sources = [layers[dz] for dz in group]
-        sources[0] = after(sources[0], *reached[-1].values())
+        sources[0] = after(sources[0], *reached[0].values())
         reached.append(grid.reach(joined(sources) if len(sources) > 1 else sources[0]))
 
     vocab_cols = head.shape[1]
@@ -284,30 +284,21 @@
     packed = squares(after(hidden, starts), norm_gain[None, :], targets[None, :], n_dp * n_t)
     fine = lax.all_to_all(packed, ("dp", "tensor"), 0, 0, tiled=True)
 
-    acc, deep = None, CORES * feat
+    acc, deep, results = None, CORES * feat, []
     for at, group in enumerate(groups):
         final = at == len(groups) - 1
-        middle = at and not final
         offsets = [2 + n_dp + dz for dz in group]
-        own = grid.sibling(reached[at][0, 0])
-        held = [layers[dz] for dz in groups[at + 1]] + [own] if middle else []
-        spread = grid.fill(dict(reached[at]), *([acc] if at == 1 else []), *held)
-        if at == 0:
-            weights = [head]
-        elif at == 1:
-            for later in groups[1:]:
-                ready = after(head, acc, *(layers[dz] for dz in groups[2]))
-                weights.append(loaded(starts, [2 + n_dp + dz for dz in later], ready, deep))
-        following = [*reached[at + 1].values(), *weights[1:3]] if middle else []
-        others = [own] + [grid.sibling(after(a, *following)) for a in spread[1:-1]]
-        others.append(grid.sibling(after(spread[-1], *([acc] if final else following))))
+        spread = grid.fill(dict(reached[at]), *(results[at - 2 : at - 1] if at >= 2 else []))
+        weights, ready = head, []
+        if len(group) > 1:
+            weights = loaded(starts, offsets, after(head, *results[-1:]), deep)
+            ready = [weights]
+        others = [grid.sibling(a) for a in spread[:-1]] + [grid.sibling(after(spread[-1], *ready))]
         blocks = spread + others
         for layer, offset in enumerate(offsets):
-            done = layer == len(offsets) - 1
-            if middle and done:
-                blocks[0] = after(blocks[0], *reached[at + 1].values())
-            last = final and done
-            acc = layer_product(tok, n_t, starts, layer, offset, fine, blocks, place, weights[at], acc, last)
+            last = final and layer == len(offsets) - 1
+            acc = layer_product(tok, n_t, starts, layer, offset, fine, blocks, place, weights, acc, last)
+        results.append(acc)
 
     parts = lax.all_to_all(acc.reshape(n_dp * n_t, 3, tok), ("dp", "tensor"), 0, 0, tiled=True)
     top = jnp.max(parts[:, 0], axis=0)

time: 86.4 us -> 89.7 us (1.038)
  waiting for transfers between devices: 18.8 us -> 24.4 us
  starting transfers between devices: 32.5 us -> 31 us
    ppermute x24, waiting for transfers between devices: 10.7 us -> 15.3 us  [permute(): return lax.ppermute(a, ('dp', 'tensor'), perm)]
    ppermute x24, starting transfers between devices: 22.5 us -> 19.5 us  [permute(): return lax.ppermute(a, ('dp', 'tensor'), perm)]
    pallas_call x2 -> x1, Pallas kernels: 7.23 us -> 4.34 us  [loaded(): pl.pallas_call(functools.partial(load_kernel, offsets), out_shape=pltpu.V...]
    all_to_all x1, starting transfers between devices: 5.05 us -> 7.27 us  [body(): fine = lax.all_to_all(packed, ('dp', 'tensor'), 0, 0, tiled=True)]
    pallas_call x4, Pallas kernels: 21 us -> 23 us  [layer_product(): pl.pallas_call(functools.partial(layer_kernel, n, n_t, place, layer, offs...]
    all_to_all x1, waiting for transfers between devices: 1.27 us -> 2.32 us  [body(): fine = lax.all_to_all(packed, ('dp', 'tensor'), 0, 0, tiled=True)]
  transfers between devices with their start and end apart: 26 -> 26, of which waited for: 10 -> 12; matrix products, arithmetic and copies ran while one was open for 0% -> 0% of each run, Pallas kernels for 28% -> 22%
where the time goes in v7:
time: 89.7 us; the launch traced here: 89.2 us
  starting transfers between devices  31 us (35%)
  Pallas kernels  29.2 us (33%)
  waiting for transfers between devices  24.4 us (27%)
  local copies, waits for them, and re-layouts  2.68 us (3%)
  between operations  1.41 us (2%)
    pallas_call x4, Pallas kernels, layer_product(): pl.pallas_call(functools.partial(layer_kernel, n, n_t, place, layer, offs...  23 us
    ppermute x24, starting transfers between devices, permute(): return lax.ppermute(a, ('dp', 'tensor'), perm)  19.5 us
    ppermute x24, waiting for transfers between devices, permute(): return lax.ppermute(a, ('dp', 'tensor'), perm)  15.3 us
    all_to_all x1, starting transfers between devices, body(): fine = lax.all_to_all(packed, ('dp', 'tensor'), 0, 0, tiled=True)  7.27 us
    all_to_all x1, waiting for transfers between devices, body(): lax.all_to_all(acc.reshape(n_dp * n_t, 3, tok), ('dp', 'tensor'), 0, 0, t...  6.74 us
    pallas_call x1, Pallas kernels, loaded(): pl.pallas_call(functools.partial(load_kernel, offsets), out_shape=pltpu.V...  4.34 us
    all_to_all x1, starting transfers between devices, body(): lax.all_to_all(acc.reshape(n_dp * n_t, 3, tok), ('dp', 'tensor'), 0, 0, t...  4.25 us
    unnamed x8, local copies, waits for them, and re-layouts  2.6 us
  transfers between devices with their start and end apart: 26, of which 12 were waited for; matrix products, arithmetic and copies ran while one was open for 0% of the time, Pallas kernels for 22%

profile of v7, /device:TPU:0, one launch (start us, length us, event | category | flops | bytes accessed | tf_op | source)
XLA Modules:
  0.0 89.2 jit_solution(4907236502073074828)
XLA Ops:
  0.6 3.1 %collective-permute-start = (bf16[128,1024]{1,0:T(8,128)(2,1)}, bf16[128,1024]{1,0:T(8,128)(2,1)S(1)}, u32[]{:S(2)}, u32[]{:S(2)}) collective-permute-start(bf16[128,1024]{1,0:T(8,128)(2,1)} %refs_2_.1), channel_id=1, source_target_pairs={{0,2},{1,3},{2,4},{3,5},{4,6},{5,7},{6,0},{7,1},{8,10},{9,11},{10,... | collective-permute-start | bytes 786440 | tf_op jit(solution)/shard_map/ppermute | solution.py:38
  3.7 1.5 %collective-permute-start.2 = (bf16[128,1024]{1,0:T(8,128)(2,1)}, bf16[128,1024]{1,0:T(8,128)(2,1)S(1)}, u32[]{:S(2)}, u32[]{:S(2)}) collective-permute-start(bf16[128,1024]{1,0:T(8,128)(2,1)} %refs_2_.1), channel_id=1, source_target_pairs={{0,8},{1,17},{2,10},{3,19},{4,12},{5,21},{6,14},{7,23},{8,0},{9,25... | collective-permute-start | bytes 786440 | tf_op jit(solution)/shard_map/ppermute | solution.py:38
  5.2 1.5 %collective-permute-start.3 = (bf16[128,1024]{1,0:T(8,128)(2,1)}, bf16[128,1024]{1,0:T(8,128)(2,1)S(1)}, u32[]{:S(2)}, u32[]{:S(2)}) collective-permute-start(bf16[128,1024]{1,0:T(8,128)(2,1)} %refs_2_.1), channel_id=1, source_target_pairs={{0,16},{1,9},{2,18},{3,11},{4,20},{5,13},{6,22},{7,15},{8,24},{9,1... | collective-permute-start | bytes 786440 | tf_op jit(solution)/shard_map/ppermute | solution.py:38
  6.7 5.5 %collective-permute-done.refs_2_ = bf16[128,1024]{1,0:T(8,128)(2,1)S(1)} collective-permute-done((bf16[128,1024]{1,0:T(8,128)(2,1)}, bf16[128,1024]{1,0:T(8,128)(2,1)S(1)}, u32[]{:S(2)}, u32[]{:S(2)}) %collective-permute-start) | collective-permute-done | bytes 262176 | tf_op jit(solution)/shard_map/ppermute | solution.py:38
  12.2 1.7 %collective-permute-start.1 = (bf16[128,1024]{1,0:T(8,128)(2,1)}, bf16[128,1024]{1,0:T(8,128)(2,1)S(1)}, u32[]{:S(2)}, u32[]{:S(2)}) collective-permute-start(bf16[128,1024]{1,0:T(8,128)(2,1)} %refs_2_.1), channel_id=1, source_target_pairs={{0,6},{1,7},{2,0},{3,1},{4,2},{5,3},{6,4},{7,5},{8,14},{9,15},{10,... | collective-permute-start | bytes 786440 | tf_op jit(solution)/shard_map/ppermute | solution.py:38
  14.0 0.0 collective-permute-start.4
  14.0 1.6 %collective-permute-start.7 = (bf16[128,1024]{1,0:T(8,128)(2,1)S(1)}, bf16[128,1024]{1,0:T(8,128)(2,1)}, u32[]{:S(2)}, u32[]{:S(2)}) collective-permute-start(bf16[128,1024]{1,0:T(8,128)(2,1)S(1)} %collective-permute-done.2.refs_3_), channel_id=1, source_target_pairs={{0,16},{1,9},{2,18},{3,11},{4,20},{5,13},{6,22},{7,15},{8,24},{9,1... | collective-permute-start | bytes 786440 | tf_op jit(solution)/shard_map/ppermute | solution.py:38
  15.6 1.5 %collective-permute-start.16 = (bf16[128,1024]{1,0:T(8,128)(2,1)S(1)}, bf16[128,1024]{1,0:T(8,128)(2,1)S(1)}, u32[]{:S(2)}, u32[]{:S(2)}) collective-permute-start(bf16[128,1024]{1,0:T(8,128)(2,1)S(1)} %collective-permute-done.refs_2_), channel_id=1, source_target_pairs={{0,8},{1,17},{2,10},{3,19},{4,12},{5,21},{6,14},{7,23},{8,0},{9,25... | collective-permute-start | bytes 786440 | tf_op jit(solution)/shard_map/ppermute | solution.py:38
  17.1 4.3 %collective-permute-done.1.refs_0_ = bf16[128,1024]{1,0:T(8,128)(2,1)S(1)} collective-permute-done((bf16[128,1024]{1,0:T(8,128)(2,1)}, bf16[128,1024]{1,0:T(8,128)(2,1)S(1)}, u32[]{:S(2)}, u32[]{:S(2)}) %collective-permute-start.1) | collective-permute-done | bytes 262176 | tf_op jit(solution)/shard_map/ppermute | solution.py:38
  21.4 1.2 %collective-permute-start.17 = (bf16[128,1024]{1,0:T(8,128)(2,1)S(1)}, bf16[128,1024]{1,0:T(8,128)(2,1)S(1)}, u32[]{:S(2)}, u32[]{:S(2)}) collective-permute-start(bf16[128,1024]{1,0:T(8,128)(2,1)S(1)} %collective-permute-done.refs_2_), channel_id=1, source_target_pairs={{0,16},{1,9},{2,18},{3,11},{4,20},{5,13},{6,22},{7,15},{8,24},{9,1... | collective-permute-start | bytes 786440 | tf_op jit(solution)/shard_map/ppermute | solution.py:38
  22.6 0.1 stack.43.refs_0_.start_ref
  22.7 1.8 %shard_map.77 = f32[32,1,1280]{2,1,0:T(1,128)} custom-call(bf16[128,1024]{1,0:T(8,128)(2,1)} %refs_2_.1, f32[1,1024]{1,0:T(1,128)} %bitcast.22, s32[1,128]{1,0:T(1,128)} %bitcast.23), custom_call_target="tpu_custom_call" | custom-call | tf_op jit(solution)/shard_map/pallas_call | solution.py:243
  24.5 7.3 %all-to-all-start = ((f32[32,1,1280]{2,1,0:T(1,128)}), f32[32,1,1280]{2,1,0:T(1,128)S(1)}, u32[]{:S(2)}, u32[]{:S(2)}) async-start(f32[32,1,1280]{2,1,0:T(1,128)} %shard_map.77), calls=%async_computation | async-start | bytes 327680 | tf_op jit(solution)/shard_map/all_to_all | solution.py:285
  31.8 1.8 %collective-permute-start.5 = (bf16[256,1024]{1,0:T(8,128)(2,1)S(1)}, bf16[256,1024]{1,0:T(8,128)(2,1)S(1)}, u32[]{:S(2)}, u32[]{:S(2)}) collective-permute-start(bf16[256,1024]{1,0:T(8,128)(2,1)S(1)} %shard_map.78.refs_2_), channel_id=1, source_target_pairs={{0,8},{1,17},{2,10},{3,19},{4,12},{5,21},{6,14},{7,23},{8,0},{9,25... | collective-permute-start | bytes 1572872 | tf_op jit(solution)/shard_map/ppermute | solution.py:38
  33.6 1.5 %collective-permute-start.6 = (bf16[256,1024]{1,0:T(8,128)(2,1)S(1)}, bf16[256,1024]{1,0:T(8,128)(2,1)S(1)}, u32[]{:S(2)}, u32[]{:S(2)}) collective-permute-start(bf16[256,1024]{1,0:T(8,128)(2,1)S(1)} %shard_map.78.refs_2_), channel_id=1, source_target_pairs={{0,16},{1,9},{2,18},{3,11},{4,20},{5,13},{6,22},{7,15},{8,24},{9,1... | collective-permute-start | bytes 1572872 | tf_op jit(solution)/shard_map/ppermute | solution.py:38
  35.1 0.5 collective-permute-start.9
  35.6 0.1 collective-permute-start.11
  35.7 0.9 %collective-permute-done.10.refs_8_ = bf16[128,1024]{1,0:T(8,128)(2,1)S(1)} collective-permute-done((bf16[128,1024]{1,0:T(8,128)(2,1)S(1)}, bf16[128,1024]{1,0:T(8,128)(2,1)S(1)}, u32[]{:S(2)}, u32[]{:S(2)}) %collective-permute-start.10) | collective-permute-done | bytes 262176 | tf_op jit(solution)/shard_map/ppermute | solution.py:38
  36.7 0.7 copy-done.1
  37.3 0.6 collective-permute-start.18
  37.9 2.3 %all-to-all-done.refs_1_ = f32[32,1,1280]{2,1,0:T(1,128)S(1)} async-done(((f32[32,1,1280]{2,1,0:T(1,128)}), f32[32,1,1280]{2,1,0:T(1,128)S(1)}, u32[]{:S(2)}, u32[]{:S(2)}) %all-to-all-start) | async-done | bytes 163872 | tf_op jit(solution)/shard_map/all_to_all | solution.py:285
  40.2 0.9 %copy-done = bf16[128,1024]{1,0:T(8,128)(2,1)S(1)} copy-done((bf16[128,1024]{1,0:T(8,128)(2,1)S(1)}, bf16[128,1024]{1,0:T(8,128)(2,1)}, u32[]{:S(2)}) %copy-start) | copy-done | bytes 262168
  41.2 0.9 %copy-done.2 = bf16[128,1024]{1,0:T(8,128)(2,1)S(1)} copy-done((bf16[128,1024]{1,0:T(8,128)(2,1)S(1)}, bf16[128,1024]{1,0:T(8,128)(2,1)}, u32[]{:S(2)}) %copy-start.2) | copy-done | bytes 262168
  42.1 6.8 %shard_map.79.refs_11_ = f32[512,1152]{1,0:T(8,128)S(1)} custom-call(s32[10]{0:T(128)S(1)} %stack.43.refs_0_.start_ref, f32[32,1,1280]{2,1,0:T(1,128)S(1)} %all-to-all-done.refs_1_, bf16[128,1024]{1,0:T(8,128)(2,1)S(1)} %copy-done, bf16[128,1024]{1,0:T(8,128)(2,1)S(1)} %collective-permute-done.2.refs_3_, ...), custom_call_target="tpu_custom_call" | custom-call | flops 2415919104 | bytes 4718592 | tf_op jit(solution)/shard_map/pallas_call | solution.py:211
  48.9 1.1 %collective-permute-start.12 = (bf16[256,1024]{1,0:T(8,128)(2,1)S(1)}, bf16[256,1024]{1,0:T(8,128)(2,1)S(1)}, u32[]{:S(2)}, u32[]{:S(2)}) collective-permute-start(bf16[256,1024]{1,0:T(8,128)(2,1)S(1)} %collective-permute-done.5.refs_3_), channel_id=1, source_target_pairs={{0,16},{1,9},{2,18},{3,11},{4,20},{5,13},{6,22},{7,15},{8,24},{9,1... | collective-permute-start | bytes 1572872 | tf_op jit(solution)/shard_map/ppermute | solution.py:38
  50.0 0.5 collective-permute-start.20
  50.5 0.0 collective-permute-done.18.refs_5_
  50.6 0.5 collective-permute-start.22
  51.0 0.5 collective-permute-done.19.refs_6_
  51.6 0.1 collective-permute-start.13
  51.7 0.2 collective-permute-done.20.refs_7_
  51.9 0.7 collective-permute-done.21.refs_8_
  52.7 0.2 collective-permute-done.22.refs_9_
  52.9 6.5 %shard_map.80.refs_11_ = f32[512,1152]{1,0:T(8,128)S(1)} custom-call(s32[10]{0:T(128)S(1)} %stack.43.refs_0_.start_ref, f32[32,1,1280]{2,1,0:T(1,128)S(1)} %all-to-all-done.refs_1_, bf16[128,1024]{1,0:T(8,128)(2,1)S(1)} %collective-permute-done.refs_2_, bf16[128,1024]{1,0:T(8,128)(2,1)S(1)} %collective-permute-done.16.refs_3_, ...), custom_call_target="tpu_custom_call" | custom-call | flops 2415919104 | bytes 4718592 | tf_op jit(solution)/shard_map/pallas_call | solution.py:211
  59.4 4.3 %shard_map.81.refs_10_ = bf16[2,2048,1152]{2,1,0:T(8,128)(2,1)S(1)} custom-call(s32[10]{0:T(128)S(1)} %stack.43.refs_0_.start_ref, bf16[8192,1152]{1,0:T(8,128)(2,1)} %head_ref), custom_call_target="tpu_custom_call" | custom-call | tf_op jit(solution)/shard_map/pallas_call | solution.py:116
  63.8 0.2 collective-permute-start.14
  64.0 0.4 collective-permute-start.15
  64.3 0.1 collective-permute-start.23
  64.5 1.3 %collective-permute-done.14.refs_7_ = bf16[256,1024]{1,0:T(8,128)(2,1)S(1)} collective-permute-done((bf16[256,1024]{1,0:T(8,128)(2,1)S(1)}, bf16[256,1024]{1,0:T(8,128)(2,1)S(1)}, u32[]{:S(2)}, u32[]{:S(2)}) %collective-permute-start.14) | collective-permute-done | bytes 524320 | tf_op jit(solution)/shard_map/ppermute | solution.py:38
  65.7 0.7 collective-permute-done.15.refs_8_
  66.5 0.7 collective-permute-done.23.refs_9_
  67.2 4.2 %shard_map.82.refs_11_ = f32[512,1152]{1,0:T(8,128)S(1)} custom-call(s32[10]{0:T(128)S(1)} %stack.43.refs_0_.start_ref, f32[32,1,1280]{2,1,0:T(1,128)S(1)} %all-to-all-done.refs_1_, bf16[256,1024]{1,0:T(8,128)(2,1)S(1)} %shard_map.78.refs_2_, bf16[256,1024]{1,0:T(8,128)(2,1)S(1)} %collective-permute-done.5.refs_3_, ...), custom_call_target="tpu_custom_call" | custom-call | flops 2415919104 | bytes 4718592 | tf_op jit(solution)/shard_map/pallas_call | solution.py:211
  71.4 0.0 copy-start.3
  71.5 5.5 %shard_map.83 = f32[4,8,3,128]{3,2,1,0:T(4,128)} custom-call(s32[10]{0:T(128)S(1)} %stack.43.refs_0_.start_ref, f32[32,1,1280]{2,1,0:T(1,128)S(1)} %all-to-all-done.refs_1_, bf16[256,1024]{1,0:T(8,128)(2,1)S(1)} %shard_map.78.refs_2_, bf16[256,1024]{1,0:T(8,128)(2,1)S(1)} %collective-permute-done.5.refs_3_, ...), custom_call_target="tpu_custom_call" | custom-call | flops 2415919104 | bytes 4718592 | tf_op jit(solution)/shard_map/pallas_call | solution.py:211
  77.0 4.2 %all-to-all-start.1 = ((f32[32,3,128]{2,1,0:T(4,128)}), f32[32,3,128]{2,1,0:T(4,128)S(1)}, u32[]{:S(2)}, u32[]{:S(2)}) async-start(f32[32,3,128]{2,1,0:T(4,128)} %bitcast.13), calls=%async_computation.1 | async-start | bytes 131072 | tf_op jit(solution)/shard_map/all_to_all | solution.py:303
  81.9 6.7 %all-to-all-done.1 = f32[32,3,128]{2,1,0:T(4,128)S(1)} async-done(((f32[32,3,128]{2,1,0:T(4,128)}), f32[32,3,128]{2,1,0:T(4,128)S(1)}, u32[]{:S(2)}, u32[]{:S(2)}) %all-to-all-start.1) | async-done | bytes 49184 | tf_op jit(solution)/shard_map/all_to_all | solution.py:303
  88.6 0.1 slice_reduce_fusion
  88.7 0.5 compare_select_fusion
  (24 shorter events, 0.1 us)
Async XLA Ops:
  0.6 11.6 %collective-permute-start = (bf16[128,1024]{1,0:T(8,128)(2,1)}, bf16[128,1024]{1,0:T(8,128)(2,1)S(1)}, u32[]{:S(2)}, u32[]{:S(2)}) collective-permute-start(bf16[128,1024]{1,0:T(8,128)(2,1)} %refs_2_.1), channel_id=1, source_target_pairs={{0,2},{1,3},{2,4},{3,5},{4,6},{5,7},{6,0},{7,1},{8,10},{9,11},{10,... | collective-permute-start | bytes 786440 | tf_op jit(solution)/shard_map/ppermute | solution.py:38
  3.7 10.3 %collective-permute-start.2 = (bf16[128,1024]{1,0:T(8,128)(2,1)}, bf16[128,1024]{1,0:T(8,128)(2,1)S(1)}, u32[]{:S(2)}, u32[]{:S(2)}) collective-permute-start(bf16[128,1024]{1,0:T(8,128)(2,1)} %refs_2_.1), channel_id=1, source_target_pairs={{0,8},{1,17},{2,10},{3,19},{4,12},{5,21},{6,14},{7,23},{8,0},{9,25... | collective-permute-start | bytes 786440 | tf_op jit(solution)/shard_map/ppermute | solution.py:38
  5.2 8.8 %collective-permute-start.3 = (bf16[128,1024]{1,0:T(8,128)(2,1)}, bf16[128,1024]{1,0:T(8,128)(2,1)S(1)}, u32[]{:S(2)}, u32[]{:S(2)}) collective-permute-start(bf16[128,1024]{1,0:T(8,128)(2,1)} %refs_2_.1), channel_id=1, source_target_pairs={{0,16},{1,9},{2,18},{3,11},{4,20},{5,13},{6,22},{7,15},{8,24},{9,1... | collective-permute-start | bytes 786440 | tf_op jit(solution)/shard_map/ppermute | solution.py:38
  12.2 9.1 %collective-permute-start.1 = (bf16[128,1024]{1,0:T(8,128)(2,1)}, bf16[128,1024]{1,0:T(8,128)(2,1)S(1)}, u32[]{:S(2)}, u32[]{:S(2)}) collective-permute-start(bf16[128,1024]{1,0:T(8,128)(2,1)} %refs_2_.1), channel_id=1, source_target_pairs={{0,6},{1,7},{2,0},{3,1},{4,2},{5,3},{6,4},{7,5},{8,14},{9,15},{10,... | collective-permute-start | bytes 786440 | tf_op jit(solution)/shard_map/ppermute | solution.py:38
  14.0 17.8 %collective-permute-start.4 = (bf16[128,1024]{1,0:T(8,128)(2,1)}, bf16[128,1024]{1,0:T(8,128)(2,1)S(1)}, u32[]{:S(2)}, u32[]{:S(2)}) collective-permute-start(bf16[128,1024]{1,0:T(8,128)(2,1)} %refs_2_.1), channel_id=1, source_target_pairs={{0,4},{1,5},{2,6},{3,7},{4,0},{5,1},{6,2},{7,3},{8,12},{9,13},{10,... | collective-permute-start | bytes 786440 | tf_op jit(solution)/shard_map/ppermute | solution.py:38
  14.0 19.7 %collective-permute-start.8 = (bf16[128,1024]{1,0:T(8,128)(2,1)}, bf16[128,1024]{1,0:T(8,128)(2,1)S(1)}, u32[]{:S(2)}, u32[]{:S(2)}) collective-permute-start(bf16[128,1024]{1,0:T(8,128)(2,1)} %refs_2_.1), channel_id=1, source_target_pairs={{0,1},{1,0},{2,3},{3,2},{4,5},{5,4},{6,7},{7,6},{8,9},{9,8},{10,11... | collective-permute-start | bytes 786440 | tf_op jit(solution)/shard_map/ppermute | solution.py:38
  14.0 21.1 %collective-permute-start.7 = (bf16[128,1024]{1,0:T(8,128)(2,1)S(1)}, bf16[128,1024]{1,0:T(8,128)(2,1)}, u32[]{:S(2)}, u32[]{:S(2)}) collective-permute-start(bf16[128,1024]{1,0:T(8,128)(2,1)S(1)} %collective-permute-done.2.refs_3_), channel_id=1, source_target_pairs={{0,16},{1,9},{2,18},{3,11},{4,20},{5,13},{6,22},{7,15},{8,24},{9,1... | collective-permute-start | bytes 786440 | tf_op jit(solution)/shard_map/ppermute | solution.py:38
  15.6 19.5 %collective-permute-start.16 = (bf16[128,1024]{1,0:T(8,128)(2,1)S(1)}, bf16[128,1024]{1,0:T(8,128)(2,1)S(1)}, u32[]{:S(2)}, u32[]{:S(2)}) collective-permute-start(bf16[128,1024]{1,0:T(8,128)(2,1)S(1)} %collective-permute-done.refs_2_), channel_id=1, source_target_pairs={{0,8},{1,17},{2,10},{3,19},{4,12},{5,21},{6,14},{7,23},{8,0},{9,25... | collective-permute-start | bytes 786440 | tf_op jit(solution)/shard_map/ppermute | solution.py:38
  21.4 14.3 %collective-permute-start.17 = (bf16[128,1024]{1,0:T(8,128)(2,1)S(1)}, bf16[128,1024]{1,0:T(8,128)(2,1)S(1)}, u32[]{:S(2)}, u32[]{:S(2)}) collective-permute-start(bf16[128,1024]{1,0:T(8,128)(2,1)S(1)} %collective-permute-done.refs_2_), channel_id=1, source_target_pairs={{0,16},{1,9},{2,18},{3,11},{4,20},{5,13},{6,22},{7,15},{8,24},{9,1... | collective-permute-start | bytes 786440 | tf_op jit(solution)/shard_map/ppermute | solution.py:38
  24.5 15.8 %all-to-all-start = ((f32[32,1,1280]{2,1,0:T(1,128)}), f32[32,1,1280]{2,1,0:T(1,128)S(1)}, u32[]{:S(2)}, u32[]{:S(2)}) async-start(f32[32,1,1280]{2,1,0:T(1,128)} %shard_map.77), calls=%async_computation | async-start | bytes 327680 | tf_op jit(solution)/shard_map/all_to_all | solution.py:285
  31.8 17.1 %collective-permute-start.5 = (bf16[256,1024]{1,0:T(8,128)(2,1)S(1)}, bf16[256,1024]{1,0:T(8,128)(2,1)S(1)}, u32[]{:S(2)}, u32[]{:S(2)}) collective-permute-start(bf16[256,1024]{1,0:T(8,128)(2,1)S(1)} %shard_map.78.refs_2_), channel_id=1, source_target_pairs={{0,8},{1,17},{2,10},{3,19},{4,12},{5,21},{6,14},{7,23},{8,0},{9,25... | collective-permute-start | bytes 1572872 | tf_op jit(solution)/shard_map/ppermute | solution.py:38
  33.6 15.3 %collective-permute-start.6 = (bf16[256,1024]{1,0:T(8,128)(2,1)S(1)}, bf16[256,1024]{1,0:T(8,128)(2,1)S(1)}, u32[]{:S(2)}, u32[]{:S(2)}) collective-permute-start(bf16[256,1024]{1,0:T(8,128)(2,1)S(1)} %shard_map.78.refs_2_), channel_id=1, source_target_pairs={{0,16},{1,9},{2,18},{3,11},{4,20},{5,13},{6,22},{7,15},{8,24},{9,1... | collective-permute-start | bytes 1572872 | tf_op jit(solution)/shard_map/ppermute | solution.py:38
  35.1 1.5 %collective-permute-start.10 = (bf16[128,1024]{1,0:T(8,128)(2,1)S(1)}, bf16[128,1024]{1,0:T(8,128)(2,1)S(1)}, u32[]{:S(2)}, u32[]{:S(2)}) collective-permute-start(bf16[128,1024]{1,0:T(8,128)(2,1)S(1)} %collective-permute-done.3.refs_4_), channel_id=1, source_target_pairs={{0,1},{1,0},{2,3},{3,2},{4,5},{5,4},{6,7},{7,6},{8,9},{9,8},{10,11... | collective-permute-start | bytes 786440 | tf_op jit(solution)/shard_map/ppermute | solution.py:38
  35.1 5.1 %collective-permute-start.9 = (bf16[128,1024]{1,0:T(8,128)(2,1)S(1)}, bf16[128,1024]{1,0:T(8,128)(2,1)}, u32[]{:S(2)}, u32[]{:S(2)}) collective-permute-start(bf16[128,1024]{1,0:T(8,128)(2,1)S(1)} %collective-permute-done.2.refs_3_), channel_id=1, source_target_pairs={{0,1},{1,0},{2,3},{3,2},{4,5},{5,4},{6,7},{7,6},{8,9},{9,8},{10,11... | collective-permute-start | bytes 786440 | tf_op jit(solution)/shard_map/ppermute | solution.py:38
  35.6 4.6 %collective-permute-start.11 = (bf16[128,1024]{1,0:T(8,128)(2,1)}, bf16[128,1024]{1,0:T(8,128)(2,1)}, u32[]{:S(2)}, u32[]{:S(2)}) collective-permute-start(bf16[128,1024]{1,0:T(8,128)(2,1)} %collective-permute-done.7.refs_5_), channel_id=1, source_target_pairs={{0,1},{1,0},{2,3},{3,2},{4,5},{5,4},{6,7},{7,6},{8,9},{9,8},{10,11... | collective-permute-start | bytes 786440 | tf_op jit(solution)/shard_map/ppermute | solution.py:38
  36.6 0.7 copy-start.1
  37.3 13.2 %collective-permute-start.18 = (bf16[128,1024]{1,0:T(8,128)(2,1)S(1)}, bf16[128,1024]{1,0:T(8,128)(2,1)}, u32[]{:S(2)}, u32[]{:S(2)}) collective-permute-start(bf16[128,1024]{1,0:T(8,128)(2,1)S(1)} %collective-permute-done.16.refs_3_), channel_id=1, source_target_pairs={{0,16},{1,9},{2,18},{3,11},{4,20},{5,13},{6,22},{7,15},{8,24},{9,1... | collective-permute-start | bytes 786440 | tf_op jit(solution)/shard_map/ppermute | solution.py:38
  40.2 1.0 %copy-start = (bf16[128,1024]{1,0:T(8,128)(2,1)S(1)}, bf16[128,1024]{1,0:T(8,128)(2,1)}, u32[]{:S(2)}) copy-start(bf16[128,1024]{1,0:T(8,128)(2,1)} %refs_2_.1) | copy-start | bytes 786436
  41.2 0.9 %copy-start.2 = (bf16[128,1024]{1,0:T(8,128)(2,1)S(1)}, bf16[128,1024]{1,0:T(8,128)(2,1)}, u32[]{:S(2)}) copy-start(bf16[128,1024]{1,0:T(8,128)(2,1)} %copy-done.1) | copy-start | bytes 786436
  48.9 15.4 %collective-permute-start.12 = (bf16[256,1024]{1,0:T(8,128)(2,1)S(1)}, bf16[256,1024]{1,0:T(8,128)(2,1)S(1)}, u32[]{:S(2)}, u32[]{:S(2)}) collective-permute-start(bf16[256,1024]{1,0:T(8,128)(2,1)S(1)} %collective-permute-done.5.refs_3_), channel_id=1, source_target_pairs={{0,16},{1,9},{2,18},{3,11},{4,20},{5,13},{6,22},{7,15},{8,24},{9,1... | collective-permute-start | bytes 1572872 | tf_op jit(solution)/shard_map/ppermute | solution.py:38
  50.0 1.5 %collective-permute-start.19 = (bf16[128,1024]{1,0:T(8,128)(2,1)S(1)}, bf16[128,1024]{1,0:T(8,128)(2,1)S(1)}, u32[]{:S(2)}, u32[]{:S(2)}) collective-permute-start(bf16[128,1024]{1,0:T(8,128)(2,1)S(1)} %collective-permute-done.refs_2_), channel_id=1, source_target_pairs={{0,1},{1,0},{2,3},{3,2},{4,5},{5,4},{6,7},{7,6},{8,9},{9,8},{10,11... | collective-permute-start | bytes 786440 | tf_op jit(solution)/shard_map/ppermute | solution.py:38
  50.0 1.9 %collective-permute-start.20 = (bf16[128,1024]{1,0:T(8,128)(2,1)S(1)}, bf16[128,1024]{1,0:T(8,128)(2,1)S(1)}, u32[]{:S(2)}, u32[]{:S(2)}) collective-permute-start(bf16[128,1024]{1,0:T(8,128)(2,1)S(1)} %collective-permute-done.16.refs_3_), channel_id=1, source_target_pairs={{0,1},{1,0},{2,3},{3,2},{4,5},{5,4},{6,7},{7,6},{8,9},{9,8},{10,11... | collective-permute-start | bytes 786440 | tf_op jit(solution)/shard_map/ppermute | solution.py:38
  50.5 2.1 %collective-permute-start.21 = (bf16[128,1024]{1,0:T(8,128)(2,1)S(1)}, bf16[128,1024]{1,0:T(8,128)(2,1)S(1)}, u32[]{:S(2)}, u32[]{:S(2)}) collective-permute-start(bf16[128,1024]{1,0:T(8,128)(2,1)S(1)} %collective-permute-done.17.refs_4_), channel_id=1, source_target_pairs={{0,1},{1,0},{2,3},{3,2},{4,5},{5,4},{6,7},{7,6},{8,9},{9,8},{10,11... | collective-permute-start | bytes 786440 | tf_op jit(solution)/shard_map/ppermute | solution.py:38
  50.6 2.3 %collective-permute-start.22 = (bf16[128,1024]{1,0:T(8,128)(2,1)}, bf16[128,1024]{1,0:T(8,128)(2,1)S(1)}, u32[]{:S(2)}, u32[]{:S(2)}) collective-permute-start(bf16[128,1024]{1,0:T(8,128)(2,1)} %collective-permute-done.18.refs_5_), channel_id=1, source_target_pairs={{0,1},{1,0},{2,3},{3,2},{4,5},{5,4},{6,7},{7,6},{8,9},{9,8},{10,11... | collective-permute-start | bytes 786440 | tf_op jit(solution)/shard_map/ppermute | solution.py:38
  51.6 12.9 %collective-permute-start.13 = (bf16[256,1024]{1,0:T(8,128)(2,1)S(1)}, bf16[256,1024]{1,0:T(8,128)(2,1)S(1)}, u32[]{:S(2)}, u32[]{:S(2)}) collective-permute-start(bf16[256,1024]{1,0:T(8,128)(2,1)S(1)} %shard_map.78.refs_2_), channel_id=1, source_target_pairs={{0,1},{1,0},{2,3},{3,2},{4,5},{5,4},{6,7},{7,6},{8,9},{9,8},{10,11... | collective-permute-start | bytes 1572872 | tf_op jit(solution)/shard_map/ppermute | solution.py:38
  63.8 2.0 %collective-permute-start.14 = (bf16[256,1024]{1,0:T(8,128)(2,1)S(1)}, bf16[256,1024]{1,0:T(8,128)(2,1)S(1)}, u32[]{:S(2)}, u32[]{:S(2)}) collective-permute-start(bf16[256,1024]{1,0:T(8,128)(2,1)S(1)} %collective-permute-done.5.refs_3_), channel_id=1, source_target_pairs={{0,1},{1,0},{2,3},{3,2},{4,5},{5,4},{6,7},{7,6},{8,9},{9,8},{10,11... | collective-permute-start | bytes 1572872 | tf_op jit(solution)/shard_map/ppermute | solution.py:38
  64.0 2.5 %collective-permute-start.15 = (bf16[256,1024]{1,0:T(8,128)(2,1)S(1)}, bf16[256,1024]{1,0:T(8,128)(2,1)S(1)}, u32[]{:S(2)}, u32[]{:S(2)}) collective-permute-start(bf16[256,1024]{1,0:T(8,128)(2,1)S(1)} %collective-permute-done.6.refs_4_), channel_id=1, source_target_pairs={{0,1},{1,0},{2,3},{3,2},{4,5},{5,4},{6,7},{7,6},{8,9},{9,8},{10,11... | collective-permute-start | bytes 1572872 | tf_op jit(solution)/shard_map/ppermute | solution.py:38
  64.3 2.9 %collective-permute-start.23 = (bf16[256,1024]{1,0:T(8,128)(2,1)S(1)}, bf16[256,1024]{1,0:T(8,128)(2,1)S(1)}, u32[]{:S(2)}, u32[]{:S(2)}) collective-permute-start(bf16[256,1024]{1,0:T(8,128)(2,1)S(1)} %collective-permute-done.12.refs_5_), channel_id=1, source_target_pairs={{0,1},{1,0},{2,3},{3,2},{4,5},{5,4},{6,7},{7,6},{8,9},{9,8},{10,11... | collective-permute-start | bytes 1572872 | tf_op jit(solution)/shard_map/ppermute | solution.py:38
  71.4 17.3 %copy-start.3 = (f32[128]{0:T(128)S(1)}, f32[128]{0:T(128)}, u32[]{:S(2)}) copy-start(f32[128]{0:T(128)} %param.10) | copy-start | bytes 1540
  77.0 11.6 %all-to-all-start.1 = ((f32[32,3,128]{2,1,0:T(4,128)}), f32[32,3,128]{2,1,0:T(4,128)S(1)}, u32[]{:S(2)}, u32[]{:S(2)}) async-start(f32[32,3,128]{2,1,0:T(4,128)} %bitcast.13), calls=%async_computation.1 | async-start | bytes 131072 | tf_op jit(solution)/shard_map/all_to_all | solution.py:303

commit v8 on v6

--- a/solution.py
+++ b/solution.py
@@ -268,43 +268,47 @@
 
     layers = {0: hidden}
     reached = [grid.reach(hidden)]
-    before = []
-    for group in groups[1:]:
+    for at, group in enumerate(groups[1:], 1):
         for dz in group:
-            layers[dz] = grid.along(after(hidden, *before), dz)
-        before = list(reached[0].values()) if len(before) == 0 else [layers[dz] for dz in group]
-    for group in groups[1:]:
-        sources = [layers[dz] for dz in group]
-        sources[0] = after(sources[0], *reached[-1].values())
-        reached.append(grid.reach(joined(sources) if len(sources) > 1 else sources[0]))
-
+            step = 1 if dz <= depth // 2 else -1
+            layers[dz] = grid.along(layers[dz - step], step) if at > 1 else grid.along(hidden, dz)
+
+    def reach_next(at, *late):
+        if at < len(groups):
+            sources = [layers[dz] for dz in groups[at]]
+            sources[0] = after(sources[0], *late)
+            reached.append(grid.reach(joined(sources) if len(sources) > 1 else sources[0]))
+
+    reach_next(1, *reached[0].values())
     vocab_cols = head.shape[1]
     vocab_start = lax.axis_index(("dp", "tensor")) * vocab_cols
     starts = jnp.stack([c_me, vocab_start] + owners + [(z_me - dz) % depth for dz in range(depth)])
     packed = squares(after(hidden, starts), norm_gain[None, :], targets[None, :], n_dp * n_t)
     fine = lax.all_to_all(packed, ("dp", "tensor"), 0, 0, tiled=True)
 
-    acc, deep = None, CORES * feat
+    acc, deep, half = None, CORES * feat, []
     for at, group in enumerate(groups):
         final = at == len(groups) - 1
         middle = at and not final
         offsets = [2 + n_dp + dz for dz in group]
         own = grid.sibling(reached[at][0, 0])
-        held = [layers[dz] for dz in groups[at + 1]] + [own] if middle else []
-        spread = grid.fill(dict(reached[at]), *([acc] if at == 1 else []), *held)
+        held = [acc, own, *(layers[dz] for dz in groups[2])] if at == 1 else half
+        spread = grid.fill(dict(reached[at]), *held)
+        if at:
+            reach_next(at + 1, spread[-1])
         if at == 0:
             weights = [head]
         elif at == 1:
             for later in groups[1:]:
                 ready = after(head, acc, *(layers[dz] for dz in groups[2]))
                 weights.append(loaded(starts, [2 + n_dp + dz for dz in later], ready, deep))
-        following = [*reached[at + 1].values(), *weights[1:3]] if middle else []
-        others = [own] + [grid.sibling(after(a, *following)) for a in spread[1:-1]]
-        others.append(grid.sibling(after(spread[-1], *([acc] if final else following))))
+        others = [own] + [grid.sibling(a) for a in spread[1:-1]]
+        others.append(grid.sibling(after(spread[-1], *([acc] if final else weights[1:3] if middle else []))))
         blocks = spread + others
         for layer, offset in enumerate(offsets):
             done = layer == len(offsets) - 1
             if middle and done:
+                half = [acc]
                 blocks[0] = after(blocks[0], *reached[at + 1].values())
             last = final and done
             acc = layer_product(tok, n_t, starts, layer, offset, fine, blocks, place, weights[at], acc, last)

time: 86.4 us -> 81.8 us (0.947)
  waiting for transfers between devices: 18.8 us -> 15.4 us
  starting transfers between devices: 32.5 us -> 30.7 us
    ppermute x24, waiting for transfers between devices: 10.7 us -> 6.84 us  [permute(): return lax.ppermute(a, ('dp', 'tensor'), perm)]
    ppermute x24, starting transfers between devices: 22.5 us -> 21.3 us  [permute(): return lax.ppermute(a, ('dp', 'tensor'), perm)]
    unnamed x8 -> x10, local copies, waits for them, and re-layouts: 2.62 us -> 3.3 us
  transfers between devices with their start and end apart: 26 -> 26, of which waited for: 10 -> 8; matrix products, arithmetic and copies ran while one was open for 0% -> 0% of each run, Pallas kernels for 28% -> 30%
where the time goes in v8:
time: 81.8 us; the launch traced here: 81.4 us
  starting transfers between devices  30.7 us (38%)
  Pallas kernels  29.8 us (36%)
  waiting for transfers between devices  15.4 us (19%)
  local copies, waits for them, and re-layouts  3.39 us (4%)
  between operations  1.46 us (2%)
    ppermute x24, starting transfers between devices, permute(): return lax.ppermute(a, ('dp', 'tensor'), perm)  21.3 us
    pallas_call x4, Pallas kernels, layer_product(): pl.pallas_call(functools.partial(layer_kernel, n, n_t, place, layer, offs...  20.8 us
    pallas_call x2, Pallas kernels, loaded(): pl.pallas_call(functools.partial(load_kernel, offsets), out_shape=pltpu.V...  7.23 us
    ppermute x24, waiting for transfers between devices, permute(): return lax.ppermute(a, ('dp', 'tensor'), perm)  6.84 us
    all_to_all x1, waiting for transfers between devices, body(): lax.all_to_all(acc.reshape(n_dp * n_t, 3, tok), ('dp', 'tensor'), 0, 0, t...  6.74 us
    all_to_all x1, starting transfers between devices, body(): fine = lax.all_to_all(packed, ('dp', 'tensor'), 0, 0, tiled=True)  5.05 us
    all_to_all x1, starting transfers between devices, body(): lax.all_to_all(acc.reshape(n_dp * n_t, 3, tok), ('dp', 'tensor'), 0, 0, t...  4.42 us
    unnamed x10, local copies, waits for them, and re-layouts  3.3 us
  transfers between devices with their start and end apart: 26, of which 8 were waited for; matrix products, arithmetic and copies ran while one was open for 0% of the time, Pallas kernels for 30%

profile of v8, /device:TPU:0, one launch (start us, length us, event | category | flops | bytes accessed | tf_op | source)
XLA Modules:
  0.0 81.4 jit_solution(14406184964853355850)
XLA Ops:
  0.6 3.0 %collective-permute-start.2 = (bf16[128,1024]{1,0:T(8,128)(2,1)}, bf16[128,1024]{1,0:T(8,128)(2,1)S(1)}, u32[]{:S(2)}, u32[]{:S(2)}) collective-permute-start(bf16[128,1024]{1,0:T(8,128)(2,1)} %refs_2_.1), channel_id=1, source_target_pairs={{0,8},{1,17},{2,10},{3,19},{4,12},{5,21},{6,14},{7,23},{8,0},{9,25... | collective-permute-start | bytes 786440 | tf_op jit(solution)/shard_map/ppermute | solution.py:38
  3.6 1.5 %collective-permute-start.3 = (bf16[128,1024]{1,0:T(8,128)(2,1)}, bf16[128,1024]{1,0:T(8,128)(2,1)S(1)}, u32[]{:S(2)}, u32[]{:S(2)}) collective-permute-start(bf16[128,1024]{1,0:T(8,128)(2,1)} %refs_2_.1), channel_id=1, source_target_pairs={{0,16},{1,9},{2,18},{3,11},{4,20},{5,13},{6,22},{7,15},{8,24},{9,1... | collective-permute-start | bytes 786440 | tf_op jit(solution)/shard_map/ppermute | solution.py:38
  5.2 1.6 %collective-permute-start = (bf16[128,1024]{1,0:T(8,128)(2,1)}, bf16[128,1024]{1,0:T(8,128)(2,1)S(1)}, u32[]{:S(2)}, u32[]{:S(2)}) collective-permute-start(bf16[128,1024]{1,0:T(8,128)(2,1)} %refs_2_.1), channel_id=1, source_target_pairs={{0,2},{1,3},{2,4},{3,5},{4,6},{5,7},{6,0},{7,1},{8,10},{9,11},{10,... | collective-permute-start | bytes 786440 | tf_op jit(solution)/shard_map/ppermute | solution.py:38
  6.7 2.2 %collective-permute-start.4 = (bf16[128,1024]{1,0:T(8,128)(2,1)}, bf16[128,1024]{1,0:T(8,128)(2,1)S(1)}, u32[]{:S(2)}, u32[]{:S(2)}) collective-permute-start(bf16[128,1024]{1,0:T(8,128)(2,1)} %refs_2_.1), channel_id=1, source_target_pairs={{0,6},{1,7},{2,0},{3,1},{4,2},{5,3},{6,4},{7,5},{8,14},{9,15},{10,... | collective-permute-start | bytes 786440 | tf_op jit(solution)/shard_map/ppermute | solution.py:38
  9.0 0.0 collective-permute-start.7
  9.0 1.6 %collective-permute-done.2.refs_3_ = bf16[128,1024]{1,0:T(8,128)(2,1)S(1)} collective-permute-done((bf16[128,1024]{1,0:T(8,128)(2,1)}, bf16[128,1024]{1,0:T(8,128)(2,1)S(1)}, u32[]{:S(2)}, u32[]{:S(2)}) %collective-permute-start.2) | collective-permute-done | bytes 262176 | tf_op jit(solution)/shard_map/ppermute | solution.py:38
  10.5 1.5 %collective-permute-start.6 = (bf16[128,1024]{1,0:T(8,128)(2,1)S(1)}, bf16[128,1024]{1,0:T(8,128)(2,1)S(1)}, u32[]{:S(2)}, u32[]{:S(2)}) collective-permute-start(bf16[128,1024]{1,0:T(8,128)(2,1)S(1)} %collective-permute-done.2.refs_3_), channel_id=1, source_target_pairs={{0,16},{1,9},{2,18},{3,11},{4,20},{5,13},{6,22},{7,15},{8,24},{9,1... | collective-permute-start | bytes 786440 | tf_op jit(solution)/shard_map/ppermute | solution.py:38
  12.0 0.9 %collective-permute-start.8 = (bf16[128,1024]{1,0:T(8,128)(2,1)S(1)}, bf16[128,1024]{1,0:T(8,128)(2,1)}, u32[]{:S(2)}, u32[]{:S(2)}) collective-permute-start(bf16[128,1024]{1,0:T(8,128)(2,1)S(1)} %collective-permute-done.2.refs_3_), channel_id=1, source_target_pairs={{0,1},{1,0},{2,3},{3,2},{4,5},{5,4},{6,7},{7,6},{8,9},{9,8},{10,11... | collective-permute-start | bytes 786440 | tf_op jit(solution)/shard_map/ppermute | solution.py:38
  12.9 0.1 stack.43.refs_0_.start_ref
  12.9 1.8 %shard_map.77 = f32[32,1,1280]{2,1,0:T(1,128)} custom-call(bf16[128,1024]{1,0:T(8,128)(2,1)} %refs_2_.1, f32[1,1024]{1,0:T(1,128)} %bitcast.22, s32[1,128]{1,0:T(1,128)} %bitcast.23), custom_call_target="tpu_custom_call" | custom-call | tf_op jit(solution)/shard_map/pallas_call | solution.py:243
  14.7 5.0 %all-to-all-start = ((f32[32,1,1280]{2,1,0:T(1,128)}), f32[32,1,1280]{2,1,0:T(1,128)S(1)}, u32[]{:S(2)}, u32[]{:S(2)}) async-start(f32[32,1,1280]{2,1,0:T(1,128)} %shard_map.77), calls=%async_computation | async-start | bytes 327680 | tf_op jit(solution)/shard_map/all_to_all | solution.py:287
  19.8 0.0 collective-permute-done.refs_0_
  19.8 0.0 collective-permute-done.4.refs_1_
  19.9 0.7 copy-done.3
  20.6 1.8 %collective-permute-start.12 = (bf16[256,1024]{1,0:T(8,128)(2,1)S(1)}, bf16[256,1024]{1,0:T(8,128)(2,1)S(1)}, u32[]{:S(2)}, u32[]{:S(2)}) collective-permute-start(bf16[256,1024]{1,0:T(8,128)(2,1)S(1)} %shard_map.78.refs_2_), channel_id=1, source_target_pairs={{0,16},{1,9},{2,18},{3,11},{4,20},{5,13},{6,22},{7,15},{8,24},{9,1... | collective-permute-start | bytes 1572872 | tf_op jit(solution)/shard_map/ppermute | solution.py:38
  22.3 0.0 collective-permute-start.9
  22.3 0.0 collective-permute-done.7.refs_6_
  22.3 1.5 %collective-permute-start.5 = (bf16[256,1024]{1,0:T(8,128)(2,1)S(1)}, bf16[256,1024]{1,0:T(8,128)(2,1)S(1)}, u32[]{:S(2)}, u32[]{:S(2)}) collective-permute-start(bf16[256,1024]{1,0:T(8,128)(2,1)S(1)} %shard_map.78.refs_2_), channel_id=1, source_target_pairs={{0,8},{1,17},{2,10},{3,19},{4,12},{5,21},{6,14},{7,23},{8,0},{9,25... | collective-permute-start | bytes 1572872 | tf_op jit(solution)/shard_map/ppermute | solution.py:38
  23.8 0.0 collective-permute-done.6.refs_5_
  23.8 0.5 collective-permute-start.10
  24.3 0.7 copy-done.1
  25.0 1.5 %collective-permute-start.1 = (bf16[128,1024]{1,0:T(8,128)(2,1)}, bf16[128,1024]{1,0:T(8,128)(2,1)}, u32[]{:S(2)}, u32[]{:S(2)}) collective-permute-start(bf16[128,1024]{1,0:T(8,128)(2,1)} %copy-done.3), channel_id=1, source_target_pairs={{0,2},{1,3},{2,4},{3,5},{4,6},{5,7},{6,0},{7,1},{8,10},{9,11},{10,... | collective-permute-start | bytes 786440 | tf_op jit(solution)/shard_map/ppermute | solution.py:38
  26.5 1.8 %all-to-all-done.refs_1_ = f32[32,1,1280]{2,1,0:T(1,128)S(1)} async-done(((f32[32,1,1280]{2,1,0:T(1,128)}), f32[32,1,1280]{2,1,0:T(1,128)S(1)}, u32[]{:S(2)}, u32[]{:S(2)}) %all-to-all-start) | async-done | bytes 163872 | tf_op jit(solution)/shard_map/all_to_all | solution.py:287
  28.3 0.9 %copy-done = bf16[128,1024]{1,0:T(8,128)(2,1)S(1)} copy-done((bf16[128,1024]{1,0:T(8,128)(2,1)S(1)}, bf16[128,1024]{1,0:T(8,128)(2,1)}, u32[]{:S(2)}) %copy-start) | copy-done | bytes 262168
  29.2 0.9 %copy-done.2 = bf16[128,1024]{1,0:T(8,128)(2,1)S(1)} copy-done((bf16[128,1024]{1,0:T(8,128)(2,1)S(1)}, bf16[128,1024]{1,0:T(8,128)(2,1)}, u32[]{:S(2)}) %copy-start.2) | copy-done | bytes 262168
  30.2 6.7 %shard_map.79.refs_11_ = f32[512,1152]{1,0:T(8,128)S(1)} custom-call(s32[10]{0:T(128)S(1)} %stack.43.refs_0_.start_ref, f32[32,1,1280]{2,1,0:T(1,128)S(1)} %all-to-all-done.refs_1_, bf16[128,1024]{1,0:T(8,128)(2,1)S(1)} %copy-done, bf16[128,1024]{1,0:T(8,128)(2,1)S(1)} %collective-permute-done.2.refs_3_, ...), custom_call_target="tpu_custom_call" | custom-call | flops 2415919104 | bytes 4718592 | tf_op jit(solution)/shard_map/pallas_call | solution.py:211
  36.9 1.1 %collective-permute-start.13 = (bf16[256,1024]{1,0:T(8,128)(2,1)S(1)}, bf16[256,1024]{1,0:T(8,128)(2,1)S(1)}, u32[]{:S(2)}, u32[]{:S(2)}) collective-permute-start(bf16[256,1024]{1,0:T(8,128)(2,1)S(1)} %collective-permute-done.5.refs_3_), channel_id=1, source_target_pairs={{0,16},{1,9},{2,18},{3,11},{4,20},{5,13},{6,22},{7,15},{8,24},{9,1... | collective-permute-start | bytes 1572872 | tf_op jit(solution)/shard_map/ppermute | solution.py:38
  38.0 4.3 %shard_map.80.refs_10_ = bf16[2,2048,1152]{2,1,0:T(8,128)(2,1)S(1)} custom-call(s32[10]{0:T(128)S(1)} %stack.43.refs_0_.start_ref, bf16[8192,1152]{1,0:T(8,128)(2,1)} %head_ref.1), custom_call_target="tpu_custom_call" | custom-call | tf_op jit(solution)/shard_map/pallas_call | solution.py:116
  42.3 2.9 %shard_map.81.refs_10_ = bf16[1,2048,1152]{2,1,0:T(8,128)(2,1)S(1)} custom-call(s32[10]{0:T(128)S(1)} %stack.43.refs_0_.start_ref, bf16[8192,1152]{1,0:T(8,128)(2,1)} %head_ref.1), custom_call_target="tpu_custom_call" | custom-call | tf_op jit(solution)/shard_map/pallas_call | solution.py:116
  45.2 0.1 collective-permute-start.16
  45.3 0.5 collective-permute-start.17
  45.8 0.3 collective-permute-done.13.refs_5_
  46.2 1.0 %collective-permute-start.14 = (bf16[128,1024]{1,0:T(8,128)(2,1)}, bf16[128,1024]{1,0:T(8,128)(2,1)S(1)}, u32[]{:S(2)}, u32[]{:S(2)}) collective-permute-start(bf16[128,1024]{1,0:T(8,128)(2,1)} %collective-permute-done.1.refs_2_), channel_id=1, source_target_pairs={{0,8},{1,17},{2,10},{3,19},{4,12},{5,21},{6,14},{7,23},{8,0},{9,25... | collective-permute-start | bytes 786440 | tf_op jit(solution)/shard_map/ppermute | solution.py:38
  47.2 1.1 %collective-permute-start.15 = (bf16[128,1024]{1,0:T(8,128)(2,1)}, bf16[128,1024]{1,0:T(8,128)(2,1)S(1)}, u32[]{:S(2)}, u32[]{:S(2)}) collective-permute-start(bf16[128,1024]{1,0:T(8,128)(2,1)} %collective-permute-done.1.refs_2_), channel_id=1, source_target_pairs={{0,16},{1,9},{2,18},{3,11},{4,20},{5,13},{6,22},{7,15},{8,24},{9,1... | collective-permute-start | bytes 786440 | tf_op jit(solution)/shard_map/ppermute | solution.py:38
  48.3 0.4 collective-permute-done.18.refs_9_
  48.7 4.2 %shard_map.82.refs_11_ = f32[512,1152]{1,0:T(8,128)S(1)} custom-call(s32[10]{0:T(128)S(1)} %stack.43.refs_0_.start_ref, f32[32,1,1280]{2,1,0:T(1,128)S(1)} %all-to-all-done.refs_1_, bf16[256,1024]{1,0:T(8,128)(2,1)S(1)} %shard_map.78.refs_2_, bf16[256,1024]{1,0:T(8,128)(2,1)S(1)} %collective-permute-done.5.refs_3_, ...), custom_call_target="tpu_custom_call" | custom-call | flops 2415919104 | bytes 4718592 | tf_op jit(solution)/shard_map/pallas_call | solution.py:211
  52.9 2.4 %collective-permute-done.14.refs_3_ = bf16[128,1024]{1,0:T(8,128)(2,1)S(1)} collective-permute-done((bf16[128,1024]{1,0:T(8,128)(2,1)}, bf16[128,1024]{1,0:T(8,128)(2,1)S(1)}, u32[]{:S(2)}, u32[]{:S(2)}) %collective-permute-start.14) | collective-permute-done | bytes 262176 | tf_op jit(solution)/shard_map/ppermute | solution.py:38
  55.3 1.0 %collective-permute-start.19 = (bf16[128,1024]{1,0:T(8,128)(2,1)S(1)}, bf16[128,1024]{1,0:T(8,128)(2,1)S(1)}, u32[]{:S(2)}, u32[]{:S(2)}) collective-permute-start(bf16[128,1024]{1,0:T(8,128)(2,1)S(1)} %collective-permute-done.14.refs_3_), channel_id=1, source_target_pairs={{0,16},{1,9},{2,18},{3,11},{4,20},{5,13},{6,22},{7,15},{8,24},{9,1... | collective-permute-start | bytes 786440 | tf_op jit(solution)/shard_map/ppermute | solution.py:38
  56.3 0.5 collective-permute-start.21
  56.8 4.2 %shard_map.83.refs_11_ = f32[512,1152]{1,0:T(8,128)S(1)} custom-call(s32[10]{0:T(128)S(1)} %stack.43.refs_0_.start_ref, f32[32,1,1280]{2,1,0:T(1,128)S(1)} %all-to-all-done.refs_1_, bf16[256,1024]{1,0:T(8,128)(2,1)S(1)} %shard_map.78.refs_2_, bf16[256,1024]{1,0:T(8,128)(2,1)S(1)} %collective-permute-done.5.refs_3_, ...), custom_call_target="tpu_custom_call" | custom-call | flops 2415919104 | bytes 4718592 | tf_op jit(solution)/shard_map/pallas_call | solution.py:211
  61.0 0.0 copy-start.4
  61.0 0.6 collective-permute-done.19.refs_5_
  61.7 1.5 %collective-permute-done.23.refs_9_ = bf16[128,1024]{1,0:T(8,128)(2,1)S(1)} collective-permute-done((bf16[128,1024]{1,0:T(8,128)(2,1)S(1)}, bf16[128,1024]{1,0:T(8,128)(2,1)S(1)}, u32[]{:S(2)}, u32[]{:S(2)}) %collective-permute-start.23) | collective-permute-done | bytes 262176 | tf_op jit(solution)/shard_map/ppermute | solution.py:38
  63.2 5.8 %shard_map.84 = f32[4,8,3,128]{3,2,1,0:T(4,128)} custom-call(s32[10]{0:T(128)S(1)} %stack.43.refs_0_.start_ref, f32[32,1,1280]{2,1,0:T(1,128)S(1)} %all-to-all-done.refs_1_, bf16[128,1024]{1,0:T(8,128)(2,1)} %collective-permute-done.1.refs_2_, bf16[128,1024]{1,0:T(8,128)(2,1)S(1)} %collective-permute-done.14.refs_3_, ...), custom_call_target="tpu_custom_call" | custom-call | flops 2415919104 | bytes 4718592 | tf_op jit(solution)/shard_map/pallas_call | solution.py:211
  69.0 4.4 %all-to-all-start.1 = ((f32[32,3,128]{2,1,0:T(4,128)}), f32[32,3,128]{2,1,0:T(4,128)S(1)}, u32[]{:S(2)}, u32[]{:S(2)}) async-start(f32[32,3,128]{2,1,0:T(4,128)} %bitcast.13), calls=%async_computation.1 | async-start | bytes 131072 | tf_op jit(solution)/shard_map/all_to_all | solution.py:316
  74.0 6.7 %all-to-all-done.1 = f32[32,3,128]{2,1,0:T(4,128)S(1)} async-done(((f32[32,3,128]{2,1,0:T(4,128)}), f32[32,3,128]{2,1,0:T(4,128)S(1)}, u32[]{:S(2)}, u32[]{:S(2)}) %all-to-all-start.1) | async-done | bytes 49184 | tf_op jit(solution)/shard_map/all_to_all | solution.py:316
  80.8 0.1 slice_reduce_fusion
  80.9 0.5 compare_select_fusion
  (27 shorter events, 0.1 us)
Async XLA Ops:
  0.6 9.9 %collective-permute-start.2 = (bf16[128,1024]{1,0:T(8,128)(2,1)}, bf16[128,1024]{1,0:T(8,128)(2,1)S(1)}, u32[]{:S(2)}, u32[]{:S(2)}) collective-permute-start(bf16[128,1024]{1,0:T(8,128)(2,1)} %refs_2_.1), channel_id=1, source_target_pairs={{0,8},{1,17},{2,10},{3,19},{4,12},{5,21},{6,14},{7,23},{8,0},{9,25... | collective-permute-start | bytes 786440 | tf_op jit(solution)/shard_map/ppermute | solution.py:38
  3.6 6.9 %collective-permute-start.3 = (bf16[128,1024]{1,0:T(8,128)(2,1)}, bf16[128,1024]{1,0:T(8,128)(2,1)S(1)}, u32[]{:S(2)}, u32[]{:S(2)}) collective-permute-start(bf16[128,1024]{1,0:T(8,128)(2,1)} %refs_2_.1), channel_id=1, source_target_pairs={{0,16},{1,9},{2,18},{3,11},{4,20},{5,13},{6,22},{7,15},{8,24},{9,1... | collective-permute-start | bytes 786440 | tf_op jit(solution)/shard_map/ppermute | solution.py:38
  5.2 14.6 %collective-permute-start = (bf16[128,1024]{1,0:T(8,128)(2,1)}, bf16[128,1024]{1,0:T(8,128)(2,1)S(1)}, u32[]{:S(2)}, u32[]{:S(2)}) collective-permute-start(bf16[128,1024]{1,0:T(8,128)(2,1)} %refs_2_.1), channel_id=1, source_target_pairs={{0,2},{1,3},{2,4},{3,5},{4,6},{5,7},{6,0},{7,1},{8,10},{9,11},{10,... | collective-permute-start | bytes 786440 | tf_op jit(solution)/shard_map/ppermute | solution.py:38
  6.7 13.1 %collective-permute-start.4 = (bf16[128,1024]{1,0:T(8,128)(2,1)}, bf16[128,1024]{1,0:T(8,128)(2,1)S(1)}, u32[]{:S(2)}, u32[]{:S(2)}) collective-permute-start(bf16[128,1024]{1,0:T(8,128)(2,1)} %refs_2_.1), channel_id=1, source_target_pairs={{0,6},{1,7},{2,0},{3,1},{4,2},{5,3},{6,4},{7,5},{8,14},{9,15},{10,... | collective-permute-start | bytes 786440 | tf_op jit(solution)/shard_map/ppermute | solution.py:38
  9.0 13.4 %collective-permute-start.7 = (bf16[128,1024]{1,0:T(8,128)(2,1)}, bf16[128,1024]{1,0:T(8,128)(2,1)S(1)}, u32[]{:S(2)}, u32[]{:S(2)}) collective-permute-start(bf16[128,1024]{1,0:T(8,128)(2,1)} %refs_2_.1), channel_id=1, source_target_pairs={{0,1},{1,0},{2,3},{3,2},{4,5},{5,4},{6,7},{7,6},{8,9},{9,8},{10,11... | collective-permute-start | bytes 786440 | tf_op jit(solution)/shard_map/ppermute | solution.py:38
  10.5 13.3 %collective-permute-start.6 = (bf16[128,1024]{1,0:T(8,128)(2,1)S(1)}, bf16[128,1024]{1,0:T(8,128)(2,1)S(1)}, u32[]{:S(2)}, u32[]{:S(2)}) collective-permute-start(bf16[128,1024]{1,0:T(8,128)(2,1)S(1)} %collective-permute-done.2.refs_3_), channel_id=1, source_target_pairs={{0,16},{1,9},{2,18},{3,11},{4,20},{5,13},{6,22},{7,15},{8,24},{9,1... | collective-permute-start | bytes 786440 | tf_op jit(solution)/shard_map/ppermute | solution.py:38
  12.0 11.8 %collective-permute-start.8 = (bf16[128,1024]{1,0:T(8,128)(2,1)S(1)}, bf16[128,1024]{1,0:T(8,128)(2,1)}, u32[]{:S(2)}, u32[]{:S(2)}) collective-permute-start(bf16[128,1024]{1,0:T(8,128)(2,1)S(1)} %collective-permute-done.2.refs_3_), channel_id=1, source_target_pairs={{0,1},{1,0},{2,3},{3,2},{4,5},{5,4},{6,7},{7,6},{8,9},{9,8},{10,11... | collective-permute-start | bytes 786440 | tf_op jit(solution)/shard_map/ppermute | solution.py:38
  14.7 13.5 %all-to-all-start = ((f32[32,1,1280]{2,1,0:T(1,128)}), f32[32,1,1280]{2,1,0:T(1,128)S(1)}, u32[]{:S(2)}, u32[]{:S(2)}) async-start(f32[32,1,1280]{2,1,0:T(1,128)} %shard_map.77), calls=%async_computation | async-start | bytes 327680 | tf_op jit(solution)/shard_map/all_to_all | solution.py:287
  19.9 0.7 copy-start.3
  20.6 16.3 %collective-permute-start.12 = (bf16[256,1024]{1,0:T(8,128)(2,1)S(1)}, bf16[256,1024]{1,0:T(8,128)(2,1)S(1)}, u32[]{:S(2)}, u32[]{:S(2)}) collective-permute-start(bf16[256,1024]{1,0:T(8,128)(2,1)S(1)} %shard_map.78.refs_2_), channel_id=1, source_target_pairs={{0,16},{1,9},{2,18},{3,11},{4,20},{5,13},{6,22},{7,15},{8,24},{9,1... | collective-permute-start | bytes 1572872 | tf_op jit(solution)/shard_map/ppermute | solution.py:38
  22.3 2.0 %collective-permute-start.9 = (bf16[128,1024]{1,0:T(8,128)(2,1)S(1)}, bf16[128,1024]{1,0:T(8,128)(2,1)S(1)}, u32[]{:S(2)}, u32[]{:S(2)}) collective-permute-start(bf16[128,1024]{1,0:T(8,128)(2,1)S(1)} %collective-permute-done.3.refs_4_), channel_id=1, source_target_pairs={{0,1},{1,0},{2,3},{3,2},{4,5},{5,4},{6,7},{7,6},{8,9},{9,8},{10,11... | collective-permute-start | bytes 786440 | tf_op jit(solution)/shard_map/ppermute | solution.py:38
  22.3 14.6 %collective-permute-start.5 = (bf16[256,1024]{1,0:T(8,128)(2,1)S(1)}, bf16[256,1024]{1,0:T(8,128)(2,1)S(1)}, u32[]{:S(2)}, u32[]{:S(2)}) collective-permute-start(bf16[256,1024]{1,0:T(8,128)(2,1)S(1)} %shard_map.78.refs_2_), channel_id=1, source_target_pairs={{0,8},{1,17},{2,10},{3,19},{4,12},{5,21},{6,14},{7,23},{8,0},{9,25... | collective-permute-start | bytes 1572872 | tf_op jit(solution)/shard_map/ppermute | solution.py:38
  23.8 13.1 %collective-permute-start.11 = (bf16[256,1024]{1,0:T(8,128)(2,1)S(1)}, bf16[256,1024]{1,0:T(8,128)(2,1)S(1)}, u32[]{:S(2)}, u32[]{:S(2)}) collective-permute-start(bf16[256,1024]{1,0:T(8,128)(2,1)S(1)} %shard_map.78.refs_2_), channel_id=1, source_target_pairs={{0,1},{1,0},{2,3},{3,2},{4,5},{5,4},{6,7},{7,6},{8,9},{9,8},{10,11... | collective-permute-start | bytes 1572872 | tf_op jit(solution)/shard_map/ppermute | solution.py:38
  23.8 4.5 %collective-permute-start.10 = (bf16[128,1024]{1,0:T(8,128)(2,1)S(1)}, bf16[128,1024]{1,0:T(8,128)(2,1)}, u32[]{:S(2)}, u32[]{:S(2)}) collective-permute-start(bf16[128,1024]{1,0:T(8,128)(2,1)S(1)} %collective-permute-done.6.refs_5_), channel_id=1, source_target_pairs={{0,1},{1,0},{2,3},{3,2},{4,5},{5,4},{6,7},{7,6},{8,9},{9,8},{10,11... | collective-permute-start | bytes 786440 | tf_op jit(solution)/shard_map/ppermute | solution.py:38
  24.3 0.7 copy-start.1
  25.0 11.8 %collective-permute-start.1 = (bf16[128,1024]{1,0:T(8,128)(2,1)}, bf16[128,1024]{1,0:T(8,128)(2,1)}, u32[]{:S(2)}, u32[]{:S(2)}) collective-permute-start(bf16[128,1024]{1,0:T(8,128)(2,1)} %copy-done.3), channel_id=1, source_target_pairs={{0,2},{1,3},{2,4},{3,5},{4,6},{5,7},{6,0},{7,1},{8,10},{9,11},{10,... | collective-permute-start | bytes 786440 | tf_op jit(solution)/shard_map/ppermute | solution.py:38
  28.3 1.0 %copy-start = (bf16[128,1024]{1,0:T(8,128)(2,1)S(1)}, bf16[128,1024]{1,0:T(8,128)(2,1)}, u32[]{:S(2)}) copy-start(bf16[128,1024]{1,0:T(8,128)(2,1)} %refs_2_.1) | copy-start | bytes 786436
  29.2 0.9 %copy-start.2 = (bf16[128,1024]{1,0:T(8,128)(2,1)S(1)}, bf16[128,1024]{1,0:T(8,128)(2,1)}, u32[]{:S(2)}) copy-start(bf16[128,1024]{1,0:T(8,128)(2,1)} %copy-done.1) | copy-start | bytes 786436
  36.9 9.2 %collective-permute-start.13 = (bf16[256,1024]{1,0:T(8,128)(2,1)S(1)}, bf16[256,1024]{1,0:T(8,128)(2,1)S(1)}, u32[]{:S(2)}, u32[]{:S(2)}) collective-permute-start(bf16[256,1024]{1,0:T(8,128)(2,1)S(1)} %collective-permute-done.5.refs_3_), channel_id=1, source_target_pairs={{0,16},{1,9},{2,18},{3,11},{4,20},{5,13},{6,22},{7,15},{8,24},{9,1... | collective-permute-start | bytes 1572872 | tf_op jit(solution)/shard_map/ppermute | solution.py:38
  45.2 3.1 %collective-permute-start.16 = (bf16[256,1024]{1,0:T(8,128)(2,1)S(1)}, bf16[256,1024]{1,0:T(8,128)(2,1)S(1)}, u32[]{:S(2)}, u32[]{:S(2)}) collective-permute-start(bf16[256,1024]{1,0:T(8,128)(2,1)S(1)} %collective-permute-done.5.refs_3_), channel_id=1, source_target_pairs={{0,1},{1,0},{2,3},{3,2},{4,5},{5,4},{6,7},{7,6},{8,9},{9,8},{10,11... | collective-permute-start | bytes 1572872 | tf_op jit(solution)/shard_map/ppermute | solution.py:38
  45.3 3.0 %collective-permute-start.17 = (bf16[256,1024]{1,0:T(8,128)(2,1)S(1)}, bf16[256,1024]{1,0:T(8,128)(2,1)S(1)}, u32[]{:S(2)}, u32[]{:S(2)}) collective-permute-start(bf16[256,1024]{1,0:T(8,128)(2,1)S(1)} %collective-permute-done.12.refs_4_), channel_id=1, source_target_pairs={{0,1},{1,0},{2,3},{3,2},{4,5},{5,4},{6,7},{7,6},{8,9},{9,8},{10,11... | collective-permute-start | bytes 1572872 | tf_op jit(solution)/shard_map/ppermute | solution.py:38
  46.1 2.6 %collective-permute-start.18 = (bf16[256,1024]{1,0:T(8,128)(2,1)S(1)}, bf16[256,1024]{1,0:T(8,128)(2,1)S(1)}, u32[]{:S(2)}, u32[]{:S(2)}) collective-permute-start(bf16[256,1024]{1,0:T(8,128)(2,1)S(1)} %collective-permute-done.13.refs_5_), channel_id=1, source_target_pairs={{0,1},{1,0},{2,3},{3,2},{4,5},{5,4},{6,7},{7,6},{8,9},{9,8},{10,11... | collective-permute-start | bytes 1572872 | tf_op jit(solution)/shard_map/ppermute | solution.py:38
  46.2 9.1 %collective-permute-start.14 = (bf16[128,1024]{1,0:T(8,128)(2,1)}, bf16[128,1024]{1,0:T(8,128)(2,1)S(1)}, u32[]{:S(2)}, u32[]{:S(2)}) collective-permute-start(bf16[128,1024]{1,0:T(8,128)(2,1)} %collective-permute-done.1.refs_2_), channel_id=1, source_target_pairs={{0,8},{1,17},{2,10},{3,19},{4,12},{5,21},{6,14},{7,23},{8,0},{9,25... | collective-permute-start | bytes 786440 | tf_op jit(solution)/shard_map/ppermute | solution.py:38
  47.2 8.1 %collective-permute-start.15 = (bf16[128,1024]{1,0:T(8,128)(2,1)}, bf16[128,1024]{1,0:T(8,128)(2,1)S(1)}, u32[]{:S(2)}, u32[]{:S(2)}) collective-permute-start(bf16[128,1024]{1,0:T(8,128)(2,1)} %collective-permute-done.1.refs_2_), channel_id=1, source_target_pairs={{0,16},{1,9},{2,18},{3,11},{4,20},{5,13},{6,22},{7,15},{8,24},{9,1... | collective-permute-start | bytes 786440 | tf_op jit(solution)/shard_map/ppermute | solution.py:38
  55.3 6.4 %collective-permute-start.19 = (bf16[128,1024]{1,0:T(8,128)(2,1)S(1)}, bf16[128,1024]{1,0:T(8,128)(2,1)S(1)}, u32[]{:S(2)}, u32[]{:S(2)}) collective-permute-start(bf16[128,1024]{1,0:T(8,128)(2,1)S(1)} %collective-permute-done.14.refs_3_), channel_id=1, source_target_pairs={{0,16},{1,9},{2,18},{3,11},{4,20},{5,13},{6,22},{7,15},{8,24},{9,1... | collective-permute-start | bytes 786440 | tf_op jit(solution)/shard_map/ppermute | solution.py:38
  56.3 5.3 %collective-permute-start.20 = (bf16[128,1024]{1,0:T(8,128)(2,1)}, bf16[128,1024]{1,0:T(8,128)(2,1)S(1)}, u32[]{:S(2)}, u32[]{:S(2)}) collective-permute-start(bf16[128,1024]{1,0:T(8,128)(2,1)} %collective-permute-done.1.refs_2_), channel_id=1, source_target_pairs={{0,1},{1,0},{2,3},{3,2},{4,5},{5,4},{6,7},{7,6},{8,9},{9,8},{10,11... | collective-permute-start | bytes 786440 | tf_op jit(solution)/shard_map/ppermute | solution.py:38
  56.3 5.3 %collective-permute-start.21 = (bf16[128,1024]{1,0:T(8,128)(2,1)S(1)}, bf16[128,1024]{1,0:T(8,128)(2,1)S(1)}, u32[]{:S(2)}, u32[]{:S(2)}) collective-permute-start(bf16[128,1024]{1,0:T(8,128)(2,1)S(1)} %collective-permute-done.14.refs_3_), channel_id=1, source_target_pairs={{0,1},{1,0},{2,3},{3,2},{4,5},{5,4},{6,7},{7,6},{8,9},{9,8},{10,11... | collective-permute-start | bytes 786440 | tf_op jit(solution)/shard_map/ppermute | solution.py:38
  56.8 4.8 %collective-permute-start.22 = (bf16[128,1024]{1,0:T(8,128)(2,1)S(1)}, bf16[128,1024]{1,0:T(8,128)(2,1)S(1)}, u32[]{:S(2)}, u32[]{:S(2)}) collective-permute-start(bf16[128,1024]{1,0:T(8,128)(2,1)S(1)} %collective-permute-done.15.refs_4_), channel_id=1, source_target_pairs={{0,1},{1,0},{2,3},{3,2},{4,5},{5,4},{6,7},{7,6},{8,9},{9,8},{10,11... | collective-permute-start | bytes 786440 | tf_op jit(solution)/shard_map/ppermute | solution.py:38
  61.0 19.9 %copy-start.4 = (f32[128]{0:T(128)S(1)}, f32[128]{0:T(128)}, u32[]{:S(2)}) copy-start(f32[128]{0:T(128)} %param.10) | copy-start | bytes 1540
  61.6 1.5 %collective-permute-start.23 = (bf16[128,1024]{1,0:T(8,128)(2,1)S(1)}, bf16[128,1024]{1,0:T(8,128)(2,1)S(1)}, u32[]{:S(2)}, u32[]{:S(2)}) collective-permute-start(bf16[128,1024]{1,0:T(8,128)(2,1)S(1)} %collective-permute-done.19.refs_5_), channel_id=1, source_target_pairs={{0,1},{1,0},{2,3},{3,2},{4,5},{5,4},{6,7},{7,6},{8,9},{9,8},{10,11... | collective-permute-start | bytes 786440 | tf_op jit(solution)/shard_map/ppermute | solution.py:38
  69.0 11.8 %all-to-all-start.1 = ((f32[32,3,128]{2,1,0:T(4,128)}), f32[32,3,128]{2,1,0:T(4,128)S(1)}, u32[]{:S(2)}, u32[]{:S(2)}) async-start(f32[32,3,128]{2,1,0:T(4,128)} %bitcast.13), calls=%async_computation.1 | async-start | bytes 131072 | tf_op jit(solution)/shard_map/all_to_all | solution.py:316

commit v9 on v8

--- a/solution.py
+++ b/solution.py
@@ -292,16 +292,16 @@
         middle = at and not final
         offsets = [2 + n_dp + dz for dz in group]
         own = grid.sibling(reached[at][0, 0])
-        held = [acc, own, *(layers[dz] for dz in groups[2])] if at == 1 else half
+        held = [acc, own, *(layers[dz] for dz in groups[2])] if at == 1 else half if at else [packed]
         spread = grid.fill(dict(reached[at]), *held)
-        if at:
-            reach_next(at + 1, spread[-1])
         if at == 0:
             weights = [head]
         elif at == 1:
             for later in groups[1:]:
                 ready = after(head, acc, *(layers[dz] for dz in groups[2]))
                 weights.append(loaded(starts, [2 + n_dp + dz for dz in later], ready, deep))
+        if at:
+            reach_next(at + 1, weights[1] if at == 1 else spread[-1])
         others = [own] + [grid.sibling(a) for a in spread[1:-1]]
         others.append(grid.sibling(after(spread[-1], *([acc] if final else weights[1:3] if middle else []))))
         blocks = spread + others

time: 81.8 us -> 79.2 us (0.968)
  starting transfers between devices: 30.7 us -> 24.8 us
  waiting for transfers between devices: 15.4 us -> 19.4 us
    ppermute x24, waiting for transfers between devices: 6.84 us -> 11.5 us  [permute(): return lax.ppermute(a, ('dp', 'tensor'), perm)]
    ppermute x24, starting transfers between devices: 21.3 us -> 17.2 us  [permute(): return lax.ppermute(a, ('dp', 'tensor'), perm)]
    all_to_all x1, starting transfers between devices: 4.42 us -> 2.55 us  [body(): lax.all_to_all(acc.reshape(n_dp * n_t, 3, tok), ('dp', 'tensor'), 0, 0, t...]
  transfers between devices with their start and end apart: 26 -> 26, of which waited for: 8 -> 11; matrix products, arithmetic and copies ran while one was open for 0% -> 0% of each run, Pallas kernels for 30% -> 31%
where the time goes in v9:
time: 79.2 us; the launch traced here: 78.8 us
  Pallas kernels  29.8 us (38%)
  starting transfers between devices  24.8 us (31%)
  waiting for transfers between devices  19.4 us (24%)
  local copies, waits for them, and re-layouts  2.71 us (3%)
  between operations  1.43 us (2%)
    pallas_call x4, Pallas kernels, layer_product(): pl.pallas_call(functools.partial(layer_kernel, n, n_t, place, layer, offs...  20.8 us
    ppermute x24, starting transfers between devices, permute(): return lax.ppermute(a, ('dp', 'tensor'), perm)  17.2 us
    ppermute x24, waiting for transfers between devices, permute(): return lax.ppermute(a, ('dp', 'tensor'), perm)  11.5 us
    pallas_call x2, Pallas kernels, loaded(): pl.pallas_call(functools.partial(load_kernel, offsets), out_shape=pltpu.V...  7.23 us
    all_to_all x1, waiting for transfers between devices, body(): lax.all_to_all(acc.reshape(n_dp * n_t, 3, tok), ('dp', 'tensor'), 0, 0, t...  6.74 us
    all_to_all x1, starting transfers between devices, body(): fine = lax.all_to_all(packed, ('dp', 'tensor'), 0, 0, tiled=True)  5.04 us
    unnamed x10, local copies, waits for them, and re-layouts  2.62 us
    all_to_all x1, starting transfers between devices, body(): lax.all_to_all(acc.reshape(n_dp * n_t, 3, tok), ('dp', 'tensor'), 0, 0, t...  2.55 us
  transfers between devices with their start and end apart: 26, of which 11 were waited for; matrix products, arithmetic and copies ran while one was open for 0% of the time, Pallas kernels for 31%

profile of v9, /device:TPU:0, one launch (start us, length us, event | category | flops | bytes accessed | tf_op | source)
XLA Modules:
  0.0 78.8 jit_solution(2647503467927205103)
XLA Ops:
  0.6 3.0 %collective-permute-start.2 = (bf16[128,1024]{1,0:T(8,128)(2,1)}, bf16[128,1024]{1,0:T(8,128)(2,1)S(1)}, u32[]{:S(2)}, u32[]{:S(2)}) collective-permute-start(bf16[128,1024]{1,0:T(8,128)(2,1)} %refs_2_.1), channel_id=1, source_target_pairs={{0,8},{1,17},{2,10},{3,19},{4,12},{5,21},{6,14},{7,23},{8,0},{9,25... | collective-permute-start | bytes 786440 | tf_op jit(solution)/shard_map/ppermute | solution.py:38
  3.6 1.5 %collective-permute-start.3 = (bf16[128,1024]{1,0:T(8,128)(2,1)}, bf16[128,1024]{1,0:T(8,128)(2,1)S(1)}, u32[]{:S(2)}, u32[]{:S(2)}) collective-permute-start(bf16[128,1024]{1,0:T(8,128)(2,1)} %refs_2_.1), channel_id=1, source_target_pairs={{0,16},{1,9},{2,18},{3,11},{4,20},{5,13},{6,22},{7,15},{8,24},{9,1... | collective-permute-start | bytes 786440 | tf_op jit(solution)/shard_map/ppermute | solution.py:38
  5.2 0.0 collective-permute-start.5
  5.2 1.6 %collective-permute-start = (bf16[128,1024]{1,0:T(8,128)(2,1)}, bf16[128,1024]{1,0:T(8,128)(2,1)S(1)}, u32[]{:S(2)}, u32[]{:S(2)}) collective-permute-start(bf16[128,1024]{1,0:T(8,128)(2,1)} %refs_2_.1), channel_id=1, source_target_pairs={{0,2},{1,3},{2,4},{3,5},{4,6},{5,7},{6,0},{7,1},{8,10},{9,11},{10,... | collective-permute-start | bytes 786440 | tf_op jit(solution)/shard_map/ppermute | solution.py:38
  6.7 2.2 %collective-permute-start.11 = (bf16[128,1024]{1,0:T(8,128)(2,1)}, bf16[128,1024]{1,0:T(8,128)(2,1)S(1)}, u32[]{:S(2)}, u32[]{:S(2)}) collective-permute-start(bf16[128,1024]{1,0:T(8,128)(2,1)} %refs_2_.1), channel_id=1, source_target_pairs={{0,6},{1,7},{2,0},{3,1},{4,2},{5,3},{6,4},{7,5},{8,14},{9,15},{10,... | collective-permute-start | bytes 786440 | tf_op jit(solution)/shard_map/ppermute | solution.py:38
  9.0 0.1 stack.43.refs_0_.start_ref
  9.1 1.8 %shard_map.77 = f32[32,1,1280]{2,1,0:T(1,128)} custom-call(bf16[128,1024]{1,0:T(8,128)(2,1)} %refs_2_.1, f32[1,1024]{1,0:T(1,128)} %bitcast.22, s32[1,128]{1,0:T(1,128)} %bitcast.23), custom_call_target="tpu_custom_call" | custom-call | tf_op jit(solution)/shard_map/pallas_call | solution.py:243
  10.9 0.0 collective-permute-done.2.refs_3_
  10.9 0.0 collective-permute-done.3.refs_4_
  10.9 1.1 %collective-permute-start.4 = (bf16[128,1024]{1,0:T(8,128)(2,1)S(1)}, bf16[128,1024]{1,0:T(8,128)(2,1)S(1)}, u32[]{:S(2)}, u32[]{:S(2)}) collective-permute-start(bf16[128,1024]{1,0:T(8,128)(2,1)S(1)} %collective-permute-done.2.refs_3_), channel_id=1, source_target_pairs={{0,16},{1,9},{2,18},{3,11},{4,20},{5,13},{6,22},{7,15},{8,24},{9,1... | collective-permute-start | bytes 786440 | tf_op jit(solution)/shard_map/ppermute | solution.py:38
  12.0 0.9 %collective-permute-start.6 = (bf16[128,1024]{1,0:T(8,128)(2,1)S(1)}, bf16[128,1024]{1,0:T(8,128)(2,1)}, u32[]{:S(2)}, u32[]{:S(2)}) collective-permute-start(bf16[128,1024]{1,0:T(8,128)(2,1)S(1)} %collective-permute-done.2.refs_3_), channel_id=1, source_target_pairs={{0,1},{1,0},{2,3},{3,2},{4,5},{5,4},{6,7},{7,6},{8,9},{9,8},{10,11... | collective-permute-start | bytes 786440 | tf_op jit(solution)/shard_map/ppermute | solution.py:38
  12.9 5.0 %all-to-all-start = ((f32[32,1,1280]{2,1,0:T(1,128)}), f32[32,1,1280]{2,1,0:T(1,128)S(1)}, u32[]{:S(2)}, u32[]{:S(2)}) async-start(f32[32,1,1280]{2,1,0:T(1,128)} %shard_map.77), calls=%async_computation | async-start | bytes 327680 | tf_op jit(solution)/shard_map/all_to_all | solution.py:287
  17.9 3.2 %collective-permute-done.11.refs_1_ = bf16[128,1024]{1,0:T(8,128)(2,1)S(1)} collective-permute-done((bf16[128,1024]{1,0:T(8,128)(2,1)}, bf16[128,1024]{1,0:T(8,128)(2,1)S(1)}, u32[]{:S(2)}, u32[]{:S(2)}) %collective-permute-start.11) | collective-permute-done | bytes 262176 | tf_op jit(solution)/shard_map/ppermute | solution.py:38
  21.2 0.4 collective-permute-start.12
  21.7 0.7 collective-permute-start.13
  22.4 1.2 %collective-permute-start.14 = (bf16[256,1024]{1,0:T(8,128)(2,1)S(1)}, bf16[256,1024]{1,0:T(8,128)(2,1)S(1)}, u32[]{:S(2)}, u32[]{:S(2)}) collective-permute-start(bf16[256,1024]{1,0:T(8,128)(2,1)S(1)} %shard_map.80.refs_2_), channel_id=1, source_target_pairs={{0,1},{1,0},{2,3},{3,2},{4,5},{5,4},{6,7},{7,6},{8,9},{9,8},{10,11... | collective-permute-start | bytes 1572872 | tf_op jit(solution)/shard_map/ppermute | solution.py:38
  23.5 0.1 collective-permute-start.8
  23.6 0.7 copy-done.1
  24.3 1.0 %collective-permute-start.1 = (bf16[128,1024]{1,0:T(8,128)(2,1)}, bf16[128,1024]{1,0:T(8,128)(2,1)}, u32[]{:S(2)}, u32[]{:S(2)}) collective-permute-start(bf16[128,1024]{1,0:T(8,128)(2,1)} %copy-done.3), channel_id=1, source_target_pairs={{0,2},{1,3},{2,4},{3,5},{4,6},{5,7},{6,0},{7,1},{8,10},{9,11},{10,... | collective-permute-start | bytes 786440 | tf_op jit(solution)/shard_map/ppermute | solution.py:38
  25.3 1.1 %all-to-all-done.refs_1_ = f32[32,1,1280]{2,1,0:T(1,128)S(1)} async-done(((f32[32,1,1280]{2,1,0:T(1,128)}), f32[32,1,1280]{2,1,0:T(1,128)S(1)}, u32[]{:S(2)}, u32[]{:S(2)}) %all-to-all-start) | async-done | bytes 163872 | tf_op jit(solution)/shard_map/all_to_all | solution.py:287
  26.4 0.9 %copy-done = bf16[128,1024]{1,0:T(8,128)(2,1)S(1)} copy-done((bf16[128,1024]{1,0:T(8,128)(2,1)S(1)}, bf16[128,1024]{1,0:T(8,128)(2,1)}, u32[]{:S(2)}) %copy-start) | copy-done | bytes 262168
  27.3 0.9 %copy-done.2 = bf16[128,1024]{1,0:T(8,128)(2,1)S(1)} copy-done((bf16[128,1024]{1,0:T(8,128)(2,1)S(1)}, bf16[128,1024]{1,0:T(8,128)(2,1)}, u32[]{:S(2)}) %copy-start.2) | copy-done | bytes 262168
  28.3 6.7 %shard_map.78.refs_11_ = f32[512,1152]{1,0:T(8,128)S(1)} custom-call(s32[10]{0:T(128)S(1)} %stack.43.refs_0_.start_ref, f32[32,1,1280]{2,1,0:T(1,128)S(1)} %all-to-all-done.refs_1_, bf16[128,1024]{1,0:T(8,128)(2,1)S(1)} %copy-done, bf16[128,1024]{1,0:T(8,128)(2,1)S(1)} %collective-permute-done.2.refs_3_, ...), custom_call_target="tpu_custom_call" | custom-call | flops 2415919104 | bytes 4718592 | tf_op jit(solution)/shard_map/pallas_call | solution.py:211
  35.0 0.1 collective-permute-done.1.refs_2_
  35.1 1.3 %collective-permute-done.12.refs_3_ = bf16[256,1024]{1,0:T(8,128)(2,1)S(1)} collective-permute-done((bf16[256,1024]{1,0:T(8,128)(2,1)S(1)}, bf16[256,1024]{1,0:T(8,128)(2,1)S(1)}, u32[]{:S(2)}, u32[]{:S(2)}) %collective-permute-start.12) | collective-permute-done | bytes 524320 | tf_op jit(solution)/shard_map/ppermute | solution.py:38
  36.4 0.6 collective-permute-start.15
  37.0 4.3 %shard_map.79.refs_10_ = bf16[2,2048,1152]{2,1,0:T(8,128)(2,1)S(1)} custom-call(s32[10]{0:T(128)S(1)} %stack.43.refs_0_.start_ref, bf16[8192,1152]{1,0:T(8,128)(2,1)} %head_ref.1), custom_call_target="tpu_custom_call" | custom-call | tf_op jit(solution)/shard_map/pallas_call | solution.py:116
  41.3 2.9 %shard_map.81.refs_10_ = bf16[1,2048,1152]{2,1,0:T(8,128)(2,1)S(1)} custom-call(s32[10]{0:T(128)S(1)} %stack.43.refs_0_.start_ref, bf16[8192,1152]{1,0:T(8,128)(2,1)} %head_ref.1), custom_call_target="tpu_custom_call" | custom-call | tf_op jit(solution)/shard_map/pallas_call | solution.py:116
  44.2 0.1 collective-permute-start.16
  44.3 0.5 collective-permute-start.17
  44.8 0.7 collective-permute-done.15.refs_5_
  45.5 0.7 collective-permute-start.10
  46.3 0.4 collective-permute-start.9
  46.7 0.3 collective-permute-done.17.refs_8_
  47.0 0.7 collective-permute-done.18.refs_9_
  47.7 4.2 %shard_map.82.refs_11_ = f32[512,1152]{1,0:T(8,128)S(1)} custom-call(s32[10]{0:T(128)S(1)} %stack.43.refs_0_.start_ref, f32[32,1,1280]{2,1,0:T(1,128)S(1)} %all-to-all-done.refs_1_, bf16[256,1024]{1,0:T(8,128)(2,1)S(1)} %shard_map.80.refs_2_, bf16[256,1024]{1,0:T(8,128)(2,1)S(1)} %collective-permute-done.12.refs_3_, ...), custom_call_target="tpu_custom_call" | custom-call | flops 2415919104 | bytes 4718592 | tf_op jit(solution)/shard_map/pallas_call | solution.py:211
  51.9 2.6 %collective-permute-done.10.refs_4_ = bf16[128,1024]{1,0:T(8,128)(2,1)S(1)} collective-permute-done((bf16[128,1024]{1,0:T(8,128)(2,1)}, bf16[128,1024]{1,0:T(8,128)(2,1)S(1)}, u32[]{:S(2)}, u32[]{:S(2)}) %collective-permute-start.10) | collective-permute-done | bytes 262176 | tf_op jit(solution)/shard_map/ppermute | solution.py:38
  54.5 0.7 collective-permute-start.19
  55.2 0.5 collective-permute-start.21
  55.7 4.2 %shard_map.83.refs_11_ = f32[512,1152]{1,0:T(8,128)S(1)} custom-call(s32[10]{0:T(128)S(1)} %stack.43.refs_0_.start_ref, f32[32,1,1280]{2,1,0:T(1,128)S(1)} %all-to-all-done.refs_1_, bf16[256,1024]{1,0:T(8,128)(2,1)S(1)} %shard_map.80.refs_2_, bf16[256,1024]{1,0:T(8,128)(2,1)S(1)} %collective-permute-done.12.refs_3_, ...), custom_call_target="tpu_custom_call" | custom-call | flops 2415919104 | bytes 4718592 | tf_op jit(solution)/shard_map/pallas_call | solution.py:211
  59.8 0.0 copy-start.4
  59.8 1.0 %collective-permute-done.19.refs_5_ = bf16[128,1024]{1,0:T(8,128)(2,1)S(1)} collective-permute-done((bf16[128,1024]{1,0:T(8,128)(2,1)S(1)}, bf16[128,1024]{1,0:T(8,128)(2,1)S(1)}, u32[]{:S(2)}, u32[]{:S(2)}) %collective-permute-start.19) | collective-permute-done | bytes 262176 | tf_op jit(solution)/shard_map/ppermute | solution.py:38
  60.9 1.5 %collective-permute-done.23.refs_9_ = bf16[128,1024]{1,0:T(8,128)(2,1)S(1)} collective-permute-done((bf16[128,1024]{1,0:T(8,128)(2,1)S(1)}, bf16[128,1024]{1,0:T(8,128)(2,1)S(1)}, u32[]{:S(2)}, u32[]{:S(2)}) %collective-permute-start.23) | collective-permute-done | bytes 262176 | tf_op jit(solution)/shard_map/ppermute | solution.py:38
  62.4 5.8 %shard_map.84 = f32[4,8,3,128]{3,2,1,0:T(4,128)} custom-call(s32[10]{0:T(128)S(1)} %stack.43.refs_0_.start_ref, f32[32,1,1280]{2,1,0:T(1,128)S(1)} %all-to-all-done.refs_1_, bf16[128,1024]{1,0:T(8,128)(2,1)} %collective-permute-done.1.refs_2_, bf16[128,1024]{1,0:T(8,128)(2,1)S(1)} %collective-permute-done.9.refs_3_, ...), custom_call_target="tpu_custom_call" | custom-call | flops 2415919104 | bytes 4718592 | tf_op jit(solution)/shard_map/pallas_call | solution.py:211
  68.2 2.5 %all-to-all-start.1 = ((f32[32,3,128]{2,1,0:T(4,128)}), f32[32,3,128]{2,1,0:T(4,128)S(1)}, u32[]{:S(2)}, u32[]{:S(2)}) async-start(f32[32,3,128]{2,1,0:T(4,128)} %bitcast.13), calls=%async_computation.1 | async-start | bytes 131072 | tf_op jit(solution)/shard_map/all_to_all | solution.py:316
  71.4 6.7 %all-to-all-done.1 = f32[32,3,128]{2,1,0:T(4,128)S(1)} async-done(((f32[32,3,128]{2,1,0:T(4,128)}), f32[32,3,128]{2,1,0:T(4,128)S(1)}, u32[]{:S(2)}, u32[]{:S(2)}) %all-to-all-start.1) | async-done | bytes 49184 | tf_op jit(solution)/shard_map/all_to_all | solution.py:316
  78.1 0.1 slice_reduce_fusion
  78.2 0.5 compare_select_fusion
  (27 shorter events, 0.1 us)
Async XLA Ops:
  0.6 10.2 %collective-permute-start.2 = (bf16[128,1024]{1,0:T(8,128)(2,1)}, bf16[128,1024]{1,0:T(8,128)(2,1)S(1)}, u32[]{:S(2)}, u32[]{:S(2)}) collective-permute-start(bf16[128,1024]{1,0:T(8,128)(2,1)} %refs_2_.1), channel_id=1, source_target_pairs={{0,8},{1,17},{2,10},{3,19},{4,12},{5,21},{6,14},{7,23},{8,0},{9,25... | collective-permute-start | bytes 786440 | tf_op jit(solution)/shard_map/ppermute | solution.py:38
  3.6 7.2 %collective-permute-start.3 = (bf16[128,1024]{1,0:T(8,128)(2,1)}, bf16[128,1024]{1,0:T(8,128)(2,1)S(1)}, u32[]{:S(2)}, u32[]{:S(2)}) collective-permute-start(bf16[128,1024]{1,0:T(8,128)(2,1)} %refs_2_.1), channel_id=1, source_target_pairs={{0,16},{1,9},{2,18},{3,11},{4,20},{5,13},{6,22},{7,15},{8,24},{9,1... | collective-permute-start | bytes 786440 | tf_op jit(solution)/shard_map/ppermute | solution.py:38
  5.2 16.5 %collective-permute-start.5 = (bf16[128,1024]{1,0:T(8,128)(2,1)}, bf16[128,1024]{1,0:T(8,128)(2,1)S(1)}, u32[]{:S(2)}, u32[]{:S(2)}) collective-permute-start(bf16[128,1024]{1,0:T(8,128)(2,1)} %refs_2_.1), channel_id=1, source_target_pairs={{0,1},{1,0},{2,3},{3,2},{4,5},{5,4},{6,7},{7,6},{8,9},{9,8},{10,11... | collective-permute-start | bytes 786440 | tf_op jit(solution)/shard_map/ppermute | solution.py:38
  5.2 12.8 %collective-permute-start = (bf16[128,1024]{1,0:T(8,128)(2,1)}, bf16[128,1024]{1,0:T(8,128)(2,1)S(1)}, u32[]{:S(2)}, u32[]{:S(2)}) collective-permute-start(bf16[128,1024]{1,0:T(8,128)(2,1)} %refs_2_.1), channel_id=1, source_target_pairs={{0,2},{1,3},{2,4},{3,5},{4,6},{5,7},{6,0},{7,1},{8,10},{9,11},{10,... | collective-permute-start | bytes 786440 | tf_op jit(solution)/shard_map/ppermute | solution.py:38
  6.7 14.4 %collective-permute-start.11 = (bf16[128,1024]{1,0:T(8,128)(2,1)}, bf16[128,1024]{1,0:T(8,128)(2,1)S(1)}, u32[]{:S(2)}, u32[]{:S(2)}) collective-permute-start(bf16[128,1024]{1,0:T(8,128)(2,1)} %refs_2_.1), channel_id=1, source_target_pairs={{0,6},{1,7},{2,0},{3,1},{4,2},{5,3},{6,4},{7,5},{8,14},{9,15},{10,... | collective-permute-start | bytes 786440 | tf_op jit(solution)/shard_map/ppermute | solution.py:38
  10.9 11.5 %collective-permute-start.4 = (bf16[128,1024]{1,0:T(8,128)(2,1)S(1)}, bf16[128,1024]{1,0:T(8,128)(2,1)S(1)}, u32[]{:S(2)}, u32[]{:S(2)}) collective-permute-start(bf16[128,1024]{1,0:T(8,128)(2,1)S(1)} %collective-permute-done.2.refs_3_), channel_id=1, source_target_pairs={{0,16},{1,9},{2,18},{3,11},{4,20},{5,13},{6,22},{7,15},{8,24},{9,1... | collective-permute-start | bytes 786440 | tf_op jit(solution)/shard_map/ppermute | solution.py:38
  12.0 11.5 %collective-permute-start.6 = (bf16[128,1024]{1,0:T(8,128)(2,1)S(1)}, bf16[128,1024]{1,0:T(8,128)(2,1)}, u32[]{:S(2)}, u32[]{:S(2)}) collective-permute-start(bf16[128,1024]{1,0:T(8,128)(2,1)S(1)} %collective-permute-done.2.refs_3_), channel_id=1, source_target_pairs={{0,1},{1,0},{2,3},{3,2},{4,5},{5,4},{6,7},{7,6},{8,9},{9,8},{10,11... | collective-permute-start | bytes 786440 | tf_op jit(solution)/shard_map/ppermute | solution.py:38
  12.9 13.5 %all-to-all-start = ((f32[32,1,1280]{2,1,0:T(1,128)}), f32[32,1,1280]{2,1,0:T(1,128)S(1)}, u32[]{:S(2)}, u32[]{:S(2)}) async-start(f32[32,1,1280]{2,1,0:T(1,128)} %shard_map.77), calls=%async_computation | async-start | bytes 327680 | tf_op jit(solution)/shard_map/all_to_all | solution.py:287
  17.9 3.7 %copy-start.3 = (bf16[128,1024]{1,0:T(8,128)(2,1)}, bf16[128,1024]{1,0:T(8,128)(2,1)S(1)}, u32[]{:S(2)}) copy-start(bf16[128,1024]{1,0:T(8,128)(2,1)S(1)} %collective-permute-done.refs_0_) | copy-start | bytes 786436
  21.2 15.2 %collective-permute-start.12 = (bf16[256,1024]{1,0:T(8,128)(2,1)S(1)}, bf16[256,1024]{1,0:T(8,128)(2,1)S(1)}, u32[]{:S(2)}, u32[]{:S(2)}) collective-permute-start(bf16[256,1024]{1,0:T(8,128)(2,1)S(1)} %shard_map.80.refs_2_), channel_id=1, source_target_pairs={{0,8},{1,17},{2,10},{3,19},{4,12},{5,21},{6,14},{7,23},{8,0},{9,25... | collective-permute-start | bytes 1572872 | tf_op jit(solution)/shard_map/ppermute | solution.py:38
  21.6 2.0 %collective-permute-start.7 = (bf16[128,1024]{1,0:T(8,128)(2,1)S(1)}, bf16[128,1024]{1,0:T(8,128)(2,1)S(1)}, u32[]{:S(2)}, u32[]{:S(2)}) collective-permute-start(bf16[128,1024]{1,0:T(8,128)(2,1)S(1)} %collective-permute-done.3.refs_4_), channel_id=1, source_target_pairs={{0,1},{1,0},{2,3},{3,2},{4,5},{5,4},{6,7},{7,6},{8,9},{9,8},{10,11... | collective-permute-start | bytes 786440 | tf_op jit(solution)/shard_map/ppermute | solution.py:38
  21.7 14.7 %collective-permute-start.13 = (bf16[256,1024]{1,0:T(8,128)(2,1)S(1)}, bf16[256,1024]{1,0:T(8,128)(2,1)S(1)}, u32[]{:S(2)}, u32[]{:S(2)}) collective-permute-start(bf16[256,1024]{1,0:T(8,128)(2,1)S(1)} %shard_map.80.refs_2_), channel_id=1, source_target_pairs={{0,16},{1,9},{2,18},{3,11},{4,20},{5,13},{6,22},{7,15},{8,24},{9,1... | collective-permute-start | bytes 1572872 | tf_op jit(solution)/shard_map/ppermute | solution.py:38
  22.4 14.0 %collective-permute-start.14 = (bf16[256,1024]{1,0:T(8,128)(2,1)S(1)}, bf16[256,1024]{1,0:T(8,128)(2,1)S(1)}, u32[]{:S(2)}, u32[]{:S(2)}) collective-permute-start(bf16[256,1024]{1,0:T(8,128)(2,1)S(1)} %shard_map.80.refs_2_), channel_id=1, source_target_pairs={{0,1},{1,0},{2,3},{3,2},{4,5},{5,4},{6,7},{7,6},{8,9},{9,8},{10,11... | collective-permute-start | bytes 1572872 | tf_op jit(solution)/shard_map/ppermute | solution.py:38
  23.5 2.8 %collective-permute-start.8 = (bf16[128,1024]{1,0:T(8,128)(2,1)S(1)}, bf16[128,1024]{1,0:T(8,128)(2,1)}, u32[]{:S(2)}, u32[]{:S(2)}) collective-permute-start(bf16[128,1024]{1,0:T(8,128)(2,1)S(1)} %collective-permute-done.4.refs_5_), channel_id=1, source_target_pairs={{0,1},{1,0},{2,3},{3,2},{4,5},{5,4},{6,7},{7,6},{8,9},{9,8},{10,11... | collective-permute-start | bytes 786440 | tf_op jit(solution)/shard_map/ppermute | solution.py:38
  23.6 0.7 copy-start.1
  24.3 10.8 %collective-permute-start.1 = (bf16[128,1024]{1,0:T(8,128)(2,1)}, bf16[128,1024]{1,0:T(8,128)(2,1)}, u32[]{:S(2)}, u32[]{:S(2)}) collective-permute-start(bf16[128,1024]{1,0:T(8,128)(2,1)} %copy-done.3), channel_id=1, source_target_pairs={{0,2},{1,3},{2,4},{3,5},{4,6},{5,7},{6,0},{7,1},{8,10},{9,11},{10,... | collective-permute-start | bytes 786440 | tf_op jit(solution)/shard_map/ppermute | solution.py:38
  26.4 1.0 %copy-start = (bf16[128,1024]{1,0:T(8,128)(2,1)S(1)}, bf16[128,1024]{1,0:T(8,128)(2,1)}, u32[]{:S(2)}) copy-start(bf16[128,1024]{1,0:T(8,128)(2,1)} %refs_2_.1) | copy-start | bytes 786436
  27.3 0.9 %copy-start.2 = (bf16[128,1024]{1,0:T(8,128)(2,1)S(1)}, bf16[128,1024]{1,0:T(8,128)(2,1)}, u32[]{:S(2)}) copy-start(bf16[128,1024]{1,0:T(8,128)(2,1)} %copy-done.1) | copy-start | bytes 786436
  36.4 9.2 %collective-permute-start.15 = (bf16[256,1024]{1,0:T(8,128)(2,1)S(1)}, bf16[256,1024]{1,0:T(8,128)(2,1)S(1)}, u32[]{:S(2)}, u32[]{:S(2)}) collective-permute-start(bf16[256,1024]{1,0:T(8,128)(2,1)S(1)} %collective-permute-done.12.refs_3_), channel_id=1, source_target_pairs={{0,16},{1,9},{2,18},{3,11},{4,20},{5,13},{6,22},{7,15},{8,24},{9,1... | collective-permute-start | bytes 1572872 | tf_op jit(solution)/shard_map/ppermute | solution.py:38
  44.2 2.4 %collective-permute-start.16 = (bf16[256,1024]{1,0:T(8,128)(2,1)S(1)}, bf16[256,1024]{1,0:T(8,128)(2,1)S(1)}, u32[]{:S(2)}, u32[]{:S(2)}) collective-permute-start(bf16[256,1024]{1,0:T(8,128)(2,1)S(1)} %collective-permute-done.12.refs_3_), channel_id=1, source_target_pairs={{0,1},{1,0},{2,3},{3,2},{4,5},{5,4},{6,7},{7,6},{8,9},{9,8},{10,11... | collective-permute-start | bytes 1572872 | tf_op jit(solution)/shard_map/ppermute | solution.py:38
  44.3 2.6 %collective-permute-start.17 = (bf16[256,1024]{1,0:T(8,128)(2,1)S(1)}, bf16[256,1024]{1,0:T(8,128)(2,1)S(1)}, u32[]{:S(2)}, u32[]{:S(2)}) collective-permute-start(bf16[256,1024]{1,0:T(8,128)(2,1)S(1)} %collective-permute-done.13.refs_4_), channel_id=1, source_target_pairs={{0,1},{1,0},{2,3},{3,2},{4,5},{5,4},{6,7},{7,6},{8,9},{9,8},{10,11... | collective-permute-start | bytes 1572872 | tf_op jit(solution)/shard_map/ppermute | solution.py:38
  45.5 2.2 %collective-permute-start.18 = (bf16[256,1024]{1,0:T(8,128)(2,1)S(1)}, bf16[256,1024]{1,0:T(8,128)(2,1)S(1)}, u32[]{:S(2)}, u32[]{:S(2)}) collective-permute-start(bf16[256,1024]{1,0:T(8,128)(2,1)S(1)} %collective-permute-done.15.refs_5_), channel_id=1, source_target_pairs={{0,1},{1,0},{2,3},{3,2},{4,5},{5,4},{6,7},{7,6},{8,9},{9,8},{10,11... | collective-permute-start | bytes 1572872 | tf_op jit(solution)/shard_map/ppermute | solution.py:38
  45.5 8.9 %collective-permute-start.10 = (bf16[128,1024]{1,0:T(8,128)(2,1)}, bf16[128,1024]{1,0:T(8,128)(2,1)S(1)}, u32[]{:S(2)}, u32[]{:S(2)}) collective-permute-start(bf16[128,1024]{1,0:T(8,128)(2,1)} %collective-permute-done.1.refs_2_), channel_id=1, source_target_pairs={{0,16},{1,9},{2,18},{3,11},{4,20},{5,13},{6,22},{7,15},{8,24},{9,1... | collective-permute-start | bytes 786440 | tf_op jit(solution)/shard_map/ppermute | solution.py:38
  46.3 8.2 %collective-permute-start.9 = (bf16[128,1024]{1,0:T(8,128)(2,1)}, bf16[128,1024]{1,0:T(8,128)(2,1)S(1)}, u32[]{:S(2)}, u32[]{:S(2)}) collective-permute-start(bf16[128,1024]{1,0:T(8,128)(2,1)} %collective-permute-done.1.refs_2_), channel_id=1, source_target_pairs={{0,8},{1,17},{2,10},{3,19},{4,12},{5,21},{6,14},{7,23},{8,0},{9,25... | collective-permute-start | bytes 786440 | tf_op jit(solution)/shard_map/ppermute | solution.py:38
  54.5 6.4 %collective-permute-start.19 = (bf16[128,1024]{1,0:T(8,128)(2,1)S(1)}, bf16[128,1024]{1,0:T(8,128)(2,1)S(1)}, u32[]{:S(2)}, u32[]{:S(2)}) collective-permute-start(bf16[128,1024]{1,0:T(8,128)(2,1)S(1)} %collective-permute-done.9.refs_3_), channel_id=1, source_target_pairs={{0,16},{1,9},{2,18},{3,11},{4,20},{5,13},{6,22},{7,15},{8,24},{9,1... | collective-permute-start | bytes 786440 | tf_op jit(solution)/shard_map/ppermute | solution.py:38
  55.1 5.7 %collective-permute-start.20 = (bf16[128,1024]{1,0:T(8,128)(2,1)}, bf16[128,1024]{1,0:T(8,128)(2,1)S(1)}, u32[]{:S(2)}, u32[]{:S(2)}) collective-permute-start(bf16[128,1024]{1,0:T(8,128)(2,1)} %collective-permute-done.1.refs_2_), channel_id=1, source_target_pairs={{0,1},{1,0},{2,3},{3,2},{4,5},{5,4},{6,7},{7,6},{8,9},{9,8},{10,11... | collective-permute-start | bytes 786440 | tf_op jit(solution)/shard_map/ppermute | solution.py:38
  55.2 5.7 %collective-permute-start.21 = (bf16[128,1024]{1,0:T(8,128)(2,1)S(1)}, bf16[128,1024]{1,0:T(8,128)(2,1)S(1)}, u32[]{:S(2)}, u32[]{:S(2)}) collective-permute-start(bf16[128,1024]{1,0:T(8,128)(2,1)S(1)} %collective-permute-done.9.refs_3_), channel_id=1, source_target_pairs={{0,1},{1,0},{2,3},{3,2},{4,5},{5,4},{6,7},{7,6},{8,9},{9,8},{10,11... | collective-permute-start | bytes 786440 | tf_op jit(solution)/shard_map/ppermute | solution.py:38
  55.7 5.2 %collective-permute-start.22 = (bf16[128,1024]{1,0:T(8,128)(2,1)S(1)}, bf16[128,1024]{1,0:T(8,128)(2,1)S(1)}, u32[]{:S(2)}, u32[]{:S(2)}) collective-permute-start(bf16[128,1024]{1,0:T(8,128)(2,1)S(1)} %collective-permute-done.10.refs_4_), channel_id=1, source_target_pairs={{0,1},{1,0},{2,3},{3,2},{4,5},{5,4},{6,7},{7,6},{8,9},{9,8},{10,11... | collective-permute-start | bytes 786440 | tf_op jit(solution)/shard_map/ppermute | solution.py:38
  59.8 18.4 %copy-start.4 = (f32[128]{0:T(128)S(1)}, f32[128]{0:T(128)}, u32[]{:S(2)}) copy-start(f32[128]{0:T(128)} %param.10) | copy-start | bytes 1540
  60.9 1.5 %collective-permute-start.23 = (bf16[128,1024]{1,0:T(8,128)(2,1)S(1)}, bf16[128,1024]{1,0:T(8,128)(2,1)S(1)}, u32[]{:S(2)}, u32[]{:S(2)}) collective-permute-start(bf16[128,1024]{1,0:T(8,128)(2,1)S(1)} %collective-permute-done.19.refs_5_), channel_id=1, source_target_pairs={{0,1},{1,0},{2,3},{3,2},{4,5},{5,4},{6,7},{7,6},{8,9},{9,8},{10,11... | collective-permute-start | bytes 786440 | tf_op jit(solution)/shard_map/ppermute | solution.py:38
  68.2 9.9 %all-to-all-start.1 = ((f32[32,3,128]{2,1,0:T(4,128)}), f32[32,3,128]{2,1,0:T(4,128)S(1)}, u32[]{:S(2)}, u32[]{:S(2)}) async-start(f32[32,3,128]{2,1,0:T(4,128)} %bitcast.13), calls=%async_computation.1 | async-start | bytes 131072 | tf_op jit(solution)/shard_map/all_to_all | solution.py:316

commit v10 on v9

--- a/solution.py
+++ b/solution.py
@@ -63,6 +63,16 @@
             for i in range(1, self.cols):
                 got[j, i] = self.plane(after(got[0, i], *late), self.second, j)
         return [got[s] for s in self.spots]
+
+    def leap(self, got):
+        def place_of(j, i):
+            def place(y, x, z, c):
+                (fy, fx), (sy, sx) = self.first[c], self.second[c]
+                return y + fy * i + sy * j, x + fx * i + sx * j, z, c
+
+            return place
+
+        return [got[s] if s in got else self.permute(got[0, 0], place_of(*s)) for s in self.spots]
 
     def owners(self, y, x, c):
         ways = [(self.first[k], self.second[k]) for k in range(CORES)]
@@ -186,10 +196,10 @@
         target = fine[owners[b] * n_t, :, feat + tok : feat + 2 * tok]
         target = to_column(target).astype(jnp.int32)
         pick = jnp.sum(jnp.where(entry == target, logits, 0.0), axis=1, keepdims=True)
+        stats = [to_row(top), to_row(total), to_row(pick)]
         for peer in range(n_t):
-            out_ref[owners[b], peer, 0:1, :] = to_row(top)
-            out_ref[owners[b], peer, 1:2, :] = to_row(total)
-            out_ref[owners[b], peer, 2:3, :] = to_row(pick)
+            for i, row in enumerate(stats):
+                out_ref[owners[b], peer, i : i + 1, :] = row
 
 
 def layer_product(tok, n_t, starts, layer, offset, fine, blocks, place, weights, acc, last):
@@ -286,30 +296,28 @@
     packed = squares(after(hidden, starts), norm_gain[None, :], targets[None, :], n_dp * n_t)
     fine = lax.all_to_all(packed, ("dp", "tensor"), 0, 0, tiled=True)
 
-    acc, deep, half = None, CORES * feat, []
+    acc, deep = None, CORES * feat
     for at, group in enumerate(groups):
         final = at == len(groups) - 1
         middle = at and not final
         offsets = [2 + n_dp + dz for dz in group]
         own = grid.sibling(reached[at][0, 0])
-        held = [acc, own, *(layers[dz] for dz in groups[2])] if at == 1 else half if at else [packed]
-        spread = grid.fill(dict(reached[at]), *held)
+        held = [acc, own, *(layers[dz] for dz in groups[2])] if at == 1 else [] if at else [packed]
+        spread = grid.leap(reached[at]) if final else grid.fill(dict(reached[at]), *held)
+        early = [grid.sibling(after(a, acc)) for a in spread[1:-1]] if middle else []
         if at == 0:
             weights = [head]
         elif at == 1:
             for later in groups[1:]:
-                ready = after(head, acc, *(layers[dz] for dz in groups[2]))
+                ready = after(head, acc, *early, *(layers[dz] for dz in groups[2]))
                 weights.append(loaded(starts, [2 + n_dp + dz for dz in later], ready, deep))
         if at:
             reach_next(at + 1, weights[1] if at == 1 else spread[-1])
-        others = [own] + [grid.sibling(a) for a in spread[1:-1]]
+        others = [own] + (early or [grid.sibling(after(a, acc) if final else a) for a in spread[1:-1]])
         others.append(grid.sibling(after(spread[-1], *([acc] if final else weights[1:3] if middle else []))))
         blocks = spread + others
         for layer, offset in enumerate(offsets):
             done = layer == len(offsets) - 1
-            if middle and done:
-                half = [acc]
-                blocks[0] = after(blocks[0], *reached[at + 1].values())
             last = final and done
             acc = layer_product(tok, n_t, starts, layer, offset, fine, blocks, place, weights[at], acc, last)
 

time: 79.2 us -> 80.9 us (1.021)
  starting transfers between devices: 24.8 us -> 28.2 us
  waiting for transfers between devices: 19.4 us -> 17.7 us
    ppermute x24, starting transfers between devices: 17.2 us -> 19.3 us  [permute(): return lax.ppermute(a, ('dp', 'tensor'), perm)]
    ppermute x24, waiting for transfers between devices: 11.5 us -> 10.1 us  [permute(): return lax.ppermute(a, ('dp', 'tensor'), perm)]
    all_to_all x1, starting transfers between devices: 2.55 us -> 3.85 us  [body(): lax.all_to_all(acc.reshape(n_dp * n_t, 3, tok), ('dp', 'tensor'), 0, 0, t...]
  transfers between devices with their start and end apart: 26 -> 26, of which waited for: 11 -> 10; matrix products, arithmetic and copies ran while one was open for 0% -> 0% of each run, Pallas kernels for 31% -> 30%
where the time goes in v10:
time: 80.9 us; the launch traced here: 80.5 us
  Pallas kernels  29.8 us (37%)
  starting transfers between devices  28.2 us (35%)
  waiting for transfers between devices  17.7 us (22%)
  local copies, waits for them, and re-layouts  2.71 us (3%)
  between operations  1.43 us (2%)
    pallas_call x4, Pallas kernels, layer_product(): pl.pallas_call(functools.partial(layer_kernel, n, n_t, place, layer, offs...  20.8 us
    ppermute x24, starting transfers between devices, permute(): return lax.ppermute(a, ('dp', 'tensor'), perm)  19.3 us
    ppermute x24, waiting for transfers between devices, permute(): return lax.ppermute(a, ('dp', 'tensor'), perm)  10.1 us
    pallas_call x2, Pallas kernels, loaded(): pl.pallas_call(functools.partial(load_kernel, offsets), out_shape=pltpu.V...  7.23 us
    all_to_all x1, waiting for transfers between devices, body(): lax.all_to_all(acc.reshape(n_dp * n_t, 3, tok), ('dp', 'tensor'), 0, 0, t...  6.74 us
    all_to_all x1, starting transfers between devices, body(): fine = lax.all_to_all(packed, ('dp', 'tensor'), 0, 0, tiled=True)  5.04 us
    all_to_all x1, starting transfers between devices, body(): lax.all_to_all(acc.reshape(n_dp * n_t, 3, tok), ('dp', 'tensor'), 0, 0, t...  3.85 us
    unnamed x10, local copies, waits for them, and re-layouts  2.62 us
  transfers between devices with their start and end apart: 26, of which 10 were waited for; matrix products, arithmetic and copies ran while one was open for 0% of the time, Pallas kernels for 30%

profile of v10, /device:TPU:0, one launch (start us, length us, event | category | flops | bytes accessed | tf_op | source)
XLA Modules:
  0.0 80.5 jit_solution(5903876899537760160)
XLA Ops:
  0.6 3.0 %collective-permute-start.2 = (bf16[128,1024]{1,0:T(8,128)(2,1)}, bf16[128,1024]{1,0:T(8,128)(2,1)S(1)}, u32[]{:S(2)}, u32[]{:S(2)}) collective-permute-start(bf16[128,1024]{1,0:T(8,128)(2,1)} %refs_2_.1), channel_id=1, source_target_pairs={{0,8},{1,17},{2,10},{3,19},{4,12},{5,21},{6,14},{7,23},{8,0},{9,25... | collective-permute-start | bytes 786440 | tf_op jit(solution)/shard_map/ppermute | solution.py:38
  3.6 1.5 %collective-permute-start.3 = (bf16[128,1024]{1,0:T(8,128)(2,1)}, bf16[128,1024]{1,0:T(8,128)(2,1)S(1)}, u32[]{:S(2)}, u32[]{:S(2)}) collective-permute-start(bf16[128,1024]{1,0:T(8,128)(2,1)} %refs_2_.1), channel_id=1, source_target_pairs={{0,16},{1,9},{2,18},{3,11},{4,20},{5,13},{6,22},{7,15},{8,24},{9,1... | collective-permute-start | bytes 786440 | tf_op jit(solution)/shard_map/ppermute | solution.py:38
  5.2 0.0 collective-permute-start.5
  5.2 1.6 %collective-permute-start = (bf16[128,1024]{1,0:T(8,128)(2,1)}, bf16[128,1024]{1,0:T(8,128)(2,1)S(1)}, u32[]{:S(2)}, u32[]{:S(2)}) collective-permute-start(bf16[128,1024]{1,0:T(8,128)(2,1)} %refs_2_.1), channel_id=1, source_target_pairs={{0,2},{1,3},{2,4},{3,5},{4,6},{5,7},{6,0},{7,1},{8,10},{9,11},{10,... | collective-permute-start | bytes 786440 | tf_op jit(solution)/shard_map/ppermute | solution.py:38
  6.7 2.2 %collective-permute-start.9 = (bf16[128,1024]{1,0:T(8,128)(2,1)}, bf16[128,1024]{1,0:T(8,128)(2,1)S(1)}, u32[]{:S(2)}, u32[]{:S(2)}) collective-permute-start(bf16[128,1024]{1,0:T(8,128)(2,1)} %refs_2_.1), channel_id=1, source_target_pairs={{0,6},{1,7},{2,0},{3,1},{4,2},{5,3},{6,4},{7,5},{8,14},{9,15},{10,... | collective-permute-start | bytes 786440 | tf_op jit(solution)/shard_map/ppermute | solution.py:38
  9.0 0.1 stack.43.refs_0_.start_ref
  9.1 1.8 %shard_map.77 = f32[32,1,1280]{2,1,0:T(1,128)} custom-call(bf16[128,1024]{1,0:T(8,128)(2,1)} %refs_2_.1, f32[1,1024]{1,0:T(1,128)} %bitcast.22, s32[1,128]{1,0:T(1,128)} %bitcast.23), custom_call_target="tpu_custom_call" | custom-call | tf_op jit(solution)/shard_map/pallas_call | solution.py:253
  10.9 0.0 collective-permute-done.2.refs_3_
  10.9 1.1 %collective-permute-start.4 = (bf16[128,1024]{1,0:T(8,128)(2,1)S(1)}, bf16[128,1024]{1,0:T(8,128)(2,1)S(1)}, u32[]{:S(2)}, u32[]{:S(2)}) collective-permute-start(bf16[128,1024]{1,0:T(8,128)(2,1)S(1)} %collective-permute-done.2.refs_3_), channel_id=1, source_target_pairs={{0,16},{1,9},{2,18},{3,11},{4,20},{5,13},{6,22},{7,15},{8,24},{9,1... | collective-permute-start | bytes 786440 | tf_op jit(solution)/shard_map/ppermute | solution.py:38
  12.0 0.9 %collective-permute-start.6 = (bf16[128,1024]{1,0:T(8,128)(2,1)S(1)}, bf16[128,1024]{1,0:T(8,128)(2,1)}, u32[]{:S(2)}, u32[]{:S(2)}) collective-permute-start(bf16[128,1024]{1,0:T(8,128)(2,1)S(1)} %collective-permute-done.2.refs_3_), channel_id=1, source_target_pairs={{0,1},{1,0},{2,3},{3,2},{4,5},{5,4},{6,7},{7,6},{8,9},{9,8},{10,11... | collective-permute-start | bytes 786440 | tf_op jit(solution)/shard_map/ppermute | solution.py:38
  12.9 5.0 %all-to-all-start = ((f32[32,1,1280]{2,1,0:T(1,128)}), f32[32,1,1280]{2,1,0:T(1,128)S(1)}, u32[]{:S(2)}, u32[]{:S(2)}) async-start(f32[32,1,1280]{2,1,0:T(1,128)} %shard_map.77), calls=%async_computation | async-start | bytes 327680 | tf_op jit(solution)/shard_map/all_to_all | solution.py:297
  17.9 3.2 %collective-permute-done.9.refs_1_ = bf16[128,1024]{1,0:T(8,128)(2,1)S(1)} collective-permute-done((bf16[128,1024]{1,0:T(8,128)(2,1)}, bf16[128,1024]{1,0:T(8,128)(2,1)S(1)}, u32[]{:S(2)}, u32[]{:S(2)}) %collective-permute-start.9) | collective-permute-done | bytes 262176 | tf_op jit(solution)/shard_map/ppermute | solution.py:38
  21.2 0.4 collective-permute-start.12
  21.6 0.5 collective-permute-start.10
  22.2 0.5 collective-permute-start.18
  22.7 0.1 collective-permute-start.8
  22.7 0.9 %collective-permute-done.7.refs_8_ = bf16[128,1024]{1,0:T(8,128)(2,1)S(1)} collective-permute-done((bf16[128,1024]{1,0:T(8,128)(2,1)S(1)}, bf16[128,1024]{1,0:T(8,128)(2,1)S(1)}, u32[]{:S(2)}, u32[]{:S(2)}) %collective-permute-start.7) | collective-permute-done | bytes 262176 | tf_op jit(solution)/shard_map/ppermute | solution.py:38
  23.7 0.7 copy-done.1
  24.4 1.2 %collective-permute-start.1 = (bf16[128,1024]{1,0:T(8,128)(2,1)}, bf16[128,1024]{1,0:T(8,128)(2,1)}, u32[]{:S(2)}, u32[]{:S(2)}) collective-permute-start(bf16[128,1024]{1,0:T(8,128)(2,1)} %copy-done.3), channel_id=1, source_target_pairs={{0,2},{1,3},{2,4},{3,5},{4,6},{5,7},{6,0},{7,1},{8,10},{9,11},{10,... | collective-permute-start | bytes 786440 | tf_op jit(solution)/shard_map/ppermute | solution.py:38
  25.6 0.8 %all-to-all-done.refs_1_ = f32[32,1,1280]{2,1,0:T(1,128)S(1)} async-done(((f32[32,1,1280]{2,1,0:T(1,128)}), f32[32,1,1280]{2,1,0:T(1,128)S(1)}, u32[]{:S(2)}, u32[]{:S(2)}) %all-to-all-start) | async-done | bytes 163872 | tf_op jit(solution)/shard_map/all_to_all | solution.py:297
  26.4 0.9 %copy-done = bf16[128,1024]{1,0:T(8,128)(2,1)S(1)} copy-done((bf16[128,1024]{1,0:T(8,128)(2,1)S(1)}, bf16[128,1024]{1,0:T(8,128)(2,1)}, u32[]{:S(2)}) %copy-start) | copy-done | bytes 262168
  27.3 0.9 %copy-done.2 = bf16[128,1024]{1,0:T(8,128)(2,1)S(1)} copy-done((bf16[128,1024]{1,0:T(8,128)(2,1)S(1)}, bf16[128,1024]{1,0:T(8,128)(2,1)}, u32[]{:S(2)}) %copy-start.2) | copy-done | bytes 262168
  28.3 6.7 %shard_map.78.refs_11_ = f32[512,1152]{1,0:T(8,128)S(1)} custom-call(s32[10]{0:T(128)S(1)} %stack.43.refs_0_.start_ref, f32[32,1,1280]{2,1,0:T(1,128)S(1)} %all-to-all-done.refs_1_, bf16[128,1024]{1,0:T(8,128)(2,1)S(1)} %copy-done, bf16[128,1024]{1,0:T(8,128)(2,1)S(1)} %collective-permute-done.2.refs_3_, ...), custom_call_target="tpu_custom_call" | custom-call | flops 2415919104 | bytes 4718592 | tf_op jit(solution)/shard_map/pallas_call | solution.py:221
  35.0 0.5 collective-permute-done.12.refs_4_
  35.5 0.2 collective-permute-start.13
  35.7 0.3 collective-permute-start.11
  36.0 0.9 %collective-permute-start.19 = (bf16[256,1024]{1,0:T(8,128)(2,1)S(1)}, bf16[256,1024]{1,0:T(8,128)(2,1)S(1)}, u32[]{:S(2)}, u32[]{:S(2)}) collective-permute-start(bf16[256,1024]{1,0:T(8,128)(2,1)S(1)} %collective-permute-done.10.refs_3_), channel_id=1, source_target_pairs={{0,16},{1,9},{2,18},{3,11},{4,20},{5,13},{6,22},{7,15},{8,24},{9,1... | collective-permute-start | bytes 1572872 | tf_op jit(solution)/shard_map/ppermute | solution.py:38
  36.8 0.5 collective-permute-done.13.refs_8_
  37.4 0.7 collective-permute-done.11.refs_7_
  38.1 4.3 %shard_map.80.refs_10_ = bf16[2,2048,1152]{2,1,0:T(8,128)(2,1)S(1)} custom-call(s32[10]{0:T(128)S(1)} %stack.43.refs_0_.start_ref, bf16[8192,1152]{1,0:T(8,128)(2,1)} %head_ref.1), custom_call_target="tpu_custom_call" | custom-call | tf_op jit(solution)/shard_map/pallas_call | solution.py:126
  42.5 2.9 %shard_map.81.refs_10_ = bf16[1,2048,1152]{2,1,0:T(8,128)(2,1)S(1)} custom-call(s32[10]{0:T(128)S(1)} %stack.43.refs_0_.start_ref, bf16[8192,1152]{1,0:T(8,128)(2,1)} %head_ref.1), custom_call_target="tpu_custom_call" | custom-call | tf_op jit(solution)/shard_map/pallas_call | solution.py:126
  45.4 0.3 collective-permute-start.20
  45.7 1.2 %collective-permute-start.16 = (bf16[128,1024]{1,0:T(8,128)(2,1)}, bf16[128,1024]{1,0:T(8,128)(2,1)S(1)}, u32[]{:S(2)}, u32[]{:S(2)}) collective-permute-start(bf16[128,1024]{1,0:T(8,128)(2,1)} %collective-permute-done.1.refs_2_), channel_id=1, source_target_pairs={{0,24},{1,25},{2,26},{3,27},{4,28},{5,29},{6,30},{7,31},{8,16},{9,... | collective-permute-start | bytes 786440 | tf_op jit(solution)/shard_map/ppermute | solution.py:38
  46.9 1.5 %collective-permute-start.15 = (bf16[128,1024]{1,0:T(8,128)(2,1)}, bf16[128,1024]{1,0:T(8,128)(2,1)S(1)}, u32[]{:S(2)}, u32[]{:S(2)}) collective-permute-start(bf16[128,1024]{1,0:T(8,128)(2,1)} %collective-permute-done.1.refs_2_), channel_id=1, source_target_pairs={{0,16},{1,9},{2,18},{3,11},{4,20},{5,13},{6,22},{7,15},{8,24},{9,1... | collective-permute-start | bytes 786440 | tf_op jit(solution)/shard_map/ppermute | solution.py:38
  48.4 0.7 collective-permute-start.14
  49.2 4.2 %shard_map.82.refs_11_ = f32[512,1152]{1,0:T(8,128)S(1)} custom-call(s32[10]{0:T(128)S(1)} %stack.43.refs_0_.start_ref, f32[32,1,1280]{2,1,0:T(1,128)S(1)} %all-to-all-done.refs_1_, bf16[256,1024]{1,0:T(8,128)(2,1)S(1)} %shard_map.79.refs_2_, bf16[256,1024]{1,0:T(8,128)(2,1)S(1)} %collective-permute-done.10.refs_3_, ...), custom_call_target="tpu_custom_call" | custom-call | flops 2415919104 | bytes 4718592 | tf_op jit(solution)/shard_map/pallas_call | solution.py:221
  53.3 4.2 %shard_map.83.refs_11_ = f32[512,1152]{1,0:T(8,128)S(1)} custom-call(s32[10]{0:T(128)S(1)} %stack.43.refs_0_.start_ref, f32[32,1,1280]{2,1,0:T(1,128)S(1)} %all-to-all-done.refs_1_, bf16[256,1024]{1,0:T(8,128)(2,1)S(1)} %shard_map.79.refs_2_, bf16[256,1024]{1,0:T(8,128)(2,1)S(1)} %collective-permute-done.10.refs_3_, ...), custom_call_target="tpu_custom_call" | custom-call | flops 2415919104 | bytes 4718592 | tf_op jit(solution)/shard_map/pallas_call | solution.py:221
  57.5 0.0 copy-start.4
  57.5 0.6 collective-permute-start.23
  58.1 2.8 %collective-permute-done.15.refs_4_ = bf16[128,1024]{1,0:T(8,128)(2,1)S(1)} collective-permute-done((bf16[128,1024]{1,0:T(8,128)(2,1)}, bf16[128,1024]{1,0:T(8,128)(2,1)S(1)}, u32[]{:S(2)}, u32[]{:S(2)}) %collective-permute-start.15) | collective-permute-done | bytes 262176 | tf_op jit(solution)/shard_map/ppermute | solution.py:38
  60.9 0.5 collective-permute-start.21
  61.4 1.0 %collective-permute-done.22.refs_8_ = bf16[128,1024]{1,0:T(8,128)(2,1)S(1)} collective-permute-done((bf16[128,1024]{1,0:T(8,128)(2,1)S(1)}, bf16[128,1024]{1,0:T(8,128)(2,1)S(1)}, u32[]{:S(2)}, u32[]{:S(2)}) %collective-permute-start.22) | collective-permute-done | bytes 262176 | tf_op jit(solution)/shard_map/ppermute | solution.py:38
  62.4 0.4 collective-permute-done.21.refs_7_
  62.8 5.8 %shard_map.84 = f32[4,8,3,128]{3,2,1,0:T(4,128)} custom-call(s32[10]{0:T(128)S(1)} %stack.43.refs_0_.start_ref, f32[32,1,1280]{2,1,0:T(1,128)S(1)} %all-to-all-done.refs_1_, bf16[128,1024]{1,0:T(8,128)(2,1)} %collective-permute-done.1.refs_2_, bf16[128,1024]{1,0:T(8,128)(2,1)S(1)} %collective-permute-done.14.refs_3_, ...), custom_call_target="tpu_custom_call" | custom-call | flops 2415919104 | bytes 4718592 | tf_op jit(solution)/shard_map/pallas_call | solution.py:221
  68.6 3.8 %all-to-all-start.1 = ((f32[32,3,128]{2,1,0:T(4,128)}), f32[32,3,128]{2,1,0:T(4,128)S(1)}, u32[]{:S(2)}, u32[]{:S(2)}) async-start(f32[32,3,128]{2,1,0:T(4,128)} %bitcast.13), calls=%async_computation.1 | async-start | bytes 131072 | tf_op jit(solution)/shard_map/all_to_all | solution.py:324
  73.1 6.7 %all-to-all-done.1 = f32[32,3,128]{2,1,0:T(4,128)S(1)} async-done(((f32[32,3,128]{2,1,0:T(4,128)}), f32[32,3,128]{2,1,0:T(4,128)S(1)}, u32[]{:S(2)}, u32[]{:S(2)}) %all-to-all-start.1) | async-done | bytes 49184 | tf_op jit(solution)/shard_map/all_to_all | solution.py:324
  79.8 0.1 slice_reduce_fusion
  79.9 0.5 compare_select_fusion
  (27 shorter events, 0.1 us)
Async XLA Ops:
  0.6 10.2 %collective-permute-start.2 = (bf16[128,1024]{1,0:T(8,128)(2,1)}, bf16[128,1024]{1,0:T(8,128)(2,1)S(1)}, u32[]{:S(2)}, u32[]{:S(2)}) collective-permute-start(bf16[128,1024]{1,0:T(8,128)(2,1)} %refs_2_.1), channel_id=1, source_target_pairs={{0,8},{1,17},{2,10},{3,19},{4,12},{5,21},{6,14},{7,23},{8,0},{9,25... | collective-permute-start | bytes 786440 | tf_op jit(solution)/shard_map/ppermute | solution.py:38
  3.6 7.2 %collective-permute-start.3 = (bf16[128,1024]{1,0:T(8,128)(2,1)}, bf16[128,1024]{1,0:T(8,128)(2,1)S(1)}, u32[]{:S(2)}, u32[]{:S(2)}) collective-permute-start(bf16[128,1024]{1,0:T(8,128)(2,1)} %refs_2_.1), channel_id=1, source_target_pairs={{0,16},{1,9},{2,18},{3,11},{4,20},{5,13},{6,22},{7,15},{8,24},{9,1... | collective-permute-start | bytes 786440 | tf_op jit(solution)/shard_map/ppermute | solution.py:38
  5.2 17.0 %collective-permute-start.5 = (bf16[128,1024]{1,0:T(8,128)(2,1)}, bf16[128,1024]{1,0:T(8,128)(2,1)S(1)}, u32[]{:S(2)}, u32[]{:S(2)}) collective-permute-start(bf16[128,1024]{1,0:T(8,128)(2,1)} %refs_2_.1), channel_id=1, source_target_pairs={{0,1},{1,0},{2,3},{3,2},{4,5},{5,4},{6,7},{7,6},{8,9},{9,8},{10,11... | collective-permute-start | bytes 786440 | tf_op jit(solution)/shard_map/ppermute | solution.py:38
  5.2 12.8 %collective-permute-start = (bf16[128,1024]{1,0:T(8,128)(2,1)}, bf16[128,1024]{1,0:T(8,128)(2,1)S(1)}, u32[]{:S(2)}, u32[]{:S(2)}) collective-permute-start(bf16[128,1024]{1,0:T(8,128)(2,1)} %refs_2_.1), channel_id=1, source_target_pairs={{0,2},{1,3},{2,4},{3,5},{4,6},{5,7},{6,0},{7,1},{8,10},{9,11},{10,... | collective-permute-start | bytes 786440 | tf_op jit(solution)/shard_map/ppermute | solution.py:38
  6.7 14.4 %collective-permute-start.9 = (bf16[128,1024]{1,0:T(8,128)(2,1)}, bf16[128,1024]{1,0:T(8,128)(2,1)S(1)}, u32[]{:S(2)}, u32[]{:S(2)}) collective-permute-start(bf16[128,1024]{1,0:T(8,128)(2,1)} %refs_2_.1), channel_id=1, source_target_pairs={{0,6},{1,7},{2,0},{3,1},{4,2},{5,3},{6,4},{7,5},{8,14},{9,15},{10,... | collective-permute-start | bytes 786440 | tf_op jit(solution)/shard_map/ppermute | solution.py:38
  10.9 11.3 %collective-permute-start.4 = (bf16[128,1024]{1,0:T(8,128)(2,1)S(1)}, bf16[128,1024]{1,0:T(8,128)(2,1)S(1)}, u32[]{:S(2)}, u32[]{:S(2)}) collective-permute-start(bf16[128,1024]{1,0:T(8,128)(2,1)S(1)} %collective-permute-done.2.refs_3_), channel_id=1, source_target_pairs={{0,16},{1,9},{2,18},{3,11},{4,20},{5,13},{6,22},{7,15},{8,24},{9,1... | collective-permute-start | bytes 786440 | tf_op jit(solution)/shard_map/ppermute | solution.py:38
  12.0 10.7 %collective-permute-start.6 = (bf16[128,1024]{1,0:T(8,128)(2,1)S(1)}, bf16[128,1024]{1,0:T(8,128)(2,1)}, u32[]{:S(2)}, u32[]{:S(2)}) collective-permute-start(bf16[128,1024]{1,0:T(8,128)(2,1)S(1)} %collective-permute-done.2.refs_3_), channel_id=1, source_target_pairs={{0,1},{1,0},{2,3},{3,2},{4,5},{5,4},{6,7},{7,6},{8,9},{9,8},{10,11... | collective-permute-start | bytes 786440 | tf_op jit(solution)/shard_map/ppermute | solution.py:38
  12.9 13.5 %all-to-all-start = ((f32[32,1,1280]{2,1,0:T(1,128)}), f32[32,1,1280]{2,1,0:T(1,128)S(1)}, u32[]{:S(2)}, u32[]{:S(2)}) async-start(f32[32,1,1280]{2,1,0:T(1,128)} %shard_map.77), calls=%async_computation | async-start | bytes 327680 | tf_op jit(solution)/shard_map/all_to_all | solution.py:297
  17.9 3.3 %copy-start.3 = (bf16[128,1024]{1,0:T(8,128)(2,1)}, bf16[128,1024]{1,0:T(8,128)(2,1)S(1)}, u32[]{:S(2)}) copy-start(bf16[128,1024]{1,0:T(8,128)(2,1)S(1)} %collective-permute-done.refs_0_) | copy-start | bytes 786436
  21.2 14.2 %collective-permute-start.12 = (bf16[256,1024]{1,0:T(8,128)(2,1)S(1)}, bf16[256,1024]{1,0:T(8,128)(2,1)S(1)}, u32[]{:S(2)}, u32[]{:S(2)}) collective-permute-start(bf16[256,1024]{1,0:T(8,128)(2,1)S(1)} %shard_map.79.refs_2_), channel_id=1, source_target_pairs={{0,16},{1,9},{2,18},{3,11},{4,20},{5,13},{6,22},{7,15},{8,24},{9,1... | collective-permute-start | bytes 1572872 | tf_op jit(solution)/shard_map/ppermute | solution.py:38
  21.6 14.1 %collective-permute-start.10 = (bf16[256,1024]{1,0:T(8,128)(2,1)S(1)}, bf16[256,1024]{1,0:T(8,128)(2,1)S(1)}, u32[]{:S(2)}, u32[]{:S(2)}) collective-permute-start(bf16[256,1024]{1,0:T(8,128)(2,1)S(1)} %shard_map.79.refs_2_), channel_id=1, source_target_pairs={{0,8},{1,17},{2,10},{3,19},{4,12},{5,21},{6,14},{7,23},{8,0},{9,25... | collective-permute-start | bytes 1572872 | tf_op jit(solution)/shard_map/ppermute | solution.py:38
  22.2 1.5 %collective-permute-start.7 = (bf16[128,1024]{1,0:T(8,128)(2,1)S(1)}, bf16[128,1024]{1,0:T(8,128)(2,1)S(1)}, u32[]{:S(2)}, u32[]{:S(2)}) collective-permute-start(bf16[128,1024]{1,0:T(8,128)(2,1)S(1)} %collective-permute-done.3.refs_4_), channel_id=1, source_target_pairs={{0,1},{1,0},{2,3},{3,2},{4,5},{5,4},{6,7},{7,6},{8,9},{9,8},{10,11... | collective-permute-start | bytes 786440 | tf_op jit(solution)/shard_map/ppermute | solution.py:38
  22.2 13.8 %collective-permute-start.18 = (bf16[256,1024]{1,0:T(8,128)(2,1)S(1)}, bf16[256,1024]{1,0:T(8,128)(2,1)S(1)}, u32[]{:S(2)}, u32[]{:S(2)}) collective-permute-start(bf16[256,1024]{1,0:T(8,128)(2,1)S(1)} %shard_map.79.refs_2_), channel_id=1, source_target_pairs={{0,1},{1,0},{2,3},{3,2},{4,5},{5,4},{6,7},{7,6},{8,9},{9,8},{10,11... | collective-permute-start | bytes 1572872 | tf_op jit(solution)/shard_map/ppermute | solution.py:38
  22.7 3.7 %collective-permute-start.8 = (bf16[128,1024]{1,0:T(8,128)(2,1)S(1)}, bf16[128,1024]{1,0:T(8,128)(2,1)}, u32[]{:S(2)}, u32[]{:S(2)}) collective-permute-start(bf16[128,1024]{1,0:T(8,128)(2,1)S(1)} %collective-permute-done.4.refs_5_), channel_id=1, source_target_pairs={{0,1},{1,0},{2,3},{3,2},{4,5},{5,4},{6,7},{7,6},{8,9},{9,8},{10,11... | collective-permute-start | bytes 786440 | tf_op jit(solution)/shard_map/ppermute | solution.py:38
  23.7 0.7 copy-start.1
  24.4 11.6 %collective-permute-start.1 = (bf16[128,1024]{1,0:T(8,128)(2,1)}, bf16[128,1024]{1,0:T(8,128)(2,1)}, u32[]{:S(2)}, u32[]{:S(2)}) collective-permute-start(bf16[128,1024]{1,0:T(8,128)(2,1)} %copy-done.3), channel_id=1, source_target_pairs={{0,2},{1,3},{2,4},{3,5},{4,6},{5,7},{6,0},{7,1},{8,10},{9,11},{10,... | collective-permute-start | bytes 786440 | tf_op jit(solution)/shard_map/ppermute | solution.py:38
  26.4 1.0 %copy-start = (bf16[128,1024]{1,0:T(8,128)(2,1)S(1)}, bf16[128,1024]{1,0:T(8,128)(2,1)}, u32[]{:S(2)}) copy-start(bf16[128,1024]{1,0:T(8,128)(2,1)} %refs_2_.1) | copy-start | bytes 786436
  27.3 0.9 %copy-start.2 = (bf16[128,1024]{1,0:T(8,128)(2,1)S(1)}, bf16[128,1024]{1,0:T(8,128)(2,1)}, u32[]{:S(2)}) copy-start(bf16[128,1024]{1,0:T(8,128)(2,1)} %copy-done.1) | copy-start | bytes 786436
  35.5 1.9 %collective-permute-start.13 = (bf16[256,1024]{1,0:T(8,128)(2,1)S(1)}, bf16[256,1024]{1,0:T(8,128)(2,1)S(1)}, u32[]{:S(2)}, u32[]{:S(2)}) collective-permute-start(bf16[256,1024]{1,0:T(8,128)(2,1)S(1)} %collective-permute-done.12.refs_4_), channel_id=1, source_target_pairs={{0,1},{1,0},{2,3},{3,2},{4,5},{5,4},{6,7},{7,6},{8,9},{9,8},{10,11... | collective-permute-start | bytes 1572872 | tf_op jit(solution)/shard_map/ppermute | solution.py:38
  35.7 2.4 %collective-permute-start.11 = (bf16[256,1024]{1,0:T(8,128)(2,1)S(1)}, bf16[256,1024]{1,0:T(8,128)(2,1)S(1)}, u32[]{:S(2)}, u32[]{:S(2)}) collective-permute-start(bf16[256,1024]{1,0:T(8,128)(2,1)S(1)} %collective-permute-done.10.refs_3_), channel_id=1, source_target_pairs={{0,1},{1,0},{2,3},{3,2},{4,5},{5,4},{6,7},{7,6},{8,9},{9,8},{10,11... | collective-permute-start | bytes 1572872 | tf_op jit(solution)/shard_map/ppermute | solution.py:38
  36.0 9.4 %collective-permute-start.19 = (bf16[256,1024]{1,0:T(8,128)(2,1)S(1)}, bf16[256,1024]{1,0:T(8,128)(2,1)S(1)}, u32[]{:S(2)}, u32[]{:S(2)}) collective-permute-start(bf16[256,1024]{1,0:T(8,128)(2,1)S(1)} %collective-permute-done.10.refs_3_), channel_id=1, source_target_pairs={{0,16},{1,9},{2,18},{3,11},{4,20},{5,13},{6,22},{7,15},{8,24},{9,1... | collective-permute-start | bytes 1572872 | tf_op jit(solution)/shard_map/ppermute | solution.py:38
  45.4 3.8 %collective-permute-start.20 = (bf16[256,1024]{1,0:T(8,128)(2,1)S(1)}, bf16[256,1024]{1,0:T(8,128)(2,1)S(1)}, u32[]{:S(2)}, u32[]{:S(2)}) collective-permute-start(bf16[256,1024]{1,0:T(8,128)(2,1)S(1)} %collective-permute-done.19.refs_5_), channel_id=1, source_target_pairs={{0,1},{1,0},{2,3},{3,2},{4,5},{5,4},{6,7},{7,6},{8,9},{9,8},{10,11... | collective-permute-start | bytes 1572872 | tf_op jit(solution)/shard_map/ppermute | solution.py:38
  45.7 11.9 %collective-permute-start.16 = (bf16[128,1024]{1,0:T(8,128)(2,1)}, bf16[128,1024]{1,0:T(8,128)(2,1)S(1)}, u32[]{:S(2)}, u32[]{:S(2)}) collective-permute-start(bf16[128,1024]{1,0:T(8,128)(2,1)} %collective-permute-done.1.refs_2_), channel_id=1, source_target_pairs={{0,24},{1,25},{2,26},{3,27},{4,28},{5,29},{6,30},{7,31},{8,16},{9,... | collective-permute-start | bytes 786440 | tf_op jit(solution)/shard_map/ppermute | solution.py:38
  46.9 14.0 %collective-permute-start.15 = (bf16[128,1024]{1,0:T(8,128)(2,1)}, bf16[128,1024]{1,0:T(8,128)(2,1)S(1)}, u32[]{:S(2)}, u32[]{:S(2)}) collective-permute-start(bf16[128,1024]{1,0:T(8,128)(2,1)} %collective-permute-done.1.refs_2_), channel_id=1, source_target_pairs={{0,16},{1,9},{2,18},{3,11},{4,20},{5,13},{6,22},{7,15},{8,24},{9,1... | collective-permute-start | bytes 786440 | tf_op jit(solution)/shard_map/ppermute | solution.py:38
  48.4 12.5 %collective-permute-start.14 = (bf16[128,1024]{1,0:T(8,128)(2,1)}, bf16[128,1024]{1,0:T(8,128)(2,1)S(1)}, u32[]{:S(2)}, u32[]{:S(2)}) collective-permute-start(bf16[128,1024]{1,0:T(8,128)(2,1)} %collective-permute-done.1.refs_2_), channel_id=1, source_target_pairs={{0,8},{1,17},{2,10},{3,19},{4,12},{5,21},{6,14},{7,23},{8,0},{9,25... | collective-permute-start | bytes 786440 | tf_op jit(solution)/shard_map/ppermute | solution.py:38
  49.2 12.2 %collective-permute-start.17 = (bf16[128,1024]{1,0:T(8,128)(2,1)}, bf16[128,1024]{1,0:T(8,128)(2,1)S(1)}, u32[]{:S(2)}, u32[]{:S(2)}) collective-permute-start(bf16[128,1024]{1,0:T(8,128)(2,1)} %collective-permute-done.1.refs_2_), channel_id=1, source_target_pairs={{0,1},{1,0},{2,3},{3,2},{4,5},{5,4},{6,7},{7,6},{8,9},{9,8},{10,11... | collective-permute-start | bytes 786440 | tf_op jit(solution)/shard_map/ppermute | solution.py:38
  57.5 22.4 %copy-start.4 = (f32[128]{0:T(128)S(1)}, f32[128]{0:T(128)}, u32[]{:S(2)}) copy-start(f32[128]{0:T(128)} %param.10) | copy-start | bytes 1540
  57.5 3.9 %collective-permute-start.23 = (bf16[128,1024]{1,0:T(8,128)(2,1)S(1)}, bf16[128,1024]{1,0:T(8,128)(2,1)S(1)}, u32[]{:S(2)}, u32[]{:S(2)}) collective-permute-start(bf16[128,1024]{1,0:T(8,128)(2,1)S(1)} %collective-permute-done.16.refs_5_), channel_id=1, source_target_pairs={{0,1},{1,0},{2,3},{3,2},{4,5},{5,4},{6,7},{7,6},{8,9},{9,8},{10,11... | collective-permute-start | bytes 786440 | tf_op jit(solution)/shard_map/ppermute | solution.py:38
  60.9 1.5 %collective-permute-start.22 = (bf16[128,1024]{1,0:T(8,128)(2,1)S(1)}, bf16[128,1024]{1,0:T(8,128)(2,1)S(1)}, u32[]{:S(2)}, u32[]{:S(2)}) collective-permute-start(bf16[128,1024]{1,0:T(8,128)(2,1)S(1)} %collective-permute-done.15.refs_4_), channel_id=1, source_target_pairs={{0,1},{1,0},{2,3},{3,2},{4,5},{5,4},{6,7},{7,6},{8,9},{9,8},{10,11... | collective-permute-start | bytes 786440 | tf_op jit(solution)/shard_map/ppermute | solution.py:38
  60.9 1.9 %collective-permute-start.21 = (bf16[128,1024]{1,0:T(8,128)(2,1)S(1)}, bf16[128,1024]{1,0:T(8,128)(2,1)S(1)}, u32[]{:S(2)}, u32[]{:S(2)}) collective-permute-start(bf16[128,1024]{1,0:T(8,128)(2,1)S(1)} %collective-permute-done.14.refs_3_), channel_id=1, source_target_pairs={{0,1},{1,0},{2,3},{3,2},{4,5},{5,4},{6,7},{7,6},{8,9},{9,8},{10,11... | collective-permute-start | bytes 786440 | tf_op jit(solution)/shard_map/ppermute | solution.py:38
  68.6 11.2 %all-to-all-start.1 = ((f32[32,3,128]{2,1,0:T(4,128)}), f32[32,3,128]{2,1,0:T(4,128)S(1)}, u32[]{:S(2)}, u32[]{:S(2)}) async-start(f32[32,3,128]{2,1,0:T(4,128)} %bitcast.13), calls=%async_computation.1 | async-start | bytes 131072 | tf_op jit(solution)/shard_map/all_to_all | solution.py:324

commit v11 on v7

--- a/solution.py
+++ b/solution.py
@@ -121,24 +121,6 @@
         scratch_shapes=[pltpu.SemaphoreType.DMA((len(offsets),))],
         compiler_params=pltpu.CompilerParams(vmem_limit_bytes=SMALL_LIMIT),
     )(starts, far(head))
-
-
-def join_kernel(*refs):
-    tok = refs[0].shape[0]
-    for j, ref in enumerate(refs[:-1]):
-        refs[-1][j * tok : (j + 1) * tok, :] = ref[...]
-
-
-def joined(blocks):
-    tok, feat = blocks[0].shape
-    vmem = pl.BlockSpec(memory_space=pltpu.VMEM)
-    return pl.pallas_call(
-        join_kernel,
-        out_shape=jax.ShapeDtypeStruct((len(blocks) * tok, feat), blocks[0].dtype),
-        in_specs=[vmem] * len(blocks),
-        out_specs=vmem,
-        compiler_params=pltpu.CompilerParams(vmem_limit_bytes=SMALL_LIMIT),
-    )(*blocks)
 
 
 def layer_kernel(n, n_t, place, layer, offset, own, first, last, *refs):
@@ -263,20 +245,21 @@
     plane, tensor = lax.axis_index("dp"), lax.axis_index("tensor")
     z_me, c_me = tensor // CORES, tensor % CORES
     owners = grid.owners(plane // grid.cols, plane % grid.cols, c_me)
-    rest = [depth - 1, *range(2, depth - 1)]
-    groups = [[0], [1]] + [rest[k : k + 2] for k in range(0, len(rest), 2)]
+    order = [0] + [d for k in range(1, depth // 2) for d in (k, depth - k)] + [depth // 2]
     place = [grid.sibling_spot(k) for k in range(n_dp)]
 
     layers = {0: hidden}
     reached = [grid.reach(hidden)]
-    for at, group in enumerate(groups[1:], 1):
-        for dz in group:
-            before = [layers[d] for d in groups[at - 1]] if at > 1 else []
-            layers[dz] = grid.along(after(hidden, *before), dz)
-    for group in groups[1:]:
-        sources = [layers[dz] for dz in group]
-        sources[0] = after(sources[0], *reached[0].values())
-        reached.append(grid.reach(joined(sources) if len(sources) > 1 else sources[0]))
+    for dz in order[1:]:
+        step = 1 if dz <= depth // 2 else -1
+        layers[dz] = grid.along(layers[(dz - step) % depth], step)
+
+    def reach_next(at, *late):
+        if at < depth:
+            reached.append(grid.reach(after(layers[order[at]], *late)))
+
+    reach_next(1, *reached[0].values())
+    reach_next(2, layers[1])
 
     vocab_cols = head.shape[1]
     vocab_start = lax.axis_index(("dp", "tensor")) * vocab_cols
@@ -284,20 +267,26 @@
     packed = squares(after(hidden, starts), norm_gain[None, :], targets[None, :], n_dp * n_t)
     fine = lax.all_to_all(packed, ("dp", "tensor"), 0, 0, tiled=True)
 
-    acc, deep, results = None, CORES * feat, []
-    for at, group in enumerate(groups):
-        final = at == len(groups) - 1
-        offsets = [2 + n_dp + dz for dz in group]
-        spread = grid.fill(dict(reached[at]), *(results[at - 2 : at - 1] if at >= 2 else []))
-        weights, ready = head, []
-        if len(group) > 1:
-            weights = loaded(starts, offsets, after(head, *results[-1:]), deep)
-            ready = [weights]
-        others = [grid.sibling(a) for a in spread[:-1]] + [grid.sibling(after(spread[-1], *ready))]
+    acc, deep, results, weights = None, CORES * feat, [], [head]
+    for at, dz in enumerate(order):
+        final = at == depth - 1
+        own = grid.sibling(reached[at][0, 0])
+        if at == 1:
+            for later in order[1:]:
+                ready = after(head, acc, layers[order[3]])
+                weights.append(loaded(starts, [2 + n_dp + later], ready, deep))
+        held = [packed] if at == 0 else [] if at == 1 else [acc if at == 2 else results[at - 2]]
+        if at == 2:
+            held = [results[0], own, layers[order[3]]]
+        spread = grid.fill(dict(reached[at]), *held)
+        if at >= 2:
+            reach_next(at + 1, spread[-1])
+        others = [own] + [grid.sibling(a) for a in spread[1:-1]]
+        others.append(grid.sibling(after(spread[-1], *([acc] if final else weights[1:4] if at == 2 else []))))
         blocks = spread + others
-        for layer, offset in enumerate(offsets):
-            last = final and layer == len(offsets) - 1
-            acc = layer_product(tok, n_t, starts, layer, offset, fine, blocks, place, weights, acc, last)
+        if at >= 2 and not final:
+            blocks[0] = after(blocks[0], *reached[at + 1].values())
+        acc = layer_product(tok, n_t, starts, 0, 2 + n_dp + dz, fine, blocks, place, weights[at], acc, final)
         results.append(acc)
 
     parts = lax.all_to_all(acc.reshape(n_dp * n_t, 3, tok), ("dp", "tensor"), 0, 0, tiled=True)

time: 89.7 us -> 88.3 us (0.984)
  waiting for transfers between devices: 24.4 us -> 20.3 us
  Pallas kernels: 29.2 us -> 31.5 us
  starting transfers between devices: 31 us -> 33 us
  local copies, waits for them, and re-layouts: 2.68 us -> 1.05 us
    pallas_call x1 -> x3, Pallas kernels: 4.34 us -> 8.67 us  [loaded(): pl.pallas_call(functools.partial(load_kernel, offsets), out_shape=pltpu.V...]
    ppermute x24 -> x31, starting transfers between devices: 19.5 us -> 23.3 us  [permute(): return lax.ppermute(a, ('dp', 'tensor'), perm)]
    all_to_all x1, waiting for transfers between devices: 2.32 us -> 0.01 us  [body(): fine = lax.all_to_all(packed, ('dp', 'tensor'), 0, 0, tiled=True)]
    pallas_call x4, Pallas kernels: 23 us -> 21 us  [layer_product(): pl.pallas_call(functools.partial(layer_kernel, n, n_t, place, layer, offs...]
    ppermute x24 -> x31, waiting for transfers between devices: 15.3 us -> 13.5 us  [permute(): return lax.ppermute(a, ('dp', 'tensor'), perm)]
    unnamed x8, local copies, waits for them, and re-layouts: 2.6 us -> 0.96 us
    all_to_all x1, starting transfers between devices: 7.27 us -> 5.78 us  [body(): fine = lax.all_to_all(packed, ('dp', 'tensor'), 0, 0, tiled=True)]
  transfers between devices with their start and end apart: 26 -> 33, of which waited for: 12 -> 6; matrix products, arithmetic and copies ran while one was open for 0% -> 0% of each run, Pallas kernels for 22% -> 30%
where the time goes in v11:
time: 88.3 us; the launch traced here: 87.9 us
  starting transfers between devices  33 us (37%)
  Pallas kernels  31.5 us (36%)
  waiting for transfers between devices  20.3 us (23%)
  between operations  1.48 us (2%)
  local copies, waits for them, and re-layouts  1.05 us (1%)
    ppermute x31, starting transfers between devices, permute(): return lax.ppermute(a, ('dp', 'tensor'), perm)  23.3 us
    pallas_call x4, Pallas kernels, layer_product(): pl.pallas_call(functools.partial(layer_kernel, n, n_t, place, layer, offs...  21 us
    ppermute x31, waiting for transfers between devices, permute(): return lax.ppermute(a, ('dp', 'tensor'), perm)  13.5 us
    pallas_call x3, Pallas kernels, loaded(): pl.pallas_call(functools.partial(load_kernel, offsets), out_shape=pltpu.V...  8.67 us
    all_to_all x1, waiting for transfers between devices, body(): lax.all_to_all(acc.reshape(n_dp * n_t, 3, tok), ('dp', 'tensor'), 0, 0, t...  6.74 us
    all_to_all x1, starting transfers between devices, body(): fine = lax.all_to_all(packed, ('dp', 'tensor'), 0, 0, tiled=True)  5.78 us
    all_to_all x1, starting transfers between devices, body(): lax.all_to_all(acc.reshape(n_dp * n_t, 3, tok), ('dp', 'tensor'), 0, 0, t...  3.86 us
    pallas_call x1, Pallas kernels, squares(): pl.pallas_call(squares_kernel, out_shape=jax.ShapeDtypeStruct((peers, 1,...  1.79 us
  transfers between devices with their start and end apart: 33, of which 6 were waited for; matrix products, arithmetic and copies ran while one was open for 0% of the time, Pallas kernels for 30%

profile of v11, /device:TPU:0, one launch (start us, length us, event | category | flops | bytes accessed | tf_op | source)
XLA Modules:
  0.0 87.9 jit_solution(1025657866405769745)
XLA Ops:
  0.6 3.0 %collective-permute-start.4 = (bf16[128,1024]{1,0:T(8,128)(2,1)}, bf16[128,1024]{1,0:T(8,128)(2,1)S(1)}, u32[]{:S(2)}, u32[]{:S(2)}) collective-permute-start(bf16[128,1024]{1,0:T(8,128)(2,1)} %refs_2_.1), channel_id=1, source_target_pairs={{0,8},{1,17},{2,10},{3,19},{4,12},{5,21},{6,14},{7,23},{8,0},{9,25... | collective-permute-start | bytes 786440 | tf_op jit(solution)/shard_map/ppermute | solution.py:38
  3.6 1.5 %collective-permute-start.5 = (bf16[128,1024]{1,0:T(8,128)(2,1)}, bf16[128,1024]{1,0:T(8,128)(2,1)S(1)}, u32[]{:S(2)}, u32[]{:S(2)}) collective-permute-start(bf16[128,1024]{1,0:T(8,128)(2,1)} %refs_2_.1), channel_id=1, source_target_pairs={{0,16},{1,9},{2,18},{3,11},{4,20},{5,13},{6,22},{7,15},{8,24},{9,1... | collective-permute-start | bytes 786440 | tf_op jit(solution)/shard_map/ppermute | solution.py:38
  5.2 1.6 %collective-permute-start = (bf16[128,1024]{1,0:T(8,128)(2,1)}, bf16[128,1024]{1,0:T(8,128)(2,1)S(1)}, u32[]{:S(2)}, u32[]{:S(2)}) collective-permute-start(bf16[128,1024]{1,0:T(8,128)(2,1)} %refs_2_.1), channel_id=1, source_target_pairs={{0,2},{1,3},{2,4},{3,5},{4,6},{5,7},{6,0},{7,1},{8,10},{9,11},{10,... | collective-permute-start | bytes 786440 | tf_op jit(solution)/shard_map/ppermute | solution.py:38
  6.7 2.2 %collective-permute-start.2 = (bf16[128,1024]{1,0:T(8,128)(2,1)}, bf16[128,1024]{1,0:T(8,128)(2,1)S(1)}, u32[]{:S(2)}, u32[]{:S(2)}) collective-permute-start(bf16[128,1024]{1,0:T(8,128)(2,1)} %refs_2_.1), channel_id=1, source_target_pairs={{0,6},{1,7},{2,0},{3,1},{4,2},{5,3},{6,4},{7,5},{8,14},{9,15},{10,... | collective-permute-start | bytes 786440 | tf_op jit(solution)/shard_map/ppermute | solution.py:38
  9.0 0.0 collective-permute-start.7
  9.0 0.1 stack.43.refs_0_.start_ref
  9.1 1.8 %shard_map.77 = f32[32,1,1280]{2,1,0:T(1,128)} custom-call(bf16[128,1024]{1,0:T(8,128)(2,1)} %refs_2_.1, f32[1,1024]{1,0:T(1,128)} %bitcast.22, s32[1,128]{1,0:T(1,128)} %bitcast.23), custom_call_target="tpu_custom_call" | custom-call | tf_op jit(solution)/shard_map/pallas_call | solution.py:225
  10.9 1.1 %collective-permute-start.6 = (bf16[128,1024]{1,0:T(8,128)(2,1)S(1)}, bf16[128,1024]{1,0:T(8,128)(2,1)S(1)}, u32[]{:S(2)}, u32[]{:S(2)}) collective-permute-start(bf16[128,1024]{1,0:T(8,128)(2,1)S(1)} %collective-permute-done.4.refs_3_), channel_id=1, source_target_pairs={{0,16},{1,9},{2,18},{3,11},{4,20},{5,13},{6,22},{7,15},{8,24},{9,1... | collective-permute-start | bytes 786440 | tf_op jit(solution)/shard_map/ppermute | solution.py:38
  12.0 5.8 %all-to-all-start = ((f32[32,1,1280]{2,1,0:T(1,128)}), f32[32,1,1280]{2,1,0:T(1,128)S(1)}, u32[]{:S(2)}, u32[]{:S(2)}) async-start(f32[32,1,1280]{2,1,0:T(1,128)} %shard_map.77), calls=%async_computation | async-start | bytes 327680 | tf_op jit(solution)/shard_map/all_to_all | solution.py:268
  17.8 0.3 collective-permute-start.8
  18.1 0.3 collective-permute-start.9
  18.4 1.4 %collective-permute-done.2.refs_2_ = bf16[128,1024]{1,0:T(8,128)(2,1)S(1)} collective-permute-done((bf16[128,1024]{1,0:T(8,128)(2,1)}, bf16[128,1024]{1,0:T(8,128)(2,1)S(1)}, u32[]{:S(2)}, u32[]{:S(2)}) %collective-permute-start.2) | collective-permute-done | bytes 262176 | tf_op jit(solution)/shard_map/ppermute | solution.py:38
  19.8 0.5 collective-permute-start.16
  20.3 1.3 %collective-permute-start.17 = (bf16[128,1024]{1,0:T(8,128)(2,1)S(1)}, bf16[128,1024]{1,0:T(8,128)(2,1)S(1)}, u32[]{:S(2)}, u32[]{:S(2)}) collective-permute-start(bf16[128,1024]{1,0:T(8,128)(2,1)S(1)} %collective-permute-done.refs_2_), channel_id=1, source_target_pairs={{0,16},{1,9},{2,18},{3,11},{4,20},{5,13},{6,22},{7,15},{8,24},{9,1... | collective-permute-start | bytes 786440 | tf_op jit(solution)/shard_map/ppermute | solution.py:38
  21.6 0.8 collective-permute-start.3
  22.4 1.3 %collective-permute-start.1 = (bf16[128,1024]{1,0:T(8,128)(2,1)S(1)}, bf16[128,1024]{1,0:T(8,128)(2,1)S(1)}, u32[]{:S(2)}, u32[]{:S(2)}) collective-permute-start(bf16[128,1024]{1,0:T(8,128)(2,1)S(1)} %collective-permute-done.refs_2_), channel_id=1, source_target_pairs={{0,2},{1,3},{2,4},{3,5},{4,6},{5,7},{6,0},{7,1},{8,10},{9,11},{10,... | collective-permute-start | bytes 786440 | tf_op jit(solution)/shard_map/ppermute | solution.py:38
  23.7 5.5 %collective-permute-done.16.refs_3_ = bf16[128,1024]{1,0:T(8,128)(2,1)} collective-permute-done((bf16[128,1024]{1,0:T(8,128)(2,1)S(1)}, bf16[128,1024]{1,0:T(8,128)(2,1)}, u32[]{:S(2)}, u32[]{:S(2)}) %collective-permute-start.16) | collective-permute-done | bytes 262176 | tf_op jit(solution)/shard_map/ppermute | solution.py:38
  29.2 1.1 %collective-permute-done.17.refs_4_ = bf16[128,1024]{1,0:T(8,128)(2,1)S(1)} collective-permute-done((bf16[128,1024]{1,0:T(8,128)(2,1)S(1)}, bf16[128,1024]{1,0:T(8,128)(2,1)S(1)}, u32[]{:S(2)}, u32[]{:S(2)}) %collective-permute-start.17) | collective-permute-done | bytes 262176 | tf_op jit(solution)/shard_map/ppermute | solution.py:38
  30.3 1.0 %collective-permute-start.12 = (bf16[128,1024]{1,0:T(8,128)(2,1)S(1)}, bf16[128,1024]{1,0:T(8,128)(2,1)}, u32[]{:S(2)}, u32[]{:S(2)}) collective-permute-start(bf16[128,1024]{1,0:T(8,128)(2,1)S(1)} %collective-permute-done.2.refs_2_), channel_id=1, source_target_pairs={{0,16},{1,9},{2,18},{3,11},{4,20},{5,13},{6,22},{7,15},{8,24},{9,1... | collective-permute-start | bytes 786440 | tf_op jit(solution)/shard_map/ppermute | solution.py:38
  31.3 1.0 %collective-permute-start.18 = (bf16[128,1024]{1,0:T(8,128)(2,1)}, bf16[128,1024]{1,0:T(8,128)(2,1)}, u32[]{:S(2)}, u32[]{:S(2)}) collective-permute-start(bf16[128,1024]{1,0:T(8,128)(2,1)} %collective-permute-done.16.refs_3_), channel_id=1, source_target_pairs={{0,16},{1,9},{2,18},{3,11},{4,20},{5,13},{6,22},{7,15},{8,24},{9,1... | collective-permute-start | bytes 786440 | tf_op jit(solution)/shard_map/ppermute | solution.py:38
  32.3 0.9 %copy-done = bf16[128,1024]{1,0:T(8,128)(2,1)S(1)} copy-done((bf16[128,1024]{1,0:T(8,128)(2,1)S(1)}, bf16[128,1024]{1,0:T(8,128)(2,1)}, u32[]{:S(2)}) %copy-start) | copy-done | bytes 262168
  33.3 6.2 %shard_map.78.refs_11_ = f32[512,1152]{1,0:T(8,128)S(1)} custom-call(s32[10]{0:T(128)S(1)} %stack.43.refs_0_.start_ref, f32[32,1,1280]{2,1,0:T(1,128)S(1)} %all-to-all-done.refs_1_, bf16[128,1024]{1,0:T(8,128)(2,1)S(1)} %copy-done, bf16[128,1024]{1,0:T(8,128)(2,1)S(1)} %collective-permute-done.4.refs_3_, ...), custom_call_target="tpu_custom_call" | custom-call | flops 2415919104 | bytes 4718592 | tf_op jit(solution)/shard_map/pallas_call | solution.py:193
  39.5 1.1 %collective-permute-start.13 = (bf16[128,1024]{1,0:T(8,128)(2,1)S(1)}, bf16[128,1024]{1,0:T(8,128)(2,1)S(1)}, u32[]{:S(2)}, u32[]{:S(2)}) collective-permute-start(bf16[128,1024]{1,0:T(8,128)(2,1)S(1)} %collective-permute-done.3.refs_3_), channel_id=1, source_target_pairs={{0,16},{1,9},{2,18},{3,11},{4,20},{5,13},{6,22},{7,15},{8,24},{9,1... | collective-permute-start | bytes 786440 | tf_op jit(solution)/shard_map/ppermute | solution.py:38
  40.6 0.5 collective-permute-start.20
  41.1 0.0 collective-permute-start.21
  41.1 0.5 collective-permute-start.22
  41.6 4.3 %collective-permute-done.13.refs_5_ = bf16[128,1024]{1,0:T(8,128)(2,1)S(1)} collective-permute-done((bf16[128,1024]{1,0:T(8,128)(2,1)S(1)}, bf16[128,1024]{1,0:T(8,128)(2,1)S(1)}, u32[]{:S(2)}, u32[]{:S(2)}) %collective-permute-start.13) | collective-permute-done | bytes 262176 | tf_op jit(solution)/shard_map/ppermute | solution.py:38
  46.0 1.4 %collective-permute-start.14 = (bf16[128,1024]{1,0:T(8,128)(2,1)S(1)}, bf16[128,1024]{1,0:T(8,128)(2,1)S(1)}, u32[]{:S(2)}, u32[]{:S(2)}) collective-permute-start(bf16[128,1024]{1,0:T(8,128)(2,1)S(1)} %collective-permute-done.1.refs_2_), channel_id=1, source_target_pairs={{0,8},{1,17},{2,10},{3,19},{4,12},{5,21},{6,14},{7,23},{8,0},{9,25... | collective-permute-start | bytes 786440 | tf_op jit(solution)/shard_map/ppermute | solution.py:38
  47.3 0.7 collective-permute-start.15
  48.0 2.9 %shard_map.79.refs_10_ = bf16[1,2048,1152]{2,1,0:T(8,128)(2,1)S(1)} custom-call(s32[10]{0:T(128)S(1)} %stack.43.refs_0_.start_ref, bf16[8192,1152]{1,0:T(8,128)(2,1)} %head_ref.2), custom_call_target="tpu_custom_call" | custom-call | tf_op jit(solution)/shard_map/pallas_call | solution.py:116
  50.9 2.9 %shard_map.81.refs_10_ = bf16[1,2048,1152]{2,1,0:T(8,128)(2,1)S(1)} custom-call(s32[10]{0:T(128)S(1)} %stack.43.refs_0_.start_ref, bf16[8192,1152]{1,0:T(8,128)(2,1)} %head_ref.2), custom_call_target="tpu_custom_call" | custom-call | tf_op jit(solution)/shard_map/pallas_call | solution.py:116
  53.8 2.9 %shard_map.82.refs_10_ = bf16[1,2048,1152]{2,1,0:T(8,128)(2,1)S(1)} custom-call(s32[10]{0:T(128)S(1)} %stack.43.refs_0_.start_ref, bf16[8192,1152]{1,0:T(8,128)(2,1)} %head_ref.2), custom_call_target="tpu_custom_call" | custom-call | tf_op jit(solution)/shard_map/pallas_call | solution.py:116
  56.8 0.1 collective-permute-start.27
  56.8 0.5 collective-permute-start.28
  57.3 0.1 collective-permute-start.29
  57.4 4.7 %shard_map.80.refs_11_ = f32[512,1152]{1,0:T(8,128)S(1)} custom-call(s32[10]{0:T(128)S(1)} %stack.43.refs_0_.start_ref, f32[32,1,1280]{2,1,0:T(1,128)S(1)} %all-to-all-done.refs_1_, bf16[128,1024]{1,0:T(8,128)(2,1)S(1)} %collective-permute-done.refs_2_, bf16[128,1024]{1,0:T(8,128)(2,1)} %collective-permute-done.16.refs_3_, bf16[128,1024]{1,0:T(8,128)(2,1)S(1)} %copy-done.2, ...), custom_call_target="tpu_custom_call" | custom-call | flops 2415919104 | bytes 4718592 | tf_op jit(solution)/shard_map/pallas_call | solution.py:193
  62.1 1.4 %collective-permute-start.23 = (bf16[128,1024]{1,0:T(8,128)(2,1)S(1)}, bf16[128,1024]{1,0:T(8,128)(2,1)S(1)}, u32[]{:S(2)}, u32[]{:S(2)}) collective-permute-start(bf16[128,1024]{1,0:T(8,128)(2,1)S(1)} %collective-permute-done.14.refs_3_), channel_id=1, source_target_pairs={{0,16},{1,9},{2,18},{3,11},{4,20},{5,13},{6,22},{7,15},{8,24},{9,1... | collective-permute-start | bytes 786440 | tf_op jit(solution)/shard_map/ppermute | solution.py:38
  63.5 0.5 collective-permute-start.25
  64.1 0.1 collective-permute-start.26
  64.1 4.6 %shard_map.83.refs_11_ = f32[512,1152]{1,0:T(8,128)S(1)} custom-call(s32[10]{0:T(128)S(1)} %stack.43.refs_0_.start_ref, f32[32,1,1280]{2,1,0:T(1,128)S(1)} %all-to-all-done.refs_1_, bf16[128,1024]{1,0:T(8,128)(2,1)S(1)} %collective-permute-done.2.refs_2_, bf16[128,1024]{1,0:T(8,128)(2,1)S(1)} %collective-permute-done.3.refs_3_, ...), custom_call_target="tpu_custom_call" | custom-call | flops 2415919104 | bytes 4718592 | tf_op jit(solution)/shard_map/pallas_call | solution.py:193
  68.7 0.0 copy-start.3
  68.8 0.5 collective-permute-start.30
  69.3 1.1 %collective-permute-done.30.refs_9_ = bf16[128,1024]{1,0:T(8,128)(2,1)S(1)} collective-permute-done((bf16[128,1024]{1,0:T(8,128)(2,1)S(1)}, bf16[128,1024]{1,0:T(8,128)(2,1)S(1)}, u32[]{:S(2)}, u32[]{:S(2)}) %collective-permute-start.30) | collective-permute-done | bytes 262176 | tf_op jit(solution)/shard_map/ppermute | solution.py:38
  70.4 5.5 %shard_map.84 = f32[4,8,3,128]{3,2,1,0:T(4,128)} custom-call(s32[10]{0:T(128)S(1)} %stack.43.refs_0_.start_ref, f32[32,1,1280]{2,1,0:T(1,128)S(1)} %all-to-all-done.refs_1_, bf16[128,1024]{1,0:T(8,128)(2,1)S(1)} %collective-permute-done.1.refs_2_, bf16[128,1024]{1,0:T(8,128)(2,1)S(1)} %collective-permute-done.14.refs_3_, ...), custom_call_target="tpu_custom_call" | custom-call | flops 2415919104 | bytes 4718592 | tf_op jit(solution)/shard_map/pallas_call | solution.py:193
  76.0 3.9 %all-to-all-start.1 = ((f32[32,3,128]{2,1,0:T(4,128)}), f32[32,3,128]{2,1,0:T(4,128)S(1)}, u32[]{:S(2)}, u32[]{:S(2)}) async-start(f32[32,3,128]{2,1,0:T(4,128)} %bitcast.13), calls=%async_computation.1 | async-start | bytes 131072 | tf_op jit(solution)/shard_map/all_to_all | solution.py:292
  80.5 6.7 %all-to-all-done.1 = f32[32,3,128]{2,1,0:T(4,128)S(1)} async-done(((f32[32,3,128]{2,1,0:T(4,128)}), f32[32,3,128]{2,1,0:T(4,128)S(1)}, u32[]{:S(2)}, u32[]{:S(2)}) %all-to-all-start.1) | async-done | bytes 49184 | tf_op jit(solution)/shard_map/all_to_all | solution.py:292
  87.2 0.1 slice_reduce_fusion
  87.3 0.5 compare_select_fusion
  (39 shorter events, 0.1 us)
Async XLA Ops:
  0.6 10.2 %collective-permute-start.4 = (bf16[128,1024]{1,0:T(8,128)(2,1)}, bf16[128,1024]{1,0:T(8,128)(2,1)S(1)}, u32[]{:S(2)}, u32[]{:S(2)}) collective-permute-start(bf16[128,1024]{1,0:T(8,128)(2,1)} %refs_2_.1), channel_id=1, source_target_pairs={{0,8},{1,17},{2,10},{3,19},{4,12},{5,21},{6,14},{7,23},{8,0},{9,25... | collective-permute-start | bytes 786440 | tf_op jit(solution)/shard_map/ppermute | solution.py:38
  3.6 7.2 %collective-permute-start.5 = (bf16[128,1024]{1,0:T(8,128)(2,1)}, bf16[128,1024]{1,0:T(8,128)(2,1)S(1)}, u32[]{:S(2)}, u32[]{:S(2)}) collective-permute-start(bf16[128,1024]{1,0:T(8,128)(2,1)} %refs_2_.1), channel_id=1, source_target_pairs={{0,16},{1,9},{2,18},{3,11},{4,20},{5,13},{6,22},{7,15},{8,24},{9,1... | collective-permute-start | bytes 786440 | tf_op jit(solution)/shard_map/ppermute | solution.py:38
  5.2 13.0 %collective-permute-start = (bf16[128,1024]{1,0:T(8,128)(2,1)}, bf16[128,1024]{1,0:T(8,128)(2,1)S(1)}, u32[]{:S(2)}, u32[]{:S(2)}) collective-permute-start(bf16[128,1024]{1,0:T(8,128)(2,1)} %refs_2_.1), channel_id=1, source_target_pairs={{0,2},{1,3},{2,4},{3,5},{4,6},{5,7},{6,0},{7,1},{8,10},{9,11},{10,... | collective-permute-start | bytes 786440 | tf_op jit(solution)/shard_map/ppermute | solution.py:38
  6.7 13.0 %collective-permute-start.2 = (bf16[128,1024]{1,0:T(8,128)(2,1)}, bf16[128,1024]{1,0:T(8,128)(2,1)S(1)}, u32[]{:S(2)}, u32[]{:S(2)}) collective-permute-start(bf16[128,1024]{1,0:T(8,128)(2,1)} %refs_2_.1), channel_id=1, source_target_pairs={{0,6},{1,7},{2,0},{3,1},{4,2},{5,3},{6,4},{7,5},{8,14},{9,15},{10,... | collective-permute-start | bytes 786440 | tf_op jit(solution)/shard_map/ppermute | solution.py:38
  9.0 11.3 %collective-permute-start.7 = (bf16[128,1024]{1,0:T(8,128)(2,1)}, bf16[128,1024]{1,0:T(8,128)(2,1)S(1)}, u32[]{:S(2)}, u32[]{:S(2)}) collective-permute-start(bf16[128,1024]{1,0:T(8,128)(2,1)} %refs_2_.1), channel_id=1, source_target_pairs={{0,1},{1,0},{2,3},{3,2},{4,5},{5,4},{6,7},{7,6},{8,9},{9,8},{10,11... | collective-permute-start | bytes 786440 | tf_op jit(solution)/shard_map/ppermute | solution.py:38
  10.9 10.7 %collective-permute-start.6 = (bf16[128,1024]{1,0:T(8,128)(2,1)S(1)}, bf16[128,1024]{1,0:T(8,128)(2,1)S(1)}, u32[]{:S(2)}, u32[]{:S(2)}) collective-permute-start(bf16[128,1024]{1,0:T(8,128)(2,1)S(1)} %collective-permute-done.4.refs_3_), channel_id=1, source_target_pairs={{0,16},{1,9},{2,18},{3,11},{4,20},{5,13},{6,22},{7,15},{8,24},{9,1... | collective-permute-start | bytes 786440 | tf_op jit(solution)/shard_map/ppermute | solution.py:38
  12.0 20.3 %all-to-all-start = ((f32[32,1,1280]{2,1,0:T(1,128)}), f32[32,1,1280]{2,1,0:T(1,128)S(1)}, u32[]{:S(2)}, u32[]{:S(2)}) async-start(f32[32,1,1280]{2,1,0:T(1,128)} %shard_map.77), calls=%async_computation | async-start | bytes 327680 | tf_op jit(solution)/shard_map/all_to_all | solution.py:268
  17.8 3.8 %collective-permute-start.8 = (bf16[128,1024]{1,0:T(8,128)(2,1)S(1)}, bf16[128,1024]{1,0:T(8,128)(2,1)S(1)}, u32[]{:S(2)}, u32[]{:S(2)}) collective-permute-start(bf16[128,1024]{1,0:T(8,128)(2,1)S(1)} %collective-permute-done.4.refs_3_), channel_id=1, source_target_pairs={{0,1},{1,0},{2,3},{3,2},{4,5},{5,4},{6,7},{7,6},{8,9},{9,8},{10,11... | collective-permute-start | bytes 786440 | tf_op jit(solution)/shard_map/ppermute | solution.py:38
  18.1 4.3 %collective-permute-start.9 = (bf16[128,1024]{1,0:T(8,128)(2,1)S(1)}, bf16[128,1024]{1,0:T(8,128)(2,1)S(1)}, u32[]{:S(2)}, u32[]{:S(2)}) collective-permute-start(bf16[128,1024]{1,0:T(8,128)(2,1)S(1)} %collective-permute-done.5.refs_4_), channel_id=1, source_target_pairs={{0,1},{1,0},{2,3},{3,2},{4,5},{5,4},{6,7},{7,6},{8,9},{9,8},{10,11... | collective-permute-start | bytes 786440 | tf_op jit(solution)/shard_map/ppermute | solution.py:38
  19.8 9.4 %collective-permute-start.16 = (bf16[128,1024]{1,0:T(8,128)(2,1)S(1)}, bf16[128,1024]{1,0:T(8,128)(2,1)}, u32[]{:S(2)}, u32[]{:S(2)}) collective-permute-start(bf16[128,1024]{1,0:T(8,128)(2,1)S(1)} %collective-permute-done.refs_2_), channel_id=1, source_target_pairs={{0,8},{1,17},{2,10},{3,19},{4,12},{5,21},{6,14},{7,23},{8,0},{9,25... | collective-permute-start | bytes 786440 | tf_op jit(solution)/shard_map/ppermute | solution.py:38
  20.3 10.0 %collective-permute-start.17 = (bf16[128,1024]{1,0:T(8,128)(2,1)S(1)}, bf16[128,1024]{1,0:T(8,128)(2,1)S(1)}, u32[]{:S(2)}, u32[]{:S(2)}) collective-permute-start(bf16[128,1024]{1,0:T(8,128)(2,1)S(1)} %collective-permute-done.refs_2_), channel_id=1, source_target_pairs={{0,16},{1,9},{2,18},{3,11},{4,20},{5,13},{6,22},{7,15},{8,24},{9,1... | collective-permute-start | bytes 786440 | tf_op jit(solution)/shard_map/ppermute | solution.py:38
  21.6 9.7 %collective-permute-start.10 = (bf16[128,1024]{1,0:T(8,128)(2,1)S(1)}, bf16[128,1024]{1,0:T(8,128)(2,1)S(1)}, u32[]{:S(2)}, u32[]{:S(2)}) collective-permute-start(bf16[128,1024]{1,0:T(8,128)(2,1)S(1)} %collective-permute-done.6.refs_5_), channel_id=1, source_target_pairs={{0,1},{1,0},{2,3},{3,2},{4,5},{5,4},{6,7},{7,6},{8,9},{9,8},{10,11... | collective-permute-start | bytes 786440 | tf_op jit(solution)/shard_map/ppermute | solution.py:38
  21.6 17.9 %collective-permute-start.3 = (bf16[128,1024]{1,0:T(8,128)(2,1)S(1)}, bf16[128,1024]{1,0:T(8,128)(2,1)S(1)}, u32[]{:S(2)}, u32[]{:S(2)}) collective-permute-start(bf16[128,1024]{1,0:T(8,128)(2,1)S(1)} %collective-permute-done.2.refs_2_), channel_id=1, source_target_pairs={{0,8},{1,17},{2,10},{3,19},{4,12},{5,21},{6,14},{7,23},{8,0},{9,25... | collective-permute-start | bytes 786440 | tf_op jit(solution)/shard_map/ppermute | solution.py:38
  22.4 17.1 %collective-permute-start.1 = (bf16[128,1024]{1,0:T(8,128)(2,1)S(1)}, bf16[128,1024]{1,0:T(8,128)(2,1)S(1)}, u32[]{:S(2)}, u32[]{:S(2)}) collective-permute-start(bf16[128,1024]{1,0:T(8,128)(2,1)S(1)} %collective-permute-done.refs_2_), channel_id=1, source_target_pairs={{0,2},{1,3},{2,4},{3,5},{4,6},{5,7},{6,0},{7,1},{8,10},{9,11},{10,... | collective-permute-start | bytes 786440 | tf_op jit(solution)/shard_map/ppermute | solution.py:38
  29.2 10.3 %collective-permute-start.11 = (bf16[128,1024]{1,0:T(8,128)(2,1)S(1)}, bf16[128,1024]{1,0:T(8,128)(2,1)S(1)}, u32[]{:S(2)}, u32[]{:S(2)}) collective-permute-start(bf16[128,1024]{1,0:T(8,128)(2,1)S(1)} %collective-permute-done.2.refs_2_), channel_id=1, source_target_pairs={{0,1},{1,0},{2,3},{3,2},{4,5},{5,4},{6,7},{7,6},{8,9},{9,8},{10,11... | collective-permute-start | bytes 786440 | tf_op jit(solution)/shard_map/ppermute | solution.py:38
  30.3 1.0 %copy-start.1 = (bf16[128,1024]{1,0:T(8,128)(2,1)}, bf16[128,1024]{1,0:T(8,128)(2,1)S(1)}, u32[]{:S(2)}) copy-start(bf16[128,1024]{1,0:T(8,128)(2,1)S(1)} %collective-permute-done.17.refs_4_) | copy-start | bytes 786436
  30.3 9.2 %collective-permute-start.12 = (bf16[128,1024]{1,0:T(8,128)(2,1)S(1)}, bf16[128,1024]{1,0:T(8,128)(2,1)}, u32[]{:S(2)}, u32[]{:S(2)}) collective-permute-start(bf16[128,1024]{1,0:T(8,128)(2,1)S(1)} %collective-permute-done.2.refs_2_), channel_id=1, source_target_pairs={{0,16},{1,9},{2,18},{3,11},{4,20},{5,13},{6,22},{7,15},{8,24},{9,1... | collective-permute-start | bytes 786440 | tf_op jit(solution)/shard_map/ppermute | solution.py:38
  31.3 9.8 %collective-permute-start.18 = (bf16[128,1024]{1,0:T(8,128)(2,1)}, bf16[128,1024]{1,0:T(8,128)(2,1)}, u32[]{:S(2)}, u32[]{:S(2)}) collective-permute-start(bf16[128,1024]{1,0:T(8,128)(2,1)} %collective-permute-done.16.refs_3_), channel_id=1, source_target_pairs={{0,16},{1,9},{2,18},{3,11},{4,20},{5,13},{6,22},{7,15},{8,24},{9,1... | collective-permute-start | bytes 786440 | tf_op jit(solution)/shard_map/ppermute | solution.py:38
  32.3 1.0 %copy-start = (bf16[128,1024]{1,0:T(8,128)(2,1)S(1)}, bf16[128,1024]{1,0:T(8,128)(2,1)}, u32[]{:S(2)}) copy-start(bf16[128,1024]{1,0:T(8,128)(2,1)} %refs_2_.1) | copy-start | bytes 786436
  33.3 7.8 %copy-start.2 = (bf16[128,1024]{1,0:T(8,128)(2,1)S(1)}, bf16[128,1024]{1,0:T(8,128)(2,1)}, u32[]{:S(2)}) copy-start(bf16[128,1024]{1,0:T(8,128)(2,1)} %copy-done.1) | copy-start | bytes 786436
  39.5 6.4 %collective-permute-start.13 = (bf16[128,1024]{1,0:T(8,128)(2,1)S(1)}, bf16[128,1024]{1,0:T(8,128)(2,1)S(1)}, u32[]{:S(2)}, u32[]{:S(2)}) collective-permute-start(bf16[128,1024]{1,0:T(8,128)(2,1)S(1)} %collective-permute-done.3.refs_3_), channel_id=1, source_target_pairs={{0,16},{1,9},{2,18},{3,11},{4,20},{5,13},{6,22},{7,15},{8,24},{9,1... | collective-permute-start | bytes 786440 | tf_op jit(solution)/shard_map/ppermute | solution.py:38
  40.6 6.7 %collective-permute-start.19 = (bf16[128,1024]{1,0:T(8,128)(2,1)S(1)}, bf16[128,1024]{1,0:T(8,128)(2,1)S(1)}, u32[]{:S(2)}, u32[]{:S(2)}) collective-permute-start(bf16[128,1024]{1,0:T(8,128)(2,1)S(1)} %collective-permute-done.refs_2_), channel_id=1, source_target_pairs={{0,1},{1,0},{2,3},{3,2},{4,5},{5,4},{6,7},{7,6},{8,9},{9,8},{10,11... | collective-permute-start | bytes 786440 | tf_op jit(solution)/shard_map/ppermute | solution.py:38
  40.6 16.1 %collective-permute-start.20 = (bf16[128,1024]{1,0:T(8,128)(2,1)}, bf16[128,1024]{1,0:T(8,128)(2,1)S(1)}, u32[]{:S(2)}, u32[]{:S(2)}) collective-permute-start(bf16[128,1024]{1,0:T(8,128)(2,1)} %collective-permute-done.16.refs_3_), channel_id=1, source_target_pairs={{0,1},{1,0},{2,3},{3,2},{4,5},{5,4},{6,7},{7,6},{8,9},{9,8},{10,11... | collective-permute-start | bytes 786440 | tf_op jit(solution)/shard_map/ppermute | solution.py:38
  41.1 15.7 %collective-permute-start.21 = (bf16[128,1024]{1,0:T(8,128)(2,1)S(1)}, bf16[128,1024]{1,0:T(8,128)(2,1)S(1)}, u32[]{:S(2)}, u32[]{:S(2)}) collective-permute-start(bf16[128,1024]{1,0:T(8,128)(2,1)S(1)} %copy-done.2), channel_id=1, source_target_pairs={{0,1},{1,0},{2,3},{3,2},{4,5},{5,4},{6,7},{7,6},{8,9},{9,8},{10,11... | collective-permute-start | bytes 786440 | tf_op jit(solution)/shard_map/ppermute | solution.py:38
  41.1 16.2 %collective-permute-start.22 = (bf16[128,1024]{1,0:T(8,128)(2,1)}, bf16[128,1024]{1,0:T(8,128)(2,1)S(1)}, u32[]{:S(2)}, u32[]{:S(2)}) collective-permute-start(bf16[128,1024]{1,0:T(8,128)(2,1)} %collective-permute-done.18.refs_5_), channel_id=1, source_target_pairs={{0,1},{1,0},{2,3},{3,2},{4,5},{5,4},{6,7},{7,6},{8,9},{9,8},{10,11... | collective-permute-start | bytes 786440 | tf_op jit(solution)/shard_map/ppermute | solution.py:38
  46.0 16.2 %collective-permute-start.14 = (bf16[128,1024]{1,0:T(8,128)(2,1)S(1)}, bf16[128,1024]{1,0:T(8,128)(2,1)S(1)}, u32[]{:S(2)}, u32[]{:S(2)}) collective-permute-start(bf16[128,1024]{1,0:T(8,128)(2,1)S(1)} %collective-permute-done.1.refs_2_), channel_id=1, source_target_pairs={{0,8},{1,17},{2,10},{3,19},{4,12},{5,21},{6,14},{7,23},{8,0},{9,25... | collective-permute-start | bytes 786440 | tf_op jit(solution)/shard_map/ppermute | solution.py:38
  47.3 14.8 %collective-permute-start.15 = (bf16[128,1024]{1,0:T(8,128)(2,1)S(1)}, bf16[128,1024]{1,0:T(8,128)(2,1)S(1)}, u32[]{:S(2)}, u32[]{:S(2)}) collective-permute-start(bf16[128,1024]{1,0:T(8,128)(2,1)S(1)} %collective-permute-done.1.refs_2_), channel_id=1, source_target_pairs={{0,16},{1,9},{2,18},{3,11},{4,20},{5,13},{6,22},{7,15},{8,24},{9,1... | collective-permute-start | bytes 786440 | tf_op jit(solution)/shard_map/ppermute | solution.py:38
  56.8 6.8 %collective-permute-start.27 = (bf16[128,1024]{1,0:T(8,128)(2,1)S(1)}, bf16[128,1024]{1,0:T(8,128)(2,1)S(1)}, u32[]{:S(2)}, u32[]{:S(2)}) collective-permute-start(bf16[128,1024]{1,0:T(8,128)(2,1)S(1)} %collective-permute-done.3.refs_3_), channel_id=1, source_target_pairs={{0,1},{1,0},{2,3},{3,2},{4,5},{5,4},{6,7},{7,6},{8,9},{9,8},{10,11... | collective-permute-start | bytes 786440 | tf_op jit(solution)/shard_map/ppermute | solution.py:38
  56.8 7.2 %collective-permute-start.28 = (bf16[128,1024]{1,0:T(8,128)(2,1)}, bf16[128,1024]{1,0:T(8,128)(2,1)S(1)}, u32[]{:S(2)}, u32[]{:S(2)}) collective-permute-start(bf16[128,1024]{1,0:T(8,128)(2,1)} %collective-permute-done.12.refs_4_), channel_id=1, source_target_pairs={{0,1},{1,0},{2,3},{3,2},{4,5},{5,4},{6,7},{7,6},{8,9},{9,8},{10,11... | collective-permute-start | bytes 786440 | tf_op jit(solution)/shard_map/ppermute | solution.py:38
  57.3 6.8 %collective-permute-start.29 = (bf16[128,1024]{1,0:T(8,128)(2,1)S(1)}, bf16[128,1024]{1,0:T(8,128)(2,1)S(1)}, u32[]{:S(2)}, u32[]{:S(2)}) collective-permute-start(bf16[128,1024]{1,0:T(8,128)(2,1)S(1)} %collective-permute-done.13.refs_5_), channel_id=1, source_target_pairs={{0,1},{1,0},{2,3},{3,2},{4,5},{5,4},{6,7},{7,6},{8,9},{9,8},{10,11... | collective-permute-start | bytes 786440 | tf_op jit(solution)/shard_map/ppermute | solution.py:38
  62.1 6.6 %collective-permute-start.23 = (bf16[128,1024]{1,0:T(8,128)(2,1)S(1)}, bf16[128,1024]{1,0:T(8,128)(2,1)S(1)}, u32[]{:S(2)}, u32[]{:S(2)}) collective-permute-start(bf16[128,1024]{1,0:T(8,128)(2,1)S(1)} %collective-permute-done.14.refs_3_), channel_id=1, source_target_pairs={{0,16},{1,9},{2,18},{3,11},{4,20},{5,13},{6,22},{7,15},{8,24},{9,1... | collective-permute-start | bytes 786440 | tf_op jit(solution)/shard_map/ppermute | solution.py:38
  63.5 5.7 %collective-permute-start.24 = (bf16[128,1024]{1,0:T(8,128)(2,1)S(1)}, bf16[128,1024]{1,0:T(8,128)(2,1)S(1)}, u32[]{:S(2)}, u32[]{:S(2)}) collective-permute-start(bf16[128,1024]{1,0:T(8,128)(2,1)S(1)} %collective-permute-done.1.refs_2_), channel_id=1, source_target_pairs={{0,1},{1,0},{2,3},{3,2},{4,5},{5,4},{6,7},{7,6},{8,9},{9,8},{10,11... | collective-permute-start | bytes 786440 | tf_op jit(solution)/shard_map/ppermute | solution.py:38
  63.5 5.7 %collective-permute-start.25 = (bf16[128,1024]{1,0:T(8,128)(2,1)S(1)}, bf16[128,1024]{1,0:T(8,128)(2,1)S(1)}, u32[]{:S(2)}, u32[]{:S(2)}) collective-permute-start(bf16[128,1024]{1,0:T(8,128)(2,1)S(1)} %collective-permute-done.14.refs_3_), channel_id=1, source_target_pairs={{0,1},{1,0},{2,3},{3,2},{4,5},{5,4},{6,7},{7,6},{8,9},{9,8},{10,11... | collective-permute-start | bytes 786440 | tf_op jit(solution)/shard_map/ppermute | solution.py:38
  64.1 5.2 %collective-permute-start.26 = (bf16[128,1024]{1,0:T(8,128)(2,1)S(1)}, bf16[128,1024]{1,0:T(8,128)(2,1)S(1)}, u32[]{:S(2)}, u32[]{:S(2)}) collective-permute-start(bf16[128,1024]{1,0:T(8,128)(2,1)S(1)} %collective-permute-done.15.refs_4_), channel_id=1, source_target_pairs={{0,1},{1,0},{2,3},{3,2},{4,5},{5,4},{6,7},{7,6},{8,9},{9,8},{10,11... | collective-permute-start | bytes 786440 | tf_op jit(solution)/shard_map/ppermute | solution.py:38
  68.7 18.6 %copy-start.3 = (f32[128]{0:T(128)S(1)}, f32[128]{0:T(128)}, u32[]{:S(2)}) copy-start(f32[128]{0:T(128)} %param.10) | copy-start | bytes 1540
  68.8 1.7 %collective-permute-start.30 = (bf16[128,1024]{1,0:T(8,128)(2,1)S(1)}, bf16[128,1024]{1,0:T(8,128)(2,1)S(1)}, u32[]{:S(2)}, u32[]{:S(2)}) collective-permute-start(bf16[128,1024]{1,0:T(8,128)(2,1)S(1)} %collective-permute-done.23.refs_5_), channel_id=1, source_target_pairs={{0,1},{1,0},{2,3},{3,2},{4,5},{5,4},{6,7},{7,6},{8,9},{9,8},{10,11... | collective-permute-start | bytes 786440 | tf_op jit(solution)/shard_map/ppermute | solution.py:38
  76.0 11.3 %all-to-all-start.1 = ((f32[32,3,128]{2,1,0:T(4,128)}), f32[32,3,128]{2,1,0:T(4,128)S(1)}, u32[]{:S(2)}, u32[]{:S(2)}) async-start(f32[32,3,128]{2,1,0:T(4,128)} %bitcast.13), calls=%async_computation.1 | async-start | bytes 131072 | tf_op jit(solution)/shard_map/all_to_all | solution.py:292

commit v12 on v9

--- a/solution.py
+++ b/solution.py
@@ -286,30 +286,35 @@
     packed = squares(after(hidden, starts), norm_gain[None, :], targets[None, :], n_dp * n_t)
     fine = lax.all_to_all(packed, ("dp", "tensor"), 0, 0, tiled=True)
 
-    acc, deep, half = None, CORES * feat, []
+    acc, deep, spreads, half = None, CORES * feat, {}, []
     for at, group in enumerate(groups):
         final = at == len(groups) - 1
         middle = at and not final
         offsets = [2 + n_dp + dz for dz in group]
-        own = grid.sibling(reached[at][0, 0])
-        held = [acc, own, *(layers[dz] for dz in groups[2])] if at == 1 else half if at else [packed]
-        spread = grid.fill(dict(reached[at]), *held)
+        own = grid.sibling(after(reached[at][0, 0], *(half if final else [])))
+        if at == 1:
+            held = [acc, own, *(layers[dz] for dz in groups[2])]
+        else:
+            held = [] if at else [packed]
+        spread = spreads.get(at) or grid.fill(dict(reached[at]), *held)
         if at == 0:
             weights = [head]
         elif at == 1:
             for later in groups[1:]:
                 ready = after(head, acc, *(layers[dz] for dz in groups[2]))
                 weights.append(loaded(starts, [2 + n_dp + dz for dz in later], ready, deep))
-        if at:
-            reach_next(at + 1, weights[1] if at == 1 else spread[-1])
-        others = [own] + [grid.sibling(a) for a in spread[1:-1]]
-        others.append(grid.sibling(after(spread[-1], *([acc] if final else weights[1:3] if middle else []))))
+        following = half if final else []
+        if middle:
+            reach_next(at + 1, *reached[at].values())
+            following = [*reached[at + 1].values(), *weights[1:3]]
+            spreads[at + 1] = grid.fill(dict(reached[at + 1]))
+        others = [own] + [grid.sibling(after(a, *following)) for a in spread[1:]]
         blocks = spread + others
         for layer, offset in enumerate(offsets):
             done = layer == len(offsets) - 1
             if middle and done:
                 half = [acc]
-                blocks[0] = after(blocks[0], *reached[at + 1].values())
+                blocks[0] = after(blocks[0], spreads[at + 1][-1])
             last = final and done
             acc = layer_product(tok, n_t, starts, layer, offset, fine, blocks, place, weights[at], acc, last)
 

time: 79.2 us -> 80.5 us (1.016)
  starting transfers between devices: 24.8 us -> 25.9 us
    ppermute x24, starting transfers between devices: 17.2 us -> 18 us  [permute(): return lax.ppermute(a, ('dp', 'tensor'), perm)]
  transfers between devices with their start and end apart: 26 -> 26, of which waited for: 11 -> 10; matrix products, arithmetic and copies ran while one was open for 0% -> 0% of each run, Pallas kernels for 31% -> 30%
where the time goes in v12:
time: 80.5 us; the launch traced here: 80.1 us
  Pallas kernels  29.8 us (37%)
  starting transfers between devices  25.9 us (32%)
  waiting for transfers between devices  19.5 us (24%)
  local copies, waits for them, and re-layouts  2.71 us (3%)
  between operations  1.45 us (2%)
    pallas_call x4, Pallas kernels, layer_product(): pl.pallas_call(functools.partial(layer_kernel, n, n_t, place, layer, offs...  20.8 us
    ppermute x24, starting transfers between devices, permute(): return lax.ppermute(a, ('dp', 'tensor'), perm)  18 us
    ppermute x24, waiting for transfers between devices, permute(): return lax.ppermute(a, ('dp', 'tensor'), perm)  11.7 us
    pallas_call x2, Pallas kernels, loaded(): pl.pallas_call(functools.partial(load_kernel, offsets), out_shape=pltpu.V...  7.23 us
    all_to_all x1, waiting for transfers between devices, body(): lax.all_to_all(acc.reshape(n_dp * n_t, 3, tok), ('dp', 'tensor'), 0, 0, t...  6.74 us
    all_to_all x1, starting transfers between devices, body(): fine = lax.all_to_all(packed, ('dp', 'tensor'), 0, 0, tiled=True)  5.04 us
    all_to_all x1, starting transfers between devices, body(): lax.all_to_all(acc.reshape(n_dp * n_t, 3, tok), ('dp', 'tensor'), 0, 0, t...  2.86 us
    unnamed x10, local copies, waits for them, and re-layouts  2.62 us
  transfers between devices with their start and end apart: 26, of which 10 were waited for; matrix products, arithmetic and copies ran while one was open for 0% of the time, Pallas kernels for 30%

profile of v12, /device:TPU:0, one launch (start us, length us, event | category | flops | bytes accessed | tf_op | source)
XLA Modules:
  0.0 80.1 jit_solution(9899347484931097801)
XLA Ops:
  0.6 3.0 %collective-permute-start.2 = (bf16[128,1024]{1,0:T(8,128)(2,1)}, bf16[128,1024]{1,0:T(8,128)(2,1)S(1)}, u32[]{:S(2)}, u32[]{:S(2)}) collective-permute-start(bf16[128,1024]{1,0:T(8,128)(2,1)} %refs_2_.1), channel_id=1, source_target_pairs={{0,8},{1,17},{2,10},{3,19},{4,12},{5,21},{6,14},{7,23},{8,0},{9,25... | collective-permute-start | bytes 786440 | tf_op jit(solution)/shard_map/ppermute | solution.py:38
  3.6 1.5 %collective-permute-start.3 = (bf16[128,1024]{1,0:T(8,128)(2,1)}, bf16[128,1024]{1,0:T(8,128)(2,1)S(1)}, u32[]{:S(2)}, u32[]{:S(2)}) collective-permute-start(bf16[128,1024]{1,0:T(8,128)(2,1)} %refs_2_.1), channel_id=1, source_target_pairs={{0,16},{1,9},{2,18},{3,11},{4,20},{5,13},{6,22},{7,15},{8,24},{9,1... | collective-permute-start | bytes 786440 | tf_op jit(solution)/shard_map/ppermute | solution.py:38
  5.2 0.0 collective-permute-start.11
  5.2 1.6 %collective-permute-start = (bf16[128,1024]{1,0:T(8,128)(2,1)}, bf16[128,1024]{1,0:T(8,128)(2,1)S(1)}, u32[]{:S(2)}, u32[]{:S(2)}) collective-permute-start(bf16[128,1024]{1,0:T(8,128)(2,1)} %refs_2_.1), channel_id=1, source_target_pairs={{0,2},{1,3},{2,4},{3,5},{4,6},{5,7},{6,0},{7,1},{8,10},{9,11},{10,... | collective-permute-start | bytes 786440 | tf_op jit(solution)/shard_map/ppermute | solution.py:38
  6.7 2.2 %collective-permute-start.4 = (bf16[128,1024]{1,0:T(8,128)(2,1)}, bf16[128,1024]{1,0:T(8,128)(2,1)S(1)}, u32[]{:S(2)}, u32[]{:S(2)}) collective-permute-start(bf16[128,1024]{1,0:T(8,128)(2,1)} %refs_2_.1), channel_id=1, source_target_pairs={{0,6},{1,7},{2,0},{3,1},{4,2},{5,3},{6,4},{7,5},{8,14},{9,15},{10,... | collective-permute-start | bytes 786440 | tf_op jit(solution)/shard_map/ppermute | solution.py:38
  9.0 0.1 stack.43.refs_0_.start_ref
  9.1 1.8 %shard_map.77 = f32[32,1,1280]{2,1,0:T(1,128)} custom-call(bf16[128,1024]{1,0:T(8,128)(2,1)} %refs_2_.1, f32[1,1024]{1,0:T(1,128)} %bitcast.22, s32[1,128]{1,0:T(1,128)} %bitcast.23), custom_call_target="tpu_custom_call" | custom-call | tf_op jit(solution)/shard_map/pallas_call | solution.py:243
  10.9 1.1 %collective-permute-start.10 = (bf16[128,1024]{1,0:T(8,128)(2,1)S(1)}, bf16[128,1024]{1,0:T(8,128)(2,1)S(1)}, u32[]{:S(2)}, u32[]{:S(2)}) collective-permute-start(bf16[128,1024]{1,0:T(8,128)(2,1)S(1)} %collective-permute-done.2.refs_3_), channel_id=1, source_target_pairs={{0,16},{1,9},{2,18},{3,11},{4,20},{5,13},{6,22},{7,15},{8,24},{9,1... | collective-permute-start | bytes 786440 | tf_op jit(solution)/shard_map/ppermute | solution.py:38
  12.0 0.9 %collective-permute-start.12 = (bf16[128,1024]{1,0:T(8,128)(2,1)S(1)}, bf16[128,1024]{1,0:T(8,128)(2,1)}, u32[]{:S(2)}, u32[]{:S(2)}) collective-permute-start(bf16[128,1024]{1,0:T(8,128)(2,1)S(1)} %collective-permute-done.2.refs_3_), channel_id=1, source_target_pairs={{0,1},{1,0},{2,3},{3,2},{4,5},{5,4},{6,7},{7,6},{8,9},{9,8},{10,11... | collective-permute-start | bytes 786440 | tf_op jit(solution)/shard_map/ppermute | solution.py:38
  12.9 5.0 %all-to-all-start = ((f32[32,1,1280]{2,1,0:T(1,128)}), f32[32,1,1280]{2,1,0:T(1,128)S(1)}, u32[]{:S(2)}, u32[]{:S(2)}) async-start(f32[32,1,1280]{2,1,0:T(1,128)} %shard_map.77), calls=%async_computation | async-start | bytes 327680 | tf_op jit(solution)/shard_map/all_to_all | solution.py:287
  17.9 3.2 %collective-permute-done.4.refs_1_ = bf16[128,1024]{1,0:T(8,128)(2,1)S(1)} collective-permute-done((bf16[128,1024]{1,0:T(8,128)(2,1)}, bf16[128,1024]{1,0:T(8,128)(2,1)S(1)}, u32[]{:S(2)}, u32[]{:S(2)}) %collective-permute-start.4) | collective-permute-done | bytes 262176 | tf_op jit(solution)/shard_map/ppermute | solution.py:38
  21.2 0.4 collective-permute-start.5
  21.7 0.7 collective-permute-start.6
  22.4 1.2 %collective-permute-start.15 = (bf16[256,1024]{1,0:T(8,128)(2,1)S(1)}, bf16[256,1024]{1,0:T(8,128)(2,1)S(1)}, u32[]{:S(2)}, u32[]{:S(2)}) collective-permute-start(bf16[256,1024]{1,0:T(8,128)(2,1)S(1)} %shard_map.78.refs_2_), channel_id=1, source_target_pairs={{0,1},{1,0},{2,3},{3,2},{4,5},{5,4},{6,7},{7,6},{8,9},{9,8},{10,11... | collective-permute-start | bytes 1572872 | tf_op jit(solution)/shard_map/ppermute | solution.py:38
  23.5 0.1 collective-permute-start.14
  23.6 0.7 copy-done.1
  24.3 1.0 %collective-permute-start.1 = (bf16[128,1024]{1,0:T(8,128)(2,1)}, bf16[128,1024]{1,0:T(8,128)(2,1)}, u32[]{:S(2)}, u32[]{:S(2)}) collective-permute-start(bf16[128,1024]{1,0:T(8,128)(2,1)} %copy-done.3), channel_id=1, source_target_pairs={{0,2},{1,3},{2,4},{3,5},{4,6},{5,7},{6,0},{7,1},{8,10},{9,11},{10,... | collective-permute-start | bytes 786440 | tf_op jit(solution)/shard_map/ppermute | solution.py:38
  25.3 1.1 %all-to-all-done.refs_1_ = f32[32,1,1280]{2,1,0:T(1,128)S(1)} async-done(((f32[32,1,1280]{2,1,0:T(1,128)}), f32[32,1,1280]{2,1,0:T(1,128)S(1)}, u32[]{:S(2)}, u32[]{:S(2)}) %all-to-all-start) | async-done | bytes 163872 | tf_op jit(solution)/shard_map/all_to_all | solution.py:287
  26.4 0.9 %copy-done = bf16[128,1024]{1,0:T(8,128)(2,1)S(1)} copy-done((bf16[128,1024]{1,0:T(8,128)(2,1)S(1)}, bf16[128,1024]{1,0:T(8,128)(2,1)}, u32[]{:S(2)}) %copy-start) | copy-done | bytes 262168
  27.3 0.9 %copy-done.2 = bf16[128,1024]{1,0:T(8,128)(2,1)S(1)} copy-done((bf16[128,1024]{1,0:T(8,128)(2,1)S(1)}, bf16[128,1024]{1,0:T(8,128)(2,1)}, u32[]{:S(2)}) %copy-start.2) | copy-done | bytes 262168
  28.3 6.7 %shard_map.79.refs_11_ = f32[512,1152]{1,0:T(8,128)S(1)} custom-call(s32[10]{0:T(128)S(1)} %stack.43.refs_0_.start_ref, f32[32,1,1280]{2,1,0:T(1,128)S(1)} %all-to-all-done.refs_1_, bf16[128,1024]{1,0:T(8,128)(2,1)S(1)} %copy-done, bf16[128,1024]{1,0:T(8,128)(2,1)S(1)} %collective-permute-done.2.refs_3_, ...), custom_call_target="tpu_custom_call" | custom-call | flops 2415919104 | bytes 4718592 | tf_op jit(solution)/shard_map/pallas_call | solution.py:211
  35.0 0.1 collective-permute-done.1.refs_2_
  35.1 1.3 %collective-permute-done.5.refs_3_ = bf16[256,1024]{1,0:T(8,128)(2,1)S(1)} collective-permute-done((bf16[256,1024]{1,0:T(8,128)(2,1)S(1)}, bf16[256,1024]{1,0:T(8,128)(2,1)S(1)}, u32[]{:S(2)}, u32[]{:S(2)}) %collective-permute-start.5) | collective-permute-done | bytes 524320 | tf_op jit(solution)/shard_map/ppermute | solution.py:38
  36.4 0.6 collective-permute-start.16
  37.0 0.1 collective-permute-start.7
  37.1 1.3 %collective-permute-start.8 = (bf16[128,1024]{1,0:T(8,128)(2,1)}, bf16[128,1024]{1,0:T(8,128)(2,1)S(1)}, u32[]{:S(2)}, u32[]{:S(2)}) collective-permute-start(bf16[128,1024]{1,0:T(8,128)(2,1)} %collective-permute-done.1.refs_2_), channel_id=1, source_target_pairs={{0,16},{1,9},{2,18},{3,11},{4,20},{5,13},{6,22},{7,15},{8,24},{9,1... | collective-permute-start | bytes 786440 | tf_op jit(solution)/shard_map/ppermute | solution.py:38
  38.4 4.3 %shard_map.80.refs_10_ = bf16[2,2048,1152]{2,1,0:T(8,128)(2,1)S(1)} custom-call(s32[10]{0:T(128)S(1)} %stack.43.refs_0_.start_ref, bf16[8192,1152]{1,0:T(8,128)(2,1)} %head_ref.1), custom_call_target="tpu_custom_call" | custom-call | tf_op jit(solution)/shard_map/pallas_call | solution.py:116
  42.7 2.9 %shard_map.81.refs_10_ = bf16[1,2048,1152]{2,1,0:T(8,128)(2,1)S(1)} custom-call(s32[10]{0:T(128)S(1)} %stack.43.refs_0_.start_ref, bf16[8192,1152]{1,0:T(8,128)(2,1)} %head_ref.1), custom_call_target="tpu_custom_call" | custom-call | tf_op jit(solution)/shard_map/pallas_call | solution.py:116
  45.6 0.8 %collective-permute-done.7.refs_3_ = bf16[128,1024]{1,0:T(8,128)(2,1)S(1)} collective-permute-done((bf16[128,1024]{1,0:T(8,128)(2,1)}, bf16[128,1024]{1,0:T(8,128)(2,1)S(1)}, u32[]{:S(2)}, u32[]{:S(2)}) %collective-permute-start.7) | collective-permute-done | bytes 262176 | tf_op jit(solution)/shard_map/ppermute | solution.py:38
  46.4 4.0 %collective-permute-done.8.refs_4_ = bf16[128,1024]{1,0:T(8,128)(2,1)S(1)} collective-permute-done((bf16[128,1024]{1,0:T(8,128)(2,1)}, bf16[128,1024]{1,0:T(8,128)(2,1)S(1)}, u32[]{:S(2)}, u32[]{:S(2)}) %collective-permute-start.8) | collective-permute-done | bytes 262176 | tf_op jit(solution)/shard_map/ppermute | solution.py:38
  50.5 0.5 collective-permute-start.17
  51.0 0.0 collective-permute-start.19
  51.0 0.7 collective-permute-start.9
  51.7 0.7 collective-permute-done.18.refs_8_
  52.4 0.7 collective-permute-done.17.refs_7_
  53.1 0.7 collective-permute-done.19.refs_9_
  53.9 4.2 %shard_map.82.refs_11_ = f32[512,1152]{1,0:T(8,128)S(1)} custom-call(s32[10]{0:T(128)S(1)} %stack.43.refs_0_.start_ref, f32[32,1,1280]{2,1,0:T(1,128)S(1)} %all-to-all-done.refs_1_, bf16[256,1024]{1,0:T(8,128)(2,1)S(1)} %shard_map.78.refs_2_, bf16[256,1024]{1,0:T(8,128)(2,1)S(1)} %collective-permute-done.5.refs_3_, ...), custom_call_target="tpu_custom_call" | custom-call | flops 2415919104 | bytes 4718592 | tf_op jit(solution)/shard_map/pallas_call | solution.py:211
  58.1 0.2 collective-permute-start.23
  58.3 0.4 collective-permute-start.22
  58.6 0.1 collective-permute-start.21
  58.8 0.4 collective-permute-start.20
  59.1 4.2 %shard_map.83.refs_11_ = f32[512,1152]{1,0:T(8,128)S(1)} custom-call(s32[10]{0:T(128)S(1)} %stack.43.refs_0_.start_ref, f32[32,1,1280]{2,1,0:T(1,128)S(1)} %all-to-all-done.refs_1_, bf16[256,1024]{1,0:T(8,128)(2,1)S(1)} %shard_map.78.refs_2_, bf16[256,1024]{1,0:T(8,128)(2,1)S(1)} %collective-permute-done.5.refs_3_, ...), custom_call_target="tpu_custom_call" | custom-call | flops 2415919104 | bytes 4718592 | tf_op jit(solution)/shard_map/pallas_call | solution.py:211
  63.3 0.0 copy-start.4
  63.4 5.8 %shard_map.84 = f32[4,8,3,128]{3,2,1,0:T(4,128)} custom-call(s32[10]{0:T(128)S(1)} %stack.43.refs_0_.start_ref, f32[32,1,1280]{2,1,0:T(1,128)S(1)} %all-to-all-done.refs_1_, bf16[128,1024]{1,0:T(8,128)(2,1)} %collective-permute-done.1.refs_2_, bf16[128,1024]{1,0:T(8,128)(2,1)S(1)} %collective-permute-done.7.refs_3_, ...), custom_call_target="tpu_custom_call" | custom-call | flops 2415919104 | bytes 4718592 | tf_op jit(solution)/shard_map/pallas_call | solution.py:211
  69.2 2.9 %all-to-all-start.1 = ((f32[32,3,128]{2,1,0:T(4,128)}), f32[32,3,128]{2,1,0:T(4,128)S(1)}, u32[]{:S(2)}, u32[]{:S(2)}) async-start(f32[32,3,128]{2,1,0:T(4,128)} %bitcast.13), calls=%async_computation.1 | async-start | bytes 131072 | tf_op jit(solution)/shard_map/all_to_all | solution.py:321
  72.7 6.7 %all-to-all-done.1 = f32[32,3,128]{2,1,0:T(4,128)S(1)} async-done(((f32[32,3,128]{2,1,0:T(4,128)}), f32[32,3,128]{2,1,0:T(4,128)S(1)}, u32[]{:S(2)}, u32[]{:S(2)}) %all-to-all-start.1) | async-done | bytes 49184 | tf_op jit(solution)/shard_map/all_to_all | solution.py:321
  79.4 0.1 slice_reduce_fusion
  79.5 0.5 compare_select_fusion
  (27 shorter events, 0.1 us)
Async XLA Ops:
  0.6 10.2 %collective-permute-start.2 = (bf16[128,1024]{1,0:T(8,128)(2,1)}, bf16[128,1024]{1,0:T(8,128)(2,1)S(1)}, u32[]{:S(2)}, u32[]{:S(2)}) collective-permute-start(bf16[128,1024]{1,0:T(8,128)(2,1)} %refs_2_.1), channel_id=1, source_target_pairs={{0,8},{1,17},{2,10},{3,19},{4,12},{5,21},{6,14},{7,23},{8,0},{9,25... | collective-permute-start | bytes 786440 | tf_op jit(solution)/shard_map/ppermute | solution.py:38
  3.6 7.2 %collective-permute-start.3 = (bf16[128,1024]{1,0:T(8,128)(2,1)}, bf16[128,1024]{1,0:T(8,128)(2,1)S(1)}, u32[]{:S(2)}, u32[]{:S(2)}) collective-permute-start(bf16[128,1024]{1,0:T(8,128)(2,1)} %refs_2_.1), channel_id=1, source_target_pairs={{0,16},{1,9},{2,18},{3,11},{4,20},{5,13},{6,22},{7,15},{8,24},{9,1... | collective-permute-start | bytes 786440 | tf_op jit(solution)/shard_map/ppermute | solution.py:38
  5.2 16.5 %collective-permute-start.11 = (bf16[128,1024]{1,0:T(8,128)(2,1)}, bf16[128,1024]{1,0:T(8,128)(2,1)S(1)}, u32[]{:S(2)}, u32[]{:S(2)}) collective-permute-start(bf16[128,1024]{1,0:T(8,128)(2,1)} %refs_2_.1), channel_id=1, source_target_pairs={{0,1},{1,0},{2,3},{3,2},{4,5},{5,4},{6,7},{7,6},{8,9},{9,8},{10,11... | collective-permute-start | bytes 786440 | tf_op jit(solution)/shard_map/ppermute | solution.py:38
  5.2 12.8 %collective-permute-start = (bf16[128,1024]{1,0:T(8,128)(2,1)}, bf16[128,1024]{1,0:T(8,128)(2,1)S(1)}, u32[]{:S(2)}, u32[]{:S(2)}) collective-permute-start(bf16[128,1024]{1,0:T(8,128)(2,1)} %refs_2_.1), channel_id=1, source_target_pairs={{0,2},{1,3},{2,4},{3,5},{4,6},{5,7},{6,0},{7,1},{8,10},{9,11},{10,... | collective-permute-start | bytes 786440 | tf_op jit(solution)/shard_map/ppermute | solution.py:38
  6.7 14.4 %collective-permute-start.4 = (bf16[128,1024]{1,0:T(8,128)(2,1)}, bf16[128,1024]{1,0:T(8,128)(2,1)S(1)}, u32[]{:S(2)}, u32[]{:S(2)}) collective-permute-start(bf16[128,1024]{1,0:T(8,128)(2,1)} %refs_2_.1), channel_id=1, source_target_pairs={{0,6},{1,7},{2,0},{3,1},{4,2},{5,3},{6,4},{7,5},{8,14},{9,15},{10,... | collective-permute-start | bytes 786440 | tf_op jit(solution)/shard_map/ppermute | solution.py:38
  10.9 11.5 %collective-permute-start.10 = (bf16[128,1024]{1,0:T(8,128)(2,1)S(1)}, bf16[128,1024]{1,0:T(8,128)(2,1)S(1)}, u32[]{:S(2)}, u32[]{:S(2)}) collective-permute-start(bf16[128,1024]{1,0:T(8,128)(2,1)S(1)} %collective-permute-done.2.refs_3_), channel_id=1, source_target_pairs={{0,16},{1,9},{2,18},{3,11},{4,20},{5,13},{6,22},{7,15},{8,24},{9,1... | collective-permute-start | bytes 786440 | tf_op jit(solution)/shard_map/ppermute | solution.py:38
  12.0 11.5 %collective-permute-start.12 = (bf16[128,1024]{1,0:T(8,128)(2,1)S(1)}, bf16[128,1024]{1,0:T(8,128)(2,1)}, u32[]{:S(2)}, u32[]{:S(2)}) collective-permute-start(bf16[128,1024]{1,0:T(8,128)(2,1)S(1)} %collective-permute-done.2.refs_3_), channel_id=1, source_target_pairs={{0,1},{1,0},{2,3},{3,2},{4,5},{5,4},{6,7},{7,6},{8,9},{9,8},{10,11... | collective-permute-start | bytes 786440 | tf_op jit(solution)/shard_map/ppermute | solution.py:38
  12.9 13.5 %all-to-all-start = ((f32[32,1,1280]{2,1,0:T(1,128)}), f32[32,1,1280]{2,1,0:T(1,128)S(1)}, u32[]{:S(2)}, u32[]{:S(2)}) async-start(f32[32,1,1280]{2,1,0:T(1,128)} %shard_map.77), calls=%async_computation | async-start | bytes 327680 | tf_op jit(solution)/shard_map/all_to_all | solution.py:287
  17.9 3.7 %copy-start.3 = (bf16[128,1024]{1,0:T(8,128)(2,1)}, bf16[128,1024]{1,0:T(8,128)(2,1)S(1)}, u32[]{:S(2)}) copy-start(bf16[128,1024]{1,0:T(8,128)(2,1)S(1)} %collective-permute-done.refs_0_) | copy-start | bytes 786436
  21.2 15.2 %collective-permute-start.5 = (bf16[256,1024]{1,0:T(8,128)(2,1)S(1)}, bf16[256,1024]{1,0:T(8,128)(2,1)S(1)}, u32[]{:S(2)}, u32[]{:S(2)}) collective-permute-start(bf16[256,1024]{1,0:T(8,128)(2,1)S(1)} %shard_map.78.refs_2_), channel_id=1, source_target_pairs={{0,8},{1,17},{2,10},{3,19},{4,12},{5,21},{6,14},{7,23},{8,0},{9,25... | collective-permute-start | bytes 1572872 | tf_op jit(solution)/shard_map/ppermute | solution.py:38
  21.6 2.0 %collective-permute-start.13 = (bf16[128,1024]{1,0:T(8,128)(2,1)S(1)}, bf16[128,1024]{1,0:T(8,128)(2,1)S(1)}, u32[]{:S(2)}, u32[]{:S(2)}) collective-permute-start(bf16[128,1024]{1,0:T(8,128)(2,1)S(1)} %collective-permute-done.3.refs_4_), channel_id=1, source_target_pairs={{0,1},{1,0},{2,3},{3,2},{4,5},{5,4},{6,7},{7,6},{8,9},{9,8},{10,11... | collective-permute-start | bytes 786440 | tf_op jit(solution)/shard_map/ppermute | solution.py:38
  21.7 14.7 %collective-permute-start.6 = (bf16[256,1024]{1,0:T(8,128)(2,1)S(1)}, bf16[256,1024]{1,0:T(8,128)(2,1)S(1)}, u32[]{:S(2)}, u32[]{:S(2)}) collective-permute-start(bf16[256,1024]{1,0:T(8,128)(2,1)S(1)} %shard_map.78.refs_2_), channel_id=1, source_target_pairs={{0,16},{1,9},{2,18},{3,11},{4,20},{5,13},{6,22},{7,15},{8,24},{9,1... | collective-permute-start | bytes 1572872 | tf_op jit(solution)/shard_map/ppermute | solution.py:38
  22.4 14.0 %collective-permute-start.15 = (bf16[256,1024]{1,0:T(8,128)(2,1)S(1)}, bf16[256,1024]{1,0:T(8,128)(2,1)S(1)}, u32[]{:S(2)}, u32[]{:S(2)}) collective-permute-start(bf16[256,1024]{1,0:T(8,128)(2,1)S(1)} %shard_map.78.refs_2_), channel_id=1, source_target_pairs={{0,1},{1,0},{2,3},{3,2},{4,5},{5,4},{6,7},{7,6},{8,9},{9,8},{10,11... | collective-permute-start | bytes 1572872 | tf_op jit(solution)/shard_map/ppermute | solution.py:38
  23.5 2.8 %collective-permute-start.14 = (bf16[128,1024]{1,0:T(8,128)(2,1)S(1)}, bf16[128,1024]{1,0:T(8,128)(2,1)}, u32[]{:S(2)}, u32[]{:S(2)}) collective-permute-start(bf16[128,1024]{1,0:T(8,128)(2,1)S(1)} %collective-permute-done.10.refs_5_), channel_id=1, source_target_pairs={{0,1},{1,0},{2,3},{3,2},{4,5},{5,4},{6,7},{7,6},{8,9},{9,8},{10,11... | collective-permute-start | bytes 786440 | tf_op jit(solution)/shard_map/ppermute | solution.py:38
  23.6 0.7 copy-start.1
  24.3 10.8 %collective-permute-start.1 = (bf16[128,1024]{1,0:T(8,128)(2,1)}, bf16[128,1024]{1,0:T(8,128)(2,1)}, u32[]{:S(2)}, u32[]{:S(2)}) collective-permute-start(bf16[128,1024]{1,0:T(8,128)(2,1)} %copy-done.3), channel_id=1, source_target_pairs={{0,2},{1,3},{2,4},{3,5},{4,6},{5,7},{6,0},{7,1},{8,10},{9,11},{10,... | collective-permute-start | bytes 786440 | tf_op jit(solution)/shard_map/ppermute | solution.py:38
  26.4 1.0 %copy-start = (bf16[128,1024]{1,0:T(8,128)(2,1)S(1)}, bf16[128,1024]{1,0:T(8,128)(2,1)}, u32[]{:S(2)}) copy-start(bf16[128,1024]{1,0:T(8,128)(2,1)} %refs_2_.1) | copy-start | bytes 786436
  27.3 0.9 %copy-start.2 = (bf16[128,1024]{1,0:T(8,128)(2,1)S(1)}, bf16[128,1024]{1,0:T(8,128)(2,1)}, u32[]{:S(2)}) copy-start(bf16[128,1024]{1,0:T(8,128)(2,1)} %copy-done.1) | copy-start | bytes 786436
  36.4 14.6 %collective-permute-start.16 = (bf16[256,1024]{1,0:T(8,128)(2,1)S(1)}, bf16[256,1024]{1,0:T(8,128)(2,1)S(1)}, u32[]{:S(2)}, u32[]{:S(2)}) collective-permute-start(bf16[256,1024]{1,0:T(8,128)(2,1)S(1)} %collective-permute-done.5.refs_3_), channel_id=1, source_target_pairs={{0,16},{1,9},{2,18},{3,11},{4,20},{5,13},{6,22},{7,15},{8,24},{9,1... | collective-permute-start | bytes 1572872 | tf_op jit(solution)/shard_map/ppermute | solution.py:38
  37.0 9.5 %collective-permute-start.7 = (bf16[128,1024]{1,0:T(8,128)(2,1)}, bf16[128,1024]{1,0:T(8,128)(2,1)S(1)}, u32[]{:S(2)}, u32[]{:S(2)}) collective-permute-start(bf16[128,1024]{1,0:T(8,128)(2,1)} %collective-permute-done.1.refs_2_), channel_id=1, source_target_pairs={{0,8},{1,17},{2,10},{3,19},{4,12},{5,21},{6,14},{7,23},{8,0},{9,25... | collective-permute-start | bytes 786440 | tf_op jit(solution)/shard_map/ppermute | solution.py:38
  37.1 13.4 %collective-permute-start.8 = (bf16[128,1024]{1,0:T(8,128)(2,1)}, bf16[128,1024]{1,0:T(8,128)(2,1)S(1)}, u32[]{:S(2)}, u32[]{:S(2)}) collective-permute-start(bf16[128,1024]{1,0:T(8,128)(2,1)} %collective-permute-done.1.refs_2_), channel_id=1, source_target_pairs={{0,16},{1,9},{2,18},{3,11},{4,20},{5,13},{6,22},{7,15},{8,24},{9,1... | collective-permute-start | bytes 786440 | tf_op jit(solution)/shard_map/ppermute | solution.py:38
  50.5 1.9 %collective-permute-start.18 = (bf16[256,1024]{1,0:T(8,128)(2,1)S(1)}, bf16[256,1024]{1,0:T(8,128)(2,1)S(1)}, u32[]{:S(2)}, u32[]{:S(2)}) collective-permute-start(bf16[256,1024]{1,0:T(8,128)(2,1)S(1)} %collective-permute-done.6.refs_4_), channel_id=1, source_target_pairs={{0,1},{1,0},{2,3},{3,2},{4,5},{5,4},{6,7},{7,6},{8,9},{9,8},{10,11... | collective-permute-start | bytes 1572872 | tf_op jit(solution)/shard_map/ppermute | solution.py:38
  50.5 2.7 %collective-permute-start.17 = (bf16[256,1024]{1,0:T(8,128)(2,1)S(1)}, bf16[256,1024]{1,0:T(8,128)(2,1)S(1)}, u32[]{:S(2)}, u32[]{:S(2)}) collective-permute-start(bf16[256,1024]{1,0:T(8,128)(2,1)S(1)} %collective-permute-done.5.refs_3_), channel_id=1, source_target_pairs={{0,1},{1,0},{2,3},{3,2},{4,5},{5,4},{6,7},{7,6},{8,9},{9,8},{10,11... | collective-permute-start | bytes 1572872 | tf_op jit(solution)/shard_map/ppermute | solution.py:38
  51.0 2.9 %collective-permute-start.19 = (bf16[256,1024]{1,0:T(8,128)(2,1)S(1)}, bf16[256,1024]{1,0:T(8,128)(2,1)S(1)}, u32[]{:S(2)}, u32[]{:S(2)}) collective-permute-start(bf16[256,1024]{1,0:T(8,128)(2,1)S(1)} %collective-permute-done.16.refs_5_), channel_id=1, source_target_pairs={{0,1},{1,0},{2,3},{3,2},{4,5},{5,4},{6,7},{7,6},{8,9},{9,8},{10,11... | collective-permute-start | bytes 1572872 | tf_op jit(solution)/shard_map/ppermute | solution.py:38
  51.0 7.1 %collective-permute-start.9 = (bf16[128,1024]{1,0:T(8,128)(2,1)S(1)}, bf16[128,1024]{1,0:T(8,128)(2,1)S(1)}, u32[]{:S(2)}, u32[]{:S(2)}) collective-permute-start(bf16[128,1024]{1,0:T(8,128)(2,1)S(1)} %collective-permute-done.7.refs_3_), channel_id=1, source_target_pairs={{0,16},{1,9},{2,18},{3,11},{4,20},{5,13},{6,22},{7,15},{8,24},{9,1... | collective-permute-start | bytes 786440 | tf_op jit(solution)/shard_map/ppermute | solution.py:38
  58.1 5.3 %collective-permute-start.23 = (bf16[128,1024]{1,0:T(8,128)(2,1)S(1)}, bf16[128,1024]{1,0:T(8,128)(2,1)S(1)}, u32[]{:S(2)}, u32[]{:S(2)}) collective-permute-start(bf16[128,1024]{1,0:T(8,128)(2,1)S(1)} %collective-permute-done.9.refs_5_), channel_id=1, source_target_pairs={{0,1},{1,0},{2,3},{3,2},{4,5},{5,4},{6,7},{7,6},{8,9},{9,8},{10,11... | collective-permute-start | bytes 786440 | tf_op jit(solution)/shard_map/ppermute | solution.py:38
  58.3 5.1 %collective-permute-start.22 = (bf16[128,1024]{1,0:T(8,128)(2,1)S(1)}, bf16[128,1024]{1,0:T(8,128)(2,1)S(1)}, u32[]{:S(2)}, u32[]{:S(2)}) collective-permute-start(bf16[128,1024]{1,0:T(8,128)(2,1)S(1)} %collective-permute-done.8.refs_4_), channel_id=1, source_target_pairs={{0,1},{1,0},{2,3},{3,2},{4,5},{5,4},{6,7},{7,6},{8,9},{9,8},{10,11... | collective-permute-start | bytes 786440 | tf_op jit(solution)/shard_map/ppermute | solution.py:38
  58.6 4.7 %collective-permute-start.21 = (bf16[128,1024]{1,0:T(8,128)(2,1)S(1)}, bf16[128,1024]{1,0:T(8,128)(2,1)S(1)}, u32[]{:S(2)}, u32[]{:S(2)}) collective-permute-start(bf16[128,1024]{1,0:T(8,128)(2,1)S(1)} %collective-permute-done.7.refs_3_), channel_id=1, source_target_pairs={{0,1},{1,0},{2,3},{3,2},{4,5},{5,4},{6,7},{7,6},{8,9},{9,8},{10,11... | collective-permute-start | bytes 786440 | tf_op jit(solution)/shard_map/ppermute | solution.py:38
  58.8 4.6 %collective-permute-start.20 = (bf16[128,1024]{1,0:T(8,128)(2,1)}, bf16[128,1024]{1,0:T(8,128)(2,1)S(1)}, u32[]{:S(2)}, u32[]{:S(2)}) collective-permute-start(bf16[128,1024]{1,0:T(8,128)(2,1)} %collective-permute-done.1.refs_2_), channel_id=1, source_target_pairs={{0,1},{1,0},{2,3},{3,2},{4,5},{5,4},{6,7},{7,6},{8,9},{9,8},{10,11... | collective-permute-start | bytes 786440 | tf_op jit(solution)/shard_map/ppermute | solution.py:38
  63.3 16.2 %copy-start.4 = (f32[128]{0:T(128)S(1)}, f32[128]{0:T(128)}, u32[]{:S(2)}) copy-start(f32[128]{0:T(128)} %param.10) | copy-start | bytes 1540
  69.2 10.3 %all-to-all-start.1 = ((f32[32,3,128]{2,1,0:T(4,128)}), f32[32,3,128]{2,1,0:T(4,128)S(1)}, u32[]{:S(2)}, u32[]{:S(2)}) async-start(f32[32,3,128]{2,1,0:T(4,128)} %bitcast.13), calls=%async_computation.1 | async-start | bytes 131072 | tf_op jit(solution)/shard_map/all_to_all | solution.py:321

commit v13 on v12

--- a/solution.py
+++ b/solution.py
@@ -297,18 +297,20 @@
         else:
             held = [] if at else [packed]
         spread = spreads.get(at) or grid.fill(dict(reached[at]), *held)
+        early = [grid.sibling(after(a, acc)) for a in spread[1:-1]] if middle else []
         if at == 0:
             weights = [head]
         elif at == 1:
             for later in groups[1:]:
-                ready = after(head, acc, *(layers[dz] for dz in groups[2]))
+                ready = after(head, acc, *early, *(layers[dz] for dz in groups[2]))
                 weights.append(loaded(starts, [2 + n_dp + dz for dz in later], ready, deep))
         following = half if final else []
         if middle:
             reach_next(at + 1, *reached[at].values())
             following = [*reached[at + 1].values(), *weights[1:3]]
             spreads[at + 1] = grid.fill(dict(reached[at + 1]))
-        others = [own] + [grid.sibling(after(a, *following)) for a in spread[1:]]
+        others = [own, *early]
+        others += [grid.sibling(after(a, *following)) for a in spread[len(others) :]]
         blocks = spread + others
         for layer, offset in enumerate(offsets):
             done = layer == len(offsets) - 1

time: 80.5 us -> 80.5 us (level)
  starting transfers between devices: 25.9 us -> 27.7 us
  waiting for transfers between devices: 19.5 us -> 17.7 us
    ppermute x24, waiting for transfers between devices: 11.7 us -> 10.2 us  [permute(): return lax.ppermute(a, ('dp', 'tensor'), perm)]
    all_to_all x1, starting transfers between devices: 2.86 us -> 3.85 us  [body(): lax.all_to_all(acc.reshape(n_dp * n_t, 3, tok), ('dp', 'tensor'), 0, 0, t...]
  transfers between devices with their start and end apart: 26 -> 26, of which waited for: 10 -> 8; matrix products, arithmetic and copies ran while one was open for 0% -> 0% of each run, Pallas kernels for 30% -> 30%
where the time goes in v13:
time: 80.5 us; the launch traced here: 80.1 us
  Pallas kernels  29.8 us (37%)
  starting transfers between devices  27.7 us (34%)
  waiting for transfers between devices  17.7 us (22%)
  local copies, waits for them, and re-layouts  2.71 us (3%)
  between operations  1.46 us (2%)
    pallas_call x4, Pallas kernels, layer_product(): pl.pallas_call(functools.partial(layer_kernel, n, n_t, place, layer, offs...  20.8 us
    ppermute x24, starting transfers between devices, permute(): return lax.ppermute(a, ('dp', 'tensor'), perm)  18.8 us
    ppermute x24, waiting for transfers between devices, permute(): return lax.ppermute(a, ('dp', 'tensor'), perm)  10.2 us
    pallas_call x2, Pallas kernels, loaded(): pl.pallas_call(functools.partial(load_kernel, offsets), out_shape=pltpu.V...  7.23 us
    all_to_all x1, waiting for transfers between devices, body(): lax.all_to_all(acc.reshape(n_dp * n_t, 3, tok), ('dp', 'tensor'), 0, 0, t...  6.74 us
    all_to_all x1, starting transfers between devices, body(): fine = lax.all_to_all(packed, ('dp', 'tensor'), 0, 0, tiled=True)  5.04 us
    all_to_all x1, starting transfers between devices, body(): lax.all_to_all(acc.reshape(n_dp * n_t, 3, tok), ('dp', 'tensor'), 0, 0, t...  3.85 us
    unnamed x10, local copies, waits for them, and re-layouts  2.62 us
  transfers between devices with their start and end apart: 26, of which 8 were waited for; matrix products, arithmetic and copies ran while one was open for 0% of the time, Pallas kernels for 30%

profile of v13, /device:TPU:0, one launch (start us, length us, event | category | flops | bytes accessed | tf_op | source)
XLA Modules:
  0.0 80.1 jit_solution(17719170497285783834)
XLA Ops:
  0.6 3.0 %collective-permute-start.2 = (bf16[128,1024]{1,0:T(8,128)(2,1)}, bf16[128,1024]{1,0:T(8,128)(2,1)S(1)}, u32[]{:S(2)}, u32[]{:S(2)}) collective-permute-start(bf16[128,1024]{1,0:T(8,128)(2,1)} %refs_2_.1), channel_id=1, source_target_pairs={{0,8},{1,17},{2,10},{3,19},{4,12},{5,21},{6,14},{7,23},{8,0},{9,25... | collective-permute-start | bytes 786440 | tf_op jit(solution)/shard_map/ppermute | solution.py:38
  3.6 1.5 %collective-permute-start.3 = (bf16[128,1024]{1,0:T(8,128)(2,1)}, bf16[128,1024]{1,0:T(8,128)(2,1)S(1)}, u32[]{:S(2)}, u32[]{:S(2)}) collective-permute-start(bf16[128,1024]{1,0:T(8,128)(2,1)} %refs_2_.1), channel_id=1, source_target_pairs={{0,16},{1,9},{2,18},{3,11},{4,20},{5,13},{6,22},{7,15},{8,24},{9,1... | collective-permute-start | bytes 786440 | tf_op jit(solution)/shard_map/ppermute | solution.py:38
  5.2 0.0 collective-permute-start.11
  5.2 1.6 %collective-permute-start = (bf16[128,1024]{1,0:T(8,128)(2,1)}, bf16[128,1024]{1,0:T(8,128)(2,1)S(1)}, u32[]{:S(2)}, u32[]{:S(2)}) collective-permute-start(bf16[128,1024]{1,0:T(8,128)(2,1)} %refs_2_.1), channel_id=1, source_target_pairs={{0,2},{1,3},{2,4},{3,5},{4,6},{5,7},{6,0},{7,1},{8,10},{9,11},{10,... | collective-permute-start | bytes 786440 | tf_op jit(solution)/shard_map/ppermute | solution.py:38
  6.7 2.2 %collective-permute-start.4 = (bf16[128,1024]{1,0:T(8,128)(2,1)}, bf16[128,1024]{1,0:T(8,128)(2,1)S(1)}, u32[]{:S(2)}, u32[]{:S(2)}) collective-permute-start(bf16[128,1024]{1,0:T(8,128)(2,1)} %refs_2_.1), channel_id=1, source_target_pairs={{0,6},{1,7},{2,0},{3,1},{4,2},{5,3},{6,4},{7,5},{8,14},{9,15},{10,... | collective-permute-start | bytes 786440 | tf_op jit(solution)/shard_map/ppermute | solution.py:38
  9.0 0.1 stack.43.refs_0_.start_ref
  9.1 1.8 %shard_map.77 = f32[32,1,1280]{2,1,0:T(1,128)} custom-call(bf16[128,1024]{1,0:T(8,128)(2,1)} %refs_2_.1, f32[1,1024]{1,0:T(1,128)} %bitcast.22, s32[1,128]{1,0:T(1,128)} %bitcast.23), custom_call_target="tpu_custom_call" | custom-call | tf_op jit(solution)/shard_map/pallas_call | solution.py:243
  10.9 0.0 collective-permute-done.2.refs_3_
  10.9 0.0 collective-permute-done.3.refs_4_
  10.9 1.1 %collective-permute-start.10 = (bf16[128,1024]{1,0:T(8,128)(2,1)S(1)}, bf16[128,1024]{1,0:T(8,128)(2,1)S(1)}, u32[]{:S(2)}, u32[]{:S(2)}) collective-permute-start(bf16[128,1024]{1,0:T(8,128)(2,1)S(1)} %collective-permute-done.2.refs_3_), channel_id=1, source_target_pairs={{0,16},{1,9},{2,18},{3,11},{4,20},{5,13},{6,22},{7,15},{8,24},{9,1... | collective-permute-start | bytes 786440 | tf_op jit(solution)/shard_map/ppermute | solution.py:38
  12.0 0.9 %collective-permute-start.12 = (bf16[128,1024]{1,0:T(8,128)(2,1)S(1)}, bf16[128,1024]{1,0:T(8,128)(2,1)}, u32[]{:S(2)}, u32[]{:S(2)}) collective-permute-start(bf16[128,1024]{1,0:T(8,128)(2,1)S(1)} %collective-permute-done.2.refs_3_), channel_id=1, source_target_pairs={{0,1},{1,0},{2,3},{3,2},{4,5},{5,4},{6,7},{7,6},{8,9},{9,8},{10,11... | collective-permute-start | bytes 786440 | tf_op jit(solution)/shard_map/ppermute | solution.py:38
  12.9 5.0 %all-to-all-start = ((f32[32,1,1280]{2,1,0:T(1,128)}), f32[32,1,1280]{2,1,0:T(1,128)S(1)}, u32[]{:S(2)}, u32[]{:S(2)}) async-start(f32[32,1,1280]{2,1,0:T(1,128)} %shard_map.77), calls=%async_computation | async-start | bytes 327680 | tf_op jit(solution)/shard_map/all_to_all | solution.py:287
  17.9 0.0 collective-permute-done.refs_0_
  17.9 3.2 %collective-permute-done.4.refs_1_ = bf16[128,1024]{1,0:T(8,128)(2,1)S(1)} collective-permute-done((bf16[128,1024]{1,0:T(8,128)(2,1)}, bf16[128,1024]{1,0:T(8,128)(2,1)S(1)}, u32[]{:S(2)}, u32[]{:S(2)}) %collective-permute-start.4) | collective-permute-done | bytes 262176 | tf_op jit(solution)/shard_map/ppermute | solution.py:38
  21.2 0.4 collective-permute-start.6
  21.6 0.5 collective-permute-start.5
  22.2 0.5 collective-permute-start.15
  22.7 0.1 collective-permute-start.14
  22.7 0.9 %collective-permute-done.13.refs_8_ = bf16[128,1024]{1,0:T(8,128)(2,1)S(1)} collective-permute-done((bf16[128,1024]{1,0:T(8,128)(2,1)S(1)}, bf16[128,1024]{1,0:T(8,128)(2,1)S(1)}, u32[]{:S(2)}, u32[]{:S(2)}) %collective-permute-start.13) | collective-permute-done | bytes 262176 | tf_op jit(solution)/shard_map/ppermute | solution.py:38
  23.7 0.7 copy-done.1
  24.4 1.2 %collective-permute-start.1 = (bf16[128,1024]{1,0:T(8,128)(2,1)}, bf16[128,1024]{1,0:T(8,128)(2,1)}, u32[]{:S(2)}, u32[]{:S(2)}) collective-permute-start(bf16[128,1024]{1,0:T(8,128)(2,1)} %copy-done.3), channel_id=1, source_target_pairs={{0,2},{1,3},{2,4},{3,5},{4,6},{5,7},{6,0},{7,1},{8,10},{9,11},{10,... | collective-permute-start | bytes 786440 | tf_op jit(solution)/shard_map/ppermute | solution.py:38
  25.6 0.8 %all-to-all-done.refs_1_ = f32[32,1,1280]{2,1,0:T(1,128)S(1)} async-done(((f32[32,1,1280]{2,1,0:T(1,128)}), f32[32,1,1280]{2,1,0:T(1,128)S(1)}, u32[]{:S(2)}, u32[]{:S(2)}) %all-to-all-start) | async-done | bytes 163872 | tf_op jit(solution)/shard_map/all_to_all | solution.py:287
  26.4 0.9 %copy-done = bf16[128,1024]{1,0:T(8,128)(2,1)S(1)} copy-done((bf16[128,1024]{1,0:T(8,128)(2,1)S(1)}, bf16[128,1024]{1,0:T(8,128)(2,1)}, u32[]{:S(2)}) %copy-start) | copy-done | bytes 262168
  27.3 0.9 %copy-done.2 = bf16[128,1024]{1,0:T(8,128)(2,1)S(1)} copy-done((bf16[128,1024]{1,0:T(8,128)(2,1)S(1)}, bf16[128,1024]{1,0:T(8,128)(2,1)}, u32[]{:S(2)}) %copy-start.2) | copy-done | bytes 262168
  28.3 6.7 %shard_map.79.refs_11_ = f32[512,1152]{1,0:T(8,128)S(1)} custom-call(s32[10]{0:T(128)S(1)} %stack.43.refs_0_.start_ref, f32[32,1,1280]{2,1,0:T(1,128)S(1)} %all-to-all-done.refs_1_, bf16[128,1024]{1,0:T(8,128)(2,1)S(1)} %copy-done, bf16[128,1024]{1,0:T(8,128)(2,1)S(1)} %collective-permute-done.2.refs_3_, ...), custom_call_target="tpu_custom_call" | custom-call | flops 2415919104 | bytes 4718592 | tf_op jit(solution)/shard_map/pallas_call | solution.py:211
  35.0 0.5 collective-permute-done.6.refs_4_
  35.5 0.2 collective-permute-start.18
  35.7 0.3 collective-permute-start.17
  36.0 0.9 %collective-permute-start.16 = (bf16[256,1024]{1,0:T(8,128)(2,1)S(1)}, bf16[256,1024]{1,0:T(8,128)(2,1)S(1)}, u32[]{:S(2)}, u32[]{:S(2)}) collective-permute-start(bf16[256,1024]{1,0:T(8,128)(2,1)S(1)} %collective-permute-done.5.refs_3_), channel_id=1, source_target_pairs={{0,16},{1,9},{2,18},{3,11},{4,20},{5,13},{6,22},{7,15},{8,24},{9,1... | collective-permute-start | bytes 1572872 | tf_op jit(solution)/shard_map/ppermute | solution.py:38
  36.8 1.2 %collective-permute-start.7 = (bf16[128,1024]{1,0:T(8,128)(2,1)}, bf16[128,1024]{1,0:T(8,128)(2,1)S(1)}, u32[]{:S(2)}, u32[]{:S(2)}) collective-permute-start(bf16[128,1024]{1,0:T(8,128)(2,1)} %collective-permute-done.1.refs_2_), channel_id=1, source_target_pairs={{0,8},{1,17},{2,10},{3,19},{4,12},{5,21},{6,14},{7,23},{8,0},{9,25... | collective-permute-start | bytes 786440 | tf_op jit(solution)/shard_map/ppermute | solution.py:38
  38.0 1.3 %collective-permute-start.8 = (bf16[128,1024]{1,0:T(8,128)(2,1)}, bf16[128,1024]{1,0:T(8,128)(2,1)S(1)}, u32[]{:S(2)}, u32[]{:S(2)}) collective-permute-start(bf16[128,1024]{1,0:T(8,128)(2,1)} %collective-permute-done.1.refs_2_), channel_id=1, source_target_pairs={{0,16},{1,9},{2,18},{3,11},{4,20},{5,13},{6,22},{7,15},{8,24},{9,1... | collective-permute-start | bytes 786440 | tf_op jit(solution)/shard_map/ppermute | solution.py:38
  39.4 4.3 %shard_map.80.refs_10_ = bf16[2,2048,1152]{2,1,0:T(8,128)(2,1)S(1)} custom-call(s32[10]{0:T(128)S(1)} %stack.43.refs_0_.start_ref, bf16[8192,1152]{1,0:T(8,128)(2,1)} %head_ref.1), custom_call_target="tpu_custom_call" | custom-call | tf_op jit(solution)/shard_map/pallas_call | solution.py:116
  43.7 2.9 %shard_map.81.refs_10_ = bf16[1,2048,1152]{2,1,0:T(8,128)(2,1)S(1)} custom-call(s32[10]{0:T(128)S(1)} %stack.43.refs_0_.start_ref, bf16[8192,1152]{1,0:T(8,128)(2,1)} %head_ref.1), custom_call_target="tpu_custom_call" | custom-call | tf_op jit(solution)/shard_map/pallas_call | solution.py:116
  46.7 4.1 %collective-permute-done.8.refs_4_ = bf16[128,1024]{1,0:T(8,128)(2,1)S(1)} collective-permute-done((bf16[128,1024]{1,0:T(8,128)(2,1)}, bf16[128,1024]{1,0:T(8,128)(2,1)S(1)}, u32[]{:S(2)}, u32[]{:S(2)}) %collective-permute-start.8) | collective-permute-done | bytes 262176 | tf_op jit(solution)/shard_map/ppermute | solution.py:38
  50.8 0.9 %collective-permute-start.9 = (bf16[128,1024]{1,0:T(8,128)(2,1)S(1)}, bf16[128,1024]{1,0:T(8,128)(2,1)S(1)}, u32[]{:S(2)}, u32[]{:S(2)}) collective-permute-start(bf16[128,1024]{1,0:T(8,128)(2,1)S(1)} %collective-permute-done.7.refs_3_), channel_id=1, source_target_pairs={{0,16},{1,9},{2,18},{3,11},{4,20},{5,13},{6,22},{7,15},{8,24},{9,1... | collective-permute-start | bytes 786440 | tf_op jit(solution)/shard_map/ppermute | solution.py:38
  51.7 1.0 %collective-permute-done.19.refs_9_ = bf16[256,1024]{1,0:T(8,128)(2,1)S(1)} collective-permute-done((bf16[256,1024]{1,0:T(8,128)(2,1)S(1)}, bf16[256,1024]{1,0:T(8,128)(2,1)S(1)}, u32[]{:S(2)}, u32[]{:S(2)}) %collective-permute-start.19) | collective-permute-done | bytes 524320 | tf_op jit(solution)/shard_map/ppermute | solution.py:38
  52.7 4.2 %shard_map.82.refs_11_ = f32[512,1152]{1,0:T(8,128)S(1)} custom-call(s32[10]{0:T(128)S(1)} %stack.43.refs_0_.start_ref, f32[32,1,1280]{2,1,0:T(1,128)S(1)} %all-to-all-done.refs_1_, bf16[256,1024]{1,0:T(8,128)(2,1)S(1)} %shard_map.78.refs_2_, bf16[256,1024]{1,0:T(8,128)(2,1)S(1)} %collective-permute-done.5.refs_3_, ...), custom_call_target="tpu_custom_call" | custom-call | flops 2415919104 | bytes 4718592 | tf_op jit(solution)/shard_map/pallas_call | solution.py:211
  56.9 0.3 collective-permute-done.9.refs_5_
  57.2 0.5 collective-permute-start.22
  57.7 0.0 collective-permute-start.21
  57.7 0.5 collective-permute-start.20
  58.2 4.2 %shard_map.83.refs_11_ = f32[512,1152]{1,0:T(8,128)S(1)} custom-call(s32[10]{0:T(128)S(1)} %stack.43.refs_0_.start_ref, f32[32,1,1280]{2,1,0:T(1,128)S(1)} %all-to-all-done.refs_1_, bf16[256,1024]{1,0:T(8,128)(2,1)S(1)} %shard_map.78.refs_2_, bf16[256,1024]{1,0:T(8,128)(2,1)S(1)} %collective-permute-done.5.refs_3_, ...), custom_call_target="tpu_custom_call" | custom-call | flops 2415919104 | bytes 4718592 | tf_op jit(solution)/shard_map/pallas_call | solution.py:211
  62.3 0.0 copy-start.4
  62.4 5.8 %shard_map.84 = f32[4,8,3,128]{3,2,1,0:T(4,128)} custom-call(s32[10]{0:T(128)S(1)} %stack.43.refs_0_.start_ref, f32[32,1,1280]{2,1,0:T(1,128)S(1)} %all-to-all-done.refs_1_, bf16[128,1024]{1,0:T(8,128)(2,1)} %collective-permute-done.1.refs_2_, bf16[128,1024]{1,0:T(8,128)(2,1)S(1)} %collective-permute-done.7.refs_3_, ...), custom_call_target="tpu_custom_call" | custom-call | flops 2415919104 | bytes 4718592 | tf_op jit(solution)/shard_map/pallas_call | solution.py:211
  68.2 3.8 %all-to-all-start.1 = ((f32[32,3,128]{2,1,0:T(4,128)}), f32[32,3,128]{2,1,0:T(4,128)S(1)}, u32[]{:S(2)}, u32[]{:S(2)}) async-start(f32[32,3,128]{2,1,0:T(4,128)} %bitcast.13), calls=%async_computation.1 | async-start | bytes 131072 | tf_op jit(solution)/shard_map/all_to_all | solution.py:323
  72.7 6.7 %all-to-all-done.1 = f32[32,3,128]{2,1,0:T(4,128)S(1)} async-done(((f32[32,3,128]{2,1,0:T(4,128)}), f32[32,3,128]{2,1,0:T(4,128)S(1)}, u32[]{:S(2)}, u32[]{:S(2)}) %all-to-all-start.1) | async-done | bytes 49184 | tf_op jit(solution)/shard_map/all_to_all | solution.py:323
  79.4 0.1 slice_reduce_fusion
  79.5 0.5 compare_select_fusion
  (27 shorter events, 0.1 us)
Async XLA Ops:
  0.6 10.2 %collective-permute-start.2 = (bf16[128,1024]{1,0:T(8,128)(2,1)}, bf16[128,1024]{1,0:T(8,128)(2,1)S(1)}, u32[]{:S(2)}, u32[]{:S(2)}) collective-permute-start(bf16[128,1024]{1,0:T(8,128)(2,1)} %refs_2_.1), channel_id=1, source_target_pairs={{0,8},{1,17},{2,10},{3,19},{4,12},{5,21},{6,14},{7,23},{8,0},{9,25... | collective-permute-start | bytes 786440 | tf_op jit(solution)/shard_map/ppermute | solution.py:38
  3.6 7.2 %collective-permute-start.3 = (bf16[128,1024]{1,0:T(8,128)(2,1)}, bf16[128,1024]{1,0:T(8,128)(2,1)S(1)}, u32[]{:S(2)}, u32[]{:S(2)}) collective-permute-start(bf16[128,1024]{1,0:T(8,128)(2,1)} %refs_2_.1), channel_id=1, source_target_pairs={{0,16},{1,9},{2,18},{3,11},{4,20},{5,13},{6,22},{7,15},{8,24},{9,1... | collective-permute-start | bytes 786440 | tf_op jit(solution)/shard_map/ppermute | solution.py:38
  5.2 17.0 %collective-permute-start.11 = (bf16[128,1024]{1,0:T(8,128)(2,1)}, bf16[128,1024]{1,0:T(8,128)(2,1)S(1)}, u32[]{:S(2)}, u32[]{:S(2)}) collective-permute-start(bf16[128,1024]{1,0:T(8,128)(2,1)} %refs_2_.1), channel_id=1, source_target_pairs={{0,1},{1,0},{2,3},{3,2},{4,5},{5,4},{6,7},{7,6},{8,9},{9,8},{10,11... | collective-permute-start | bytes 786440 | tf_op jit(solution)/shard_map/ppermute | solution.py:38
  5.2 12.8 %collective-permute-start = (bf16[128,1024]{1,0:T(8,128)(2,1)}, bf16[128,1024]{1,0:T(8,128)(2,1)S(1)}, u32[]{:S(2)}, u32[]{:S(2)}) collective-permute-start(bf16[128,1024]{1,0:T(8,128)(2,1)} %refs_2_.1), channel_id=1, source_target_pairs={{0,2},{1,3},{2,4},{3,5},{4,6},{5,7},{6,0},{7,1},{8,10},{9,11},{10,... | collective-permute-start | bytes 786440 | tf_op jit(solution)/shard_map/ppermute | solution.py:38
  6.7 14.4 %collective-permute-start.4 = (bf16[128,1024]{1,0:T(8,128)(2,1)}, bf16[128,1024]{1,0:T(8,128)(2,1)S(1)}, u32[]{:S(2)}, u32[]{:S(2)}) collective-permute-start(bf16[128,1024]{1,0:T(8,128)(2,1)} %refs_2_.1), channel_id=1, source_target_pairs={{0,6},{1,7},{2,0},{3,1},{4,2},{5,3},{6,4},{7,5},{8,14},{9,15},{10,... | collective-permute-start | bytes 786440 | tf_op jit(solution)/shard_map/ppermute | solution.py:38
  10.9 11.3 %collective-permute-start.10 = (bf16[128,1024]{1,0:T(8,128)(2,1)S(1)}, bf16[128,1024]{1,0:T(8,128)(2,1)S(1)}, u32[]{:S(2)}, u32[]{:S(2)}) collective-permute-start(bf16[128,1024]{1,0:T(8,128)(2,1)S(1)} %collective-permute-done.2.refs_3_), channel_id=1, source_target_pairs={{0,16},{1,9},{2,18},{3,11},{4,20},{5,13},{6,22},{7,15},{8,24},{9,1... | collective-permute-start | bytes 786440 | tf_op jit(solution)/shard_map/ppermute | solution.py:38
  12.0 10.7 %collective-permute-start.12 = (bf16[128,1024]{1,0:T(8,128)(2,1)S(1)}, bf16[128,1024]{1,0:T(8,128)(2,1)}, u32[]{:S(2)}, u32[]{:S(2)}) collective-permute-start(bf16[128,1024]{1,0:T(8,128)(2,1)S(1)} %collective-permute-done.2.refs_3_), channel_id=1, source_target_pairs={{0,1},{1,0},{2,3},{3,2},{4,5},{5,4},{6,7},{7,6},{8,9},{9,8},{10,11... | collective-permute-start | bytes 786440 | tf_op jit(solution)/shard_map/ppermute | solution.py:38
  12.9 13.5 %all-to-all-start = ((f32[32,1,1280]{2,1,0:T(1,128)}), f32[32,1,1280]{2,1,0:T(1,128)S(1)}, u32[]{:S(2)}, u32[]{:S(2)}) async-start(f32[32,1,1280]{2,1,0:T(1,128)} %shard_map.77), calls=%async_computation | async-start | bytes 327680 | tf_op jit(solution)/shard_map/all_to_all | solution.py:287
  17.9 3.3 %copy-start.3 = (bf16[128,1024]{1,0:T(8,128)(2,1)}, bf16[128,1024]{1,0:T(8,128)(2,1)S(1)}, u32[]{:S(2)}) copy-start(bf16[128,1024]{1,0:T(8,128)(2,1)S(1)} %collective-permute-done.refs_0_) | copy-start | bytes 786436
  21.2 14.2 %collective-permute-start.6 = (bf16[256,1024]{1,0:T(8,128)(2,1)S(1)}, bf16[256,1024]{1,0:T(8,128)(2,1)S(1)}, u32[]{:S(2)}, u32[]{:S(2)}) collective-permute-start(bf16[256,1024]{1,0:T(8,128)(2,1)S(1)} %shard_map.78.refs_2_), channel_id=1, source_target_pairs={{0,16},{1,9},{2,18},{3,11},{4,20},{5,13},{6,22},{7,15},{8,24},{9,1... | collective-permute-start | bytes 1572872 | tf_op jit(solution)/shard_map/ppermute | solution.py:38
  21.6 14.1 %collective-permute-start.5 = (bf16[256,1024]{1,0:T(8,128)(2,1)S(1)}, bf16[256,1024]{1,0:T(8,128)(2,1)S(1)}, u32[]{:S(2)}, u32[]{:S(2)}) collective-permute-start(bf16[256,1024]{1,0:T(8,128)(2,1)S(1)} %shard_map.78.refs_2_), channel_id=1, source_target_pairs={{0,8},{1,17},{2,10},{3,19},{4,12},{5,21},{6,14},{7,23},{8,0},{9,25... | collective-permute-start | bytes 1572872 | tf_op jit(solution)/shard_map/ppermute | solution.py:38
  22.2 1.5 %collective-permute-start.13 = (bf16[128,1024]{1,0:T(8,128)(2,1)S(1)}, bf16[128,1024]{1,0:T(8,128)(2,1)S(1)}, u32[]{:S(2)}, u32[]{:S(2)}) collective-permute-start(bf16[128,1024]{1,0:T(8,128)(2,1)S(1)} %collective-permute-done.3.refs_4_), channel_id=1, source_target_pairs={{0,1},{1,0},{2,3},{3,2},{4,5},{5,4},{6,7},{7,6},{8,9},{9,8},{10,11... | collective-permute-start | bytes 786440 | tf_op jit(solution)/shard_map/ppermute | solution.py:38
  22.2 13.8 %collective-permute-start.15 = (bf16[256,1024]{1,0:T(8,128)(2,1)S(1)}, bf16[256,1024]{1,0:T(8,128)(2,1)S(1)}, u32[]{:S(2)}, u32[]{:S(2)}) collective-permute-start(bf16[256,1024]{1,0:T(8,128)(2,1)S(1)} %shard_map.78.refs_2_), channel_id=1, source_target_pairs={{0,1},{1,0},{2,3},{3,2},{4,5},{5,4},{6,7},{7,6},{8,9},{9,8},{10,11... | collective-permute-start | bytes 1572872 | tf_op jit(solution)/shard_map/ppermute | solution.py:38
  22.7 3.7 %collective-permute-start.14 = (bf16[128,1024]{1,0:T(8,128)(2,1)S(1)}, bf16[128,1024]{1,0:T(8,128)(2,1)}, u32[]{:S(2)}, u32[]{:S(2)}) collective-permute-start(bf16[128,1024]{1,0:T(8,128)(2,1)S(1)} %collective-permute-done.10.refs_5_), channel_id=1, source_target_pairs={{0,1},{1,0},{2,3},{3,2},{4,5},{5,4},{6,7},{7,6},{8,9},{9,8},{10,11... | collective-permute-start | bytes 786440 | tf_op jit(solution)/shard_map/ppermute | solution.py:38
  23.7 0.7 copy-start.1
  24.4 11.6 %collective-permute-start.1 = (bf16[128,1024]{1,0:T(8,128)(2,1)}, bf16[128,1024]{1,0:T(8,128)(2,1)}, u32[]{:S(2)}, u32[]{:S(2)}) collective-permute-start(bf16[128,1024]{1,0:T(8,128)(2,1)} %copy-done.3), channel_id=1, source_target_pairs={{0,2},{1,3},{2,4},{3,5},{4,6},{5,7},{6,0},{7,1},{8,10},{9,11},{10,... | collective-permute-start | bytes 786440 | tf_op jit(solution)/shard_map/ppermute | solution.py:38
  26.4 1.0 %copy-start = (bf16[128,1024]{1,0:T(8,128)(2,1)S(1)}, bf16[128,1024]{1,0:T(8,128)(2,1)}, u32[]{:S(2)}) copy-start(bf16[128,1024]{1,0:T(8,128)(2,1)} %refs_2_.1) | copy-start | bytes 786436
  27.3 0.9 %copy-start.2 = (bf16[128,1024]{1,0:T(8,128)(2,1)S(1)}, bf16[128,1024]{1,0:T(8,128)(2,1)}, u32[]{:S(2)}) copy-start(bf16[128,1024]{1,0:T(8,128)(2,1)} %copy-done.1) | copy-start | bytes 786436
  35.5 3.9 %collective-permute-start.18 = (bf16[256,1024]{1,0:T(8,128)(2,1)S(1)}, bf16[256,1024]{1,0:T(8,128)(2,1)S(1)}, u32[]{:S(2)}, u32[]{:S(2)}) collective-permute-start(bf16[256,1024]{1,0:T(8,128)(2,1)S(1)} %collective-permute-done.6.refs_4_), channel_id=1, source_target_pairs={{0,1},{1,0},{2,3},{3,2},{4,5},{5,4},{6,7},{7,6},{8,9},{9,8},{10,11... | collective-permute-start | bytes 1572872 | tf_op jit(solution)/shard_map/ppermute | solution.py:38
  35.7 3.7 %collective-permute-start.17 = (bf16[256,1024]{1,0:T(8,128)(2,1)S(1)}, bf16[256,1024]{1,0:T(8,128)(2,1)S(1)}, u32[]{:S(2)}, u32[]{:S(2)}) collective-permute-start(bf16[256,1024]{1,0:T(8,128)(2,1)S(1)} %collective-permute-done.5.refs_3_), channel_id=1, source_target_pairs={{0,1},{1,0},{2,3},{3,2},{4,5},{5,4},{6,7},{7,6},{8,9},{9,8},{10,11... | collective-permute-start | bytes 1572872 | tf_op jit(solution)/shard_map/ppermute | solution.py:38
  36.0 14.8 %collective-permute-start.16 = (bf16[256,1024]{1,0:T(8,128)(2,1)S(1)}, bf16[256,1024]{1,0:T(8,128)(2,1)S(1)}, u32[]{:S(2)}, u32[]{:S(2)}) collective-permute-start(bf16[256,1024]{1,0:T(8,128)(2,1)S(1)} %collective-permute-done.5.refs_3_), channel_id=1, source_target_pairs={{0,16},{1,9},{2,18},{3,11},{4,20},{5,13},{6,22},{7,15},{8,24},{9,1... | collective-permute-start | bytes 1572872 | tf_op jit(solution)/shard_map/ppermute | solution.py:38
  36.8 9.8 %collective-permute-start.7 = (bf16[128,1024]{1,0:T(8,128)(2,1)}, bf16[128,1024]{1,0:T(8,128)(2,1)S(1)}, u32[]{:S(2)}, u32[]{:S(2)}) collective-permute-start(bf16[128,1024]{1,0:T(8,128)(2,1)} %collective-permute-done.1.refs_2_), channel_id=1, source_target_pairs={{0,8},{1,17},{2,10},{3,19},{4,12},{5,21},{6,14},{7,23},{8,0},{9,25... | collective-permute-start | bytes 786440 | tf_op jit(solution)/shard_map/ppermute | solution.py:38
  38.0 12.7 %collective-permute-start.8 = (bf16[128,1024]{1,0:T(8,128)(2,1)}, bf16[128,1024]{1,0:T(8,128)(2,1)S(1)}, u32[]{:S(2)}, u32[]{:S(2)}) collective-permute-start(bf16[128,1024]{1,0:T(8,128)(2,1)} %collective-permute-done.1.refs_2_), channel_id=1, source_target_pairs={{0,16},{1,9},{2,18},{3,11},{4,20},{5,13},{6,22},{7,15},{8,24},{9,1... | collective-permute-start | bytes 786440 | tf_op jit(solution)/shard_map/ppermute | solution.py:38
  50.8 1.9 %collective-permute-start.19 = (bf16[256,1024]{1,0:T(8,128)(2,1)S(1)}, bf16[256,1024]{1,0:T(8,128)(2,1)S(1)}, u32[]{:S(2)}, u32[]{:S(2)}) collective-permute-start(bf16[256,1024]{1,0:T(8,128)(2,1)S(1)} %collective-permute-done.16.refs_5_), channel_id=1, source_target_pairs={{0,1},{1,0},{2,3},{3,2},{4,5},{5,4},{6,7},{7,6},{8,9},{9,8},{10,11... | collective-permute-start | bytes 1572872 | tf_op jit(solution)/shard_map/ppermute | solution.py:38
  50.8 6.4 %collective-permute-start.9 = (bf16[128,1024]{1,0:T(8,128)(2,1)S(1)}, bf16[128,1024]{1,0:T(8,128)(2,1)S(1)}, u32[]{:S(2)}, u32[]{:S(2)}) collective-permute-start(bf16[128,1024]{1,0:T(8,128)(2,1)S(1)} %collective-permute-done.7.refs_3_), channel_id=1, source_target_pairs={{0,16},{1,9},{2,18},{3,11},{4,20},{5,13},{6,22},{7,15},{8,24},{9,1... | collective-permute-start | bytes 786440 | tf_op jit(solution)/shard_map/ppermute | solution.py:38
  57.2 5.2 %collective-permute-start.23 = (bf16[128,1024]{1,0:T(8,128)(2,1)S(1)}, bf16[128,1024]{1,0:T(8,128)(2,1)S(1)}, u32[]{:S(2)}, u32[]{:S(2)}) collective-permute-start(bf16[128,1024]{1,0:T(8,128)(2,1)S(1)} %collective-permute-done.9.refs_5_), channel_id=1, source_target_pairs={{0,1},{1,0},{2,3},{3,2},{4,5},{5,4},{6,7},{7,6},{8,9},{9,8},{10,11... | collective-permute-start | bytes 786440 | tf_op jit(solution)/shard_map/ppermute | solution.py:38
  57.2 5.2 %collective-permute-start.22 = (bf16[128,1024]{1,0:T(8,128)(2,1)S(1)}, bf16[128,1024]{1,0:T(8,128)(2,1)S(1)}, u32[]{:S(2)}, u32[]{:S(2)}) collective-permute-start(bf16[128,1024]{1,0:T(8,128)(2,1)S(1)} %collective-permute-done.8.refs_4_), channel_id=1, source_target_pairs={{0,1},{1,0},{2,3},{3,2},{4,5},{5,4},{6,7},{7,6},{8,9},{9,8},{10,11... | collective-permute-start | bytes 786440 | tf_op jit(solution)/shard_map/ppermute | solution.py:38
  57.7 4.7 %collective-permute-start.21 = (bf16[128,1024]{1,0:T(8,128)(2,1)S(1)}, bf16[128,1024]{1,0:T(8,128)(2,1)S(1)}, u32[]{:S(2)}, u32[]{:S(2)}) collective-permute-start(bf16[128,1024]{1,0:T(8,128)(2,1)S(1)} %collective-permute-done.7.refs_3_), channel_id=1, source_target_pairs={{0,1},{1,0},{2,3},{3,2},{4,5},{5,4},{6,7},{7,6},{8,9},{9,8},{10,11... | collective-permute-start | bytes 786440 | tf_op jit(solution)/shard_map/ppermute | solution.py:38
  57.7 4.7 %collective-permute-start.20 = (bf16[128,1024]{1,0:T(8,128)(2,1)}, bf16[128,1024]{1,0:T(8,128)(2,1)S(1)}, u32[]{:S(2)}, u32[]{:S(2)}) collective-permute-start(bf16[128,1024]{1,0:T(8,128)(2,1)} %collective-permute-done.1.refs_2_), channel_id=1, source_target_pairs={{0,1},{1,0},{2,3},{3,2},{4,5},{5,4},{6,7},{7,6},{8,9},{9,8},{10,11... | collective-permute-start | bytes 786440 | tf_op jit(solution)/shard_map/ppermute | solution.py:38
  62.3 17.2 %copy-start.4 = (f32[128]{0:T(128)S(1)}, f32[128]{0:T(128)}, u32[]{:S(2)}) copy-start(f32[128]{0:T(128)} %param.10) | copy-start | bytes 1540
  68.2 11.2 %all-to-all-start.1 = ((f32[32,3,128]{2,1,0:T(4,128)}), f32[32,3,128]{2,1,0:T(4,128)S(1)}, u32[]{:S(2)}, u32[]{:S(2)}) async-start(f32[32,3,128]{2,1,0:T(4,128)} %bitcast.13), calls=%async_computation.1 | async-start | bytes 131072 | tf_op jit(solution)/shard_map/all_to_all | solution.py:323
